TPU v7x, 128 devices: a whole 4x4x4 slice. The times are simulated.
128 devices in a mesh: grp: 32 (over z, x, core), nar: 4 (over y).
Axes of the slice: x: 4, y: 4, z: 4, core: 2. Of those that a mesh axis runs over, the one named last changes fastest.
Arguments:
- features: bfloat16 [1048576, 128], P(('grp', 'nar')), may hold values from -6 to 6
- requests: int32 [16384, 64], P(('grp', 'nar')), may hold values from 0 to 8191
- index_one: int32 [262144, 16], P(('grp', 'nar')), may hold values from 0 to 8191
- mask_one: int32 [262144, 15], P(('grp', 'nar')), may hold values from 0 to 1, as said below
- index_two: int32 [65536, 11], P(('grp', 'nar')), may hold values from 0 to 8191
- mask_two: int32 [65536, 10], P(('grp', 'nar')), may hold values from 0 to 1, as said below
- labels: int32 [65536], P(('grp', 'nar')), may hold values from 0 to 171
- seed_live: int32 [65536], P(('grp', 'nar')), may hold values from 0 to 1
- w_first: float32 [256, 256], P('nar'), may hold values from -0.5 to 0.5
- w_second: float32 [512, 172], P('nar'), may hold values from -0.375 to 0.375
- mom_first: float32 [256, 256], P('nar')
- mom_second: float32 [512, 172], P('nar')
- biases: float32 [428], replicated, may hold values from -4 to 4
- bias_m: float32 [428], replicated, may hold values from -0.0004272461 to 0.0004272461
- bias_v: float32 [428], replicated, may hold values from 8.871389e-11 to 3.5485556e-10
Outputs:
- loss: float32 [], replicated
- first_new: float32 [256, 256], P('nar')
- second_new: float32 [512, 172], P('nar')
- mom_first_new: float32 [256, 256], P('nar')
- mom_second_new: float32 [512, 172], P('nar')
- first_low: bfloat16 [256, 256], P('nar')
- second_low: bfloat16 [512, 172], P('nar')
- biases_new: float32 [428], replicated
- bias_m_new: float32 [428], replicated
- bias_v_new: float32 [428], replicated
Inputs may be any that keep to these rules, and one draw needn't show every extreme that they name: `index_one`: column 0 names the node's own row, the others its sampled neighbours. `index_two`: column 0 names the seed's own first-layer row in its group. `mask_one`: some rows have no live slot. `mask_two`: some rows have no live slot.
All inputs are finite; a program needn't handle non-finite values.
Results may differ from a plain program's by a relative error of at most 0.0031.
Values may be sent and summed in bfloat16 or wider, within the bound.
A program may use at most 128 MiB of HBM per device.

v0:
```python
import jax
import jax.numpy as jnp
from jax import lax
from jax.sharding import PartitionSpec as P

HID = 256
NS_ITERS = 5
STEP = 10


LAM = 0.5
MU = 0.95
WDECAY = 0.01
LR_BIAS = 0.05
BETA_ONE = 0.9
BETA_TWO = 0.999
EPSILON = 1e-08
NS_A = 3.4445
NS_B = -4.775
NS_C = 2.0315
HIGH = lax.Precision.HIGHEST


def pull_rows(features, requests):
    served = lax.all_to_all(
        features[lax.all_to_all(requests, ("grp", "nar"), split_axis=0, concat_axis=0, tiled=True)],
        ("grp", "nar"),
        split_axis=0,
        concat_axis=0,
        tiled=True,
    )
    return served.reshape(-1, features.shape[1])


def layer_forward(table, index, mask, weight, bias_part):
    self_rows = table[index[:, 0]]
    near_rows = table[index[:, 1:]]
    total = jnp.einsum(
        "mk,mkd->md", mask.astype(jnp.bfloat16), near_rows, preferred_element_type=jnp.float32
    )
    count = jnp.maximum(jnp.sum(mask.astype(jnp.float32), axis=1), 1.0)
    near_mean = (total / count[:, None]).astype(jnp.bfloat16)
    act = jnp.concatenate([self_rows, near_mean], axis=1)
    out = jnp.dot(act, weight, preferred_element_type=jnp.float32) + bias_part
    return (act, out, self_rows, near_mean, count)


def layer_backward(act, grad_out, weight):
    grad_weight = jnp.dot(act.T, grad_out, preferred_element_type=jnp.float32)
    grad_bias = jnp.sum(grad_out.astype(jnp.float32), axis=0)
    grad_act = jnp.dot(grad_out, weight.T, preferred_element_type=jnp.float32)
    return (grad_weight, grad_bias, grad_act)


def add_grads(grad_total, targets, grad_self, grad_near, share):
    grad_total = grad_total.at[targets[:, 0]].add(grad_self, mode="drop")
    for slot in range(targets.shape[1] - 1):
        grad_total = grad_total.at[targets[:, 1 + slot]].add(
            share[:, slot : slot + 1] * grad_near, mode="drop"
        )
    return grad_total


def newton_schulz(first_mom, second_mom):
    norm_one, norm_two = lax.psum(
        (jnp.sum(first_mom * first_mom), jnp.sum(second_mom * second_mom)), "nar"
    )
    x_one = first_mom / (jnp.sqrt(norm_one) + 1e-07)
    x_two = second_mom / (jnp.sqrt(norm_two) + 1e-07)
    for _ in range(NS_ITERS):
        gram_one, gram_two = lax.psum(
            (jnp.dot(x_one.T, x_one, precision=HIGH), jnp.dot(x_two.T, x_two, precision=HIGH)),
            "nar",
        )
        mix_one = NS_B * gram_one + NS_C * jnp.dot(gram_one, gram_one, precision=HIGH)
        mix_two = NS_B * gram_two + NS_C * jnp.dot(gram_two, gram_two, precision=HIGH)
        x_one = NS_A * x_one + jnp.dot(x_one, mix_one, precision=HIGH)
        x_two = NS_A * x_two + jnp.dot(x_two, mix_two, precision=HIGH)
    return (x_one, x_two)


def per_device(
    features,
    requests,
    index_one,
    mask_one,
    index_two,
    mask_two,
    labels,
    seed_live,
    w_first,
    w_second,
    mom_first,
    mom_second,
    biases,
    bias_m,
    bias_v,
):
    narrow = lax.axis_size("nar")
    seeds_all = lax.axis_size("grp") * narrow * labels.shape[0]
    live = seed_live.astype(jnp.float32)
    weight_one, weight_two = (
        lax.all_gather(w_first.astype(jnp.bfloat16), "nar", axis=0, tiled=True),
        lax.all_gather(w_second.astype(jnp.bfloat16), "nar", axis=0, tiled=True),
    )
    pulled = pull_rows(features, requests)
    act_one, z_one, unused_self, unused_near, unused_count = layer_forward(
        pulled, index_one, mask_one, weight_one, biases[:HID]
    )
    hidden = jax.nn.silu(z_one).astype(jnp.bfloat16)
    group = lax.all_gather(hidden, "nar", axis=0, tiled=True)
    act_two, logits, self_two, near_two, count_two = layer_forward(
        group, index_two, mask_two, weight_two, biases[HID:]
    )
    lse = jax.nn.logsumexp(logits, axis=1)
    picked = jnp.take_along_axis(logits, labels[:, None], axis=1)[:, 0]
    diff = self_two.astype(jnp.float32) - near_two.astype(jnp.float32)
    terms = lse - picked + LAM / HID * jnp.sum(diff * diff, axis=1)
    loss_local = jnp.sum(live * terms)
    onehot = (labels[:, None] == jnp.arange(logits.shape[1], dtype=jnp.int32)[None, :]).astype(
        jnp.float32
    )
    grad_logits = (live[:, None] * (jnp.exp(logits - lse[:, None]) - onehot) / seeds_all).astype(
        jnp.bfloat16
    )
    grad_two, bias_two, grad_act = layer_backward(act_two, grad_logits, weight_two)
    reg = 2.0 * LAM / HID / seeds_all * live[:, None] * diff
    grad_self = grad_act[:, :HID] + reg
    grad_near = grad_act[:, HID:] - reg
    share = mask_two.astype(jnp.float32) / count_two[:, None]
    grad_group = add_grads(
        jnp.zeros((group.shape[0], HID), jnp.float32), index_two, grad_self, grad_near, share
    )
    grad_hidden = lax.psum_scatter(grad_group, "nar", scatter_dimension=0, tiled=True)
    sig = jax.nn.sigmoid(z_one)
    grad_z = (grad_hidden * sig * (1.0 + z_one * (1.0 - sig))).astype(jnp.bfloat16)
    grad_one, bias_one, unused_act = layer_backward(act_one, grad_z, weight_one)
    whole_one, whole_two = lax.psum((grad_one, grad_two), "grp")
    sum_one, sum_two = (
        lax.psum_scatter(whole_one, "nar", scatter_dimension=0, tiled=True),
        lax.psum_scatter(whole_two, "nar", scatter_dimension=0, tiled=True),
    )
    grad_bias, loss = lax.psum((jnp.concatenate([bias_one, bias_two]), loss_local), ("grp", "nar"))
    mom_one_new = MU * mom_first + sum_one
    mom_two_new = MU * mom_second + sum_two
    ortho_one, ortho_two = newton_schulz(mom_one_new, mom_two_new)
    rows_one = w_first.shape[0] * narrow
    rows_two = w_second.shape[0] * narrow
    scale_one = max(1.0, rows_one / w_first.shape[1]) ** 0.5
    scale_two = max(1.0, rows_two / w_second.shape[1]) ** 0.5
    first_new = w_first * (1.0 - WDECAY) - scale_one * ortho_one
    second_new = w_second * (1.0 - WDECAY) - scale_two * ortho_two
    m_new = BETA_ONE * bias_m + (1.0 - BETA_ONE) * grad_bias
    v_new = BETA_TWO * bias_v + (1.0 - BETA_TWO) * grad_bias * grad_bias
    m_hat = m_new / (1.0 - BETA_ONE**STEP)
    v_hat = v_new / (1.0 - BETA_TWO**STEP)
    bias_new = biases * (1.0 - LR_BIAS * WDECAY) - LR_BIAS * m_hat / (jnp.sqrt(v_hat) + EPSILON)
    return (
        loss,
        first_new,
        second_new,
        mom_one_new,
        mom_two_new,
        first_new.astype(jnp.bfloat16),
        second_new.astype(jnp.bfloat16),
        bias_new,
        m_new,
        v_new,
    )


def solution(mesh):
    placed = (
        P(("grp", "nar"), None),
        P(("grp", "nar"), None),
        P(("grp", "nar"), None),
        P(("grp", "nar"), None),
        P(("grp", "nar"), None),
        P(("grp", "nar"), None),
        P(("grp", "nar")),
        P(("grp", "nar")),
        P("nar", None),
        P("nar", None),
        P("nar", None),
        P("nar", None),
        P(),
        P(),
        P(),
    )
    return jax.shard_map(
        per_device,
        mesh=mesh,
        in_specs=placed,
        out_specs=(
            P(),
            P("nar", None),
            P("nar", None),
            P("nar", None),
            P("nar", None),
            P("nar", None),
            P("nar", None),
            P(),
            P(),
            P(),
        ),
        check_vma=False,
    )
```

profile of v0, /device:TPU:1, one launch (start us, length us, event | category | flops | bytes accessed | tf_op | source)
XLA Modules:
  0.0 951.3 jit_solution(5732921527281336856)
XLA Ops:
  7.2 1.6 copy.28
  8.8 11.5 %all-to-all-start = ((s32[128,1,64]{2,1,0:T(1,128)}), s32[128,1,64]{2,1,0:T(1,128)S(1)}, u32[]{:S(2)}, u32[]{:S(2)}) async-start(s32[128,1,64]{2,1,0:T(1,128)} %bitcast), calls=%async_computation | async-start | bytes 131072 | tf_op jit(solution)/shard_map/all_to_all | solution.py:26
  21.3 8.6 all-to-all-done
  30.0 29.2 %gather_fusion = bf16[8192,128]{1,0:T(8,128)(2,1)} fusion(bf16[8192,128]{1,0:T(8,128)(2,1)S(1)} %copy-done, s32[8192]{0:T(1024)S(1)} %broadcast_clamp_fusion.1), kind=kCustom, calls=%fused_computation | custom fusion | bytes 4227072 | tf_op jit(solution)/shard_map/gather | solution.py:26
  59.2 5.2 all-to-all-start.1
  65.5 2.0 copy.31
  67.5 23.0 %all_gather.9 = bf16[256,256]{1,0:T(8,128)(2,1)} all-gather(bf16[64,256]{1,0:T(8,128)(2,1)S(1)} %convert_element_type.62), channel_id=1, replica_groups=mesh['grp'=32,'nar'=4] {'nar'}, dimensions={0}, use_global_device_ids=true | all-gather | bytes 163840 | tf_op jit(solution)/shard_map/all_gather | solution.py:103
  91.5 3.3 all-to-all-done.1
  94.8 9.5 gather_fusion.1
  104.3 104.4 %gather_fusion.2 = bf16[30720,128]{1,0:T(8,128)(2,1)} fusion(bf16[8192,128]{1,0:T(8,128)(2,1)} %bitcast.3, s32[30720]{0:T(1024)S(1)} %broadcast_clamp_fusion), kind=kCustom, calls=%fused_computation.2 | custom fusion | bytes 15851520 | tf_op jit(solution)/shard_map/gather | solution.py:37
  208.7 12.5 %reshape.117 = bf16[2048,15,128]{2,1,0:T(8,128)(2,1)} reshape(bf16[30720,128]{1,0:T(8,128)(2,1)} %gather_fusion.2) | data formatting | bytes 15728640 | tf_op jit(solution)/shard_map/gather | solution.py:37
  221.2 5.9 fusion.67
  228.4 3.3 multiply_convert_fusion.1
  232.4 9.0 all_gather.11
  242.7 40.4 %all-gather.2.cloned.1.call-done = bf16[8192,256]{1,0:T(8,128)(2,1)} async-done(((bf16[2048,256]{1,0:T(8,128)(2,1)}), bf16[8192,256]{1,0:T(8,128)(2,1)}) %all-gather.2.cloned.1.call-update) | async-done | bytes 4194320 | tf_op jit(solution)/shard_map/all_gather | solution.py:111
  283.1 22.4 %gather_fusion.4 = bf16[5120,256]{1,0:T(8,128)(2,1)} fusion(bf16[8192,256]{1,0:T(8,128)(2,1)} %all-gather.2.cloned.1.call-done, s32[5120]{0:T(1024)S(1)} %broadcast_clamp_fusion.2), kind=kCustom, calls=%fused_computation.4 | custom fusion | bytes 5263360 | tf_op jit(solution)/shard_map/gather | solution.py:37
  305.5 6.0 reshape.133
  311.5 3.8 fusion.68
  315.2 4.3 gather_fusion.3
  321.2 4.5 gather_fusion.5
  328.7 7.6 scatter_custom_fusion
  336.4 10.0 %scatter_custom_fusion.1 = f32[8192,256]{1,0:T(8,128)} fusion(f32[8192,256]{1,0:T(8,128)} %scatter_custom_fusion, s32[512]{0:T(512)} %bitcast.134, f32[512,256]{1,0:T(8,128)S(1)} %slice_subtract_fusion, f32[512]{0:T(512)S(1)} %bitcast.121), kind=kCustom, calls=%fused_computation.84 | custom fusion | flops 262144 | bytes 8914944 | tf_op jit(solution)/shard_map/scatter-add | solution.py:58
  346.4 9.9 %scatter_custom_fusion.2 = f32[8192,256]{1,0:T(8,128)} fusion(f32[8192,256]{1,0:T(8,128)} %scatter_custom_fusion.1, s32[512]{0:T(512)} %bitcast.133, f32[512,256]{1,0:T(8,128)S(1)} %slice_subtract_fusion, f32[512]{0:T(512)S(1)} %bitcast.120), kind=kCustom, calls=%fused_computation.82 | custom fusion | flops 262144 | bytes 8914944 | tf_op jit(solution)/shard_map/scatter-add | solution.py:58
  356.2 9.8 %scatter_custom_fusion.3 = f32[8192,256]{1,0:T(8,128)} fusion(f32[8192,256]{1,0:T(8,128)} %scatter_custom_fusion.2, s32[512]{0:T(512)} %bitcast.132, f32[512,256]{1,0:T(8,128)S(1)} %slice_subtract_fusion, f32[512]{0:T(512)S(1)} %bitcast.119), kind=kCustom, calls=%fused_computation.80 | custom fusion | flops 262144 | bytes 8914944 | tf_op jit(solution)/shard_map/scatter-add | solution.py:58
  366.1 9.8 %scatter_custom_fusion.4 = f32[8192,256]{1,0:T(8,128)} fusion(f32[8192,256]{1,0:T(8,128)} %scatter_custom_fusion.3, s32[512]{0:T(512)} %bitcast.131, f32[512,256]{1,0:T(8,128)S(1)} %slice_subtract_fusion, f32[512]{0:T(512)S(1)} %bitcast.118), kind=kCustom, calls=%fused_computation.78 | custom fusion | flops 262144 | bytes 8914944 | tf_op jit(solution)/shard_map/scatter-add | solution.py:58
  375.9 9.8 %scatter_custom_fusion.5 = f32[8192,256]{1,0:T(8,128)} fusion(f32[8192,256]{1,0:T(8,128)} %scatter_custom_fusion.4, s32[512]{0:T(512)} %bitcast.130, f32[512,256]{1,0:T(8,128)S(1)} %slice_subtract_fusion, f32[512]{0:T(512)S(1)} %bitcast.117), kind=kCustom, calls=%fused_computation.76 | custom fusion | flops 262144 | bytes 8914944 | tf_op jit(solution)/shard_map/scatter-add | solution.py:58
  385.8 10.0 %scatter_custom_fusion.6 = f32[8192,256]{1,0:T(8,128)} fusion(f32[8192,256]{1,0:T(8,128)} %scatter_custom_fusion.5, s32[512]{0:T(512)} %bitcast.129, f32[512,256]{1,0:T(8,128)S(1)} %slice_subtract_fusion, f32[512]{0:T(512)S(1)} %bitcast.116), kind=kCustom, calls=%fused_computation.74 | custom fusion | flops 262144 | bytes 8914944 | tf_op jit(solution)/shard_map/scatter-add | solution.py:58
  395.8 9.9 %scatter_custom_fusion.7 = f32[8192,256]{1,0:T(8,128)} fusion(f32[8192,256]{1,0:T(8,128)} %scatter_custom_fusion.6, s32[512]{0:T(512)} %bitcast.128, f32[512,256]{1,0:T(8,128)S(1)} %slice_subtract_fusion, f32[512]{0:T(512)S(1)} %bitcast.115), kind=kCustom, calls=%fused_computation.72 | custom fusion | flops 262144 | bytes 8914944 | tf_op jit(solution)/shard_map/scatter-add | solution.py:58
  405.7 9.8 %scatter_custom_fusion.8 = f32[8192,256]{1,0:T(8,128)} fusion(f32[8192,256]{1,0:T(8,128)} %scatter_custom_fusion.7, s32[512]{0:T(512)} %bitcast.127, f32[512,256]{1,0:T(8,128)S(1)} %slice_subtract_fusion, f32[512]{0:T(512)S(1)} %bitcast.114), kind=kCustom, calls=%fused_computation.70 | custom fusion | flops 262144 | bytes 8914944 | tf_op jit(solution)/shard_map/scatter-add | solution.py:58
  415.5 9.8 %scatter_custom_fusion.9 = f32[8192,256]{1,0:T(8,128)} fusion(f32[8192,256]{1,0:T(8,128)} %scatter_custom_fusion.8, s32[512]{0:T(512)} %bitcast.126, f32[512,256]{1,0:T(8,128)S(1)} %slice_subtract_fusion, f32[512]{0:T(512)S(1)} %bitcast.113), kind=kCustom, calls=%fused_computation.68 | custom fusion | flops 262144 | bytes 8914944 | tf_op jit(solution)/shard_map/scatter-add | solution.py:58
  425.4 9.8 %scatter_custom_fusion.10 = f32[8192,256]{1,0:T(8,128)} fusion(f32[8192,256]{1,0:T(8,128)} %scatter_custom_fusion.9, s32[512]{0:T(512)} %bitcast.125, f32[512,256]{1,0:T(8,128)S(1)} %slice_subtract_fusion, f32[512]{0:T(512)S(1)} %bitcast.112), kind=kCustom, calls=%fused_computation.66 | custom fusion | flops 262144 | bytes 8914944 | tf_op jit(solution)/shard_map/scatter-add | solution.py:58
  436.4 79.9 %reduce-scatter.4.cloned.1.call-done = f32[2048,256]{1,0:T(8,128)} async-done(((f32[8192,256]{1,0:T(8,128)}), f32[2048,256]{1,0:T(8,128)}) %reduce-scatter.4.cloned.1.call-update) | async-done | bytes 2097168 | tf_op jit(solution)/shard_map/reduce_scatter | solution.py:134
  516.3 3.0 convert_reduce_fusion
  519.3 2.2 fusion.15
  521.7 15.4 %reduce-scatter.8.cloned.1.call-done = f32[128,172]{0,1:T(8,128)} async-done(((f32[512,172]{0,1:T(8,128)}), f32[128,172]{0,1:T(8,128)}) %reduce-scatter.8.cloned.1.call-update) | async-done | bytes 88080 | tf_op jit(solution)/shard_map/reduce_scatter | solution.py:141
  537.1 22.4 %reduce-scatter.6.cloned.1.call-done = f32[64,256]{1,0:T(8,128)} async-done(((f32[256,256]{1,0:T(8,128)}), f32[64,256]{1,0:T(8,128)}) %reduce-scatter.6.cloned.1.call-update) | async-done | bytes 65552 | tf_op jit(solution)/shard_map/reduce_scatter | solution.py:140
  559.6 104.4 %all-reduce.15.cloned.1.call-done = (f32[64,256]{1,0:T(8,128)}, f32[128,172]{0,1:T(8,128)}) async-done(((f32[64,256]{1,0:T(8,128)}, f32[128,172]{0,1:T(8,128)}), (f32[64,256]{1,0:T(8,128)}, f32[128,172]{0,1:T(8,128)})) %all-reduce.15.cloned.1.call-update) | async-done | bytes 153616 | tf_op jit(solution)/shard_map/psum | solution.py:138
  665.4 1.6 multiply_reduce_fusion.1
  667.0 9.3 all-reduce.2
  679.9 38.0 %all-reduce.25.cloned.1.call-done = (f32[256,256]{1,0:T(8,128)}, f32[172,172]{1,0:T(8,128)}) async-done(((f32[256,256]{1,0:T(8,128)}, f32[172,172]{1,0:T(8,128)}), (f32[256,256]{1,0:T(8,128)}, f32[172,172]{1,0:T(8,128)})) %all-reduce.25.cloned.1.call-update) | async-done | bytes 380496 | tf_op jit(solution)/shard_map/psum | solution.py:71
  717.9 1.5 fusion.6
  723.8 43.3 %all-reduce.23.cloned.1.call-done = (f32[256,256]{1,0:T(8,128)}, f32[172,172]{1,0:T(8,128)}) async-done(((f32[256,256]{1,0:T(8,128)}, f32[172,172]{1,0:T(8,128)}), (f32[256,256]{1,0:T(8,128)}, f32[172,172]{1,0:T(8,128)})) %all-reduce.23.cloned.1.call-update) | async-done | bytes 380496 | tf_op jit(solution)/shard_map/psum | solution.py:71
  773.0 43.3 %all-reduce.21.cloned.1.call-done = (f32[256,256]{1,0:T(8,128)}, f32[172,172]{1,0:T(8,128)}) async-done(((f32[256,256]{1,0:T(8,128)}, f32[172,172]{1,0:T(8,128)}), (f32[256,256]{1,0:T(8,128)}, f32[172,172]{1,0:T(8,128)})) %all-reduce.21.cloned.1.call-update) | async-done | bytes 380496 | tf_op jit(solution)/shard_map/psum | solution.py:71
  816.2 1.5 fusion.4
  822.1 43.3 %all-reduce.19.cloned.1.call-done = (f32[256,256]{1,0:T(8,128)}, f32[172,172]{1,0:T(8,128)}) async-done(((f32[256,256]{1,0:T(8,128)}, f32[172,172]{1,0:T(8,128)}), (f32[256,256]{1,0:T(8,128)}, f32[172,172]{1,0:T(8,128)})) %all-reduce.19.cloned.1.call-update) | async-done | bytes 380496 | tf_op jit(solution)/shard_map/psum | solution.py:71
  865.4 1.5 fusion.3
  871.3 67.1 %all-reduce = (f32[]{:T(128)}, f32[428]{0:T(512)S(1)}) all-reduce(f32[]{:T(128)} %get-tuple-element.37, f32[428]{0:T(512)S(1)} %pad_maximum_fusion.6), channel_id=1, replica_groups=mesh['grp'=32,'nar'=4] {'grp','nar'}, use_global_device_ids=true, to_apply=%region_6.7 | all-reduce | flops 429 | bytes 3432 | tf_op jit(solution)/shard_map/psum | solution.py:143
  939.0 1.5 fusion.2
  (144 shorter events, 38.5 us)
Async XLA Ops:
  7.2 22.8 %copy-start = (bf16[8192,128]{1,0:T(8,128)(2,1)S(1)}, bf16[8192,128]{1,0:T(8,128)(2,1)}, u32[]{:S(2)}) copy-start(bf16[8192,128]{1,0:T(8,128)(2,1)} %param.15) | copy-start | bytes 6291460
  8.8 21.1 %all-to-all-start = ((s32[128,1,64]{2,1,0:T(1,128)}), s32[128,1,64]{2,1,0:T(1,128)S(1)}, u32[]{:S(2)}, u32[]{:S(2)}) async-start(s32[128,1,64]{2,1,0:T(1,128)} %bitcast), calls=%async_computation | async-start | bytes 131072 | tf_op jit(solution)/shard_map/all_to_all | solution.py:26
  30.0 34.5 %copy-start.4 = (s32[2048,15]{0,1:T(8,128)S(1)}, s32[2048,15]{0,1:T(8,128)}, u32[]{:S(2)}) copy-start(s32[2048,15]{0,1:T(8,128)} %param.18) | copy-start | bytes 368644
  30.0 34.5 %copy-start.9 = (f32[64,256]{1,0:T(8,128)S(1)}, f32[64,256]{1,0:T(8,128)}, u32[]{:S(2)}) copy-start(f32[64,256]{1,0:T(8,128)} %param.23) | copy-start | bytes 196612
  59.2 35.6 %all-to-all-start.1 = ((bf16[128,64,128]{2,1,0:T(8,128)(2,1)}), bf16[128,64,128]{2,1,0:T(8,128)(2,1)}, u32[]{:S(2)}, u32[]{:S(2)}) async-start(bf16[128,64,128]{2,1,0:T(8,128)(2,1)} %bitcast.108), calls=%async_computation.1 | async-start | bytes 4194304 | tf_op jit(solution)/shard_map/all_to_all | solution.py:25
  64.5 218.7 %all-gather.2.cloned.1.call-start = ((), (), s32[]{:S(2)}) async-start(), calls=%async_computation.5 | async-start | bytes 5242880 | tf_op jit(solution)/shard_map/all_gather | solution.py:111
  221.2 7.2 copy-start.11
  221.2 7.2 slice-start
  227.1 4.7 copy-start.20
  227.1 4.7 copy-start.18
  227.1 4.7 copy-start.5
  227.2 4.7 copy-start.12
  227.2 5.0 copy-start.7
  227.2 14.9 %copy-start.16 = (s32[512]{0:T(512)S(1)}, s32[512]{0:T(512)}, u32[]{:S(2)}) copy-start(s32[512]{0:T(512)} %param.21) | copy-start | bytes 6148
  227.5 0.8 copy-start.3
  231.7 284.6 %reduce-scatter.4.cloned.1.call-start = ((), (), s32[]{:S(2)}) async-start(), calls=%async_computation.6 | async-start | bytes 10485760 | tf_op jit(solution)/shard_map/reduce_scatter | solution.py:134
  242.1 0.6 copy-start.17
  305.5 20.3 %copy-start.19 = (s32[512]{0:T(512)S(1)}, s32[512]{0:T(512)}, u32[]{:S(2)}) copy-start(s32[512]{0:T(512)} %param.22) | copy-start | bytes 6148
  327.5 1.1 copy-start.1
  435.2 84.1 %copy-start.2 = (bf16[2048,128]{1,0:T(8,128)(2,1)S(1)}, bf16[2048,128]{1,0:T(8,128)(2,1)}, u32[]{:S(2)}) copy-start(bf16[2048,128]{1,0:T(8,128)(2,1)} %gather_fusion.1) | copy-start | bytes 1572868
  435.2 228.8 %copy-start.15 = (f32[64,256]{1,0:T(8,128)S(1)}, f32[64,256]{1,0:T(8,128)}, u32[]{:S(2)}) copy-start(f32[64,256]{1,0:T(8,128)} %param.25) | copy-start | bytes 196612
  435.2 230.2 %copy-start.13 = (f32[128,172]{0,1:T(8,128)S(1)}, f32[128,172]{0,1:T(8,128)}, u32[]{:S(2)}) copy-start(f32[128,172]{0,1:T(8,128)} %param.26) | copy-start | bytes 264196
  435.3 101.8 %reduce-scatter.8.cloned.1.call-start = ((), (), s32[]{:S(2)}) async-start(), calls=%async_computation.8 | async-start | bytes 450560 | tf_op jit(solution)/shard_map/reduce_scatter | solution.py:141
  436.3 123.2 %reduce-scatter.6.cloned.1.call-start = ((), (), s32[]{:S(2)}) async-start(), calls=%async_computation.7 | async-start | bytes 327680 | tf_op jit(solution)/shard_map/reduce_scatter | solution.py:140
  521.6 349.7 %copy-start.22 = (f32[172]{0:T(256)S(1)}, f32[172]{0:T(256)}, u32[]{:S(2)}) copy-start(f32[172]{0:T(256)} %get-tuple-element.35) | copy-start | bytes 2068
  521.6 416.8 %copy-start.21 = (f32[428]{0:T(512)S(1)}, f32[428]{0:T(512)}, u32[]{:S(2)}) copy-start(f32[428]{0:T(512)} %param.27) | copy-start | bytes 5140
  521.6 416.8 %copy-start.23 = (f32[428]{0:T(512)S(1)}, f32[428]{0:T(512)}, u32[]{:S(2)}) copy-start(f32[428]{0:T(512)} %param.28) | copy-start | bytes 5140
  521.6 416.8 %copy-start.24 = (f32[428]{0:T(512)S(1)}, f32[428]{0:T(512)}, u32[]{:S(2)}) copy-start(f32[428]{0:T(512)} %param.29) | copy-start | bytes 5140
  521.6 419.0 %copy-start.10 = (f32[64,256]{1,0:T(8,128)S(1)}, f32[64,256]{1,0:T(8,128)}, u32[]{:S(2)}) copy-start(f32[64,256]{1,0:T(8,128)} %param.23) | copy-start | bytes 196612
  521.6 142.4 %all-reduce.15.cloned.1.call-start = ((), (), s32[]{:S(2)}) async-start(), calls=%async_computation.9 | async-start | bytes 311296 | tf_op jit(solution)/shard_map/psum | solution.py:138
  559.5 158.3 %all-reduce.25.cloned.1.call-start = ((), (), s32[]{:S(2)}) async-start(), calls=%async_computation.14 | async-start | bytes 884736 | tf_op jit(solution)/shard_map/psum | solution.py:71
  665.4 278.6 %copy-start.8 = (f32[64,256]{1,0:T(8,128)}, f32[64,256]{1,0:T(8,128)S(1)}, u32[]{:S(2)}) copy-start(f32[64,256]{1,0:T(8,128)S(1)} %get-tuple-element.32) | copy-start | bytes 196612
  665.4 277.4 %copy-start.6 = (f32[128,172]{0,1:T(8,128)S(1)}, f32[128,172]{0,1:T(8,128)}, u32[]{:S(2)}) copy-start(f32[128,172]{0,1:T(8,128)} %param.24) | copy-start | bytes 264196
  667.0 277.1 %copy-start.14 = (f32[128,172]{0,1:T(8,128)}, f32[128,172]{0,1:T(8,128)S(1)}, u32[]{:S(2)}) copy-start(f32[128,172]{0,1:T(8,128)S(1)} %get-tuple-element.30) | copy-start | bytes 264196
  679.8 87.2 %all-reduce.23.cloned.1.call-start = ((), (), s32[]{:S(2)}) async-start(), calls=%async_computation.13 | async-start | bytes 884736 | tf_op jit(solution)/shard_map/psum | solution.py:71
  723.7 92.5 %all-reduce.21.cloned.1.call-start = ((), (), s32[]{:S(2)}) async-start(), calls=%async_computation.12 | async-start | bytes 884736 | tf_op jit(solution)/shard_map/psum | solution.py:71
  772.9 92.5 %all-reduce.19.cloned.1.call-start = ((), (), s32[]{:S(2)}) async-start(), calls=%async_computation.11 | async-start | bytes 884736 | tf_op jit(solution)/shard_map/psum | solution.py:71
  822.1 116.9 %all-reduce.17.cloned.1.call-start = ((), (), s32[]{:S(2)}) async-start(), calls=%async_computation.10 | async-start | bytes 884736 | tf_op jit(solution)/shard_map/psum | solution.py:71
Sparse Core Ops, SparseCore 0:
  231.9 51.2 all-gather.1
  435.4 80.8 reduce-scatter.3
  518.7 18.3 reduce-scatter.7
  539.3 20.1 reduce-scatter.5
  563.2 100.7 all-reduce.14
  680.0 37.8 all-reduce.24
  723.9 43.1 all-reduce.22
  773.0 43.1 all-reduce.20
  822.2 43.1 all-reduce.18
  871.4 43.0 all-reduce.16
where the time goes:
time: 959 us; the launch traced here: 951 us
  waiting for transfers between devices  442 us (46%)
  local copies, waits for them, and re-layouts  200 us (21%)
  other arithmetic  119 us (12%)
  blocking collectives  108 us (11%)
  matrix products  47.2 us (5%)
  starting transfers between devices  17.1 us (2%)
  between operations  16.6 us (2%)
    psum x5, waiting for transfers between devices, newton_schulz(): lax.psum((jnp.dot(x_one.T, x_one, precision=HIGH), jnp.dot(x_two.T, x_two...  168 us
    gather x4, local copies, waits for them, and re-layouts, layer_forward(): near_rows = table[index[:, 1:]]  145 us
    psum x1, waiting for transfers between devices, per_device(): whole_one, whole_two = lax.psum((grad_one, grad_two), 'grp')  104 us
    scatter-add x10, other arithmetic, add_grads(): grad_total.at[targets[:, 1 + slot]]  98.8 us
    reduce_scatter x1, waiting for transfers between devices, per_device(): lax.psum_scatter(grad_group, 'nar', scatter_dimension=0, tiled=True)  79.9 us
    psum x1, blocking collectives, per_device(): lax.psum((jnp.concatenate([bias_one, bias_two]), loss_local), ('grp', 'na...  67.1 us
    all_gather x1, waiting for transfers between devices, per_device(): group = lax.all_gather(hidden, 'nar', axis=0, tiled=True)  40.4 us
    gather x1, local copies, waits for them, and re-layouts, pull_rows(): features[lax.all_to_all(requests, ('grp', 'nar'), split_axis=0, concat_ax...  29.2 us
  transfers between devices with their start and end apart: 12, of which 11 were waited for; matrix products, arithmetic and copies ran while one was open for 1% of the time, Pallas kernels for 0%

commit v1 on v0

v1 whole, which is shorter than its diff:
```python
import functools

import jax
import jax.numpy as jnp
from jax import lax
from jax.experimental import pallas as pl
from jax.experimental.pallas import tpu as pltpu
from jax.sharding import PartitionSpec as P

HID = 256
CLS = 172
CLS_PAD = 176
D_IN = 128
F1 = 15
F2 = 10
NS_ITERS = 5
STEP = 10
LAM = 0.5
MU = 0.95
WDECAY = 0.01
LR_BIAS = 0.05
BETA_ONE = 0.9
BETA_TWO = 0.999
EPSILON = 1e-08
NS_A = 3.4445
NS_B = -4.775
NS_C = 2.0315
HIGH = lax.Precision.HIGHEST
MESH = pl.DeviceIdType.MESH
BF = jnp.bfloat16
F32 = jnp.float32

DEV = 128
NAR = 4
OWN = 8192
CAP = 64
SRC = 8192
FRONT = 2048
SEED = 512


def all_to(t):
    return (t // NAR, t % NAR)


def pull_kernel(
    req, feat, w1, w2t, m1, m2t, idx2,
    pulled, gw1, gw2t, gm1, gm2t, gidx2,
    featb, featf, reqin, reqs, stage, sendbuf,
    feat_sem, req_send, req_recv, loc_sem, row_send, row_recv, nar_send, nar_recv,
):
    g = lax.axis_index("grp")
    y = lax.axis_index("nar")
    me = g * NAR + y

    load = pltpu.make_async_copy(feat, featb, feat_sem)
    load.start()

    barrier = pltpu.get_barrier_semaphore()

    def greet(i, c):
        pl.semaphore_signal(barrier, inc=1, device_id=all_to((me + i) % DEV), device_id_type=MESH)
        return c

    lax.fori_loop(1, DEV, greet, 0)
    pl.semaphore_wait(barrier, DEV - 1)

    def ask(i, c):
        t = (me + i * 37) % DEV
        pltpu.make_async_remote_copy(
            src_ref=req.at[t], dst_ref=reqin.at[me], send_sem=req_send, recv_sem=req_recv,
            device_id=all_to(t), device_id_type=MESH,
        ).start()
        return c

    lax.fori_loop(1, DEV, ask, 0)

    own = []
    for n, (a, b) in enumerate(((w1, gw1), (w2t, gw2t), (m1, gm1), (m2t, gm2t), (idx2, gidx2))):
        own.append(pltpu.make_async_copy(a, b.at[y], loc_sem.at[n]))
        own[-1].start()
        for d in range(1, NAR):
            pltpu.make_async_remote_copy(
                src_ref=a, dst_ref=b.at[y], send_sem=nar_send.at[n, d - 1], recv_sem=nar_recv.at[n, d - 1],
                device_id=(g, (y + d) % NAR), device_id_type=MESH,
            ).start()

    load.wait()

    def widen(i, c):
        rows = pl.ds(pl.multiple_of(i * 256, 256), 256)
        featf[rows, :] = featb[rows, :].astype(F32)
        return c

    lax.fori_loop(0, OWN // 256, widen, 0)

    mine = pltpu.make_async_copy(req.at[me], reqin.at[me], loc_sem.at[5])
    mine.start()
    mine.wait()
    got = reqin.at[pl.ds(0, DEV - 1)]
    pltpu.make_async_copy(got, got, req_recv).wait()
    fetch = pltpu.make_async_copy(reqin, reqs, loc_sem.at[6])
    fetch.start()
    fetch.wait()

    def serve(i, c):
        t = (me + i * 37) % DEV
        for r in range(CAP):
            stage[r:r + 1, :] = featf[pl.ds(reqs[t, 0, r], 1), :]
        slot = pl.ds(pl.multiple_of(i * CAP, CAP), CAP)
        sendbuf[slot, :] = stage[...].astype(BF)
        return t, slot

    def serve_far(i, c):
        t, slot = serve(i, c)
        pltpu.make_async_remote_copy(
            src_ref=sendbuf.at[slot], dst_ref=pulled.at[pl.ds(pl.multiple_of(me * CAP, CAP), CAP)],
            send_sem=row_send, recv_sem=row_recv, device_id=all_to(t), device_id_type=MESH,
        ).start()
        return c

    lax.fori_loop(1, DEV, serve_far, 0)
    serve(0, 0)
    pulled[pl.ds(pl.multiple_of(me * CAP, CAP), CAP), :] = sendbuf[0:CAP, :]

    for n, (a, b) in enumerate(((w1, gw1), (w2t, gw2t), (m1, gm1), (m2t, gm2t), (idx2, gidx2))):
        own[n].wait()
        for d in range(1, NAR):
            pltpu.make_async_remote_copy(
                src_ref=a, dst_ref=b.at[y], send_sem=nar_send.at[n, d - 1], recv_sem=nar_recv.at[n, d - 1],
                device_id=(g, (y + d) % NAR), device_id_type=MESH,
            ).wait()
    sent = req.at[pl.ds(0, DEV - 1)]
    pltpu.make_async_copy(sent, sent, req_send).wait()
    gone = sendbuf.at[pl.ds(0, (DEV - 1) * CAP)]
    pltpu.make_async_copy(gone, gone, row_send).wait()
    come = pulled.at[pl.ds(0, (DEV - 1) * CAP)]
    pltpu.make_async_copy(come, come, row_recv).wait()


def pull(req, feat, w1, w2t, m1, m2t, idx2):
    vm = pl.BlockSpec(memory_space=pltpu.VMEM)
    small = (w1, w2t, m1, m2t, idx2)
    return pl.pallas_call(
        pull_kernel,
        out_shape=[jax.ShapeDtypeStruct((SRC, D_IN), BF)]
        + [jax.ShapeDtypeStruct((NAR,) + a.shape, a.dtype) for a in small],
        in_specs=[vm, pl.BlockSpec(memory_space=pl.ANY)] + [vm] * 5,
        out_specs=[vm] * 6,
        scratch_shapes=[
            pltpu.VMEM((OWN, D_IN), BF),
            pltpu.VMEM((OWN, D_IN), F32),
            pltpu.VMEM((DEV, 1, 128), jnp.int32),
            pltpu.SMEM((DEV, 1, 128), jnp.int32),
            pltpu.VMEM((CAP, D_IN), F32),
            pltpu.VMEM((DEV * CAP, D_IN), BF),
            pltpu.SemaphoreType.DMA,
            pltpu.SemaphoreType.DMA,
            pltpu.SemaphoreType.DMA,
            pltpu.SemaphoreType.DMA((7,)),
            pltpu.SemaphoreType.DMA,
            pltpu.SemaphoreType.DMA,
            pltpu.SemaphoreType.DMA((5, 3)),
            pltpu.SemaphoreType.DMA((5, 3)),
        ],
        compiler_params=pltpu.CompilerParams(
            collective_id=0, has_side_effects=True, vmem_limit_bytes=56 * 2**20
        ),
    )(req, feat, *small)


def first_kernel(idx, inv, pulled, w1t, b1, a1, z1t, h1t, table, near, own):
    def widen(i, c):
        rows = pl.ds(pl.multiple_of(i * 256, 256), 256)
        table[rows, :] = pulled[rows, :].astype(F32)
        return c

    lax.fori_loop(0, SRC // 256, widen, 0)
    table[SRC:SRC + 8, :] = jnp.zeros((8, D_IN), F32)

    def some(i, c):
        base = pl.multiple_of(i * 8, 8)
        for j in range(8):
            m = base + j
            own[pl.ds(m, 1), :] = table[pl.ds(idx[0, m], 1), :]
            rows = [table[pl.ds(idx[1 + k, m], 1), :] for k in range(F1)]
            while len(rows) > 1:
                rows = [a + b for a, b in zip(rows[::2], rows[1::2])] + ([rows[-1]] if len(rows) % 2 else [])
            near[pl.ds(m, 1), :] = rows[0] * inv[0, m]
        return c

    lax.fori_loop(0, FRONT // 8, some, 0)

    def block(i, c):
        rows = pl.ds(pl.multiple_of(i * 256, 256), 256)
        act = jnp.concatenate([own[rows, :].astype(BF), near[rows, :].astype(BF)], axis=1)
        a1[rows, :] = act
        z = lax.dot_general(
            w1t[...], act, (((1,), (1,)), ((), ())), preferred_element_type=F32
        ) + b1[...]
        z1t[:, rows] = z
        h1t[:, rows] = (z * jax.nn.sigmoid(z)).astype(BF)
        return c

    lax.fori_loop(0, FRONT // 256, block, 0)


def first(idx, inv, pulled, w1t, b1):
    vm = pl.BlockSpec(memory_space=pltpu.VMEM)
    sm = pl.BlockSpec(memory_space=pltpu.SMEM)
    return pl.pallas_call(
        first_kernel,
        out_shape=[
            jax.ShapeDtypeStruct((FRONT, 2 * D_IN), BF),
            jax.ShapeDtypeStruct((HID, FRONT), F32),
            jax.ShapeDtypeStruct((HID, FRONT), BF),
        ],
        in_specs=[sm, sm, vm, vm, vm],
        out_specs=[vm] * 3,
        scratch_shapes=[
            pltpu.VMEM((SRC + 8, D_IN), F32),
            pltpu.VMEM((FRONT, D_IN), F32),
            pltpu.VMEM((FRONT, D_IN), F32),
        ],
        compiler_params=pltpu.CompilerParams(vmem_limit_bytes=56 * 2**20),
    )(idx, inv, pulled, w1t, b1)


def dot(a, b, dims=((1,), (0,)), precision=None):
    return lax.dot_general(a, b, (dims, ((), ())), preferred_element_type=F32, precision=precision)


def newton_schulz(x):
    x = x / (jnp.sqrt(jnp.sum(x * x)) + 1e-07)
    for _ in range(NS_ITERS):
        gram = dot(x, x, ((1,), (1,)), HIGH)
        mix = NS_B * gram + NS_C * dot(gram, gram, precision=HIGH)
        x = NS_A * x + dot(mix, x, precision=HIGH)
    return x


def per_device(
    features, requests, index_one, mask_one, index_two, mask_two, labels, seed_live,
    w_first, w_second, mom_first, mom_second, biases, bias_m, bias_v,
):
    y = lax.axis_index("nar")
    seeds_all = SEED * DEV
    live = seed_live.astype(F32)[None, :]
    idx_one, msk_one = index_one.T, mask_one.T
    idx_two, msk_two = index_two.T, mask_two.T
    idx_one = jnp.concatenate([idx_one[:1], jnp.where(msk_one > 0, idx_one[1:], SRC)], axis=0)
    inv_one = 1.0 / jnp.maximum(jnp.sum(msk_one.astype(F32), axis=0, keepdims=True), 1.0)
    idx_two = jnp.concatenate(
        [idx_two[:1], jnp.where(msk_two > 0, idx_two[1:], -1), jnp.zeros((5, SEED), jnp.int32)], axis=0
    )
    inv_two = 1.0 / jnp.maximum(jnp.sum(msk_two.astype(F32), axis=0, keepdims=True), 1.0)
    w2t = jnp.pad(w_second.astype(BF).T, ((0, CLS_PAD - CLS), (0, 0)))
    m2t = jnp.pad(mom_second.T, ((0, CLS_PAD - CLS), (0, 0)))
    req = jnp.pad(requests, ((0, 0), (0, 64))).reshape(DEV, 1, 128)
    pulled, gw1, gw2t, gm1, gm2t, gidx2 = pull(
        req, features, w_first.astype(BF), w2t, mom_first, m2t, idx_two
    )
    w1t = gw1.reshape(HID, 2 * D_IN).T
    w2t = jnp.transpose(gw2t, (1, 0, 2)).reshape(CLS_PAD, 2 * HID)[:CLS]
    b1 = biases[:HID][:, None]
    b2 = biases[HID:][:, None]
    a1, z1t, h1t = first(idx_one, inv_one, pulled, w1t, b1)

    group = lax.all_gather(h1t, "nar", axis=1, tiled=True)
    iota = jnp.arange(NAR * FRONT, dtype=jnp.int32)[:, None]
    pick_near = sum((iota == idx_two[1 + k][None, :]).astype(F32) for k in range(F2)).astype(BF)
    pick_self = (iota == idx_two[:1]).astype(BF)
    near = (dot(group, pick_near) * inv_two).astype(BF)
    self2 = dot(group, pick_self).astype(BF)
    act2 = jnp.concatenate([self2, near], axis=0)
    logits = dot(w2t, act2) + b2
    top = jnp.max(logits, axis=0, keepdims=True)
    e = jnp.exp(logits - top)
    tot = jnp.sum(e, axis=0, keepdims=True)
    lse = top + jnp.log(tot)
    hot = (jnp.arange(CLS, dtype=jnp.int32)[:, None] == labels[None, :]).astype(F32)
    picked = jnp.sum(hot * logits, axis=0, keepdims=True)
    diff = self2.astype(F32) - near.astype(F32)
    terms = lse - picked + LAM / HID * jnp.sum(diff * diff, axis=0, keepdims=True)
    loss = jnp.sum(live * terms)
    dlog = (live * (e / tot - hot) / seeds_all).astype(BF)
    g2t = dot(dlog, act2, ((1,), (1,)))
    db2 = jnp.sum(dlog.astype(F32), axis=1)
    da = dot(w2t, dlog, ((0,), (0,)))
    reg = 2.0 * LAM / HID / seeds_all * live * diff
    dself = (da[:HID] + reg).astype(BF)
    dnear = ((da[HID:] - reg) * inv_two).astype(BF)
    back = lax.all_gather(jnp.concatenate([dself, dnear], axis=0), "nar", axis=1, tiled=True)
    rows = jnp.arange(FRONT, dtype=jnp.int32)[:, None] + y * FRONT
    alls = jnp.transpose(gidx2, (1, 0, 2)).reshape(16, NAR * SEED)
    put_near = sum((rows == alls[1 + k][None, :]).astype(F32) for k in range(F2)).astype(BF)
    put_self = (rows == alls[:1]).astype(BF)
    dh1 = dot(back[:HID], put_self, ((1,), (1,))) + dot(back[HID:], put_near, ((1,), (1,)))
    sig = jax.nn.sigmoid(z1t)
    dz1 = (dh1 * sig * (1.0 + z1t * (1.0 - sig))).astype(BF)
    g1t = dot(dz1, a1)
    db1 = jnp.sum(dz1.astype(F32), axis=1)
    flat = jnp.concatenate([g1t.reshape(-1), g2t.reshape(-1), db1, db2, loss[None]])
    flat = lax.psum(flat, ("grp", "nar"))
    n1, n2 = HID * 2 * D_IN, CLS * 2 * HID
    g1 = flat[:n1].reshape(HID, 2 * D_IN).T
    g2t = flat[n1:n1 + n2].reshape(CLS, 2 * HID)
    grad_bias = flat[n1 + n2:-1]
    loss = flat[-1]
    mom1 = MU * gm1.reshape(2 * D_IN, HID) + g1
    mom2t = MU * jnp.transpose(gm2t, (1, 0, 2)).reshape(CLS_PAD, 2 * HID)[:CLS] + g2t
    x1 = newton_schulz(mom1.T).T
    x2t = newton_schulz(mom2t)
    x1 = lax.dynamic_slice_in_dim(x1, y * 64, 64, 0)
    x2 = lax.dynamic_slice_in_dim(x2t, y * 128, 128, 1).T
    mom_one_new = lax.dynamic_slice_in_dim(mom1, y * 64, 64, 0)
    mom_two_new = lax.dynamic_slice_in_dim(mom2t, y * 128, 128, 1).T
    first_new = w_first * (1.0 - WDECAY) - x1
    second_new = w_second * (1.0 - WDECAY) - (2 * HID / CLS) ** 0.5 * x2
    m_new = BETA_ONE * bias_m + (1.0 - BETA_ONE) * grad_bias
    v_new = BETA_TWO * bias_v + (1.0 - BETA_TWO) * grad_bias * grad_bias
    m_hat = m_new / (1.0 - BETA_ONE**STEP)
    v_hat = v_new / (1.0 - BETA_TWO**STEP)
    bias_new = biases * (1.0 - LR_BIAS * WDECAY) - LR_BIAS * m_hat / (jnp.sqrt(v_hat) + EPSILON)
    return (
        loss, first_new, second_new, mom_one_new, mom_two_new,
        first_new.astype(BF), second_new.astype(BF), bias_new, m_new, v_new,
    )


def solution(mesh):
    both = ("grp", "nar")
    placed = (
        P(both, None), P(both, None), P(both, None), P(both, None), P(both, None), P(both, None),
        P(both), P(both), P("nar", None), P("nar", None), P("nar", None), P("nar", None), P(), P(), P(),
    )
    nar = P("nar", None)
    return jax.shard_map(
        per_device, mesh=mesh, in_specs=placed,
        out_specs=(P(), nar, nar, nar, nar, nar, nar, P(), P(), P()), check_vma=False,
    )
```

time: 959 us -> 431 us (0.45)
  waiting for transfers between devices: 442 us -> 220 us
  local copies, waits for them, and re-layouts: 200 us -> 19 us
  blocking collectives: 108 us -> 0 us
  other arithmetic: 119 us -> 13.5 us
  Pallas kernels: 0 us -> 97.6 us
  starting transfers between devices: 17.1 us -> 0.37 us
  matrix products: 47.2 us -> 59.7 us
    gather x8 -> x0, local copies, waits for them, and re-layouts: 193 us -> none  [the longest x4 145 us: layer_forward(): near_rows = table[index[:, 1:]]]
    psum x6 -> x1, waiting for transfers between devices: 272 us -> 145 us  [per_device(): flat = lax.psum(flat, ('grp', 'nar'))]
    reduce_scatter x3 -> x0, waiting for transfers between devices: 118 us -> none  [the longest x1 79.9 us: per_device(): lax.psum_scatter(grad_group, 'nar', scatter_dimension=0, tiled=True)]
    scatter-add x11 -> x0, other arithmetic: 106 us -> none  [the longest x10 98.8 us: add_grads(): grad_total.at[targets[:, 1 + slot]]]
    pallas_call x0 -> x2, Pallas kernels: none -> 97.6 us  [the longest x1 54.4 us: pull(): pl.pallas_call(pull_kernel, out_shape=[jax.ShapeDtypeStruct((SRC, D_IN),...]
    psum x2 -> x0, blocking collectives: 76.5 us -> none  [the longest x1 67.1 us: per_device(): lax.psum((jnp.concatenate([bias_one, bias_two]), loss_local), ('grp', 'na...]
    all_gather x1 -> x2, waiting for transfers between devices: 40.4 us -> 74.9 us  [the longest x1 44.9 us: per_device(): group = lax.all_gather(h1t, 'nar', axis=1, tiled=True)]
    all_gather x2 -> x0, blocking collectives: 32 us -> none  [the longest x1 23 us: per_device(): lax.all_gather(w_first.astype(jnp.bfloat16), 'nar', axis=0, tiled=True)]
  transfers between devices with their start and end apart: 12 -> 3, of which waited for: 11 -> 3; matrix products, arithmetic and copies ran while one was open for 1% -> 0% of each run, Pallas kernels for 0% -> 0%
where the time goes in v1:
time: 431 us; the launch traced here: 426 us
  waiting for transfers between devices  220 us (51%)
  Pallas kernels  97.6 us (23%)
  matrix products  59.7 us (14%)
  local copies, waits for them, and re-layouts  19 us (4%)
  between operations  16 us (4%)
  other arithmetic  13.5 us (3%)
    psum x1, waiting for transfers between devices, per_device(): flat = lax.psum(flat, ('grp', 'nar'))  145 us
    dot_general x38, matrix products, dot(): lax.dot_general(a, b, (dims, ((), ())), preferred_element_type=F32, preci...  59.7 us
    pallas_call x1, Pallas kernels, pull(): pl.pallas_call(pull_kernel, out_shape=[jax.ShapeDtypeStruct((SRC, D_IN),...  54.4 us
    all_gather x1, waiting for transfers between devices, per_device(): group = lax.all_gather(h1t, 'nar', axis=1, tiled=True)  44.9 us
    pallas_call x1, Pallas kernels, first(): pl.pallas_call(first_kernel, out_shape=[jax.ShapeDtypeStruct((FRONT, 2 *...  43.2 us
    all_gather x1, waiting for transfers between devices, per_device(): lax.all_gather(jnp.concatenate([dself, dnear], axis=0), 'nar', axis=1, ti...  30 us
  transfers between devices with their start and end apart: 3, of which 3 were waited for; matrix products, arithmetic and copies ran while one was open for 0% of the time, Pallas kernels for 0%

profile of v1, /device:TPU:1, one launch (start us, length us, event | category | flops | bytes accessed | tf_op | source)
XLA Modules:
  0.0 426.3 jit_solution(10175551710076302264)
XLA Ops:
  7.2 0.8 slice.167
  8.1 1.0 slice_select_fusion
  9.1 0.9 convert_reduce_fusion.2
  10.0 0.7 slice.164
  10.7 0.8 slice_select_fusion.1
  11.6 0.8 copy.30
  12.4 0.6 pad.12
  13.1 0.9 convert_bitcast_fusion
  14.0 1.5 convert_element_type.128.w1
  15.5 0.6 pad.13.w2t
  16.1 1.5 pad.14.m2t
  17.6 0.7 add_add_fusion.idx2
  18.3 54.4 %shard_map.222 = (bf16[8192,128]{1,0:T(8,128)(2,1)}, bf16[4,64,256]{2,1,0:T(8,128)(2,1)}, bf16[4,176,128]{2,1,0:T(8,128)(2,1)}, f32[4,64,256]{2,1,0:T(8,128)}, f...) custom-call(s32[128,1,128]{2,1,0:T(1,128)} %bitcast.145, bf16[8192,128]{1,0:T(8,128)(2,1)} %feat.1, ...), custom_call_target="tpu_custom_call" | custom-call | tf_op jit(solution)/shard_map/pallas_call | solution.py:144
  72.7 1.7 copy.32
  74.4 0.7 slice.132
  75.1 0.8 copy.33.b1
  75.9 0.6 maximum_divide_fusion
  76.5 0.7 pad_add_fusion.idx
  77.1 43.2 %shard_map.223 = (bf16[2048,256]{1,0:T(8,128)(2,1)}, f32[256,2048]{1,0:T(8,128)}, bf16[256,2048]{1,0:T(8,128)(2,1)}) custom-call(s32[16,2048]{1,0:T(8,128)} %pad_add_fusion.idx, f32[1,2048]{1,0:T(1,128)} %bitcast.154, bf16[8192,128]{1,0:T(8,128)(2,1)} %get-tuple-element.20.pulled, bf16[256,256]{1,0:T(8,128)(2,1)} %bitcast.143, f32[256,1]{1,0:T(8,128)} %copy.33.b1), custom_call_target="tpu_custom_call" | custom-call | tf_op jit(solution)/shard_map/pallas_call | solution.py:211
  120.7 44.9 %all-gather.3.cloned.1.call-done = bf16[256,8192]{1,0:T(8,128)(2,1)} async-done(((bf16[256,2048]{1,0:T(8,128)(2,1)}), bf16[256,8192]{1,0:T(8,128)(2,1)}) %all-gather.3.cloned.1.call-update) | async-done | bytes 4194320 | tf_op jit(solution)/shard_map/all_gather | solution.py:269
  165.6 5.4 %fusion.22 = bf16[256,512]{1,0:T(8,128)(2,1)S(1)} fusion(bf16[256,8192]{1,0:T(8,128)(2,1)} %all-gather.3.cloned.1.call-done, s32[512]{0:T(512)S(1)} %bitcast.166), kind=kOutput, calls=%fused_computation.28 | convolution fusion | flops 2151809024 | bytes 4458496 | tf_op jit(solution)/shard_map/dot_general | solution.py:230
  171.0 17.1 %fusion.23 = bf16[256,512]{1,0:T(8,128)(2,1)S(1)} fusion(bf16[256,8192]{1,0:T(8,128)(2,1)S(1)} %copy-done.14, s32[512]{0:T(512)S(1)} %bitcast.169, s32[512]{0:T(512)S(1)} %bitcast.170, s32[512]{0:T(512)S(1)} %bitcast.171, s32[512]{0:T(512)S(1)} %bitcast.172, s32[512]{0:T(512)S(1)} %bitcast.173, s32[512]{0:T(512)S(1)} %bitcast.174, s32[512]{0:T(512)S(1)} %bitcast.175, ...), kind=kOutput, calls=%fused_computation.29 | convolution fusion | flops 2273574912 | bytes 4478976 | tf_op jit(solution)/shard_map/dot_general | solution.py:230
  189.3 0.8 pad_maximum_fusion.1
  191.0 0.6 multiply_reduce_fusion.3
  191.6 30.0 %all-gather.5.cloned.1.call-done = bf16[512,2048]{1,0:T(8,128)(2,1)} async-done(((bf16[512,512]{1,0:T(8,128)(2,1)}), bf16[512,2048]{1,0:T(8,128)(2,1)}) %all-gather.5.cloned.1.call-update) | async-done | bytes 2097168 | tf_op jit(solution)/shard_map/all_gather | solution.py:293
  221.6 18.7 %fusion.6 = f32[256,2048]{1,0:T(8,128)S(1)} fusion(s32[2048]{0:T(1024)S(1)} %bitcast.156, s32[2048]{0:T(1024)S(1)} %bitcast.157, s32[2048]{0:T(1024)S(1)} %bitcast.158, s32[2048]{0:T(1024)S(1)} %bitcast.159, s32[2048]{0:T(1024)S(1)} %bitcast.160, s32[2048]{0:T(1024)S(1)} %bitcast.161, s32[2048]{0:T(1024)S(1)} %bitcast.162, s32[2048]{0:T(1024)S(1)} %bitcast.163, ...), kind=kOutput, calls=%fused_computation.19 | convolution fusion | flops 2273312768 | bytes 3235840 | tf_op jit(solution)/shard_map/dot_general | solution.py:230
  240.3 4.0 convert_reduce_fusion
  244.9 6.2 %concatenate.19 = f32[154029]{0:T(1024)} concatenate(f32[65536]{0:T(1024)S(1)} %bitcast.139, f32[88064]{0:T(1024)S(1)} %reshape.139, f32[256]{0:T(256)S(1)} %get-tuple-element.89, f32[172]{0:T(256)S(1)} %get-tuple-element.59, f32[1]{0:T(128)} %bitcast.35), dimensions={0} | concatenate | bytes 1232232 | tf_op jit(solution)/shard_map/concatenate | solution.py:303
  251.7 145.1 %all-reduce.5.cloned.1.call-done = f32[154029]{0:T(1024)} async-done(((f32[154029]{0:T(1024)}), f32[154029]{0:T(1024)}) %all-reduce.5.cloned.1.call-update) | async-done | bytes 616132 | tf_op jit(solution)/shard_map/psum | solution.py:304
  396.8 1.0 slice.195
  397.9 0.7 multiply_reduce_fusion.2
  399.7 1.7 fusion.58
  403.1 0.5 convolution_add_fusion.3
  404.5 0.5 convolution_add_fusion.2
  405.7 0.5 convolution_add_fusion.1
  407.0 0.5 convolution_add_fusion
  408.3 0.5 fusion.73
  408.8 0.7 dynamic-slice_bitcast_fusion
  409.4 0.7 fusion.54
  410.6 0.6 convolution_add_fusion.8
  411.2 0.6 fusion.63
  412.7 0.6 fusion.64
  414.1 0.6 fusion.65
  415.5 0.6 fusion.66
  417.0 0.7 fusion.56
  417.7 0.7 copy.38
  418.4 0.6 slice.194
  419.0 0.6 divide_subtract_fusion
  (95 shorter events, 11.7 us)
Async XLA Ops:
  7.2 113.3 %copy-start.11 = (f32[428]{0:T(512)S(1)}, f32[428]{0:T(512)}, u32[]{:S(2)}) copy-start(f32[428]{0:T(512)} %param.27) | copy-start | bytes 5140
  7.2 158.4 %all-gather.3.cloned.1.call-start = ((), (), s32[]{:S(2)}) async-start(), calls=%async_computation | async-start | bytes 5242880 | tf_op jit(solution)/shard_map/all_gather | solution.py:269
  13.1 107.6 %copy-start.9 = (s32[512]{0:T(512)S(1)}, s32[512]{0:T(512)}, u32[]{:S(2)}) copy-start(s32[512]{0:T(512)} %param.22) | copy-start | bytes 6148
  13.1 107.6 %copy-start.7 = (s32[512,10]{0,1:T(8,128)S(1)}, s32[512,10]{0,1:T(8,128)}, u32[]{:S(2)}) copy-start(s32[512,10]{0,1:T(8,128)} %param.20) | copy-start | bytes 61444
  72.7 47.8 %copy-start.6 = (bf16[4,176,128]{2,1,0:T(8,128)(2,1)S(1)}, bf16[4,176,128]{2,1,0:T(8,128)(2,1)}, u32[]{:S(2)}) copy-start(bf16[4,176,128]{2,1,0:T(8,128)(2,1)} %get-tuple-element.19) | copy-start | bytes 540676
  120.4 101.2 %all-gather.5.cloned.1.call-start = ((), (), s32[]{:S(2)}) async-start(), calls=%async_computation.1 | async-start | bytes 2621440 | tf_op jit(solution)/shard_map/all_gather | solution.py:293
  165.6 5.4 %copy-start.14 = (bf16[256,8192]{1,0:T(8,128)(2,1)S(1)}, bf16[256,8192]{1,0:T(8,128)(2,1)}, u32[]{:S(2)}) copy-start(bf16[256,8192]{1,0:T(8,128)(2,1)} %all-gather.3.cloned.1.call-done) | copy-start | bytes 12582916
  171.0 17.5 %copy-start.10 = (s32[512]{0:T(512)S(1)}, s32[512]{0:T(512)}, u32[]{:S(2)}) copy-start(s32[512]{0:T(512)} %param.21) | copy-start | bytes 6148
  188.2 2.3 copy-start.8
  190.2 206.6 %all-reduce.5.cloned.1.call-start = ((), (), s32[]{:S(2)}) async-start(), calls=%async_computation.2 | async-start | bytes 1236992 | tf_op jit(solution)/shard_map/psum | solution.py:304
  221.6 18.7 %copy-start.15 = (f32[256,2048]{1,0:T(8,128)S(1)}, f32[256,2048]{1,0:T(8,128)}, u32[]{:S(2)}) copy-start(f32[256,2048]{1,0:T(8,128)} %get-tuple-element.24) | copy-start | bytes 6291460
  221.6 18.7 %copy-start.16 = (bf16[512,2048]{1,0:T(8,128)(2,1)S(1)}, bf16[512,2048]{1,0:T(8,128)(2,1)}, u32[]{:S(2)}) copy-start(bf16[512,2048]{1,0:T(8,128)(2,1)} %all-gather.5.cloned.1.call-done) | copy-start | bytes 6291460
  240.3 4.0 copy-start.1
  244.3 6.9 %copy-start.2 = (f32[4,176,128]{2,1,0:T(8,128)S(1)}, f32[4,176,128]{2,1,0:T(8,128)}, u32[]{:S(2)}) copy-start(f32[4,176,128]{2,1,0:T(8,128)} %get-tuple-element.27) | copy-start | bytes 1081348
  244.3 7.2 %copy-start.4 = (f32[4,64,256]{2,1,0:T(8,128)S(1)}, f32[4,64,256]{2,1,0:T(8,128)}, u32[]{:S(2)}) copy-start(f32[4,64,256]{2,1,0:T(8,128)} %get-tuple-element.26) | copy-start | bytes 786436
  396.8 5.4 %copy-start = (f32[154029]{0:T(1024)S(1)}, f32[154029]{0:T(1024)}, u32[]{:S(2)}) copy-start(f32[154029]{0:T(1024)} %all-reduce.5.cloned.1.call-done) | copy-start | bytes 1848352
  404.1 5.3 %copy-start.3 = (f32[128,172]{0,1:T(8,128)S(1)}, f32[128,172]{0,1:T(8,128)}, u32[]{:S(2)}) copy-start(f32[128,172]{0,1:T(8,128)} %param.24) | copy-start | bytes 264196
  412.2 4.8 %copy-start.5 = (f32[64,256]{1,0:T(8,128)S(1)}, f32[64,256]{1,0:T(8,128)}, u32[]{:S(2)}) copy-start(f32[64,256]{1,0:T(8,128)} %param.23) | copy-start | bytes 196612
  412.2 6.7 %copy-start.12 = (f32[428]{0:T(512)S(1)}, f32[428]{0:T(512)}, u32[]{:S(2)}) copy-start(f32[428]{0:T(512)} %param.28) | copy-start | bytes 5140
  412.3 6.7 %copy-start.13 = (f32[428]{0:T(512)S(1)}, f32[428]{0:T(512)}, u32[]{:S(2)}) copy-start(f32[428]{0:T(512)} %param.29) | copy-start | bytes 5140
Sparse Core Ops, SparseCore 0:
  120.5 45.0 all-gather.2
  190.3 31.2 all-gather.4
  251.3 145.4 all-reduce.4

commit v2 on v1

v2 whole, which is shorter than its diff:
```python
import functools

import jax
import jax.numpy as jnp
from jax import lax
from jax.experimental import pallas as pl
from jax.experimental.pallas import tpu as pltpu
from jax.sharding import PartitionSpec as P

HID = 256
CLS = 172
CLS_PAD = 176
D_IN = 128
F1 = 15
F2 = 10
NS_ITERS = 5
STEP = 10
LAM = 0.5
MU = 0.95
WDECAY = 0.01
LR_BIAS = 0.05
BETA_ONE = 0.9
BETA_TWO = 0.999
EPSILON = 1e-08
NS_A = 3.4445
NS_B = -4.775
NS_C = 2.0315
HIGH = lax.Precision.HIGHEST
MESH = pl.DeviceIdType.MESH
BF = jnp.bfloat16
F32 = jnp.float32

DEV = 128
NAR = 4
OWN = 8192
CAP = 64
SRC = 8192
FRONT = 2048
SEED = 512


def all_to(t):
    return (t // NAR, t % NAR)


def pull_kernel(
    req, feat, w1, w2t, m1, m2t, idx2,
    pulled, gw1, gw2t, gm1, gm2t, gidx2,
    featb, featf, reqin, reqs, stage, sendbuf,
    feat_sem, req_send, req_recv, loc_sem, row_send, row_recv, nar_send, nar_recv,
):
    g = lax.axis_index("grp")
    y = lax.axis_index("nar")
    me = g * NAR + y

    load = pltpu.make_async_copy(feat, featb, feat_sem)
    load.start()

    barrier = pltpu.get_barrier_semaphore()

    def greet(i, c):
        pl.semaphore_signal(barrier, inc=1, device_id=all_to((me + i) % DEV), device_id_type=MESH)
        return c

    lax.fori_loop(1, DEV, greet, 0)
    pl.semaphore_wait(barrier, DEV - 1)

    def ask(i, c):
        t = (me + i * 37) % DEV
        pltpu.make_async_remote_copy(
            src_ref=req.at[t], dst_ref=reqin.at[me], send_sem=req_send, recv_sem=req_recv,
            device_id=all_to(t), device_id_type=MESH,
        ).start()
        return c

    lax.fori_loop(1, DEV, ask, 0)

    own = []
    for n, (a, b) in enumerate(((w1, gw1), (w2t, gw2t), (m1, gm1), (m2t, gm2t), (idx2, gidx2))):
        own.append(pltpu.make_async_copy(a, b.at[y], loc_sem.at[n]))
        own[-1].start()
        for d in range(1, NAR):
            pltpu.make_async_remote_copy(
                src_ref=a, dst_ref=b.at[y], send_sem=nar_send.at[n, d - 1], recv_sem=nar_recv.at[n, d - 1],
                device_id=(g, (y + d) % NAR), device_id_type=MESH,
            ).start()

    load.wait()

    def widen(i, c):
        rows = pl.ds(pl.multiple_of(i * 256, 256), 256)
        featf[rows, :] = featb[rows, :].astype(F32)
        return c

    lax.fori_loop(0, OWN // 256, widen, 0)

    mine = pltpu.make_async_copy(req.at[me], reqin.at[me], loc_sem.at[5])
    mine.start()
    mine.wait()
    got = reqin.at[pl.ds(0, DEV - 1)]
    pltpu.make_async_copy(got, got, req_recv).wait()
    fetch = pltpu.make_async_copy(reqin, reqs, loc_sem.at[6])
    fetch.start()
    fetch.wait()

    def serve(i, c):
        t = (me + i * 37) % DEV
        for r in range(CAP):
            stage[r:r + 1, :] = featf[pl.ds(reqs[t, 0, r], 1), :]
        slot = pl.ds(pl.multiple_of(i * CAP, CAP), CAP)
        sendbuf[slot, :] = stage[...].astype(BF)
        return t, slot

    def serve_far(i, c):
        t, slot = serve(i, c)
        pltpu.make_async_remote_copy(
            src_ref=sendbuf.at[slot], dst_ref=pulled.at[pl.ds(pl.multiple_of(me * CAP, CAP), CAP)],
            send_sem=row_send, recv_sem=row_recv, device_id=all_to(t), device_id_type=MESH,
        ).start()
        return c

    lax.fori_loop(1, DEV, serve_far, 0)
    serve(0, 0)
    pulled[pl.ds(pl.multiple_of(me * CAP, CAP), CAP), :] = sendbuf[0:CAP, :]

    for n, (a, b) in enumerate(((w1, gw1), (w2t, gw2t), (m1, gm1), (m2t, gm2t), (idx2, gidx2))):
        own[n].wait()
        for d in range(1, NAR):
            pltpu.make_async_remote_copy(
                src_ref=a, dst_ref=b.at[y], send_sem=nar_send.at[n, d - 1], recv_sem=nar_recv.at[n, d - 1],
                device_id=(g, (y + d) % NAR), device_id_type=MESH,
            ).wait()
    sent = req.at[pl.ds(0, DEV - 1)]
    pltpu.make_async_copy(sent, sent, req_send).wait()
    gone = sendbuf.at[pl.ds(0, (DEV - 1) * CAP)]
    pltpu.make_async_copy(gone, gone, row_send).wait()
    come = pulled.at[pl.ds(0, (DEV - 1) * CAP)]
    pltpu.make_async_copy(come, come, row_recv).wait()


def pull(req, feat, w1, w2t, m1, m2t, idx2):
    vm = pl.BlockSpec(memory_space=pltpu.VMEM)
    small = (w1, w2t, m1, m2t, idx2)
    return pl.pallas_call(
        pull_kernel,
        out_shape=[jax.ShapeDtypeStruct((SRC, D_IN), BF)]
        + [jax.ShapeDtypeStruct((NAR,) + a.shape, a.dtype) for a in small],
        in_specs=[vm, pl.BlockSpec(memory_space=pl.ANY)] + [vm] * 5,
        out_specs=[vm] * 6,
        scratch_shapes=[
            pltpu.VMEM((OWN, D_IN), BF),
            pltpu.VMEM((OWN, D_IN), F32),
            pltpu.VMEM((DEV, 1, 128), jnp.int32),
            pltpu.SMEM((DEV, 1, 128), jnp.int32),
            pltpu.VMEM((CAP, D_IN), F32),
            pltpu.VMEM((DEV * CAP, D_IN), BF),
            pltpu.SemaphoreType.DMA,
            pltpu.SemaphoreType.DMA,
            pltpu.SemaphoreType.DMA,
            pltpu.SemaphoreType.DMA((7,)),
            pltpu.SemaphoreType.DMA,
            pltpu.SemaphoreType.DMA,
            pltpu.SemaphoreType.DMA((5, 3)),
            pltpu.SemaphoreType.DMA((5, 3)),
        ],
        compiler_params=pltpu.CompilerParams(
            collective_id=0, has_side_effects=True, vmem_limit_bytes=56 * 2**20
        ),
    )(req, feat, *small)


P1 = 33
P2 = 44
PIECES = P1 + P2
SEEDS_ALL = SEED * DEV


def dot(a, b, dims=((1,), (0,))):
    return lax.dot_general(a, b, (dims, ((), ())), preferred_element_type=F32)


NN = ((1,), (0,))
NT = ((1,), (1,))


def split(a):
    hi = a.astype(BF)
    return hi, (a - hi.astype(F32)).astype(BF)


def dot3(a, b, dims):
    (ah, al), (bh, bl) = a, b
    return dot(ah, bh, dims) + (dot(ah, bl, dims) + dot(al, bh, dims))


def ns_step(x):
    xs = split(x)
    gram = dot3(xs, xs, NT)
    gs = split(gram)
    mix = NS_B * gram + NS_C * dot3(gs, gs, NN)
    return NS_A * x + dot3(split(mix), xs, NN)


def spread(row):
    return jnp.broadcast_to(row, (128, 128)).T


def step_kernel(
    idx, inv, pulled, gw1, gw2t, gm1, gm2t, idx2, gidx2, labels, live, bias, biasm, biasv, w1own, w2own,
    o_loss, o_first, o_second, o_mom1, o_mom2, o_flow, o_slow, o_bias, o_bm, o_bv,
    table, near, own, a1, z1t, gbuf, fsel, bsel, rbuf, dbuf, dh1, w1t, w2, b1c, b2c, pay1, pay2, misc,
    inbox, res1, res2, mine, x1s, x2s,
    h_send, h_recv, r_send, r_recv, d_send, d_recv, rs_send, rs_recv, ag_send, ag_recv,
):
    g = lax.axis_index("grp")
    y = lax.axis_index("nar")
    me = g * NAR + y
    left, right, opp = (y + 3) % NAR, (y + 1) % NAR, (y + 2) % NAR

    barrier = pltpu.get_barrier_semaphore()

    def greet(i, c):
        pl.semaphore_signal(barrier, inc=1, device_id=all_to((me + i) % DEV), device_id_type=MESH)
        return c

    lax.fori_loop(1, DEV, greet, 0)

    def link(src, dst, ssem, rsem, to):
        return pltpu.make_async_remote_copy(
            src_ref=src, dst_ref=dst, send_sem=ssem, recv_sem=rsem, device_id=(g, to), device_id_type=MESH
        )

    def widen(i, c):
        rows = pl.ds(pl.multiple_of(i * 256, 256), 256)
        table[rows, :] = pulled[rows, :].astype(F32)
        return c

    lax.fori_loop(0, SRC // 256, widen, 0)
    table[SRC:SRC + 8, :] = jnp.zeros((8, D_IN), F32)
    w1t[...] = gw1[...].reshape(2 * D_IN, HID).T
    w2t = jnp.concatenate([gw2t[q] for q in range(NAR)], axis=1)
    w2[...] = w2t.T
    b1c[...] = jnp.concatenate([spread(bias[0:1, :]), spread(bias[1:2, :])], axis=0)
    b2c[...] = jnp.concatenate([spread(bias[2:3, :]), spread(bias[3:4, :])], axis=0)

    iota16 = lax.broadcasted_iota(jnp.int32, (16, 128), 0).astype(jnp.int16)
    one, zero = jnp.ones((16, 128), BF), jnp.zeros((16, 128), BF)

    def select(ids, base, groups, put):
        ids = ids - base
        rows = [
            [jnp.broadcast_to(ids[k:k + 1, c * 128:(c + 1) * 128], (16, 128)).astype(jnp.int16) for c in range(4)]
            for k in range(1 + F2)
        ]

        def body(i, carry):
            here = iota16 + jnp.full((16, 128), i * 16, jnp.int32).astype(jnp.int16)
            out = pl.ds(pl.multiple_of(i * 16, 16), 16)
            for c in range(4):
                acc = jnp.where(here == rows[1][c], one, zero)
                for k in range(2, 1 + F2):
                    acc = acc + jnp.where(here == rows[k][c], one, zero)
                put(out, c * 128, acc)
                put(out, SEED + c * 128, jnp.where(here == rows[0][c], one, zero))
            return carry

        lax.fori_loop(0, groups, body, 0)

    def put_f(rows, col, v):
        fsel[rows, col:col + 128] = v

    select(idx2[...], 0, SRC // 16, put_f)
    for q in range(NAR):
        def put_b(rows, col, v, q=q):
            bsel[q, rows, col:col + 128] = v

        select(gidx2[q], y * FRONT, FRONT // 16, put_b)

    pl.semaphore_wait(barrier, DEV - 1)

    view = table.reshape(SRC + 8, 1, D_IN)

    def cols(b):
        return pl.ds(pl.multiple_of(b * 256, 256), 256)

    def forward(b):
        @pl.when(b % 2 == 0)
        def _():
            blk = gbuf.at[left, :, cols(b)]
            link(blk, blk, h_send.at[0, b], h_recv.at[0, b], right).wait_recv()
            link(blk, blk, h_send.at[2, b], h_recv.at[2, b], right).start()

        @pl.when(b % 2 == 1)
        def _():
            blk = gbuf.at[right, :, cols(b)]
            link(blk, blk, h_send.at[1, b], h_recv.at[1, b], left).wait_recv()
            link(blk, blk, h_send.at[2, b], h_recv.at[2, b], left).start()

    def block(b, c):
        def some(i, c2):
            base = pl.multiple_of(b * 256 + i * 8, 8)
            for j in range(8):
                m = base + j
                own[pl.ds(m, 1), :] = view[idx[0, m]]
                rows = [view[idx[1 + k, m]] for k in range(F1)]
                while len(rows) > 1:
                    rows = [p + q for p, q in zip(rows[::2], rows[1::2])] + ([rows[-1]] if len(rows) % 2 else [])
                near[pl.ds(m, 1), :] = rows[0] * inv[0, m]
            return c2

        lax.fori_loop(0, 32, some, 0)
        rows = cols(b)
        act = jnp.concatenate([own[rows, :].astype(BF), near[rows, :].astype(BF)], axis=1)
        a1[rows, :] = act
        z = dot(w1t[...], act, NT) + jnp.concatenate([b1c[...], b1c[...]], axis=1)
        z1t[:, rows] = z
        gbuf[y, :, rows] = (z / (1.0 + jnp.exp(-z))).astype(BF)
        blk = gbuf.at[y, :, rows]
        link(blk, blk, h_send.at[0, b], h_recv.at[0, b], right).start()
        link(blk, blk, h_send.at[1, b], h_recv.at[1, b], left).start()

        @pl.when(b > 0)
        def _():
            forward(b - 1)

        return c

    lax.fori_loop(0, 8, block, 0)
    forward(7)

    def from_source(q):
        return dot(gbuf[q], fsel[pl.ds(pl.multiple_of(q * FRONT, FRONT), FRONT), :])

    total = from_source(y)
    for b in range(1, 8, 2):
        blk = gbuf.at[left, :, b * 256:(b + 1) * 256]
        link(blk, blk, h_send.at[0, b], h_recv.at[0, b], right).wait_recv()
    total = total + from_source(left)
    for b in range(0, 8, 2):
        blk = gbuf.at[right, :, b * 256:(b + 1) * 256]
        link(blk, blk, h_send.at[1, b], h_recv.at[1, b], left).wait_recv()
    total = total + from_source(right)
    for b in range(8):
        blk = gbuf.at[opp, :, b * 256:(b + 1) * 256]
        link(blk, blk, h_send.at[2, b], h_recv.at[2, b], right).wait_recv()
    total = total + from_source(opp)

    def inverse_count(ids):
        n = jnp.sum((ids[1:1 + F2, :] >= 0).astype(F32), axis=0, keepdims=True)
        return 1.0 / jnp.maximum(n, 1.0)

    near2 = (total[:, :SEED] * inverse_count(idx2[...])).astype(BF)
    self2 = total[:, SEED:].astype(BF)
    alive = live[...].astype(F32)
    diff = self2.astype(F32) - near2.astype(F32)

    def swap_start(buf, ssem, rsem):
        blk = buf.at[y]
        link(blk, blk, ssem.at[0], rsem.at[0], right).start()
        link(blk, blk, ssem.at[1], rsem.at[1], left).start()

    def swap_forward(buf, ssem, rsem, cut):
        blk = buf.at[left]
        link(blk, blk, ssem.at[0], rsem.at[0], right).wait_recv()
        half = buf.at[left, 0:cut, :]
        link(half, half, ssem.at[2], rsem.at[2], right).start()
        blk = buf.at[right]
        link(blk, blk, ssem.at[1], rsem.at[1], left).wait_recv()
        half = buf.at[right, cut:, :]
        link(half, half, ssem.at[3], rsem.at[3], left).start()

    def swap_end(buf, ssem, rsem, cut):
        half = buf.at[opp, 0:cut, :]
        link(half, half, ssem.at[2], rsem.at[2], right).wait_recv()
        half = buf.at[opp, cut:, :]
        link(half, half, ssem.at[3], rsem.at[3], left).wait_recv()

    def swap_sent(buf, ssem, rsem, cut):
        blk = buf.at[y]
        link(blk, blk, ssem.at[0], rsem.at[0], right).wait_send()
        link(blk, blk, ssem.at[1], rsem.at[1], left).wait_send()
        half = buf.at[left, 0:cut, :]
        link(half, half, ssem.at[2], rsem.at[2], right).wait_send()
        half = buf.at[right, cut:, :]
        link(half, half, ssem.at[3], rsem.at[3], left).wait_send()

    rbuf[y] = (2.0 * LAM / HID / SEEDS_ALL * alive * diff).astype(BF)
    swap_start(rbuf, r_send, r_recv)

    act2 = jnp.concatenate([self2, near2], axis=0)
    w2t = jnp.concatenate([gw2t[q] for q in range(NAR)], axis=1)
    cls = lax.broadcasted_iota(jnp.int32, (CLS_PAD, SEED), 0)
    b2 = b2c[0:CLS_PAD, :]
    logits = dot(w2t, act2) + jnp.concatenate([b2] * 4, axis=1)
    logits = jnp.where(cls < CLS, logits, -1e30)
    top = jnp.max(logits, axis=0, keepdims=True)
    e = jnp.exp(logits - top)
    tot = jnp.sum(e, axis=0, keepdims=True)
    hot = cls == labels[...]
    picked = jnp.sum(jnp.where(hot, logits, 0.0), axis=0, keepdims=True)
    dlog = (alive * (e * (1.0 / tot) - jnp.where(hot, 1.0, 0.0)) * (1.0 / SEEDS_ALL)).astype(BF)
    dbuf[y] = dlog
    swap_start(dbuf, d_send, d_recv)

    terms = top + jnp.log(tot) - picked + LAM / HID * jnp.sum(diff * diff, axis=0, keepdims=True)
    loss = jnp.sum(alive * terms, axis=1, keepdims=True)
    g2t = dot(dlog, act2, NT).astype(BF)
    for q in range(NAR):
        pay2[q * CLS_PAD:(q + 1) * CLS_PAD, :] = g2t[:, q * 128:(q + 1) * 128]

    my_piece = (me * 77) % DEV

    def to_owner(pay, first, count):
        def body(i, c):
            t = (me + i) % DEV
            p = (t * 77) % DEV - first

            @pl.when((p >= 0) & (p < count))
            def _():
                pltpu.make_async_remote_copy(
                    src_ref=pay.at[pl.ds(pl.multiple_of(p * 16, 16), 16)], dst_ref=inbox.at[me],
                    send_sem=rs_send, recv_sem=rs_recv, device_id=all_to(t), device_id_type=MESH,
                ).start()

            return c

        lax.fori_loop(1, DEV, body, 0)

    def add_up(pay, res, first, count, ssem, rsem):
        q = my_piece - first

        @pl.when((q >= 0) & (q < count))
        def _():
            rows16 = pl.ds(pl.multiple_of(q * 16, 16), 16)
            got = inbox.at[pl.ds(0, DEV - 1)]
            pltpu.make_async_copy(got, got, rs_recv).wait()
            inbox[me] = pay[rows16, :]

            def body(i, acc):
                part = inbox[pl.ds(pl.multiple_of(i * 8, 8), 8)].astype(F32)
                return acc + jnp.sum(part, axis=0)

            res[rows16, :] = lax.fori_loop(0, DEV // 8, body, jnp.zeros((16, 128), F32))

            def tell(i, c):
                pltpu.make_async_remote_copy(
                    src_ref=res.at[rows16], dst_ref=res.at[rows16],
                    send_sem=ssem, recv_sem=rsem, device_id=all_to((me + i) % DEV), device_id_type=MESH,
                ).start()
                return c

            lax.fori_loop(1, DEV, tell, 0)

    def take(res, first, count, rsem):
        q = my_piece - first
        holds = (q >= 0) & (q < count)

        @pl.when(holds)
        def _():
            got = res.at[pl.ds(0, (count - 1) * 16)]
            pltpu.make_async_copy(got, got, rsem).wait()

        @pl.when(jnp.logical_not(holds))
        def _():
            got = res.at[pl.ds(0, count * 16)]
            pltpu.make_async_copy(got, got, rsem).wait()

    to_owner(pay2, P1, P2)

    def grads(q):
        da = dot(w2[...], dbuf[q])
        r = rbuf[q].astype(F32)
        ds = (da[:HID] + r).astype(BF)
        dn = ((da[HID:] - r) * inverse_count(gidx2[q])).astype(BF)
        return dot(jnp.concatenate([dn, ds], axis=1), bsel[q], NT)

    swap_forward(rbuf, r_send, r_recv, 128)
    dh1[...] = grads(y)
    swap_forward(dbuf, d_send, d_recv, 96)
    dh1[...] += grads(left)
    dh1[...] += grads(right)
    swap_end(rbuf, r_send, r_recv, 128)
    swap_end(dbuf, d_send, d_recv, 96)
    dh1[...] += grads(opp)
    add_up(pay2, res2, P1, P2, ag_send.at[0], ag_recv.at[0])

    z = z1t[...]
    sig = 1.0 / (1.0 + jnp.exp(-z))
    dz = (dh1[...] * sig * (1.0 + z * (1.0 - sig))).astype(BF)
    g1 = dot(dz, a1[...]).T.astype(BF)
    pay1[0:256, :] = g1[:, :128]
    pay1[256:512, :] = g1[:, 128:]
    ones_f = jnp.ones((8, FRONT), BF)
    ones_s = jnp.ones((8, SEED), BF)
    db1 = dot(ones_f, dz, NT)[0:1, :]
    db2 = dot(ones_s, dlog, NT)[0:1, :]
    misc[...] = jnp.zeros((16, 128), F32)

    def two(rows, v):
        hi = v.astype(BF).astype(F32)
        misc[rows:rows + 1, 0:v.shape[1]] = hi
        misc[rows + 4:rows + 5, 0:v.shape[1]] = v - hi

    two(0, db1[:, :128])
    two(1, db1[:, 128:])
    two(2, db2[:, :128])
    two(3, db2[:, 128:])
    hi = loss.astype(BF).astype(F32)
    misc[8:9, 0:1] = hi
    misc[9:10, 0:1] = loss - hi
    pay1[512:528, :] = misc[...].astype(BF)
    to_owner(pay1, 0, P1)

    take(res2, P1, P2, ag_recv.at[0])
    mom2 = jnp.concatenate(
        [MU * gm2t[q] + res2[q * CLS_PAD:(q + 1) * CLS_PAD, :] for q in range(NAR)], axis=1
    )
    for q in range(NAR):
        x2s[q] = mom2[:, q * 128:(q + 1) * 128]
    o_mom2[...] = x2s[y][0:CLS, :]
    x2 = mom2 * (1.0 / (jnp.sqrt(jnp.sum(mom2 * mom2, keepdims=True)) + 1e-07))
    for _ in range(3):
        x2 = ns_step(x2)
    add_up(pay1, res1, 0, P1, ag_send.at[1], ag_recv.at[1])
    for _ in range(NS_ITERS - 3):
        x2 = ns_step(x2)
    for q in range(NAR):
        x2s[q] = x2[:, q * 128:(q + 1) * 128]
    second = w2own[...] * (1.0 - WDECAY) - (2 * HID / CLS) ** 0.5 * x2s[y][0:CLS, :]
    o_second[...] = second
    o_slow[...] = second.astype(BF)

    take(res1, 0, P1, ag_recv.at[1])
    grad1 = jnp.concatenate([res1[0:256, :], res1[256:512, :]], axis=1)
    mom1 = MU * gm1[...].reshape(2 * D_IN, HID) + grad1
    x1s[...] = mom1
    block64 = pl.ds(pl.multiple_of(y * 64, 64), 64)
    o_mom1[...] = x1s[block64, :]
    x1 = mom1 * (1.0 / (jnp.sqrt(jnp.sum(mom1 * mom1, keepdims=True)) + 1e-07))
    for _ in range(NS_ITERS):
        x1 = ns_step(x1)
    x1s[...] = x1
    first_new = w1own[...] * (1.0 - WDECAY) - x1s[block64, :]
    o_first[...] = first_new
    o_flow[...] = first_new.astype(BF)

    gb = res1[512:516, :] + res1[516:520, :]
    m_new = BETA_ONE * biasm[...] + (1.0 - BETA_ONE) * gb
    v_new = BETA_TWO * biasv[...] + (1.0 - BETA_TWO) * gb * gb
    m_hat = m_new / (1.0 - BETA_ONE**STEP)
    v_hat = v_new / (1.0 - BETA_TWO**STEP)
    o_bias[...] = bias[...] * (1.0 - LR_BIAS * WDECAY) - LR_BIAS * m_hat / (jnp.sqrt(v_hat) + EPSILON)
    o_bm[...] = m_new
    o_bv[...] = v_new
    o_loss[...] = res1[520:521, :] + res1[521:522, :]

    for b in range(8):
        blk = gbuf.at[y, :, b * 256:(b + 1) * 256]
        link(blk, blk, h_send.at[0, b], h_recv.at[0, b], right).wait_send()
        link(blk, blk, h_send.at[1, b], h_recv.at[1, b], left).wait_send()
        blk = gbuf.at[opp, :, b * 256:(b + 1) * 256]
        link(blk, blk, h_send.at[2, b], h_recv.at[2, b], right).wait_send()
    swap_sent(rbuf, r_send, r_recv, 128)
    swap_sent(dbuf, d_send, d_recv, 96)

    owner = my_piece < PIECES

    @pl.when(owner)
    def _():
        gone = inbox.at[pl.ds(0, PIECES - 1)]
        pltpu.make_async_copy(gone, gone, rs_send).wait()

    @pl.when(jnp.logical_not(owner))
    def _():
        gone = inbox.at[pl.ds(0, PIECES)]
        pltpu.make_async_copy(gone, gone, rs_send).wait()

    for n, (lo, hi) in enumerate(((P1, PIECES), (0, P1))):
        @pl.when((my_piece >= lo) & (my_piece < hi))
        def _():
            gone = mine.at[pl.ds(0, DEV - 1)]
            pltpu.make_async_copy(gone, gone, ag_send.at[n]).wait()


def step(idx, inv, pulled, gw1, gw2t, gm1, gm2t, idx2, gidx2, labels, live, bias, biasm, biasv, w1own, w2own):
    vm = pl.BlockSpec(memory_space=pltpu.VMEM)
    sm = pl.BlockSpec(memory_space=pltpu.SMEM)
    dma = pltpu.SemaphoreType.DMA
    sds = jax.ShapeDtypeStruct
    return pl.pallas_call(
        step_kernel,
        out_shape=[
            sds((1, 128), F32), sds((64, HID), F32), sds((CLS, 128), F32), sds((64, HID), F32), sds((CLS, 128), F32),
            sds((64, HID), BF), sds((CLS, 128), BF), sds((4, 128), F32), sds((4, 128), F32), sds((4, 128), F32),
        ],
        in_specs=[sm, sm] + [vm] * 14,
        out_specs=[vm] * 10,
        scratch_shapes=[
            pltpu.VMEM((SRC + 8, D_IN), F32),
            pltpu.VMEM((FRONT, D_IN), F32),
            pltpu.VMEM((FRONT, D_IN), F32),
            pltpu.VMEM((FRONT, 2 * D_IN), BF),
            pltpu.VMEM((HID, FRONT), F32),
            pltpu.VMEM((NAR, HID, FRONT), BF),
            pltpu.VMEM((SRC, 2 * SEED), BF),
            pltpu.VMEM((NAR, FRONT, 2 * SEED), BF),
            pltpu.VMEM((NAR, HID, SEED), BF),
            pltpu.VMEM((NAR, CLS_PAD, SEED), BF),
            pltpu.VMEM((HID, FRONT), F32),
            pltpu.VMEM((HID, 2 * D_IN), BF),
            pltpu.VMEM((2 * HID, CLS_PAD), BF),
            pltpu.VMEM((HID, 128), F32),
            pltpu.VMEM((HID, 128), F32),
            pltpu.VMEM((P1 * 16, 128), BF),
            pltpu.VMEM((P2 * 16, 128), BF),
            pltpu.VMEM((16, 128), F32),
            pltpu.VMEM((DEV, 16, 128), BF),
            pltpu.VMEM((P1 * 16, 128), F32),
            pltpu.VMEM((P2 * 16, 128), F32),
            pltpu.VMEM((DEV, 16, 128), F32),
            pltpu.VMEM((2 * D_IN, HID), F32),
            pltpu.VMEM((NAR, CLS_PAD, 128), F32),
            dma((3, 8)), dma((3, 8)), dma((4,)), dma((4,)), dma((4,)), dma((4,)), dma, dma, dma((2,)), dma((2,)),
        ],
        compiler_params=pltpu.CompilerParams(
            collective_id=1, has_side_effects=True, vmem_limit_bytes=62 * 2**20
        ),
    )(idx, inv, pulled, gw1, gw2t, gm1, gm2t, idx2, gidx2, labels, live, bias, biasm, biasv, w1own, w2own)


def as_rows(v):
    return jnp.pad(v, (0, 512 - v.shape[0])).reshape(4, 128)


def per_device(
    features, requests, index_one, mask_one, index_two, mask_two, labels, seed_live,
    w_first, w_second, mom_first, mom_second, biases, bias_m, bias_v,
):
    idx_one, msk_one = index_one.T, mask_one.T
    idx_two, msk_two = index_two.T, mask_two.T
    idx_one = jnp.concatenate([idx_one[:1], jnp.where(msk_one > 0, idx_one[1:], SRC)], axis=0)
    inv_one = 1.0 / jnp.maximum(jnp.sum(msk_one.astype(F32), axis=0, keepdims=True), 1.0)
    idx_two = jnp.concatenate(
        [idx_two[:1], jnp.where(msk_two > 0, idx_two[1:], -1), jnp.zeros((5, SEED), jnp.int32)], axis=0
    )
    w2t = jnp.pad(w_second.astype(BF).T, ((0, CLS_PAD - CLS), (0, 0)))
    m2t = jnp.pad(mom_second.T, ((0, CLS_PAD - CLS), (0, 0)))
    req = jnp.pad(requests, ((0, 0), (0, 64))).reshape(DEV, 1, 128)
    pulled, gw1, gw2t, gm1, gm2t, gidx2 = pull(
        req, features, w_first.astype(BF), w2t, mom_first, m2t, idx_two
    )
    loss, first_new, second_new, mom_one, mom_two, first_low, second_low, bias_new, m_new, v_new = step(
        idx_one, inv_one, pulled, gw1, gw2t, gm1, gm2t, idx_two, gidx2, labels[None, :], seed_live[None, :],
        as_rows(biases), as_rows(bias_m), as_rows(bias_v), w_first, w_second.T,
    )
    n = HID + CLS
    return (
        loss[0, 0], first_new, second_new.T, mom_one, mom_two.T, first_low, second_low.T,
        bias_new.reshape(512)[:n], m_new.reshape(512)[:n], v_new.reshape(512)[:n],
    )


def solution(mesh):
    both = ("grp", "nar")
    placed = (
        P(both, None), P(both, None), P(both, None), P(both, None), P(both, None), P(both, None),
        P(both), P(both), P("nar", None), P("nar", None), P("nar", None), P("nar", None), P(), P(), P(),
    )
    nar = P("nar", None)
    return jax.shard_map(
        per_device, mesh=mesh, in_specs=placed,
        out_specs=(P(), nar, nar, nar, nar, nar, nar, P(), P(), P()), check_vma=False,
    )
```

time: 431 us -> 223 us (0.52)
  waiting for transfers between devices: 220 us -> 0 us
  Pallas kernels: 97.6 us -> 192 us
  matrix products: 59.7 us -> 0 us
  between operations: 16 us -> 2.36 us
  other arithmetic: 13.5 us -> 7.02 us
    psum x1 -> x0, waiting for transfers between devices: 145 us -> none  [per_device(): flat = lax.psum(flat, ('grp', 'nar'))]
    pallas_call x1, Pallas kernels: 43.2 us -> 138 us  [step(): pl.pallas_call(step_kernel, out_shape=[sds((1, 128), F32), sds((64, HID),...]
    all_gather x2 -> x0, waiting for transfers between devices: 74.9 us -> none  [the longest x1 44.9 us: per_device(): group = lax.all_gather(h1t, 'nar', axis=1, tiled=True)]
    dot_general x38 -> x0, matrix products: 59.7 us -> none  [dot(): lax.dot_general(a, b, (dims, ((), ())), preferred_element_type=F32, preci...]
    unnamed x41 -> x10, local copies, waits for them, and re-layouts: 1.97 us -> 13.4 us
    concatenate x1 -> x0, local copies, waits for them, and re-layouts: 6.24 us -> none  [per_device(): jnp.concatenate([g1t.reshape(-1), g2t.reshape(-1), db1, db2, loss[None]])]
  transfers between devices with their start and end apart: 3 -> 0, of which waited for: 3 -> 0; matrix products, arithmetic and copies ran while one was open for 0% -> 0% of each run, Pallas kernels for 0% -> 0%
where the time goes in v2:
time: 223 us; the launch traced here: 222 us
  Pallas kernels  192 us (86%)
  local copies, waits for them, and re-layouts  20.4 us (9%)
  other arithmetic  7.02 us (3%)
  between operations  2.36 us (1%)
    pallas_call x1, Pallas kernels, step(): pl.pallas_call(step_kernel, out_shape=[sds((1, 128), F32), sds((64, HID),...  138 us
    pallas_call x1, Pallas kernels, pull(): pl.pallas_call(pull_kernel, out_shape=[jax.ShapeDtypeStruct((SRC, D_IN),...  54.4 us
    unnamed x10, local copies, waits for them, and re-layouts  13.4 us

profile of v2, /device:TPU:1, one launch (start us, length us, event | category | flops | bytes accessed | tf_op | source)
XLA Modules:
  0.0 222.1 jit_solution(12682613982004515953)
XLA Ops:
  0.7 0.1 pad.30.clone
  0.7 0.7 slice.34
  1.4 1.3 pad_bitcast_fusion.2.bias
  2.7 1.3 pad_bitcast_fusion
  4.0 0.8 slice.32
  4.8 0.9 convert_reduce_fusion
  5.8 0.6 maximum_divide_fusion
  6.4 0.8 slice_select_fusion.1
  7.2 0.7 add_add_fusion.idx2
  7.8 1.5 convert_element_type.19.w1
  9.3 0.9 convert_bitcast_fusion
  10.2 0.6 pad.23.w2t
  10.8 0.8 copy.25
  11.7 0.6 pad.22
  12.3 1.5 pad.24.m2t
  13.9 1.0 slice_select_fusion
  14.8 0.7 pad_add_fusion.idx
  15.5 54.4 %shard_map.222 = (bf16[8192,128]{1,0:T(8,128)(2,1)}, bf16[4,64,256]{2,1,0:T(8,128)(2,1)}, bf16[4,176,128]{2,1,0:T(8,128)(2,1)}, f32[4,64,256]{2,1,0:T(8,128)}, f...) custom-call(s32[128,1,128]{2,1,0:T(1,128)} %bitcast.32, bf16[8192,128]{1,0:T(8,128)(2,1)} %feat.1, ...), custom_call_target="tpu_custom_call" | custom-call | tf_op jit(solution)/shard_map/pallas_call | solution.py:144
  69.9 138.0 %shard_map.223 = (f32[1,128]{1,0:T(1,128)}, f32[64,256]{1,0:T(8,128)}, f32[172,128]{1,0:T(8,128)}, f32[64,256]{1,0:T(8,128)}, f32[172,128]{1,0:T(8,128)}, /*inde...) custom-call(s32[16,2048]{1,0:T(8,128)} %pad_add_fusion.idx, ...), custom_call_target="tpu_custom_call" | custom-call | tf_op jit(solution)/shard_map/pallas_call | solution.py:590
  208.4 1.5 copy.37
  209.9 1.5 copy.38
  211.4 1.5 copy.39
  212.9 1.5 copy.40
  214.4 1.4 copy.41
  215.8 1.4 copy.42
  217.2 1.2 copy.43
  218.5 1.3 copy.44
  219.7 1.3 copy.45
  (1 shorter events, 0.0 us)

commit v3 on v2

v3 whole, which is shorter than its diff:
```python
import functools

import jax
import jax.numpy as jnp
from jax import lax
from jax.experimental import pallas as pl
from jax.experimental.pallas import tpu as pltpu
from jax.sharding import PartitionSpec as P

HID = 256
CLS = 172
CLS_PAD = 176
D_IN = 128
F1 = 15
F2 = 10
NS_ITERS = 5
STEP = 10
LAM = 0.5
MU = 0.95
WDECAY = 0.01
LR_BIAS = 0.05
BETA_ONE = 0.9
BETA_TWO = 0.999
EPSILON = 1e-08
NS_A = 3.4445
NS_B = -4.775
NS_C = 2.0315
HIGH = lax.Precision.HIGHEST
MESH = pl.DeviceIdType.MESH
BF = jnp.bfloat16
F32 = jnp.float32

DEV = 128
NAR = 4
OWN = 8192
CAP = 64
SRC = 8192
FRONT = 2048
SEED = 512


def all_to(t):
    return (t // NAR, t % NAR)


P1 = 33
P2 = 44
PIECES = P1 + P2
SEEDS_ALL = SEED * DEV


def dot(a, b, dims=((1,), (0,))):
    return lax.dot_general(a, b, (dims, ((), ())), preferred_element_type=F32)


NN = ((1,), (0,))
NT = ((1,), (1,))


def split(a):
    hi = a.astype(BF)
    return hi, (a - hi.astype(F32)).astype(BF)


def dot3(a, b, dims):
    (ah, al), (bh, bl) = a, b
    return dot(ah, bh, dims) + (dot(ah, bl, dims) + dot(al, bh, dims))


def ns_step(x):
    xs = split(x)
    gram = dot3(xs, xs, NT)
    gs = split(gram)
    mix = NS_B * gram + NS_C * dot3(gs, gs, NN)
    return NS_A * x + dot3(split(mix), xs, NN)


def spread(row):
    return jnp.broadcast_to(row, (128, 128)).T


def main_kernel(
    reqt, feat, idx1t, msk1t, idx2t, msk2t, labels, live, w1, w2own, m1, m2own, bias,
    o_res1, o_gm1, o_mom2, o_x2,
    table, featb, pulled, stage, reqv, reqin, idxv, invv, near, own, a1, z1t, gbuf, fsel, bsel, rbuf, dbuf, dh1,
    gw1, gw2t, gm2t, gidx2, w1t, w2, b1c, b2c, pay1, pay2, misc, inbox, res2, x2s,
    reqs, idx, inv,
    feat_sem, loc_sem, req_send, req_recv, row_send, row_recv, nar_send, nar_recv,
    h_send, h_recv, r_send, r_recv, d_send, d_recv, rs_send, rs_recv, ag_send, ag_recv,
):
    g = lax.axis_index("grp")
    y = lax.axis_index("nar")
    me = g * NAR + y
    left, right, opp = (y + 3) % NAR, (y + 1) % NAR, (y + 2) % NAR

    load = pltpu.make_async_copy(feat, featb, feat_sem)
    load.start()

    barrier = pltpu.get_barrier_semaphore()

    def greet(i, c):
        pl.semaphore_signal(barrier, inc=1, device_id=all_to((me + i) % DEV), device_id_type=MESH)
        return c

    lax.fori_loop(1, DEV, greet, 0)

    def link(src, dst, ssem, rsem, to):
        return pltpu.make_async_remote_copy(
            src_ref=src, dst_ref=dst, send_sem=ssem, recv_sem=rsem, device_id=(g, to), device_id_type=MESH
        )

    reqv[...] = jnp.concatenate([reqt[...], jnp.zeros((DEV - CAP, DEV), jnp.int32)], axis=0).T
    ask_rows = reqv.reshape(DEV, 1, 128)
    got_rows = reqin.reshape(DEV, 1, 128)

    gw1[y] = w1[...].astype(BF)
    pad = CLS_PAD - CLS
    gw2t[y] = jnp.concatenate([w2own[...], jnp.zeros((pad, 128), F32)], axis=0).astype(BF)
    o_gm1[y] = m1[...]
    gm2t[y] = jnp.concatenate([m2own[...], jnp.zeros((pad, 128), F32)], axis=0)
    gidx2[y] = jnp.concatenate(
        [idx2t[0:1, :], jnp.where(msk2t[...] > 0, idx2t[1:, :], -1), jnp.zeros((5, SEED), jnp.int32)], axis=0
    )
    shared = (gidx2, gw1, gw2t, o_gm1, gm2t)

    pl.semaphore_wait(barrier, DEV - 1)

    def ask(i, c):
        t = (me + i * 37) % DEV
        pltpu.make_async_remote_copy(
            src_ref=ask_rows.at[t], dst_ref=got_rows.at[me], send_sem=req_send, recv_sem=req_recv,
            device_id=all_to(t), device_id_type=MESH,
        ).start()
        return c

    lax.fori_loop(1, DEV, ask, 0)
    for n, a in enumerate(shared):
        for d in range(1, NAR):
            link(a.at[y], a.at[y], nar_send.at[n, d - 1], nar_recv.at[n, d - 1], (y + d) % NAR).start()

    reqin[pl.ds(me, 1), :] = reqv[pl.ds(me, 1), :]
    msk = msk1t[...]
    idxv[0:1, :] = idx1t[0:1, :]
    idxv[1:16, :] = jnp.where(msk > 0, idx1t[1:16, :], SRC)
    invv[...] = 1.0 / jnp.maximum(jnp.sum(msk.astype(F32), axis=0, keepdims=True), 1.0)
    to_smem = [pltpu.make_async_copy(idxv, idx, loc_sem.at[0]), pltpu.make_async_copy(invv, inv, loc_sem.at[1])]
    for c in to_smem:
        c.start()

    load.wait()

    def widen_features(i, c):
        rows = pl.ds(pl.multiple_of(i * 256, 256), 256)
        table[rows, :] = featb[rows, :].astype(F32)
        return c

    lax.fori_loop(0, OWN // 256, widen_features, 0)

    got = got_rows.at[pl.ds(0, DEV - 1)]
    pltpu.make_async_copy(got, got, req_recv).wait()
    fetch = pltpu.make_async_copy(reqin, reqs, loc_sem.at[2])
    fetch.start()
    fetch.wait()

    view = table.reshape(SRC + 8, 1, D_IN)
    my_rows = pl.ds(pl.multiple_of(me * CAP, CAP), CAP)

    def serve(i, c):
        t = (me + i * 37) % DEV
        for r in range(CAP):
            stage[r:r + 1, :] = view[reqs[t, r]]
        slot = pl.ds(pl.multiple_of(i * CAP, CAP), CAP)
        featb[slot, :] = stage[...].astype(BF)

        @pl.when(i > 0)
        def _():
            pltpu.make_async_remote_copy(
                src_ref=featb.at[slot], dst_ref=pulled.at[my_rows],
                send_sem=row_send, recv_sem=row_recv, device_id=all_to(t), device_id_type=MESH,
            ).start()

        return c

    lax.fori_loop(1, DEV, serve, 0)
    serve(0, 0)
    pulled[my_rows, :] = featb[0:CAP, :]

    for n, a in enumerate(shared):
        for d in range(1, NAR):
            link(a.at[y], a.at[y], nar_send.at[n, d - 1], nar_recv.at[n, d - 1], (y + d) % NAR).wait()
    w1t[...] = gw1[...].reshape(2 * D_IN, HID).T
    w2t = jnp.concatenate([gw2t[q] for q in range(NAR)], axis=1)
    w2[...] = w2t.T
    b1c[...] = jnp.concatenate([spread(bias[0:1, 0:128]), spread(bias[0:1, 128:256])], axis=0)
    last = jnp.concatenate([bias[0:1, 384:428], jnp.zeros((1, 84), F32)], axis=1)
    b2c[...] = jnp.concatenate([spread(bias[0:1, 256:384]), spread(last)], axis=0)

    iota16 = lax.broadcasted_iota(jnp.int32, (16, 128), 0).astype(jnp.int16)
    one, zero = jnp.ones((16, 128), BF), jnp.zeros((16, 128), BF)

    def select(ids, base, groups, put):
        ids = ids - base
        rows = [
            [jnp.broadcast_to(ids[k:k + 1, c * 128:(c + 1) * 128], (16, 128)).astype(jnp.int16) for c in range(4)]
            for k in range(1 + F2)
        ]

        def body(i, carry):
            here = iota16 + jnp.full((16, 128), i * 16, jnp.int32).astype(jnp.int16)
            out = pl.ds(pl.multiple_of(i * 16, 16), 16)
            for c in range(4):
                acc = jnp.where(here == rows[1][c], one, zero)
                for k in range(2, 1 + F2):
                    acc = acc + jnp.where(here == rows[k][c], one, zero)
                put(out, c * 128, acc)
                put(out, SEED + c * 128, jnp.where(here == rows[0][c], one, zero))
            return carry

        lax.fori_loop(0, groups, body, 0)

    def put_f(rows, col, v):
        fsel[rows, col:col + 128] = v

    select(gidx2[y], 0, SRC // 16, put_f)
    for q in range(NAR):
        def put_b(rows, col, v, q=q):
            bsel[q, rows, col:col + 128] = v

        select(gidx2[q], y * FRONT, FRONT // 16, put_b)

    come = pulled.at[pl.ds(0, (DEV - 1) * CAP)]
    pltpu.make_async_copy(come, come, row_recv).wait()
    gone = featb.at[pl.ds(0, (DEV - 1) * CAP)]
    pltpu.make_async_copy(gone, gone, row_send).wait()
    sent = ask_rows.at[pl.ds(0, DEV - 1)]
    pltpu.make_async_copy(sent, sent, req_send).wait()

    def widen(i, c):
        rows = pl.ds(pl.multiple_of(i * 256, 256), 256)
        table[rows, :] = pulled[rows, :].astype(F32)
        return c

    lax.fori_loop(0, SRC // 256, widen, 0)
    table[SRC:SRC + 8, :] = jnp.zeros((8, D_IN), F32)
    for c in to_smem:
        c.wait()

    def cols(b):
        return pl.ds(pl.multiple_of(b * 256, 256), 256)

    def forward(b):
        @pl.when(b % 2 == 0)
        def _():
            blk = gbuf.at[left, :, cols(b)]
            link(blk, blk, h_send.at[0, b], h_recv.at[0, b], right).wait_recv()
            link(blk, blk, h_send.at[2, b], h_recv.at[2, b], right).start()

        @pl.when(b % 2 == 1)
        def _():
            blk = gbuf.at[right, :, cols(b)]
            link(blk, blk, h_send.at[1, b], h_recv.at[1, b], left).wait_recv()
            link(blk, blk, h_send.at[2, b], h_recv.at[2, b], left).start()

    def block(b, c):
        def some(i, c2):
            base = pl.multiple_of(b * 256 + i * 8, 8)
            for j in range(8):
                m = base + j
                here = pl.ds(pl.multiple_of(i * 8, 8) + j, 1)
                own[here, :] = view[idx[0, m]]
                rows = [view[idx[1 + k, m]] for k in range(F1)]
                while len(rows) > 1:
                    rows = [p + q for p, q in zip(rows[::2], rows[1::2])] + ([rows[-1]] if len(rows) % 2 else [])
                near[here, :] = rows[0] * inv[0, m]
            return c2

        lax.fori_loop(0, 32, some, 0)
        rows = cols(b)
        act = jnp.concatenate([own[...].astype(BF), near[...].astype(BF)], axis=1)
        a1[rows, :] = act
        z = dot(w1t[...], act, NT) + jnp.concatenate([b1c[...], b1c[...]], axis=1)
        z1t[:, rows] = z
        gbuf[y, :, rows] = (z / (1.0 + jnp.exp(-z))).astype(BF)
        blk = gbuf.at[y, :, rows]
        link(blk, blk, h_send.at[0, b], h_recv.at[0, b], right).start()
        link(blk, blk, h_send.at[1, b], h_recv.at[1, b], left).start()

        @pl.when(b > 0)
        def _():
            forward(b - 1)

        return c

    lax.fori_loop(0, 8, block, 0)
    forward(7)

    def from_source(q):
        return dot(gbuf[q], fsel[pl.ds(pl.multiple_of(q * FRONT, FRONT), FRONT), :])

    total = from_source(y)
    for b in range(1, 8, 2):
        blk = gbuf.at[left, :, b * 256:(b + 1) * 256]
        link(blk, blk, h_send.at[0, b], h_recv.at[0, b], right).wait_recv()
    total = total + from_source(left)
    for b in range(0, 8, 2):
        blk = gbuf.at[right, :, b * 256:(b + 1) * 256]
        link(blk, blk, h_send.at[1, b], h_recv.at[1, b], left).wait_recv()
    total = total + from_source(right)
    for b in range(8):
        blk = gbuf.at[opp, :, b * 256:(b + 1) * 256]
        link(blk, blk, h_send.at[2, b], h_recv.at[2, b], right).wait_recv()
    total = total + from_source(opp)

    def inverse_count(ids):
        n = jnp.sum((ids[1:1 + F2, :] >= 0).astype(F32), axis=0, keepdims=True)
        return 1.0 / jnp.maximum(n, 1.0)

    near2 = (total[:, :SEED] * inverse_count(gidx2[y])).astype(BF)
    self2 = total[:, SEED:].astype(BF)
    alive = live[...].astype(F32)
    diff = self2.astype(F32) - near2.astype(F32)

    def swap_start(buf, ssem, rsem):
        blk = buf.at[y]
        link(blk, blk, ssem.at[0], rsem.at[0], right).start()
        link(blk, blk, ssem.at[1], rsem.at[1], left).start()

    def swap_forward(buf, ssem, rsem, cut):
        blk = buf.at[left]
        link(blk, blk, ssem.at[0], rsem.at[0], right).wait_recv()
        half = buf.at[left, 0:cut, :]
        link(half, half, ssem.at[2], rsem.at[2], right).start()
        blk = buf.at[right]
        link(blk, blk, ssem.at[1], rsem.at[1], left).wait_recv()
        half = buf.at[right, cut:, :]
        link(half, half, ssem.at[3], rsem.at[3], left).start()

    def swap_end(buf, ssem, rsem, cut):
        half = buf.at[opp, 0:cut, :]
        link(half, half, ssem.at[2], rsem.at[2], right).wait_recv()
        half = buf.at[opp, cut:, :]
        link(half, half, ssem.at[3], rsem.at[3], left).wait_recv()

    def swap_sent(buf, ssem, rsem, cut):
        blk = buf.at[y]
        link(blk, blk, ssem.at[0], rsem.at[0], right).wait_send()
        link(blk, blk, ssem.at[1], rsem.at[1], left).wait_send()
        half = buf.at[left, 0:cut, :]
        link(half, half, ssem.at[2], rsem.at[2], right).wait_send()
        half = buf.at[right, cut:, :]
        link(half, half, ssem.at[3], rsem.at[3], left).wait_send()

    rbuf[y] = (2.0 * LAM / HID / SEEDS_ALL * alive * diff).astype(BF)
    swap_start(rbuf, r_send, r_recv)

    act2 = jnp.concatenate([self2, near2], axis=0)
    w2t = jnp.concatenate([gw2t[q] for q in range(NAR)], axis=1)
    cls = lax.broadcasted_iota(jnp.int32, (CLS_PAD, SEED), 0)
    b2 = b2c[0:CLS_PAD, :]
    logits = dot(w2t, act2) + jnp.concatenate([b2] * 4, axis=1)
    logits = jnp.where(cls < CLS, logits, -1e30)
    top = jnp.max(logits, axis=0, keepdims=True)
    e = jnp.exp(logits - top)
    tot = jnp.sum(e, axis=0, keepdims=True)
    hot = cls == labels[...]
    picked = jnp.sum(jnp.where(hot, logits, 0.0), axis=0, keepdims=True)
    dlog = (alive * (e * (1.0 / tot) - jnp.where(hot, 1.0, 0.0)) * (1.0 / SEEDS_ALL)).astype(BF)
    dbuf[y] = dlog
    swap_start(dbuf, d_send, d_recv)

    terms = top + jnp.log(tot) - picked + LAM / HID * jnp.sum(diff * diff, axis=0, keepdims=True)
    loss = jnp.sum(alive * terms, axis=1, keepdims=True)
    g2t = dot(dlog, act2, NT).astype(BF)
    for q in range(NAR):
        pay2[q * CLS_PAD:(q + 1) * CLS_PAD, :] = g2t[:, q * 128:(q + 1) * 128]

    my_piece = (me * 77) % DEV

    def to_owner(pay, first, count):
        def body(i, c):
            t = (me + i) % DEV
            p = (t * 77) % DEV - first

            @pl.when((p >= 0) & (p < count))
            def _():
                pltpu.make_async_remote_copy(
                    src_ref=pay.at[pl.ds(pl.multiple_of(p * 16, 16), 16)], dst_ref=inbox.at[me],
                    send_sem=rs_send, recv_sem=rs_recv, device_id=all_to(t), device_id_type=MESH,
                ).start()

            return c

        lax.fori_loop(1, DEV, body, 0)

    def add_up(pay, res, first, count, ssem, rsem):
        q = my_piece - first

        @pl.when((q >= 0) & (q < count))
        def _():
            rows16 = pl.ds(pl.multiple_of(q * 16, 16), 16)
            got = inbox.at[pl.ds(0, DEV - 1)]
            pltpu.make_async_copy(got, got, rs_recv).wait()
            inbox[me] = pay[rows16, :]

            def body(i, acc):
                part = inbox[pl.ds(pl.multiple_of(i * 8, 8), 8)].astype(F32)
                return acc + jnp.sum(part, axis=0)

            res[rows16, :] = lax.fori_loop(0, DEV // 8, body, jnp.zeros((16, 128), F32))

            def tell(i, c):
                pltpu.make_async_remote_copy(
                    src_ref=res.at[rows16], dst_ref=res.at[rows16],
                    send_sem=ssem, recv_sem=rsem, device_id=all_to((me + i) % DEV), device_id_type=MESH,
                ).start()
                return c

            lax.fori_loop(1, DEV, tell, 0)

    def take(res, first, count, rsem):
        q = my_piece - first
        holds = (q >= 0) & (q < count)

        @pl.when(holds)
        def _():
            got = res.at[pl.ds(0, (count - 1) * 16)]
            pltpu.make_async_copy(got, got, rsem).wait()

        @pl.when(jnp.logical_not(holds))
        def _():
            got = res.at[pl.ds(0, count * 16)]
            pltpu.make_async_copy(got, got, rsem).wait()

    to_owner(pay2, P1, P2)

    def grads(q):
        da = dot(w2[...], dbuf[q])
        r = rbuf[q].astype(F32)
        ds = (da[:HID] + r).astype(BF)
        dn = ((da[HID:] - r) * inverse_count(gidx2[q])).astype(BF)
        return dot(jnp.concatenate([dn, ds], axis=1), bsel[q], NT)

    swap_forward(rbuf, r_send, r_recv, 128)
    dh1[...] = grads(y)
    swap_forward(dbuf, d_send, d_recv, 96)
    dh1[...] += grads(left)
    dh1[...] += grads(right)
    swap_end(rbuf, r_send, r_recv, 128)
    swap_end(dbuf, d_send, d_recv, 96)
    dh1[...] += grads(opp)
    add_up(pay2, res2, P1, P2, ag_send.at[0], ag_recv.at[0])

    z = z1t[...]
    sig = 1.0 / (1.0 + jnp.exp(-z))
    dz = (dh1[...] * sig * (1.0 + z * (1.0 - sig))).astype(BF)
    g1 = dot(dz, a1[...]).T.astype(BF)
    pay1[0:256, :] = g1[:, :128]
    pay1[256:512, :] = g1[:, 128:]
    ones_f = jnp.ones((8, FRONT), BF)
    ones_s = jnp.ones((8, SEED), BF)
    db1 = dot(ones_f, dz, NT)[0:1, :]
    db2 = dot(ones_s, dlog, NT)[0:1, :]
    misc[...] = jnp.zeros((16, 128), F32)

    def two(rows, v):
        hi = v.astype(BF).astype(F32)
        misc[rows:rows + 1, 0:v.shape[1]] = hi
        misc[rows + 4:rows + 5, 0:v.shape[1]] = v - hi

    two(0, db1[:, :128])
    two(1, db1[:, 128:])
    two(2, db2[:, :128])
    two(3, db2[:, 128:])
    hi = loss.astype(BF).astype(F32)
    misc[8:9, 0:1] = hi
    misc[9:10, 0:1] = loss - hi
    pay1[512:528, :] = misc[...].astype(BF)
    to_owner(pay1, 0, P1)

    take(res2, P1, P2, ag_recv.at[0])
    mom2 = jnp.concatenate(
        [MU * gm2t[q] + res2[q * CLS_PAD:(q + 1) * CLS_PAD, :] for q in range(NAR)], axis=1
    )
    for q in range(NAR):
        x2s[q] = mom2[:, q * 128:(q + 1) * 128]
    o_mom2[...] = x2s[y]
    x2 = mom2 * (1.0 / (jnp.sqrt(jnp.sum(mom2 * mom2, keepdims=True)) + 1e-07))
    for _ in range(3):
        x2 = ns_step(x2)
    add_up(pay1, o_res1, 0, P1, ag_send.at[1], ag_recv.at[1])
    for _ in range(NS_ITERS - 3):
        x2 = ns_step(x2)
    for q in range(NAR):
        x2s[q] = x2[:, q * 128:(q + 1) * 128]
    o_x2[...] = x2s[y]
    take(o_res1, 0, P1, ag_recv.at[1])

    for b in range(8):
        blk = gbuf.at[y, :, b * 256:(b + 1) * 256]
        link(blk, blk, h_send.at[0, b], h_recv.at[0, b], right).wait_send()
        link(blk, blk, h_send.at[1, b], h_recv.at[1, b], left).wait_send()
        blk = gbuf.at[opp, :, b * 256:(b + 1) * 256]
        link(blk, blk, h_send.at[2, b], h_recv.at[2, b], right).wait_send()
    swap_sent(rbuf, r_send, r_recv, 128)
    swap_sent(dbuf, d_send, d_recv, 96)

    owner = my_piece < PIECES

    @pl.when(owner)
    def _():
        gone = inbox.at[pl.ds(0, PIECES - 1)]
        pltpu.make_async_copy(gone, gone, rs_send).wait()

    @pl.when(jnp.logical_not(owner))
    def _():
        gone = inbox.at[pl.ds(0, PIECES)]
        pltpu.make_async_copy(gone, gone, rs_send).wait()

    for n, (lo, hi) in enumerate(((P1, PIECES), (0, P1))):
        @pl.when((my_piece >= lo) & (my_piece < hi))
        def _():
            gone = table.at[pl.ds(0, (DEV - 1) * 16)]
            pltpu.make_async_copy(gone, gone, ag_send.at[n]).wait()


def main(reqt, feat, idx1t, msk1t, idx2t, msk2t, labels, live, w1, w2own, m1, m2own, bias):
    vm = pl.BlockSpec(memory_space=pltpu.VMEM)
    dma = pltpu.SemaphoreType.DMA
    sds = jax.ShapeDtypeStruct
    V = pltpu.VMEM
    return pl.pallas_call(
        main_kernel,
        out_shape=[
            sds((P1 * 16, 128), F32), sds((NAR, 64, HID), F32), sds((CLS_PAD, 128), F32), sds((CLS_PAD, 128), F32),
        ],
        in_specs=[vm, pl.BlockSpec(memory_space=pl.ANY)] + [vm] * 11,
        out_specs=[vm] * 4,
        scratch_shapes=[
            V((SRC + 8, D_IN), F32),
            V((OWN, D_IN), BF),
            V((SRC, D_IN), BF),
            V((CAP, D_IN), F32),
            V((DEV, 128), jnp.int32),
            V((DEV, 128), jnp.int32),
            V((16, FRONT), jnp.int32),
            V((1, FRONT), F32),
            V((256, D_IN), F32),
            V((256, D_IN), F32),
            V((FRONT, 2 * D_IN), BF),
            V((HID, FRONT), F32),
            V((NAR, HID, FRONT), BF),
            V((SRC, 2 * SEED), BF),
            V((NAR, FRONT, 2 * SEED), BF),
            V((NAR, HID, SEED), BF),
            V((NAR, CLS_PAD, SEED), BF),
            V((HID, FRONT), F32),
            V((NAR, 64, HID), BF),
            V((NAR, CLS_PAD, 128), BF),
            V((NAR, CLS_PAD, 128), F32),
            V((NAR, 16, SEED), jnp.int32),
            V((HID, 2 * D_IN), BF),
            V((2 * HID, CLS_PAD), BF),
            V((HID, 128), F32),
            V((HID, 128), F32),
            V((P1 * 16, 128), BF),
            V((P2 * 16, 128), BF),
            V((16, 128), F32),
            V((DEV, 16, 128), BF),
            V((P2 * 16, 128), F32),
            V((NAR, CLS_PAD, 128), F32),
            pltpu.SMEM((DEV, 128), jnp.int32),
            pltpu.SMEM((16, FRONT), jnp.int32),
            pltpu.SMEM((1, FRONT), F32),
            dma, dma((3,)), dma, dma, dma, dma, dma((5, 3)), dma((5, 3)),
            dma((3, 8)), dma((3, 8)), dma((4,)), dma((4,)), dma((4,)), dma((4,)), dma, dma, dma((2,)), dma((2,)),
        ],
        compiler_params=pltpu.CompilerParams(
            collective_id=0, has_side_effects=True, vmem_limit_bytes=62 * 2**20
        ),
    )(reqt, feat, idx1t, msk1t, idx2t, msk2t, labels, live, w1, w2own, m1, m2own, bias)


def update_kernel(
    res1, gm1, mom2, x2, w1own, w2own, bias, biasm, biasv,
    o_loss, o_first, o_second, o_mom1, o_mom2, o_flow, o_slow, o_bias, o_bm, o_bv,
    x1s,
):
    y = lax.axis_index("nar")
    grad1 = jnp.concatenate([res1[0:256, :], res1[256:512, :]], axis=1)
    mom1 = MU * gm1[...].reshape(2 * D_IN, HID) + grad1
    x1s[...] = mom1
    block64 = pl.ds(pl.multiple_of(y * 64, 64), 64)
    o_mom1[...] = x1s[block64, :]
    x1 = mom1 * (1.0 / (jnp.sqrt(jnp.sum(mom1 * mom1, keepdims=True)) + 1e-07))
    for _ in range(NS_ITERS):
        x1 = ns_step(x1)
    x1s[...] = x1
    first_new = w1own[...] * (1.0 - WDECAY) - x1s[block64, :]
    o_first[...] = first_new
    o_flow[...] = first_new.astype(BF)
    second = w2own[...] * (1.0 - WDECAY) - (2 * HID / CLS) ** 0.5 * x2[0:CLS, :]
    o_second[...] = second
    o_slow[...] = second.astype(BF)
    o_mom2[...] = mom2[0:CLS, :]

    gb = res1[512:516, :] + res1[516:520, :]
    gb = jnp.concatenate([gb[0:1, :], gb[1:2, :], gb[2:3, :], gb[3:4, 0:44]], axis=1)
    m_new = BETA_ONE * biasm[...] + (1.0 - BETA_ONE) * gb
    v_new = BETA_TWO * biasv[...] + (1.0 - BETA_TWO) * gb * gb
    m_hat = m_new / (1.0 - BETA_ONE**STEP)
    v_hat = v_new / (1.0 - BETA_TWO**STEP)
    o_bias[...] = bias[...] * (1.0 - LR_BIAS * WDECAY) - LR_BIAS * m_hat / (jnp.sqrt(v_hat) + EPSILON)
    o_bm[...] = m_new
    o_bv[...] = v_new
    o_loss[...] = res1[520:521, 0:1] + res1[521:522, 0:1]


def update(*args):
    vm = pl.BlockSpec(memory_space=pltpu.VMEM)
    sds = jax.ShapeDtypeStruct
    return pl.pallas_call(
        update_kernel,
        out_shape=[
            sds((1, 1), F32), sds((64, HID), F32), sds((CLS, 128), F32), sds((64, HID), F32), sds((CLS, 128), F32),
            sds((64, HID), BF), sds((CLS, 128), BF), sds((1, 428), F32), sds((1, 428), F32), sds((1, 428), F32),
        ],
        in_specs=[vm] * 9,
        out_specs=[vm] * 10,
        scratch_shapes=[pltpu.VMEM((2 * D_IN, HID), F32)],
        compiler_params=pltpu.CompilerParams(vmem_limit_bytes=32 * 2**20),
    )(*args)


def per_device(
    features, requests, index_one, mask_one, index_two, mask_two, labels, seed_live,
    w_first, w_second, mom_first, mom_second, biases, bias_m, bias_v,
):
    w2own, bias = w_second.T, biases[None, :]
    res1, gm1, mom2, x2 = main(
        requests.T, features, index_one.T, mask_one.T, index_two.T, mask_two.T, labels[None, :], seed_live[None, :],
        w_first, w2own, mom_first, mom_second.T, bias,
    )
    loss, first_new, second_new, mom_one, mom_two, first_low, second_low, bias_new, m_new, v_new = update(
        res1, gm1, mom2, x2, w_first, w2own, bias, bias_m[None, :], bias_v[None, :]
    )
    return (
        loss.reshape(()), first_new, second_new.T, mom_one, mom_two.T, first_low, second_low.T,
        bias_new.reshape(-1), m_new.reshape(-1), v_new.reshape(-1),
    )


def solution(mesh):
    both = ("grp", "nar")
    placed = (
        P(both, None), P(both, None), P(both, None), P(both, None), P(both, None), P(both, None),
        P(both), P(both), P("nar", None), P("nar", None), P("nar", None), P("nar", None), P(), P(), P(),
    )
    nar = P("nar", None)
    return jax.shard_map(
        per_device, mesh=mesh, in_specs=placed,
        out_specs=(P(), nar, nar, nar, nar, nar, nar, P(), P(), P()), check_vma=False,
    )
```

time: 223 us -> 178 us (0.80)
  Pallas kernels: 192 us -> 174 us
  local copies, waits for them, and re-layouts: 20.4 us -> 3.7 us
  other arithmetic: 7.02 us -> 0 us
    pallas_call x2, Pallas kernels: 192 us -> 174 us  [the longest x1 168 us: main(): pl.pallas_call(main_kernel, out_shape=[sds((P1 * 16, 128), F32), sds((NAR...]
    unnamed x10 -> x18, local copies, waits for them, and re-layouts: 13.4 us -> 3.7 us
    pad x3 -> x0, local copies, waits for them, and re-layouts: 2.8 us -> none  [the longest x1 1.53 us: per_device(): m2t = jnp.pad(mom_second.T, ((0, CLS_PAD - CLS), (0, 0)))]
    reshape x2 -> x0, local copies, waits for them, and re-layouts: 2.54 us -> none  [as_rows(): return jnp.pad(v, (0, 512 - v.shape[0])).reshape(4, 128)]
where the time goes in v3:
time: 178 us
  Pallas kernels  174 us (98%)
  local copies, waits for them, and re-layouts  3.7 us (2%)
    pallas_call x1, Pallas kernels, main(): pl.pallas_call(main_kernel, out_shape=[sds((P1 * 16, 128), F32), sds((NAR...  168 us
    pallas_call x1, Pallas kernels, update(): pl.pallas_call(update_kernel, out_shape=[sds((1, 1), F32), sds((64, HID),...  5.47 us
    unnamed x18, local copies, waits for them, and re-layouts  3.7 us

profile of v3, /device:TPU:1, one launch (start us, length us, event | category | flops | bytes accessed | tf_op | source)
XLA Modules:
  0.0 178.2 jit_solution(6492102375166146290)
XLA Ops:
  0.6 0.0 copy-start.3
  0.7 0.0 copy-start.8
  0.7 0.0 copy-start.7
  0.7 0.0 copy-start.6
  0.7 0.0 copy-start
  0.7 168.3 %shard_map.222 = (f32[528,128]{1,0:T(8,128)}, f32[4,64,256]{2,1,0:T(8,128)}, f32[176,128]{1,0:T(8,128)}, f32[176,128]{1,0:T(8,128)}) custom-call(s32[64,128]{1,0:T(8,128)} %bitcast.28, bf16[8192,128]{1,0:T(8,128)(2,1)} %feat.1, s32[16,2048]{1,0:T(8,128)} %bitcast.25, s32[15,2048]{1,0:T(8,128)} %bitcast.26, s32[11,512]{1,0:T(8,128)} %bitcast.29, ...), custom_call_target="tpu_custom_call" | custom-call | tf_op jit(solution)/shard_map/pallas_call | solution.py:531
  169.0 0.0 copy-done.3
  169.0 0.0 copy-done.8
  169.0 0.0 copy-done.7
  169.0 0.0 copy-done.6
  169.0 0.0 copy-done
  169.0 0.0 copy-start.1
  169.0 0.9 copy-done.1
  170.0 0.0 copy-start.2
  170.0 0.9 copy-done.2
  170.9 0.0 copy-start.4
  170.9 0.9 copy-done.4
  171.8 0.0 copy-start.5
  171.8 0.9 copy-done.5
  172.7 5.5 %shard_map.223 = (f32[1,1]{1,0:T(1,128)}, f32[64,256]{1,0:T(8,128)}, f32[172,128]{1,0:T(8,128)}, f32[64,256]{1,0:T(8,128)}, f32[172,128]{1,0:T(8,128)}, /*index=...) custom-call(f32[528,128]{1,0:T(8,128)S(1)} %copy-done.1, ...), custom_call_target="tpu_custom_call" | custom-call | tf_op jit(solution)/shard_map/pallas_call | solution.py:621
Async XLA Ops:
  0.6 168.3 %copy-start.3 = (f32[64,256]{1,0:T(8,128)S(1)}, f32[64,256]{1,0:T(8,128)}, u32[]{:S(2)}) copy-start(f32[64,256]{1,0:T(8,128)} %w1own.1) | copy-start | bytes 196612
  0.7 168.3 %copy-start.8 = (f32[428]{0:T(512)S(1)}, f32[428]{0:T(512)}, u32[]{:S(2)}) copy-start(f32[428]{0:T(512)} %param.29) | copy-start | bytes 5140
  0.7 168.3 %copy-start.7 = (f32[428]{0:T(512)S(1)}, f32[428]{0:T(512)}, u32[]{:S(2)}) copy-start(f32[428]{0:T(512)} %param.28) | copy-start | bytes 5140
  0.7 168.3 %copy-start.6 = (f32[428]{0:T(512)S(1)}, f32[428]{0:T(512)}, u32[]{:S(2)}) copy-start(f32[428]{0:T(512)} %param.27) | copy-start | bytes 5140
  0.7 168.3 %copy-start = (f32[128,172]{0,1:T(8,128)S(1)}, f32[128,172]{0,1:T(8,128)}, u32[]{:S(2)}) copy-start(f32[128,172]{0,1:T(8,128)} %param.24) | copy-start | bytes 264196
  169.0 1.0 copy-start.1
  170.0 0.9 copy-start.2
  170.9 0.9 copy-start.4
  171.8 0.9 copy-start.5

commit v4 on v3

--- a/solution.py
+++ b/solution.py
@@ -45,7 +45,11 @@
 
 P1 = 33
 P2 = 44
-PIECES = P1 + P2
+GRP = 32
+ROW_G1 = P1 * 16
+ROW_M2 = ROW_G1 + 512
+ROW_X2 = ROW_M2 + CLS_PAD
+ROWS = ROW_X2 + CLS_PAD
 SEEDS_ALL = SEED * DEV
 
 
@@ -81,13 +85,14 @@
 
 def main_kernel(
     reqt, feat, idx1t, msk1t, idx2t, msk2t, labels, live, w1, w2own, m1, m2own, bias,
-    o_res1, o_gm1, o_mom2, o_x2,
-    table, featb, pulled, stage, reqv, reqin, idxv, invv, near, own, a1, z1t, gbuf, fsel, bsel, rbuf, dbuf, dh1,
-    gw1, gw2t, gm2t, gidx2, w1t, w2, b1c, b2c, pay1, pay2, misc, inbox, res2, x2s,
+    o_all,
+    table, featb, pulled, stage, reqv, reqin, idxv, invv, near, own, z1t, gbuf, fsel, bsel, idc, rbuf, dbuf,
+    gw1, gw2t, gm1, gm2t, gidx2, w1t, w2, b1c, b2c, pay1, pay2, misc, inbox1, inbox2, ybox1, ybox2, res2, x2s,
     reqs, idx, inv,
     feat_sem, loc_sem, req_send, req_recv, row_send, row_recv, nar_send, nar_recv,
-    h_send, h_recv, r_send, r_recv, d_send, d_recv, rs_send, rs_recv, ag_send, ag_recv,
+    h_send, h_recv, r_send, r_recv, d_send, d_recv, rs_send, rs_recv, y_send, y_recv, ag_send, ag_recv,
 ):
+    a1, dh1 = pulled, table
     g = lax.axis_index("grp")
     y = lax.axis_index("nar")
     me = g * NAR + y
@@ -116,12 +121,12 @@
     gw1[y] = w1[...].astype(BF)
     pad = CLS_PAD - CLS
     gw2t[y] = jnp.concatenate([w2own[...], jnp.zeros((pad, 128), F32)], axis=0).astype(BF)
-    o_gm1[y] = m1[...]
+    gm1[y] = m1[...]
     gm2t[y] = jnp.concatenate([m2own[...], jnp.zeros((pad, 128), F32)], axis=0)
     gidx2[y] = jnp.concatenate(
         [idx2t[0:1, :], jnp.where(msk2t[...] > 0, idx2t[1:, :], -1), jnp.zeros((5, SEED), jnp.int32)], axis=0
     )
-    shared = (gidx2, gw1, gw2t, o_gm1, gm2t)
+    shared = (gidx2, gw1, gw2t, gm1, gm2t)
 
     pl.semaphore_wait(barrier, DEV - 1)
 
@@ -189,6 +194,9 @@
         for d in range(1, NAR):
             link(a.at[y], a.at[y], nar_send.at[n, d - 1], nar_recv.at[n, d - 1], (y + d) % NAR).wait()
     w1t[...] = gw1[...].reshape(2 * D_IN, HID).T
+    for q in range(NAR):
+        o_all[ROW_G1 + q * 64:ROW_G1 + q * 64 + 64, :] = MU * gm1[q, :, 0:128]
+        o_all[ROW_G1 + 256 + q * 64:ROW_G1 + 256 + q * 64 + 64, :] = MU * gm1[q, :, 128:256]
     w2t = jnp.concatenate([gw2t[q] for q in range(NAR)], axis=1)
     w2[...] = w2t.T
     b1c[...] = jnp.concatenate([spread(bias[0:1, 0:128]), spread(bias[0:1, 128:256])], axis=0)
@@ -222,11 +230,28 @@
         fsel[rows, col:col + 128] = v
 
     select(gidx2[y], 0, SRC // 16, put_f)
+    lane16 = lax.broadcasted_iota(jnp.int32, (16, 128), 1).astype(jnp.int16)
+
+    idc[...] = (jnp.concatenate([gidx2[q] for q in range(NAR)], axis=0) - y * FRONT).T
+
+    def select_rows(q, group):
+        at = pl.multiple_of(group * 16, 16)
+        blk = idc[pl.ds(at, 16), :]
+        want = [jnp.broadcast_to(blk[:, q * 16 + k:q * 16 + k + 1], (16, 128)).astype(jnp.int16) for k in range(1 + F2)]
+        for c in range(FRONT // 128):
+            here = lane16 + jnp.full((16, 128), c * 128, jnp.int32).astype(jnp.int16)
+            acc = jnp.where(here == want[1], one, zero)
+            for k in range(2, 1 + F2):
+                acc = acc + jnp.where(here == want[k], one, zero)
+            bsel[q, pl.ds(at, 16), c * 128:(c + 1) * 128] = acc
+            bsel[q, pl.ds(SEED + at, 16), c * 128:(c + 1) * 128] = jnp.where(here == want[0], one, zero)
+
     for q in range(NAR):
-        def put_b(rows, col, v, q=q):
-            bsel[q, rows, col:col + 128] = v
-
-        select(gidx2[q], y * FRONT, FRONT // 16, put_b)
+        def all_rows(i, carry, q=q):
+            select_rows(q, i)
+            return carry
+
+        lax.fori_loop(0, SEED // 16, all_rows, 0)
 
     come = pulled.at[pl.ds(0, (DEV - 1) * CAP)]
     pltpu.make_async_copy(come, come, row_recv).wait()
@@ -263,10 +288,10 @@
 
     def block(b, c):
         def some(i, c2):
-            base = pl.multiple_of(b * 256 + i * 8, 8)
-            for j in range(8):
+            base = pl.multiple_of(b * 256 + i * 16, 16)
+            for j in range(16):
                 m = base + j
-                here = pl.ds(pl.multiple_of(i * 8, 8) + j, 1)
+                here = pl.ds(pl.multiple_of(i * 16, 16) + j, 1)
                 own[here, :] = view[idx[0, m]]
                 rows = [view[idx[1 + k, m]] for k in range(F1)]
                 while len(rows) > 1:
@@ -274,10 +299,11 @@
                 near[here, :] = rows[0] * inv[0, m]
             return c2
 
-        lax.fori_loop(0, 32, some, 0)
+        lax.fori_loop(0, 16, some, 0)
         rows = cols(b)
         act = jnp.concatenate([own[...].astype(BF), near[...].astype(BF)], axis=1)
-        a1[rows, :] = act
+        a1[rows, :] = act[:, :128]
+        a1[pl.ds(pl.multiple_of(FRONT + b * 256, 256), 256), :] = act[:, 128:]
         z = dot(w1t[...], act, NT) + jnp.concatenate([b1c[...], b1c[...]], axis=1)
         z1t[:, rows] = z
         gbuf[y, :, rows] = (z / (1.0 + jnp.exp(-z))).astype(BF)
@@ -374,86 +400,109 @@
     for q in range(NAR):
         pay2[q * CLS_PAD:(q + 1) * CLS_PAD, :] = g2t[:, q * 128:(q + 1) * 128]
 
-    my_piece = (me * 77) % DEV
-
-    def to_owner(pay, first, count):
+    def plane(i):
+        return ((g + i) % GRP, y)
+
+    def to_owner(pay, inbox, count, n):
         def body(i, c):
-            t = (me + i) % DEV
-            p = (t * 77) % DEV - first
-
-            @pl.when((p >= 0) & (p < count))
+            t = (g + i) % GRP
+            for slot in range(2):
+                p = t + slot * GRP
+
+                @pl.when(p < count)
+                def _():
+                    pltpu.make_async_remote_copy(
+                        src_ref=pay.at[pl.ds(pl.multiple_of(p * 16, 16), 16)], dst_ref=inbox.at[slot, g],
+                        send_sem=rs_send.at[n], recv_sem=rs_recv.at[n, slot], device_id=(t, y), device_id_type=MESH,
+                    ).start()
+
+            return c
+
+        lax.fori_loop(1, GRP, body, 0)
+
+    def add_plane(pay, inbox, ybox, count, n):
+        for slot in range(2):
+            p = g + slot * GRP
+
+            @pl.when(p < count)
             def _():
-                pltpu.make_async_remote_copy(
-                    src_ref=pay.at[pl.ds(pl.multiple_of(p * 16, 16), 16)], dst_ref=inbox.at[me],
-                    send_sem=rs_send, recv_sem=rs_recv, device_id=all_to(t), device_id_type=MESH,
-                ).start()
-
-            return c
-
-        lax.fori_loop(1, DEV, body, 0)
-
-    def add_up(pay, res, first, count, ssem, rsem):
-        q = my_piece - first
-
-        @pl.when((q >= 0) & (q < count))
-        def _():
-            rows16 = pl.ds(pl.multiple_of(q * 16, 16), 16)
-            got = inbox.at[pl.ds(0, DEV - 1)]
-            pltpu.make_async_copy(got, got, rs_recv).wait()
-            inbox[me] = pay[rows16, :]
-
-            def body(i, acc):
-                part = inbox[pl.ds(pl.multiple_of(i * 8, 8), 8)].astype(F32)
-                return acc + jnp.sum(part, axis=0)
-
-            res[rows16, :] = lax.fori_loop(0, DEV // 8, body, jnp.zeros((16, 128), F32))
-
-            def tell(i, c):
-                pltpu.make_async_remote_copy(
-                    src_ref=res.at[rows16], dst_ref=res.at[rows16],
-                    send_sem=ssem, recv_sem=rsem, device_id=all_to((me + i) % DEV), device_id_type=MESH,
-                ).start()
-                return c
-
-            lax.fori_loop(1, DEV, tell, 0)
-
-    def take(res, first, count, rsem):
-        q = my_piece - first
-        holds = (q >= 0) & (q < count)
-
-        @pl.when(holds)
-        def _():
-            got = res.at[pl.ds(0, (count - 1) * 16)]
-            pltpu.make_async_copy(got, got, rsem).wait()
-
-        @pl.when(jnp.logical_not(holds))
-        def _():
-            got = res.at[pl.ds(0, count * 16)]
-            pltpu.make_async_copy(got, got, rsem).wait()
-
-    to_owner(pay2, P1, P2)
+                got = inbox.at[slot, pl.ds(0, GRP - 1)]
+                pltpu.make_async_copy(got, got, rs_recv.at[n, slot]).wait()
+                inbox[slot, g] = pay[pl.ds(pl.multiple_of(p * 16, 16), 16), :]
+                ybox[slot, y] = jnp.sum(inbox[slot].astype(F32), axis=0)
+                blk = ybox.at[slot, y]
+                for d in range(1, NAR):
+                    link(blk, blk, y_send.at[n, slot, d - 1], y_recv.at[n, slot, d - 1], (y + d) % NAR).start()
+
+    def add_group(ybox, res, count, n):
+        for slot in range(2):
+            p = g + slot * GRP
+
+            @pl.when(p < count)
+            def _():
+                blk = ybox.at[slot, y]
+                for d in range(1, NAR):
+                    link(blk, blk, y_send.at[n, slot, d - 1], y_recv.at[n, slot, d - 1], (y + d) % NAR).wait()
+                rows16 = pl.ds(pl.multiple_of(p * 16, 16), 16)
+                res[rows16, :] = (ybox[slot, 0] + ybox[slot, 1]) + (ybox[slot, 2] + ybox[slot, 3])
+
+                def tell(i, c):
+                    pltpu.make_async_remote_copy(
+                        src_ref=res.at[rows16], dst_ref=res.at[rows16], send_sem=ag_send.at[n], recv_sem=ag_recv.at[n],
+                        device_id=plane(i), device_id_type=MESH,
+                    ).start()
+                    return c
+
+                lax.fori_loop(1, GRP, tell, 0)
+
+    def take(res, count, n):
+        two_here = g + GRP < count
+        for own, here in ((2, two_here), (1, jnp.logical_not(two_here))):
+            @pl.when(here)
+            def _(own=own):
+                got = res.at[pl.ds(0, (count - own) * 16)]
+                pltpu.make_async_copy(got, got, ag_recv.at[n]).wait()
+
+    def sums_sent(pay, count, n):
+        two_here = g + GRP < count
+        for own, here in ((2, two_here), (1, jnp.logical_not(two_here))):
+            @pl.when(here)
+            def _(own=own):
+                gone = pay.at[pl.ds(0, (count - own) * 16)]
+                pltpu.make_async_copy(gone, gone, rs_send.at[n]).wait()
+                gone = table.at[pl.ds(0, own * (GRP - 1) * 16)]
+                pltpu.make_async_copy(gone, gone, ag_send.at[n]).wait()
+
+    to_owner(pay2, inbox2, P2, 1)
 
     def grads(q):
         da = dot(w2[...], dbuf[q])
         r = rbuf[q].astype(F32)
         ds = (da[:HID] + r).astype(BF)
         dn = ((da[HID:] - r) * inverse_count(gidx2[q])).astype(BF)
-        return dot(jnp.concatenate([dn, ds], axis=1), bsel[q], NT)
+        return dot(jnp.concatenate([dn, ds], axis=1), bsel[q])
 
     swap_forward(rbuf, r_send, r_recv, 128)
-    dh1[...] = grads(y)
+    def add_grads(q, fresh=False):
+        part = grads(q)
+        for c in range(FRONT // 128):
+            now = part[:, c * 128:(c + 1) * 128]
+            dh1[c * 256:(c + 1) * 256, :] = now if fresh else dh1[c * 256:(c + 1) * 256, :] + now
+
+    add_grads(y, True)
     swap_forward(dbuf, d_send, d_recv, 96)
-    dh1[...] += grads(left)
-    dh1[...] += grads(right)
+    add_grads(left)
+    add_grads(right)
     swap_end(rbuf, r_send, r_recv, 128)
     swap_end(dbuf, d_send, d_recv, 96)
-    dh1[...] += grads(opp)
-    add_up(pay2, res2, P1, P2, ag_send.at[0], ag_recv.at[0])
+    add_grads(opp)
+    add_plane(pay2, inbox2, ybox2, P2, 1)
 
     z = z1t[...]
     sig = 1.0 / (1.0 + jnp.exp(-z))
-    dz = (dh1[...] * sig * (1.0 + z * (1.0 - sig))).astype(BF)
-    g1 = dot(dz, a1[...]).T.astype(BF)
+    dh = jnp.concatenate([dh1[c * 256:(c + 1) * 256, :] for c in range(FRONT // 128)], axis=1)
+    dz = (dh * sig * (1.0 + z * (1.0 - sig))).astype(BF)
+    g1 = jnp.concatenate([dot(dz, a1[0:FRONT, :]), dot(dz, a1[FRONT:2 * FRONT, :])], axis=1).T.astype(BF)
     pay1[0:256, :] = g1[:, :128]
     pay1[256:512, :] = g1[:, 128:]
     ones_f = jnp.ones((8, FRONT), BF)
@@ -475,25 +524,26 @@
     misc[8:9, 0:1] = hi
     misc[9:10, 0:1] = loss - hi
     pay1[512:528, :] = misc[...].astype(BF)
-    to_owner(pay1, 0, P1)
-
-    take(res2, P1, P2, ag_recv.at[0])
+    to_owner(pay1, inbox1, P1, 0)
+    add_group(ybox2, res2, P2, 1)
+
+    add_plane(pay1, inbox1, ybox1, P1, 0)
+    take(res2, P2, 1)
     mom2 = jnp.concatenate(
         [MU * gm2t[q] + res2[q * CLS_PAD:(q + 1) * CLS_PAD, :] for q in range(NAR)], axis=1
     )
     for q in range(NAR):
         x2s[q] = mom2[:, q * 128:(q + 1) * 128]
-    o_mom2[...] = x2s[y]
+    o_all[ROW_M2:ROW_M2 + CLS_PAD, :] = x2s[y]
     x2 = mom2 * (1.0 / (jnp.sqrt(jnp.sum(mom2 * mom2, keepdims=True)) + 1e-07))
-    for _ in range(3):
-        x2 = ns_step(x2)
-    add_up(pay1, o_res1, 0, P1, ag_send.at[1], ag_recv.at[1])
-    for _ in range(NS_ITERS - 3):
+    x2 = ns_step(x2)
+    add_group(ybox1, o_all, P1, 0)
+    for _ in range(NS_ITERS - 1):
         x2 = ns_step(x2)
     for q in range(NAR):
         x2s[q] = x2[:, q * 128:(q + 1) * 128]
-    o_x2[...] = x2s[y]
-    take(o_res1, 0, P1, ag_recv.at[1])
+    o_all[ROW_X2:ROW_X2 + CLS_PAD, :] = x2s[y]
+    take(o_all, P1, 0)
 
     for b in range(8):
         blk = gbuf.at[y, :, b * 256:(b + 1) * 256]
@@ -504,23 +554,8 @@
     swap_sent(rbuf, r_send, r_recv, 128)
     swap_sent(dbuf, d_send, d_recv, 96)
 
-    owner = my_piece < PIECES
-
-    @pl.when(owner)
-    def _():
-        gone = inbox.at[pl.ds(0, PIECES - 1)]
-        pltpu.make_async_copy(gone, gone, rs_send).wait()
-
-    @pl.when(jnp.logical_not(owner))
-    def _():
-        gone = inbox.at[pl.ds(0, PIECES)]
-        pltpu.make_async_copy(gone, gone, rs_send).wait()
-
-    for n, (lo, hi) in enumerate(((P1, PIECES), (0, P1))):
-        @pl.when((my_piece >= lo) & (my_piece < hi))
-        def _():
-            gone = table.at[pl.ds(0, (DEV - 1) * 16)]
-            pltpu.make_async_copy(gone, gone, ag_send.at[n]).wait()
+    sums_sent(pay2, P2, 1)
+    sums_sent(pay1, P1, 0)
 
 
 def main(reqt, feat, idx1t, msk1t, idx2t, msk2t, labels, live, w1, w2own, m1, m2own, bias):
@@ -530,11 +565,9 @@
     V = pltpu.VMEM
     return pl.pallas_call(
         main_kernel,
-        out_shape=[
-            sds((P1 * 16, 128), F32), sds((NAR, 64, HID), F32), sds((CLS_PAD, 128), F32), sds((CLS_PAD, 128), F32),
-        ],
+        out_shape=sds((ROWS, 128), F32),
         in_specs=[vm, pl.BlockSpec(memory_space=pl.ANY)] + [vm] * 11,
-        out_specs=[vm] * 4,
+        out_specs=vm,
         scratch_shapes=[
             V((SRC + 8, D_IN), F32),
             V((OWN, D_IN), BF),
@@ -546,16 +579,16 @@
             V((1, FRONT), F32),
             V((256, D_IN), F32),
             V((256, D_IN), F32),
-            V((FRONT, 2 * D_IN), BF),
             V((HID, FRONT), F32),
             V((NAR, HID, FRONT), BF),
             V((SRC, 2 * SEED), BF),
-            V((NAR, FRONT, 2 * SEED), BF),
+            V((NAR, 2 * SEED, FRONT), BF),
+            V((SEED, 16 * NAR), jnp.int32),
             V((NAR, HID, SEED), BF),
             V((NAR, CLS_PAD, SEED), BF),
-            V((HID, FRONT), F32),
             V((NAR, 64, HID), BF),
             V((NAR, CLS_PAD, 128), BF),
+            V((NAR, 64, HID), F32),
             V((NAR, CLS_PAD, 128), F32),
             V((NAR, 16, SEED), jnp.int32),
             V((HID, 2 * D_IN), BF),
@@ -565,14 +598,18 @@
             V((P1 * 16, 128), BF),
             V((P2 * 16, 128), BF),
             V((16, 128), F32),
-            V((DEV, 16, 128), BF),
+            V((2, GRP, 16, 128), BF),
+            V((2, GRP, 16, 128), BF),
+            V((2, NAR, 16, 128), F32),
+            V((2, NAR, 16, 128), F32),
             V((P2 * 16, 128), F32),
             V((NAR, CLS_PAD, 128), F32),
             pltpu.SMEM((DEV, 128), jnp.int32),
             pltpu.SMEM((16, FRONT), jnp.int32),
             pltpu.SMEM((1, FRONT), F32),
             dma, dma((3,)), dma, dma, dma, dma, dma((5, 3)), dma((5, 3)),
-            dma((3, 8)), dma((3, 8)), dma((4,)), dma((4,)), dma((4,)), dma((4,)), dma, dma, dma((2,)), dma((2,)),
+            dma((3, 8)), dma((3, 8)), dma((4,)), dma((4,)), dma((4,)), dma((4,)),
+            dma((2,)), dma((2, 2)), dma((2, 2, 3)), dma((2, 2, 3)), dma((2,)), dma((2,)),
         ],
         compiler_params=pltpu.CompilerParams(
             collective_id=0, has_side_effects=True, vmem_limit_bytes=62 * 2**20
@@ -581,13 +618,14 @@
 
 
 def update_kernel(
-    res1, gm1, mom2, x2, w1own, w2own, bias, biasm, biasv,
+    res, w1own, w2own, bias, biasm, biasv,
     o_loss, o_first, o_second, o_mom1, o_mom2, o_flow, o_slow, o_bias, o_bm, o_bv,
     x1s,
 ):
     y = lax.axis_index("nar")
-    grad1 = jnp.concatenate([res1[0:256, :], res1[256:512, :]], axis=1)
-    mom1 = MU * gm1[...].reshape(2 * D_IN, HID) + grad1
+    mom1 = jnp.concatenate(
+        [res[i * 256:i * 256 + 256, :] + res[ROW_G1 + i * 256:ROW_G1 + i * 256 + 256, :] for i in range(2)], axis=1
+    )
     x1s[...] = mom1
     block64 = pl.ds(pl.multiple_of(y * 64, 64), 64)
     o_mom1[...] = x1s[block64, :]
@@ -598,12 +636,12 @@
     first_new = w1own[...] * (1.0 - WDECAY) - x1s[block64, :]
     o_first[...] = first_new
     o_flow[...] = first_new.astype(BF)
-    second = w2own[...] * (1.0 - WDECAY) - (2 * HID / CLS) ** 0.5 * x2[0:CLS, :]
+    second = w2own[...] * (1.0 - WDECAY) - (2 * HID / CLS) ** 0.5 * res[ROW_X2:ROW_X2 + CLS, :]
     o_second[...] = second
     o_slow[...] = second.astype(BF)
-    o_mom2[...] = mom2[0:CLS, :]
-
-    gb = res1[512:516, :] + res1[516:520, :]
+    o_mom2[...] = res[ROW_M2:ROW_M2 + CLS, :]
+
+    gb = res[512:516, :] + res[516:520, :]
     gb = jnp.concatenate([gb[0:1, :], gb[1:2, :], gb[2:3, :], gb[3:4, 0:44]], axis=1)
     m_new = BETA_ONE * biasm[...] + (1.0 - BETA_ONE) * gb
     v_new = BETA_TWO * biasv[...] + (1.0 - BETA_TWO) * gb * gb
@@ -612,7 +650,7 @@
     o_bias[...] = bias[...] * (1.0 - LR_BIAS * WDECAY) - LR_BIAS * m_hat / (jnp.sqrt(v_hat) + EPSILON)
     o_bm[...] = m_new
     o_bv[...] = v_new
-    o_loss[...] = res1[520:521, 0:1] + res1[521:522, 0:1]
+    o_loss[...] = res[520:521, 0:1] + res[521:522, 0:1]
 
 
 def update(*args):
@@ -624,7 +662,7 @@
             sds((1, 1), F32), sds((64, HID), F32), sds((CLS, 128), F32), sds((64, HID), F32), sds((CLS, 128), F32),
             sds((64, HID), BF), sds((CLS, 128), BF), sds((1, 428), F32), sds((1, 428), F32), sds((1, 428), F32),
         ],
-        in_specs=[vm] * 9,
+        in_specs=[vm] * 6,
         out_specs=[vm] * 10,
         scratch_shapes=[pltpu.VMEM((2 * D_IN, HID), F32)],
         compiler_params=pltpu.CompilerParams(vmem_limit_bytes=32 * 2**20),
@@ -636,12 +674,12 @@
     w_first, w_second, mom_first, mom_second, biases, bias_m, bias_v,
 ):
     w2own, bias = w_second.T, biases[None, :]
-    res1, gm1, mom2, x2 = main(
+    res = main(
         requests.T, features, index_one.T, mask_one.T, index_two.T, mask_two.T, labels[None, :], seed_live[None, :],
         w_first, w2own, mom_first, mom_second.T, bias,
     )
     loss, first_new, second_new, mom_one, mom_two, first_low, second_low, bias_new, m_new, v_new = update(
-        res1, gm1, mom2, x2, w_first, w2own, bias, bias_m[None, :], bias_v[None, :]
+        res, w_first, w2own, bias, bias_m[None, :], bias_v[None, :]
     )
     return (
         loss.reshape(()), first_new, second_new.T, mom_one, mom_two.T, first_low, second_low.T,

time: 178 us -> 171 us (0.961)
  Pallas kernels: 174 us -> 169 us
  local copies, waits for them, and re-layouts: 3.7 us -> 1.12 us
    pallas_call x1, Pallas kernels: 168 us -> 164 us  [main(): pl.pallas_call(main_kernel, out_shape=sds((ROWS, 128), F32), in_specs=[vm...]
    unnamed x18 -> x12, local copies, waits for them, and re-layouts: 3.7 us -> 1.12 us
where the time goes in v4:
time: 171 us
  Pallas kernels  169 us (99%)
    pallas_call x1, Pallas kernels, main(): pl.pallas_call(main_kernel, out_shape=sds((ROWS, 128), F32), in_specs=[vm...  164 us
    pallas_call x1, Pallas kernels, update(): pl.pallas_call(update_kernel, out_shape=[sds((1, 1), F32), sds((64, HID),...  5.46 us

profile of v4, /device:TPU:1, one launch (start us, length us, event | category | flops | bytes accessed | tf_op | source)
XLA Modules:
  0.0 171.2 jit_solution(1930032035475398080)
XLA Ops:
  0.6 0.0 copy-start.2
  0.7 0.0 copy-start.5
  0.7 0.0 copy-start.4
  0.7 0.0 copy-start.3
  0.7 0.0 copy-start.1
  0.7 163.9 %shard_map.222.res = f32[1392,128]{1,0:T(8,128)} custom-call(s32[64,128]{1,0:T(8,128)} %bitcast.28, bf16[8192,128]{1,0:T(8,128)(2,1)} %feat.1, s32[16,2048]{1,0:T(8,128)} %bitcast.25, s32[15,2048]{1,0:T(8,128)} %bitcast.26, s32[11,512]{1,0:T(8,128)} %bitcast.29, s32[10,512]{1,0:T(8,128)} %bitcast.30, s32[1,512]{1,0:T(1,128)} %bitcast.31, s32[1,512]{1,0:T(1,128)} %bitcast.32, ...), custom_call_target="tpu_custom_call" | custom-call | tf_op jit(solution)/shard_map/pallas_call | solution.py:566
  164.6 0.0 copy-done.2
  164.6 0.0 copy-done.5
  164.6 0.0 copy-done.4
  164.7 0.0 copy-done.3
  164.7 0.0 copy-done.1
  164.7 0.0 copy-start
  164.7 1.1 copy-done
  165.8 5.5 %shard_map.223 = (f32[1,1]{1,0:T(1,128)}, f32[64,256]{1,0:T(8,128)}, f32[172,128]{1,0:T(8,128)}, f32[64,256]{1,0:T(8,128)}, f32[172,128]{1,0:T(8,128)}, /*index=...) custom-call(f32[1392,128]{1,0:T(8,128)S(1)} %copy-done, ...), custom_call_target="tpu_custom_call" | custom-call | tf_op jit(solution)/shard_map/pallas_call | solution.py:659
Async XLA Ops:
  0.6 164.0 %copy-start.2 = (f32[64,256]{1,0:T(8,128)S(1)}, f32[64,256]{1,0:T(8,128)}, u32[]{:S(2)}) copy-start(f32[64,256]{1,0:T(8,128)} %w1own.1) | copy-start | bytes 196612
  0.7 164.0 %copy-start.5 = (f32[428]{0:T(512)S(1)}, f32[428]{0:T(512)}, u32[]{:S(2)}) copy-start(f32[428]{0:T(512)} %param.29) | copy-start | bytes 5140
  0.7 164.0 %copy-start.4 = (f32[428]{0:T(512)S(1)}, f32[428]{0:T(512)}, u32[]{:S(2)}) copy-start(f32[428]{0:T(512)} %param.28) | copy-start | bytes 5140
  0.7 164.0 %copy-start.3 = (f32[428]{0:T(512)S(1)}, f32[428]{0:T(512)}, u32[]{:S(2)}) copy-start(f32[428]{0:T(512)} %param.27) | copy-start | bytes 5140
  0.7 164.0 %copy-start.1 = (f32[128,172]{0,1:T(8,128)S(1)}, f32[128,172]{0,1:T(8,128)}, u32[]{:S(2)}) copy-start(f32[128,172]{0,1:T(8,128)} %param.24) | copy-start | bytes 264196
  164.7 1.1 copy-start

commit v5 on v4

--- a/solution.py
+++ b/solution.py
@@ -59,6 +59,7 @@
 
 NN = ((1,), (0,))
 NT = ((1,), (1,))
+TN = ((0,), (0,))
 
 
 def split(a):
@@ -86,8 +87,8 @@
 def main_kernel(
     reqt, feat, idx1t, msk1t, idx2t, msk2t, labels, live, w1, w2own, m1, m2own, bias,
     o_all,
-    table, featb, pulled, stage, reqv, reqin, idxv, invv, near, own, z1t, gbuf, fsel, bsel, idc, rbuf, dbuf,
-    gw1, gw2t, gm1, gm2t, gidx2, w1t, w2, b1c, b2c, pay1, pay2, misc, inbox1, inbox2, ybox1, ybox2, res2, x2s,
+    table, featb, pulled, stage, reqv, reqin, idxv, invv, near, own, z1, a1t, gbuf, fsel, bsel, idc, invc, livec, rbuf, dbuf,
+    gw1, gw2t, gm1, gm2t, gidx2, w2t, b2c, pay1, pay2, misc, inbox1, inbox2, ybox1, ybox2, res2, x2s,
     reqs, idx, inv,
     feat_sem, loc_sem, req_send, req_recv, row_send, row_recv, nar_send, nar_recv,
     h_send, h_recv, r_send, r_recv, d_send, d_recv, rs_send, rs_recv, y_send, y_recv, ag_send, ag_recv,
@@ -193,65 +194,65 @@
     for n, a in enumerate(shared):
         for d in range(1, NAR):
             link(a.at[y], a.at[y], nar_send.at[n, d - 1], nar_recv.at[n, d - 1], (y + d) % NAR).wait()
-    w1t[...] = gw1[...].reshape(2 * D_IN, HID).T
     for q in range(NAR):
         o_all[ROW_G1 + q * 64:ROW_G1 + q * 64 + 64, :] = MU * gm1[q, :, 0:128]
         o_all[ROW_G1 + 256 + q * 64:ROW_G1 + 256 + q * 64 + 64, :] = MU * gm1[q, :, 128:256]
-    w2t = jnp.concatenate([gw2t[q] for q in range(NAR)], axis=1)
-    w2[...] = w2t.T
-    b1c[...] = jnp.concatenate([spread(bias[0:1, 0:128]), spread(bias[0:1, 128:256])], axis=0)
+    for q in range(NAR):
+        w2t[:, q * 128:(q + 1) * 128] = gw2t[q]
     last = jnp.concatenate([bias[0:1, 384:428], jnp.zeros((1, 84), F32)], axis=1)
     b2c[...] = jnp.concatenate([spread(bias[0:1, 256:384]), spread(last)], axis=0)
 
+    def column(row):
+        return jnp.concatenate([spread(row[:, c * 128:(c + 1) * 128]) for c in range(SEED // 128)], axis=0)
+
+    for q in range(NAR):
+        n = jnp.sum((gidx2[q, 1:1 + F2, :] >= 0).astype(F32), axis=0, keepdims=True)
+        invc[q] = column(1.0 / jnp.maximum(n, 1.0))
+    livec[...] = column(2.0 * LAM / HID / SEEDS_ALL * live[...].astype(F32))
+
+    lane16 = lax.broadcasted_iota(jnp.int32, (16, 128), 1).astype(jnp.int16)
     iota16 = lax.broadcasted_iota(jnp.int32, (16, 128), 0).astype(jnp.int16)
     one, zero = jnp.ones((16, 128), BF), jnp.zeros((16, 128), BF)
 
-    def select(ids, base, groups, put):
-        ids = ids - base
-        rows = [
-            [jnp.broadcast_to(ids[k:k + 1, c * 128:(c + 1) * 128], (16, 128)).astype(jnp.int16) for c in range(4)]
-            for k in range(1 + F2)
+    def marks(here, want):
+        acc = jnp.where(here == want[1], one, zero)
+        for k in range(2, 1 + F2):
+            acc = acc + jnp.where(here == want[k], one, zero)
+        return acc, jnp.where(here == want[0], one, zero)
+
+    idc[...] = gidx2[y].T
+
+    def forward_marks(i, carry):
+        at = pl.multiple_of(i * 16, 16)
+        blk = idc[pl.ds(at, 16), :]
+        want = [jnp.broadcast_to(blk[:, k:k + 1], (16, 128)).astype(jnp.int16) for k in range(1 + F2)]
+        for q in range(NAR):
+            for c in range(FRONT // 128):
+                here = lane16 + jnp.full((16, 128), q * FRONT + c * 128, jnp.int32).astype(jnp.int16)
+                a, b = marks(here, want)
+                fsel[q, pl.ds(at, 16), c * 128:(c + 1) * 128] = a
+                fsel[q, pl.ds(SEED + at, 16), c * 128:(c + 1) * 128] = b
+        return carry
+
+    lax.fori_loop(0, SEED // 16, forward_marks, 0)
+
+    for q in range(NAR):
+        ids = gidx2[q] - y * FRONT
+        wants = [
+            [jnp.broadcast_to(ids[k:k + 1, c * 128:(c + 1) * 128], (16, 128)).astype(jnp.int16) for k in range(1 + F2)]
+            for c in range(SEED // 128)
         ]
 
-        def body(i, carry):
+        def backward_marks(i, carry, q=q, wants=wants):
             here = iota16 + jnp.full((16, 128), i * 16, jnp.int32).astype(jnp.int16)
             out = pl.ds(pl.multiple_of(i * 16, 16), 16)
-            for c in range(4):
-                acc = jnp.where(here == rows[1][c], one, zero)
-                for k in range(2, 1 + F2):
-                    acc = acc + jnp.where(here == rows[k][c], one, zero)
-                put(out, c * 128, acc)
-                put(out, SEED + c * 128, jnp.where(here == rows[0][c], one, zero))
+            for c in range(SEED // 128):
+                a, b = marks(here, wants[c])
+                bsel[q, out, c * 128:(c + 1) * 128] = a
+                bsel[q, out, SEED + c * 128:SEED + (c + 1) * 128] = b
             return carry
 
-        lax.fori_loop(0, groups, body, 0)
-
-    def put_f(rows, col, v):
-        fsel[rows, col:col + 128] = v
-
-    select(gidx2[y], 0, SRC // 16, put_f)
-    lane16 = lax.broadcasted_iota(jnp.int32, (16, 128), 1).astype(jnp.int16)
-
-    idc[...] = (jnp.concatenate([gidx2[q] for q in range(NAR)], axis=0) - y * FRONT).T
-
-    def select_rows(q, group):
-        at = pl.multiple_of(group * 16, 16)
-        blk = idc[pl.ds(at, 16), :]
-        want = [jnp.broadcast_to(blk[:, q * 16 + k:q * 16 + k + 1], (16, 128)).astype(jnp.int16) for k in range(1 + F2)]
-        for c in range(FRONT // 128):
-            here = lane16 + jnp.full((16, 128), c * 128, jnp.int32).astype(jnp.int16)
-            acc = jnp.where(here == want[1], one, zero)
-            for k in range(2, 1 + F2):
-                acc = acc + jnp.where(here == want[k], one, zero)
-            bsel[q, pl.ds(at, 16), c * 128:(c + 1) * 128] = acc
-            bsel[q, pl.ds(SEED + at, 16), c * 128:(c + 1) * 128] = jnp.where(here == want[0], one, zero)
-
-    for q in range(NAR):
-        def all_rows(i, carry, q=q):
-            select_rows(q, i)
-            return carry
-
-        lax.fori_loop(0, SEED // 16, all_rows, 0)
+        lax.fori_loop(0, FRONT // 16, backward_marks, 0)
 
     come = pulled.at[pl.ds(0, (DEV - 1) * CAP)]
     pltpu.make_async_copy(come, come, row_recv).wait()
@@ -276,13 +277,13 @@
     def forward(b):
         @pl.when(b % 2 == 0)
         def _():
-            blk = gbuf.at[left, :, cols(b)]
+            blk = gbuf.at[left, cols(b), :]
             link(blk, blk, h_send.at[0, b], h_recv.at[0, b], right).wait_recv()
             link(blk, blk, h_send.at[2, b], h_recv.at[2, b], right).start()
 
         @pl.when(b % 2 == 1)
         def _():
-            blk = gbuf.at[right, :, cols(b)]
+            blk = gbuf.at[right, cols(b), :]
             link(blk, blk, h_send.at[1, b], h_recv.at[1, b], left).wait_recv()
             link(blk, blk, h_send.at[2, b], h_recv.at[2, b], left).start()
 
@@ -304,10 +305,10 @@
         act = jnp.concatenate([own[...].astype(BF), near[...].astype(BF)], axis=1)
         a1[rows, :] = act[:, :128]
         a1[pl.ds(pl.multiple_of(FRONT + b * 256, 256), 256), :] = act[:, 128:]
-        z = dot(w1t[...], act, NT) + jnp.concatenate([b1c[...], b1c[...]], axis=1)
-        z1t[:, rows] = z
-        gbuf[y, :, rows] = (z / (1.0 + jnp.exp(-z))).astype(BF)
-        blk = gbuf.at[y, :, rows]
+        z = dot(act, gw1[...].reshape(2 * D_IN, HID)) + bias[0:1, 0:HID]
+        z1[rows, :] = z
+        gbuf[y, rows, :] = (z / (1.0 + jnp.exp(-z))).astype(BF)
+        blk = gbuf.at[y, rows, :]
         link(blk, blk, h_send.at[0, b], h_recv.at[0, b], right).start()
         link(blk, blk, h_send.at[1, b], h_recv.at[1, b], left).start()
 
@@ -321,30 +322,30 @@
     forward(7)
 
     def from_source(q):
-        return dot(gbuf[q], fsel[pl.ds(pl.multiple_of(q * FRONT, FRONT), FRONT), :])
+        return dot(fsel[q], gbuf[q])
 
     total = from_source(y)
     for b in range(1, 8, 2):
-        blk = gbuf.at[left, :, b * 256:(b + 1) * 256]
+        blk = gbuf.at[left, b * 256:(b + 1) * 256, :]
         link(blk, blk, h_send.at[0, b], h_recv.at[0, b], right).wait_recv()
     total = total + from_source(left)
     for b in range(0, 8, 2):
-        blk = gbuf.at[right, :, b * 256:(b + 1) * 256]
+        blk = gbuf.at[right, b * 256:(b + 1) * 256, :]
         link(blk, blk, h_send.at[1, b], h_recv.at[1, b], left).wait_recv()
     total = total + from_source(right)
     for b in range(8):
-        blk = gbuf.at[opp, :, b * 256:(b + 1) * 256]
+        blk = gbuf.at[opp, b * 256:(b + 1) * 256, :]
         link(blk, blk, h_send.at[2, b], h_recv.at[2, b], right).wait_recv()
     total = total + from_source(opp)
 
-    def inverse_count(ids):
-        n = jnp.sum((ids[1:1 + F2, :] >= 0).astype(F32), axis=0, keepdims=True)
-        return 1.0 / jnp.maximum(n, 1.0)
-
-    near2 = (total[:, :SEED] * inverse_count(gidx2[y])).astype(BF)
-    self2 = total[:, SEED:].astype(BF)
+    def wide(a):
+        return jnp.concatenate([a, a], axis=1)
+
+    near2 = (total[:SEED, :] * wide(invc[y])).astype(BF)
+    self2 = total[SEED:, :].astype(BF)
     alive = live[...].astype(F32)
     diff = self2.astype(F32) - near2.astype(F32)
+    pull_apart = wide(livec[...]) * diff
 
     def swap_start(buf, ssem, rsem):
         blk = buf.at[y]
@@ -376,14 +377,13 @@
         half = buf.at[right, cut:, :]
         link(half, half, ssem.at[3], rsem.at[3], left).wait_send()
 
-    rbuf[y] = (2.0 * LAM / HID / SEEDS_ALL * alive * diff).astype(BF)
+    rbuf[y] = pull_apart.astype(BF)
     swap_start(rbuf, r_send, r_recv)
 
-    act2 = jnp.concatenate([self2, near2], axis=0)
-    w2t = jnp.concatenate([gw2t[q] for q in range(NAR)], axis=1)
+    act2 = jnp.concatenate([self2, near2], axis=1)
     cls = lax.broadcasted_iota(jnp.int32, (CLS_PAD, SEED), 0)
     b2 = b2c[0:CLS_PAD, :]
-    logits = dot(w2t, act2) + jnp.concatenate([b2] * 4, axis=1)
+    logits = dot(w2t[...], act2, NT) + jnp.concatenate([b2] * 4, axis=1)
     logits = jnp.where(cls < CLS, logits, -1e30)
     top = jnp.max(logits, axis=0, keepdims=True)
     e = jnp.exp(logits - top)
@@ -394,9 +394,9 @@
     dbuf[y] = dlog
     swap_start(dbuf, d_send, d_recv)
 
-    terms = top + jnp.log(tot) - picked + LAM / HID * jnp.sum(diff * diff, axis=0, keepdims=True)
-    loss = jnp.sum(alive * terms, axis=1, keepdims=True)
-    g2t = dot(dlog, act2, NT).astype(BF)
+    loss = jnp.sum(alive * (top + jnp.log(tot) - picked), axis=1, keepdims=True)
+    loss = loss + SEEDS_ALL / 2 * jnp.sum(pull_apart * diff, keepdims=True)
+    g2t = dot(dlog, act2).astype(BF)
     for q in range(NAR):
         pay2[q * CLS_PAD:(q + 1) * CLS_PAD, :] = g2t[:, q * 128:(q + 1) * 128]
 
@@ -475,40 +475,39 @@
 
     to_owner(pay2, inbox2, P2, 1)
 
-    def grads(q):
-        da = dot(w2[...], dbuf[q])
+    def add_grads(q, fresh=False):
+        da = dot(dbuf[q], w2t[...], TN)
         r = rbuf[q].astype(F32)
-        ds = (da[:HID] + r).astype(BF)
-        dn = ((da[HID:] - r) * inverse_count(gidx2[q])).astype(BF)
-        return dot(jnp.concatenate([dn, ds], axis=1), bsel[q])
-
-    swap_forward(rbuf, r_send, r_recv, 128)
-    def add_grads(q, fresh=False):
-        part = grads(q)
-        for c in range(FRONT // 128):
+        ds = (da[:, :HID] + r).astype(BF)
+        dn = ((da[:, HID:] - r) * wide(invc[q])).astype(BF)
+        part = dot(bsel[q], jnp.concatenate([dn, ds], axis=0))
+        for c in range(2):
+            rows = slice(c * FRONT, (c + 1) * FRONT)
             now = part[:, c * 128:(c + 1) * 128]
-            dh1[c * 256:(c + 1) * 256, :] = now if fresh else dh1[c * 256:(c + 1) * 256, :] + now
-
+            dh1[rows, :] = now if fresh else dh1[rows, :] + now
+
+    for c in range(2):
+        a1t[c * 128:(c + 1) * 128, :] = a1[c * FRONT:(c + 1) * FRONT, :].T
+    db2 = jnp.sum(dlog.astype(F32), axis=1, keepdims=True)
+    db2 = jnp.broadcast_to(db2, (CLS_PAD, 128)).T[0:1, :]
+    swap_forward(rbuf, r_send, r_recv, SEED // 2)
     add_grads(y, True)
     swap_forward(dbuf, d_send, d_recv, 96)
     add_grads(left)
     add_grads(right)
-    swap_end(rbuf, r_send, r_recv, 128)
+    swap_end(rbuf, r_send, r_recv, SEED // 2)
     swap_end(dbuf, d_send, d_recv, 96)
     add_grads(opp)
     add_plane(pay2, inbox2, ybox2, P2, 1)
 
-    z = z1t[...]
+    z = z1[...]
     sig = 1.0 / (1.0 + jnp.exp(-z))
-    dh = jnp.concatenate([dh1[c * 256:(c + 1) * 256, :] for c in range(FRONT // 128)], axis=1)
+    dh = jnp.concatenate([dh1[0:FRONT, :], dh1[FRONT:2 * FRONT, :]], axis=1)
     dz = (dh * sig * (1.0 + z * (1.0 - sig))).astype(BF)
-    g1 = jnp.concatenate([dot(dz, a1[0:FRONT, :]), dot(dz, a1[FRONT:2 * FRONT, :])], axis=1).T.astype(BF)
+    g1 = dot(a1t[...], dz).astype(BF)
     pay1[0:256, :] = g1[:, :128]
     pay1[256:512, :] = g1[:, 128:]
-    ones_f = jnp.ones((8, FRONT), BF)
-    ones_s = jnp.ones((8, SEED), BF)
-    db1 = dot(ones_f, dz, NT)[0:1, :]
-    db2 = dot(ones_s, dlog, NT)[0:1, :]
+    db1 = jnp.sum(dz.astype(F32), axis=0, keepdims=True)
     misc[...] = jnp.zeros((16, 128), F32)
 
     def two(rows, v):
@@ -546,12 +545,12 @@
     take(o_all, P1, 0)
 
     for b in range(8):
-        blk = gbuf.at[y, :, b * 256:(b + 1) * 256]
+        blk = gbuf.at[y, b * 256:(b + 1) * 256, :]
         link(blk, blk, h_send.at[0, b], h_recv.at[0, b], right).wait_send()
         link(blk, blk, h_send.at[1, b], h_recv.at[1, b], left).wait_send()
-        blk = gbuf.at[opp, :, b * 256:(b + 1) * 256]
+        blk = gbuf.at[opp, b * 256:(b + 1) * 256, :]
         link(blk, blk, h_send.at[2, b], h_recv.at[2, b], right).wait_send()
-    swap_sent(rbuf, r_send, r_recv, 128)
+    swap_sent(rbuf, r_send, r_recv, SEED // 2)
     swap_sent(dbuf, d_send, d_recv, 96)
 
     sums_sent(pay2, P2, 1)
@@ -579,21 +578,22 @@
             V((1, FRONT), F32),
             V((256, D_IN), F32),
             V((256, D_IN), F32),
-            V((HID, FRONT), F32),
-            V((NAR, HID, FRONT), BF),
-            V((SRC, 2 * SEED), BF),
+            V((FRONT, HID), F32),
+            V((2 * D_IN, FRONT), BF),
+            V((NAR, FRONT, HID), BF),
             V((NAR, 2 * SEED, FRONT), BF),
-            V((SEED, 16 * NAR), jnp.int32),
-            V((NAR, HID, SEED), BF),
+            V((NAR, FRONT, 2 * SEED), BF),
+            V((SEED, 16), jnp.int32),
+            V((NAR, SEED, 128), F32),
+            V((SEED, 128), F32),
+            V((NAR, SEED, HID), BF),
             V((NAR, CLS_PAD, SEED), BF),
             V((NAR, 64, HID), BF),
             V((NAR, CLS_PAD, 128), BF),
             V((NAR, 64, HID), F32),
             V((NAR, CLS_PAD, 128), F32),
             V((NAR, 16, SEED), jnp.int32),
-            V((HID, 2 * D_IN), BF),
-            V((2 * HID, CLS_PAD), BF),
-            V((HID, 128), F32),
+            V((CLS_PAD, 2 * HID), BF),
             V((HID, 128), F32),
             V((P1 * 16, 128), BF),
             V((P2 * 16, 128), BF),

time: 171 us -> 172 us (level)
  no operation moved by 1% of the time
where the time goes in v5:
time: 172 us; the launch traced here: 171 us
  Pallas kernels  170 us (99%)
    pallas_call x1, Pallas kernels, main(): pl.pallas_call(main_kernel, out_shape=sds((ROWS, 128), F32), in_specs=[vm...  164 us
    pallas_call x1, Pallas kernels, update(): pl.pallas_call(update_kernel, out_shape=[sds((1, 1), F32), sds((64, HID),...  5.46 us

profile of v5, /device:TPU:1, one launch (start us, length us, event | category | flops | bytes accessed | tf_op | source)
XLA Modules:
  0.0 171.4 jit_solution(16560089011489621301)
XLA Ops:
  0.6 0.0 copy-start.2
  0.7 0.0 copy-start.5
  0.7 0.0 copy-start.4
  0.7 0.0 copy-start.3
  0.7 0.0 copy-start.1
  0.7 164.1 %shard_map.222.res = f32[1392,128]{1,0:T(8,128)} custom-call(s32[64,128]{1,0:T(8,128)} %bitcast.28, bf16[8192,128]{1,0:T(8,128)(2,1)} %feat.1, s32[16,2048]{1,0:T(8,128)} %bitcast.25, s32[15,2048]{1,0:T(8,128)} %bitcast.26, s32[11,512]{1,0:T(8,128)} %bitcast.29, s32[10,512]{1,0:T(8,128)} %bitcast.30, s32[1,512]{1,0:T(1,128)} %bitcast.31, s32[1,512]{1,0:T(1,128)} %bitcast.32, ...), custom_call_target="tpu_custom_call" | custom-call | tf_op jit(solution)/shard_map/pallas_call | solution.py:565
  164.8 0.0 copy-done.2
  164.8 0.0 copy-done.5
  164.8 0.0 copy-done.4
  164.8 0.0 copy-done.3
  164.8 0.0 copy-done.1
  164.8 0.0 copy-start
  164.8 1.1 copy-done
  165.9 5.5 %shard_map.223 = (f32[1,1]{1,0:T(1,128)}, f32[64,256]{1,0:T(8,128)}, f32[172,128]{1,0:T(8,128)}, f32[64,256]{1,0:T(8,128)}, f32[172,128]{1,0:T(8,128)}, /*index=...) custom-call(f32[1392,128]{1,0:T(8,128)S(1)} %copy-done, ...), custom_call_target="tpu_custom_call" | custom-call | tf_op jit(solution)/shard_map/pallas_call | solution.py:659
Async XLA Ops:
  0.6 164.1 %copy-start.2 = (f32[64,256]{1,0:T(8,128)S(1)}, f32[64,256]{1,0:T(8,128)}, u32[]{:S(2)}) copy-start(f32[64,256]{1,0:T(8,128)} %w1own.1) | copy-start | bytes 196612
  0.7 164.1 %copy-start.5 = (f32[428]{0:T(512)S(1)}, f32[428]{0:T(512)}, u32[]{:S(2)}) copy-start(f32[428]{0:T(512)} %param.29) | copy-start | bytes 5140
  0.7 164.1 %copy-start.4 = (f32[428]{0:T(512)S(1)}, f32[428]{0:T(512)}, u32[]{:S(2)}) copy-start(f32[428]{0:T(512)} %param.28) | copy-start | bytes 5140
  0.7 164.1 %copy-start.3 = (f32[428]{0:T(512)S(1)}, f32[428]{0:T(512)}, u32[]{:S(2)}) copy-start(f32[428]{0:T(512)} %param.27) | copy-start | bytes 5140
  0.7 164.1 %copy-start.1 = (f32[128,172]{0,1:T(8,128)S(1)}, f32[128,172]{0,1:T(8,128)}, u32[]{:S(2)}) copy-start(f32[128,172]{0,1:T(8,128)} %param.24) | copy-start | bytes 264196
  164.8 1.1 copy-start

commit v6 on v5

--- a/solution.py
+++ b/solution.py
@@ -87,7 +87,7 @@
 def main_kernel(
     reqt, feat, idx1t, msk1t, idx2t, msk2t, labels, live, w1, w2own, m1, m2own, bias,
     o_all,
-    table, featb, pulled, stage, reqv, reqin, idxv, invv, near, own, z1, a1t, gbuf, fsel, bsel, idc, invc, livec, rbuf, dbuf,
+    table, featb, pulled, stage, reqv, reqin, idxv, invv, near, own, z1, a1t, gbuf, fsel, bsel, wants, idc, invc, livec, rbuf, dbuf,
     gw1, gw2t, gm1, gm2t, gidx2, w2t, b2c, pay1, pay2, misc, inbox1, inbox2, ybox1, ybox2, res2, x2s,
     reqs, idx, inv,
     feat_sem, loc_sem, req_send, req_recv, row_send, row_recv, nar_send, nar_recv,
@@ -238,21 +238,19 @@
 
     for q in range(NAR):
         ids = gidx2[q] - y * FRONT
-        wants = [
-            [jnp.broadcast_to(ids[k:k + 1, c * 128:(c + 1) * 128], (16, 128)).astype(jnp.int16) for k in range(1 + F2)]
-            for c in range(SEED // 128)
-        ]
-
-        def backward_marks(i, carry, q=q, wants=wants):
-            here = iota16 + jnp.full((16, 128), i * 16, jnp.int32).astype(jnp.int16)
-            out = pl.ds(pl.multiple_of(i * 16, 16), 16)
+        for c in range(SEED // 128):
+            for k in range(1 + F2):
+                row = ids[k:k + 1, c * 128:(c + 1) * 128]
+                wants[q, c, k] = jnp.broadcast_to(row, (16, 128)).astype(jnp.int16)
+
+    def backward_marks(i):
+        here = iota16 + jnp.full((16, 128), i * 16, jnp.int32).astype(jnp.int16)
+        out = pl.ds(pl.multiple_of(i * 16, 16), 16)
+        for q in range(NAR):
             for c in range(SEED // 128):
-                a, b = marks(here, wants[c])
+                a, b = marks(here, [wants[q, c, k] for k in range(1 + F2)])
                 bsel[q, out, c * 128:(c + 1) * 128] = a
                 bsel[q, out, SEED + c * 128:SEED + (c + 1) * 128] = b
-            return carry
-
-        lax.fori_loop(0, FRONT // 16, backward_marks, 0)
 
     come = pulled.at[pl.ds(0, (DEV - 1) * CAP)]
     pltpu.make_async_copy(come, come, row_recv).wait()
@@ -289,6 +287,7 @@
 
     def block(b, c):
         def some(i, c2):
+            backward_marks(b * 16 + i)
             base = pl.multiple_of(b * 256 + i * 16, 16)
             for j in range(16):
                 m = base + j
@@ -495,10 +494,11 @@
     swap_forward(dbuf, d_send, d_recv, 96)
     add_grads(left)
     add_grads(right)
+    add_plane(pay2, inbox2, ybox2, P2, 1)
     swap_end(rbuf, r_send, r_recv, SEED // 2)
     swap_end(dbuf, d_send, d_recv, 96)
+    add_group(ybox2, res2, P2, 1)
     add_grads(opp)
-    add_plane(pay2, inbox2, ybox2, P2, 1)
 
     z = z1[...]
     sig = 1.0 / (1.0 + jnp.exp(-z))
@@ -524,9 +524,7 @@
     misc[9:10, 0:1] = loss - hi
     pay1[512:528, :] = misc[...].astype(BF)
     to_owner(pay1, inbox1, P1, 0)
-    add_group(ybox2, res2, P2, 1)
-
-    add_plane(pay1, inbox1, ybox1, P1, 0)
+
     take(res2, P2, 1)
     mom2 = jnp.concatenate(
         [MU * gm2t[q] + res2[q * CLS_PAD:(q + 1) * CLS_PAD, :] for q in range(NAR)], axis=1
@@ -536,8 +534,10 @@
     o_all[ROW_M2:ROW_M2 + CLS_PAD, :] = x2s[y]
     x2 = mom2 * (1.0 / (jnp.sqrt(jnp.sum(mom2 * mom2, keepdims=True)) + 1e-07))
     x2 = ns_step(x2)
+    add_plane(pay1, inbox1, ybox1, P1, 0)
+    x2 = ns_step(x2)
     add_group(ybox1, o_all, P1, 0)
-    for _ in range(NS_ITERS - 1):
+    for _ in range(NS_ITERS - 2):
         x2 = ns_step(x2)
     for q in range(NAR):
         x2s[q] = x2[:, q * 128:(q + 1) * 128]
@@ -583,6 +583,7 @@
             V((NAR, FRONT, HID), BF),
             V((NAR, 2 * SEED, FRONT), BF),
             V((NAR, FRONT, 2 * SEED), BF),
+            V((NAR, 4, 1 + F2, 16, 128), jnp.int16),
             V((SEED, 16), jnp.int32),
             V((NAR, SEED, 128), F32),
             V((SEED, 128), F32),

time: 172 us -> 167 us (0.971)
  Pallas kernels: 170 us -> 165 us
    pallas_call x1, Pallas kernels: 164 us -> 160 us  [main(): pl.pallas_call(main_kernel, out_shape=sds((ROWS, 128), F32), in_specs=[vm...]
where the time goes in v6:
time: 167 us
  Pallas kernels  165 us (99%)
    pallas_call x1, Pallas kernels, main(): pl.pallas_call(main_kernel, out_shape=sds((ROWS, 128), F32), in_specs=[vm...  160 us
    pallas_call x1, Pallas kernels, update(): pl.pallas_call(update_kernel, out_shape=[sds((1, 1), F32), sds((64, HID),...  5.46 us

profile of v6, /device:TPU:1, one launch (start us, length us, event | category | flops | bytes accessed | tf_op | source)
XLA Modules:
  0.0 166.9 jit_solution(4417257877804110116)
XLA Ops:
  0.6 0.0 copy-start.2
  0.7 0.0 copy-start.5
  0.7 0.0 copy-start.4
  0.7 0.0 copy-start.3
  0.7 0.0 copy-start.1
  0.7 159.6 %shard_map.222.res = f32[1392,128]{1,0:T(8,128)} custom-call(s32[64,128]{1,0:T(8,128)} %bitcast.28, bf16[8192,128]{1,0:T(8,128)(2,1)} %feat.1, s32[16,2048]{1,0:T(8,128)} %bitcast.25, s32[15,2048]{1,0:T(8,128)} %bitcast.26, s32[11,512]{1,0:T(8,128)} %bitcast.29, s32[10,512]{1,0:T(8,128)} %bitcast.30, s32[1,512]{1,0:T(1,128)} %bitcast.31, s32[1,512]{1,0:T(1,128)} %bitcast.32, ...), custom_call_target="tpu_custom_call" | custom-call | tf_op jit(solution)/shard_map/pallas_call | solution.py:565
  160.3 0.0 copy-done.2
  160.3 0.0 copy-done.5
  160.3 0.0 copy-done.4
  160.3 0.0 copy-done.3
  160.3 0.0 copy-done.1
  160.4 0.0 copy-start
  160.4 1.1 copy-done
  161.5 5.5 %shard_map.223 = (f32[1,1]{1,0:T(1,128)}, f32[64,256]{1,0:T(8,128)}, f32[172,128]{1,0:T(8,128)}, f32[64,256]{1,0:T(8,128)}, f32[172,128]{1,0:T(8,128)}, /*index=...) custom-call(f32[1392,128]{1,0:T(8,128)S(1)} %copy-done, ...), custom_call_target="tpu_custom_call" | custom-call | tf_op jit(solution)/shard_map/pallas_call | solution.py:660
Async XLA Ops:
  0.6 159.7 %copy-start.2 = (f32[64,256]{1,0:T(8,128)S(1)}, f32[64,256]{1,0:T(8,128)}, u32[]{:S(2)}) copy-start(f32[64,256]{1,0:T(8,128)} %w1own.1) | copy-start | bytes 196612
  0.7 159.7 %copy-start.5 = (f32[428]{0:T(512)S(1)}, f32[428]{0:T(512)}, u32[]{:S(2)}) copy-start(f32[428]{0:T(512)} %param.29) | copy-start | bytes 5140
  0.7 159.7 %copy-start.4 = (f32[428]{0:T(512)S(1)}, f32[428]{0:T(512)}, u32[]{:S(2)}) copy-start(f32[428]{0:T(512)} %param.28) | copy-start | bytes 5140
  0.7 159.7 %copy-start.3 = (f32[428]{0:T(512)S(1)}, f32[428]{0:T(512)}, u32[]{:S(2)}) copy-start(f32[428]{0:T(512)} %param.27) | copy-start | bytes 5140
  0.7 159.7 %copy-start.1 = (f32[128,172]{0,1:T(8,128)S(1)}, f32[128,172]{0,1:T(8,128)}, u32[]{:S(2)}) copy-start(f32[128,172]{0,1:T(8,128)} %param.24) | copy-start | bytes 264196
  160.4 1.1 copy-start

commit v7 on v6

--- a/solution.py
+++ b/solution.py
@@ -90,7 +90,7 @@
     table, featb, pulled, stage, reqv, reqin, idxv, invv, near, own, z1, a1t, gbuf, fsel, bsel, wants, idc, invc, livec, rbuf, dbuf,
     gw1, gw2t, gm1, gm2t, gidx2, w2t, b2c, pay1, pay2, misc, inbox1, inbox2, ybox1, ybox2, res2, x2s,
     reqs, idx, inv,
-    feat_sem, loc_sem, req_send, req_recv, row_send, row_recv, nar_send, nar_recv,
+    feat_sem, loc_sem, ask_sem, req_send, req_recv, row_send, row_recv, nar_send, nar_recv,
     h_send, h_recv, r_send, r_recv, d_send, d_recv, rs_send, rs_recv, y_send, y_recv, ag_send, ag_recv,
 ):
     a1, dh1 = pulled, table
@@ -104,11 +104,17 @@
 
     barrier = pltpu.get_barrier_semaphore()
 
+    ys = [(y + d) % NAR for d in range(NAR)]
+
     def greet(i, c):
-        pl.semaphore_signal(barrier, inc=1, device_id=all_to((me + i) % DEV), device_id_type=MESH)
+        t = (g + i) % GRP
+        for d in range(NAR):
+            pl.semaphore_signal(barrier, inc=1, device_id=(t, ys[d]), device_id_type=MESH)
         return c
 
-    lax.fori_loop(1, DEV, greet, 0)
+    for d in range(1, NAR):
+        pl.semaphore_signal(barrier, inc=1, device_id=(g, ys[d]), device_id_type=MESH)
+    lax.fori_loop(1, GRP, greet, 0)
 
     def link(src, dst, ssem, rsem, to):
         return pltpu.make_async_remote_copy(
@@ -131,20 +137,28 @@
 
     pl.semaphore_wait(barrier, DEV - 1)
 
+    def ask_one(t, u, n):
+        row = t * NAR + u
+        pltpu.make_async_remote_copy(
+            src_ref=ask_rows.at[row], dst_ref=got_rows.at[me], send_sem=req_send, recv_sem=req_recv.at[n],
+            device_id=(t, u), device_id_type=MESH,
+        ).start()
+
     def ask(i, c):
-        t = (me + i * 37) % DEV
-        pltpu.make_async_remote_copy(
-            src_ref=ask_rows.at[t], dst_ref=got_rows.at[me], send_sem=req_send, recv_sem=req_recv,
-            device_id=all_to(t), device_id_type=MESH,
-        ).start()
+        n = (i * 13) % GRP
+        t = (g + n) % GRP
+        for d in range(NAR):
+            ask_one(t, ys[d], n)
         return c
 
-    lax.fori_loop(1, DEV, ask, 0)
+    for d in range(1, NAR):
+        ask_one(g, ys[d], 0)
+    lax.fori_loop(1, GRP, ask, 0)
+    reqin[pl.ds(me, 1), :] = reqv[pl.ds(me, 1), :]
     for n, a in enumerate(shared):
         for d in range(1, NAR):
             link(a.at[y], a.at[y], nar_send.at[n, d - 1], nar_recv.at[n, d - 1], (y + d) % NAR).start()
 
-    reqin[pl.ds(me, 1), :] = reqv[pl.ds(me, 1), :]
     msk = msk1t[...]
     idxv[0:1, :] = idx1t[0:1, :]
     idxv[1:16, :] = jnp.where(msk > 0, idx1t[1:16, :], SRC)
@@ -162,33 +176,58 @@
 
     lax.fori_loop(0, OWN // 256, widen_features, 0)
 
-    got = got_rows.at[pl.ds(0, DEV - 1)]
-    pltpu.make_async_copy(got, got, req_recv).wait()
-    fetch = pltpu.make_async_copy(reqin, reqs, loc_sem.at[2])
-    fetch.start()
-    fetch.wait()
-
     view = table.reshape(SRC + 8, 1, D_IN)
     my_rows = pl.ds(pl.multiple_of(me * CAP, CAP), CAP)
 
+    def pick(t, u, slot):
+        for r in range(CAP):
+            stage[r:r + 1, :] = view[reqs[t * NAR + u, 0, r]]
+        featb[slot, :] = stage[...].astype(BF)
+
+    def serve_one(t, u, slot):
+        pick(t, u, slot)
+        pltpu.make_async_remote_copy(
+            src_ref=featb.at[slot], dst_ref=pulled.at[my_rows],
+            send_sem=row_send, recv_sem=row_recv, device_id=(t, u), device_id_type=MESH,
+        ).start()
+
+    def asked(count, n):
+        rows = got_rows.at[pl.ds(0, count)]
+        pltpu.make_async_copy(rows, rows, req_recv.at[n]).wait()
+
+    def to_scalars(t, n):
+        rows = pl.ds(pl.multiple_of(t * NAR, NAR), NAR)
+        return pltpu.make_async_copy(got_rows.at[rows], reqs.at[rows], ask_sem.at[n])
+
+    def whose(i):
+        n = (i * 13) % GRP
+        return n, (g + GRP - n) % GRP
+
+    def fetch(i):
+        n, t = whose(i)
+        asked(NAR, n)
+        to_scalars(t, n).start()
+
     def serve(i, c):
-        t = (me + i * 37) % DEV
-        for r in range(CAP):
-            stage[r:r + 1, :] = view[reqs[t, r]]
-        slot = pl.ds(pl.multiple_of(i * CAP, CAP), CAP)
-        featb[slot, :] = stage[...].astype(BF)
-
-        @pl.when(i > 0)
+        n, t = whose(i)
+
+        @pl.when(i < GRP - 1)
         def _():
-            pltpu.make_async_remote_copy(
-                src_ref=featb.at[slot], dst_ref=pulled.at[my_rows],
-                send_sem=row_send, recv_sem=row_recv, device_id=all_to(t), device_id_type=MESH,
-            ).start()
-
+            fetch(i + 1)
+
+        to_scalars(t, n).wait()
+        for d in range(NAR):
+            serve_one(t, ys[d], pl.ds(pl.multiple_of((i * NAR + d) * CAP, CAP), CAP))
         return c
 
-    lax.fori_loop(1, DEV, serve, 0)
-    serve(0, 0)
+    fetch(1)
+    lax.fori_loop(1, GRP, serve, 0)
+    asked(NAR - 1, 0)
+    to_scalars(g, 0).start()
+    to_scalars(g, 0).wait()
+    for d in range(1, NAR):
+        serve_one(g, ys[d], pl.ds(d * CAP, CAP))
+    pick(g, y, pl.ds(0, CAP))
     pulled[my_rows, :] = featb[0:CAP, :]
 
     for n, a in enumerate(shared):
@@ -254,7 +293,7 @@
 
     come = pulled.at[pl.ds(0, (DEV - 1) * CAP)]
     pltpu.make_async_copy(come, come, row_recv).wait()
-    gone = featb.at[pl.ds(0, (DEV - 1) * CAP)]
+    gone = featb.at[pl.ds(CAP, (DEV - 1) * CAP)]
     pltpu.make_async_copy(gone, gone, row_send).wait()
     sent = ask_rows.at[pl.ds(0, DEV - 1)]
     pltpu.make_async_copy(sent, sent, req_send).wait()
@@ -285,39 +324,47 @@
             link(blk, blk, h_send.at[1, b], h_recv.at[1, b], left).wait_recv()
             link(blk, blk, h_send.at[2, b], h_recv.at[2, b], left).start()
 
-    def block(b, c):
-        def some(i, c2):
-            backward_marks(b * 16 + i)
-            base = pl.multiple_of(b * 256 + i * 16, 16)
-            for j in range(16):
-                m = base + j
-                here = pl.ds(pl.multiple_of(i * 16, 16) + j, 1)
-                own[here, :] = view[idx[0, m]]
-                rows = [view[idx[1 + k, m]] for k in range(F1)]
-                while len(rows) > 1:
-                    rows = [p + q for p, q in zip(rows[::2], rows[1::2])] + ([rows[-1]] if len(rows) % 2 else [])
-                near[here, :] = rows[0] * inv[0, m]
-            return c2
-
-        lax.fori_loop(0, 16, some, 0)
-        rows = cols(b)
+    def finish(n):
+        rows = pl.ds(pl.multiple_of(n * 16, 16), 16)
         act = jnp.concatenate([own[...].astype(BF), near[...].astype(BF)], axis=1)
         a1[rows, :] = act[:, :128]
-        a1[pl.ds(pl.multiple_of(FRONT + b * 256, 256), 256), :] = act[:, 128:]
+        a1[pl.ds(pl.multiple_of(FRONT + n * 16, 16), 16), :] = act[:, 128:]
         z = dot(act, gw1[...].reshape(2 * D_IN, HID)) + bias[0:1, 0:HID]
         z1[rows, :] = z
         gbuf[y, rows, :] = (z / (1.0 + jnp.exp(-z))).astype(BF)
-        blk = gbuf.at[y, rows, :]
+
+    def send(b):
+        blk = gbuf.at[y, cols(b), :]
         link(blk, blk, h_send.at[0, b], h_recv.at[0, b], right).start()
         link(blk, blk, h_send.at[1, b], h_recv.at[1, b], left).start()
 
-        @pl.when(b > 0)
+    def some(n, c):
+        finish(jnp.maximum(n - 1, 0))
+        backward_marks(n)
+        for j in range(16):
+            m = n * 16 + j
+            own[j:j + 1, :] = view[idx[0, m]]
+            rows = [view[idx[1 + k, m]] for k in range(F1)]
+            while len(rows) > 1:
+                rows = [p + q for p, q in zip(rows[::2], rows[1::2])] + ([rows[-1]] if len(rows) % 2 else [])
+            near[j:j + 1, :] = rows[0] * inv[0, m]
+
+        @pl.when((n > 0) & (n % 16 == 0))
         def _():
-            forward(b - 1)
+            send(n // 16 - 1)
+
+        @pl.when((n > 16) & (n % 16 == 0))
+        def _():
+            forward(n // 16 - 2)
 
         return c
 
-    lax.fori_loop(0, 8, block, 0)
+    own[...] = jnp.zeros((16, D_IN), F32)
+    near[...] = jnp.zeros((16, D_IN), F32)
+    lax.fori_loop(0, FRONT // 16, some, 0)
+    finish(FRONT // 16 - 1)
+    send(7)
+    forward(6)
     forward(7)
 
     def from_source(q):
@@ -479,11 +526,17 @@
         r = rbuf[q].astype(F32)
         ds = (da[:, :HID] + r).astype(BF)
         dn = ((da[:, HID:] - r) * wide(invc[q])).astype(BF)
-        part = dot(bsel[q], jnp.concatenate([dn, ds], axis=0))
-        for c in range(2):
-            rows = slice(c * FRONT, (c + 1) * FRONT)
-            now = part[:, c * 128:(c + 1) * 128]
-            dh1[rows, :] = now if fresh else dh1[rows, :] + now
+        both = jnp.concatenate([dn, ds], axis=0)
+
+        def rows512(i, c):
+            part = dot(bsel[q, pl.ds(pl.multiple_of(i * 512, 512), 512), :], both)
+            for h in range(2):
+                rows = pl.ds(pl.multiple_of(h * FRONT + i * 512, 512), 512)
+                now = part[:, h * 128:(h + 1) * 128]
+                dh1[rows, :] = now if fresh else dh1[rows, :] + now
+            return c
+
+        lax.fori_loop(0, FRONT // 512, rows512, 0)
 
     for c in range(2):
         a1t[c * 128:(c + 1) * 128, :] = a1[c * FRONT:(c + 1) * FRONT, :].T
@@ -500,14 +553,23 @@
     add_group(ybox2, res2, P2, 1)
     add_grads(opp)
 
-    z = z1[...]
-    sig = 1.0 / (1.0 + jnp.exp(-z))
-    dh = jnp.concatenate([dh1[0:FRONT, :], dh1[FRONT:2 * FRONT, :]], axis=1)
-    dz = (dh * sig * (1.0 + z * (1.0 - sig))).astype(BF)
+    def to_z(i, db):
+        z = z1[pl.ds(pl.multiple_of(i * 128, 128), 128), :]
+        sig = 1.0 / (1.0 + jnp.exp(-z))
+        dh = jnp.concatenate(
+            [dh1[pl.ds(pl.multiple_of(h * FRONT + i * 128, 128), 128), :] for h in range(2)], axis=1
+        )
+        dz = dh * sig * (1.0 + z * (1.0 - sig))
+        low = dz.astype(BF)
+        for h in range(2):
+            a1[pl.ds(pl.multiple_of((2 + h) * FRONT + i * 128, 128), 128), :] = low[:, h * 128:(h + 1) * 128]
+        return db + jnp.sum(low.astype(F32), axis=0, keepdims=True)
+
+    db1 = lax.fori_loop(0, FRONT // 128, to_z, jnp.zeros((1, HID), F32))
+    dz = jnp.concatenate([a1[2 * FRONT:3 * FRONT, :], a1[3 * FRONT:4 * FRONT, :]], axis=1)
     g1 = dot(a1t[...], dz).astype(BF)
     pay1[0:256, :] = g1[:, :128]
     pay1[256:512, :] = g1[:, 128:]
-    db1 = jnp.sum(dz.astype(F32), axis=0, keepdims=True)
     misc[...] = jnp.zeros((16, 128), F32)
 
     def two(rows, v):
@@ -576,8 +638,8 @@
             V((DEV, 128), jnp.int32),
             V((16, FRONT), jnp.int32),
             V((1, FRONT), F32),
-            V((256, D_IN), F32),
-            V((256, D_IN), F32),
+            V((16, D_IN), F32),
+            V((16, D_IN), F32),
             V((FRONT, HID), F32),
             V((2 * D_IN, FRONT), BF),
             V((NAR, FRONT, HID), BF),
@@ -605,10 +667,10 @@
             V((2, NAR, 16, 128), F32),
             V((P2 * 16, 128), F32),
             V((NAR, CLS_PAD, 128), F32),
-            pltpu.SMEM((DEV, 128), jnp.int32),
+            pltpu.SMEM((DEV, 1, 128), jnp.int32),
             pltpu.SMEM((16, FRONT), jnp.int32),
             pltpu.SMEM((1, FRONT), F32),
-            dma, dma((3,)), dma, dma, dma, dma, dma((5, 3)), dma((5, 3)),
+            dma, dma((2,)), dma((GRP,)), dma, dma((GRP,)), dma, dma, dma((5, 3)), dma((5, 3)),
             dma((3, 8)), dma((3, 8)), dma((4,)), dma((4,)), dma((4,)), dma((4,)),
             dma((2,)), dma((2, 2)), dma((2, 2, 3)), dma((2, 2, 3)), dma((2,)), dma((2,)),
         ],

time: 167 us -> 180 us (1.078)
  Pallas kernels: 165 us -> 177 us
    pallas_call x1, Pallas kernels: 160 us -> 172 us  [main(): pl.pallas_call(main_kernel, out_shape=sds((ROWS, 128), F32), in_specs=[vm...]
where the time goes in v7:
time: 180 us; the launch traced here: 179 us
  Pallas kernels  177 us (98%)
    pallas_call x1, Pallas kernels, main(): pl.pallas_call(main_kernel, out_shape=sds((ROWS, 128), F32), in_specs=[vm...  172 us
    pallas_call x1, Pallas kernels, update(): pl.pallas_call(update_kernel, out_shape=[sds((1, 1), F32), sds((64, HID),...  5.47 us

profile of v7, /device:TPU:1, one launch (start us, length us, event | category | flops | bytes accessed | tf_op | source)
XLA Modules:
  0.0 179.3 jit_solution(14820710139522796016)
XLA Ops:
  0.6 0.0 copy-start.2
  0.7 0.0 copy-start.5
  0.7 0.0 copy-start.4
  0.7 0.0 copy-start.3
  0.7 0.0 copy-start.1
  0.7 172.0 %shard_map.222.res = f32[1392,128]{1,0:T(8,128)} custom-call(s32[64,128]{1,0:T(8,128)} %bitcast.28, bf16[8192,128]{1,0:T(8,128)(2,1)} %feat.1, s32[16,2048]{1,0:T(8,128)} %bitcast.25, s32[15,2048]{1,0:T(8,128)} %bitcast.26, s32[11,512]{1,0:T(8,128)} %bitcast.29, s32[10,512]{1,0:T(8,128)} %bitcast.30, s32[1,512]{1,0:T(1,128)} %bitcast.31, s32[1,512]{1,0:T(1,128)} %bitcast.32, ...), custom_call_target="tpu_custom_call" | custom-call | tf_op jit(solution)/shard_map/pallas_call | solution.py:627
  172.7 0.0 copy-done.2
  172.7 0.0 copy-done.5
  172.7 0.0 copy-done.4
  172.7 0.0 copy-done.3
  172.8 0.0 copy-done.1
  172.8 0.0 copy-start
  172.8 1.1 copy-done
  173.9 5.5 %shard_map.223 = (f32[1,1]{1,0:T(1,128)}, f32[64,256]{1,0:T(8,128)}, f32[172,128]{1,0:T(8,128)}, f32[64,256]{1,0:T(8,128)}, f32[172,128]{1,0:T(8,128)}, /*index=...) custom-call(f32[1392,128]{1,0:T(8,128)S(1)} %copy-done, ...), custom_call_target="tpu_custom_call" | custom-call | tf_op jit(solution)/shard_map/pallas_call | solution.py:722
Async XLA Ops:
  0.6 172.1 %copy-start.2 = (f32[64,256]{1,0:T(8,128)S(1)}, f32[64,256]{1,0:T(8,128)}, u32[]{:S(2)}) copy-start(f32[64,256]{1,0:T(8,128)} %w1own.1) | copy-start | bytes 196612
  0.7 172.1 %copy-start.5 = (f32[428]{0:T(512)S(1)}, f32[428]{0:T(512)}, u32[]{:S(2)}) copy-start(f32[428]{0:T(512)} %param.29) | copy-start | bytes 5140
  0.7 172.1 %copy-start.4 = (f32[428]{0:T(512)S(1)}, f32[428]{0:T(512)}, u32[]{:S(2)}) copy-start(f32[428]{0:T(512)} %param.28) | copy-start | bytes 5140
  0.7 172.1 %copy-start.3 = (f32[428]{0:T(512)S(1)}, f32[428]{0:T(512)}, u32[]{:S(2)}) copy-start(f32[428]{0:T(512)} %param.27) | copy-start | bytes 5140
  0.7 172.1 %copy-start.1 = (f32[128,172]{0,1:T(8,128)S(1)}, f32[128,172]{0,1:T(8,128)}, u32[]{:S(2)}) copy-start(f32[128,172]{0,1:T(8,128)} %param.24) | copy-start | bytes 264196
  172.8 1.1 copy-start

commit v8 on v7

--- a/solution.py
+++ b/solution.py
@@ -324,47 +324,39 @@
             link(blk, blk, h_send.at[1, b], h_recv.at[1, b], left).wait_recv()
             link(blk, blk, h_send.at[2, b], h_recv.at[2, b], left).start()
 
-    def finish(n):
-        rows = pl.ds(pl.multiple_of(n * 16, 16), 16)
+    def block(b, c):
+        def some(i, c2):
+            backward_marks(b * 16 + i)
+            base = pl.multiple_of(b * 256 + i * 16, 16)
+            for j in range(16):
+                m = base + j
+                here = pl.ds(pl.multiple_of(i * 16, 16) + j, 1)
+                own[here, :] = view[idx[0, m]]
+                rows = [view[idx[1 + k, m]] for k in range(F1)]
+                while len(rows) > 1:
+                    rows = [p + q for p, q in zip(rows[::2], rows[1::2])] + ([rows[-1]] if len(rows) % 2 else [])
+                near[here, :] = rows[0] * inv[0, m]
+            return c2
+
+        lax.fori_loop(0, 16, some, 0)
+        rows = cols(b)
         act = jnp.concatenate([own[...].astype(BF), near[...].astype(BF)], axis=1)
         a1[rows, :] = act[:, :128]
-        a1[pl.ds(pl.multiple_of(FRONT + n * 16, 16), 16), :] = act[:, 128:]
+        a1[pl.ds(pl.multiple_of(FRONT + b * 256, 256), 256), :] = act[:, 128:]
         z = dot(act, gw1[...].reshape(2 * D_IN, HID)) + bias[0:1, 0:HID]
         z1[rows, :] = z
         gbuf[y, rows, :] = (z / (1.0 + jnp.exp(-z))).astype(BF)
-
-    def send(b):
-        blk = gbuf.at[y, cols(b), :]
+        blk = gbuf.at[y, rows, :]
         link(blk, blk, h_send.at[0, b], h_recv.at[0, b], right).start()
         link(blk, blk, h_send.at[1, b], h_recv.at[1, b], left).start()
 
-    def some(n, c):
-        finish(jnp.maximum(n - 1, 0))
-        backward_marks(n)
-        for j in range(16):
-            m = n * 16 + j
-            own[j:j + 1, :] = view[idx[0, m]]
-            rows = [view[idx[1 + k, m]] for k in range(F1)]
-            while len(rows) > 1:
-                rows = [p + q for p, q in zip(rows[::2], rows[1::2])] + ([rows[-1]] if len(rows) % 2 else [])
-            near[j:j + 1, :] = rows[0] * inv[0, m]
-
-        @pl.when((n > 0) & (n % 16 == 0))
+        @pl.when(b > 0)
         def _():
-            send(n // 16 - 1)
-
-        @pl.when((n > 16) & (n % 16 == 0))
-        def _():
-            forward(n // 16 - 2)
+            forward(b - 1)
 
         return c
 
-    own[...] = jnp.zeros((16, D_IN), F32)
-    near[...] = jnp.zeros((16, D_IN), F32)
-    lax.fori_loop(0, FRONT // 16, some, 0)
-    finish(FRONT // 16 - 1)
-    send(7)
-    forward(6)
+    lax.fori_loop(0, 8, block, 0)
     forward(7)
 
     def from_source(q):
@@ -638,8 +630,8 @@
             V((DEV, 128), jnp.int32),
             V((16, FRONT), jnp.int32),
             V((1, FRONT), F32),
-            V((16, D_IN), F32),
-            V((16, D_IN), F32),
+            V((256, D_IN), F32),
+            V((256, D_IN), F32),
             V((FRONT, HID), F32),
             V((2 * D_IN, FRONT), BF),
             V((NAR, FRONT, HID), BF),

time: 180 us -> 168 us (0.933)
  Pallas kernels: 177 us -> 166 us
    pallas_call x1, Pallas kernels: 172 us -> 160 us  [main(): pl.pallas_call(main_kernel, out_shape=sds((ROWS, 128), F32), in_specs=[vm...]
where the time goes in v8:
time: 168 us; the launch traced here: 167 us
  Pallas kernels  166 us (99%)
    pallas_call x1, Pallas kernels, main(): pl.pallas_call(main_kernel, out_shape=sds((ROWS, 128), F32), in_specs=[vm...  160 us
    pallas_call x1, Pallas kernels, update(): pl.pallas_call(update_kernel, out_shape=[sds((1, 1), F32), sds((64, HID),...  5.46 us

profile of v8, /device:TPU:1, one launch (start us, length us, event | category | flops | bytes accessed | tf_op | source)
XLA Modules:
  0.0 167.4 jit_solution(6165155889739376715)
XLA Ops:
  0.6 0.0 copy-start.2
  0.7 0.0 copy-start.5
  0.7 0.0 copy-start.4
  0.7 0.0 copy-start.3
  0.7 0.0 copy-start.1
  0.7 160.1 %shard_map.222.res = f32[1392,128]{1,0:T(8,128)} custom-call(s32[64,128]{1,0:T(8,128)} %bitcast.28, bf16[8192,128]{1,0:T(8,128)(2,1)} %feat.1, s32[16,2048]{1,0:T(8,128)} %bitcast.25, s32[15,2048]{1,0:T(8,128)} %bitcast.26, s32[11,512]{1,0:T(8,128)} %bitcast.29, s32[10,512]{1,0:T(8,128)} %bitcast.30, s32[1,512]{1,0:T(1,128)} %bitcast.31, s32[1,512]{1,0:T(1,128)} %bitcast.32, ...), custom_call_target="tpu_custom_call" | custom-call | tf_op jit(solution)/shard_map/pallas_call | solution.py:619
  160.8 0.0 copy-done.2
  160.8 0.0 copy-done.5
  160.8 0.0 copy-done.4
  160.9 0.0 copy-done.3
  160.9 0.0 copy-done.1
  160.9 0.0 copy-start
  160.9 1.1 copy-done
  162.0 5.5 %shard_map.223 = (f32[1,1]{1,0:T(1,128)}, f32[64,256]{1,0:T(8,128)}, f32[172,128]{1,0:T(8,128)}, f32[64,256]{1,0:T(8,128)}, f32[172,128]{1,0:T(8,128)}, /*index=...) custom-call(f32[1392,128]{1,0:T(8,128)S(1)} %copy-done, ...), custom_call_target="tpu_custom_call" | custom-call | tf_op jit(solution)/shard_map/pallas_call | solution.py:714
Async XLA Ops:
  0.6 160.2 %copy-start.2 = (f32[64,256]{1,0:T(8,128)S(1)}, f32[64,256]{1,0:T(8,128)}, u32[]{:S(2)}) copy-start(f32[64,256]{1,0:T(8,128)} %w1own.1) | copy-start | bytes 196612
  0.7 160.2 %copy-start.5 = (f32[428]{0:T(512)S(1)}, f32[428]{0:T(512)}, u32[]{:S(2)}) copy-start(f32[428]{0:T(512)} %param.29) | copy-start | bytes 5140
  0.7 160.2 %copy-start.4 = (f32[428]{0:T(512)S(1)}, f32[428]{0:T(512)}, u32[]{:S(2)}) copy-start(f32[428]{0:T(512)} %param.28) | copy-start | bytes 5140
  0.7 160.2 %copy-start.3 = (f32[428]{0:T(512)S(1)}, f32[428]{0:T(512)}, u32[]{:S(2)}) copy-start(f32[428]{0:T(512)} %param.27) | copy-start | bytes 5140
  0.7 160.2 %copy-start.1 = (f32[128,172]{0,1:T(8,128)S(1)}, f32[128,172]{0,1:T(8,128)}, u32[]{:S(2)}) copy-start(f32[128,172]{0,1:T(8,128)} %param.24) | copy-start | bytes 264196
  160.9 1.1 copy-start

commit v9 on v8

--- a/solution.py
+++ b/solution.py
@@ -179,9 +179,11 @@
     view = table.reshape(SRC + 8, 1, D_IN)
     my_rows = pl.ds(pl.multiple_of(me * CAP, CAP), CAP)
 
+    stage_rows = stage.reshape(CAP, 1, D_IN)
+
     def pick(t, u, slot):
         for r in range(CAP):
-            stage[r:r + 1, :] = view[reqs[t * NAR + u, 0, r]]
+            stage_rows[r] = view[reqs[t * NAR + u, 0, r]]
         featb[slot, :] = stage[...].astype(BF)
 
     def serve_one(t, u, slot):
@@ -324,18 +326,20 @@
             link(blk, blk, h_send.at[1, b], h_recv.at[1, b], left).wait_recv()
             link(blk, blk, h_send.at[2, b], h_recv.at[2, b], left).start()
 
+    own_rows, near_rows = own.reshape(256, 1, D_IN), near.reshape(256, 1, D_IN)
+
     def block(b, c):
         def some(i, c2):
             backward_marks(b * 16 + i)
             base = pl.multiple_of(b * 256 + i * 16, 16)
             for j in range(16):
                 m = base + j
-                here = pl.ds(pl.multiple_of(i * 16, 16) + j, 1)
-                own[here, :] = view[idx[0, m]]
+                here = i * 16 + j
+                own_rows[here] = view[idx[0, m]]
                 rows = [view[idx[1 + k, m]] for k in range(F1)]
                 while len(rows) > 1:
                     rows = [p + q for p, q in zip(rows[::2], rows[1::2])] + ([rows[-1]] if len(rows) % 2 else [])
-                near[here, :] = rows[0] * inv[0, m]
+                near_rows[here] = rows[0] * inv[0, m]
             return c2
 
         lax.fori_loop(0, 16, some, 0)

time: 168 us -> 168 us (level)
  no operation moved by 1% of the time
where the time goes in v9:
time: 168 us; the launch traced here: 167 us
  Pallas kernels  166 us (99%)
    pallas_call x1, Pallas kernels, main(): pl.pallas_call(main_kernel, out_shape=sds((ROWS, 128), F32), in_specs=[vm...  160 us
    pallas_call x1, Pallas kernels, update(): pl.pallas_call(update_kernel, out_shape=[sds((1, 1), F32), sds((64, HID),...  5.46 us

profile of v9, /device:TPU:1, one launch (start us, length us, event | category | flops | bytes accessed | tf_op | source)
XLA Modules:
  0.0 167.4 jit_solution(6165155889739376715)
XLA Ops:
  0.6 0.0 copy-start.2
  0.7 0.0 copy-start.5
  0.7 0.0 copy-start.4
  0.7 0.0 copy-start.3
  0.7 0.0 copy-start.1
  0.7 160.1 %shard_map.222.res = f32[1392,128]{1,0:T(8,128)} custom-call(s32[64,128]{1,0:T(8,128)} %bitcast.28, bf16[8192,128]{1,0:T(8,128)(2,1)} %feat.1, s32[16,2048]{1,0:T(8,128)} %bitcast.25, s32[15,2048]{1,0:T(8,128)} %bitcast.26, s32[11,512]{1,0:T(8,128)} %bitcast.29, s32[10,512]{1,0:T(8,128)} %bitcast.30, s32[1,512]{1,0:T(1,128)} %bitcast.31, s32[1,512]{1,0:T(1,128)} %bitcast.32, ...), custom_call_target="tpu_custom_call" | custom-call | tf_op jit(solution)/shard_map/pallas_call | solution.py:623
  160.8 0.0 copy-done.2
  160.8 0.0 copy-done.5
  160.8 0.0 copy-done.4
  160.9 0.0 copy-done.3
  160.9 0.0 copy-done.1
  160.9 0.0 copy-start
  160.9 1.1 copy-done
  162.0 5.5 %shard_map.223 = (f32[1,1]{1,0:T(1,128)}, f32[64,256]{1,0:T(8,128)}, f32[172,128]{1,0:T(8,128)}, f32[64,256]{1,0:T(8,128)}, f32[172,128]{1,0:T(8,128)}, /*index=...) custom-call(f32[1392,128]{1,0:T(8,128)S(1)} %copy-done, ...), custom_call_target="tpu_custom_call" | custom-call | tf_op jit(solution)/shard_map/pallas_call | solution.py:718
Async XLA Ops:
  0.6 160.2 %copy-start.2 = (f32[64,256]{1,0:T(8,128)S(1)}, f32[64,256]{1,0:T(8,128)}, u32[]{:S(2)}) copy-start(f32[64,256]{1,0:T(8,128)} %w1own.1) | copy-start | bytes 196612
  0.7 160.2 %copy-start.5 = (f32[428]{0:T(512)S(1)}, f32[428]{0:T(512)}, u32[]{:S(2)}) copy-start(f32[428]{0:T(512)} %param.29) | copy-start | bytes 5140
  0.7 160.2 %copy-start.4 = (f32[428]{0:T(512)S(1)}, f32[428]{0:T(512)}, u32[]{:S(2)}) copy-start(f32[428]{0:T(512)} %param.28) | copy-start | bytes 5140
  0.7 160.2 %copy-start.3 = (f32[428]{0:T(512)S(1)}, f32[428]{0:T(512)}, u32[]{:S(2)}) copy-start(f32[428]{0:T(512)} %param.27) | copy-start | bytes 5140
  0.7 160.2 %copy-start.1 = (f32[128,172]{0,1:T(8,128)S(1)}, f32[128,172]{0,1:T(8,128)}, u32[]{:S(2)}) copy-start(f32[128,172]{0,1:T(8,128)} %param.24) | copy-start | bytes 264196
  160.9 1.1 copy-start

commit v10 on v8

--- a/solution.py
+++ b/solution.py
@@ -102,19 +102,7 @@
     load = pltpu.make_async_copy(feat, featb, feat_sem)
     load.start()
 
-    barrier = pltpu.get_barrier_semaphore()
-
     ys = [(y + d) % NAR for d in range(NAR)]
-
-    def greet(i, c):
-        t = (g + i) % GRP
-        for d in range(NAR):
-            pl.semaphore_signal(barrier, inc=1, device_id=(t, ys[d]), device_id_type=MESH)
-        return c
-
-    for d in range(1, NAR):
-        pl.semaphore_signal(barrier, inc=1, device_id=(g, ys[d]), device_id_type=MESH)
-    lax.fori_loop(1, GRP, greet, 0)
 
     def link(src, dst, ssem, rsem, to):
         return pltpu.make_async_remote_copy(
@@ -134,8 +122,6 @@
         [idx2t[0:1, :], jnp.where(msk2t[...] > 0, idx2t[1:, :], -1), jnp.zeros((5, SEED), jnp.int32)], axis=0
     )
     shared = (gidx2, gw1, gw2t, gm1, gm2t)
-
-    pl.semaphore_wait(barrier, DEV - 1)
 
     def ask_one(t, u, n):
         row = t * NAR + u
@@ -667,7 +653,7 @@
             dma((2,)), dma((2, 2)), dma((2, 2, 3)), dma((2, 2, 3)), dma((2,)), dma((2,)),
         ],
         compiler_params=pltpu.CompilerParams(
-            collective_id=0, has_side_effects=True, vmem_limit_bytes=62 * 2**20
+            has_side_effects=True, vmem_limit_bytes=62 * 2**20
         ),
     )(reqt, feat, idx1t, msk1t, idx2t, msk2t, labels, live, w1, w2own, m1, m2own, bias)
 

time: 168 us -> 171 us (1.018)
  Pallas kernels: 166 us -> 169 us
    pallas_call x1, Pallas kernels: 160 us -> 164 us  [main(): pl.pallas_call(main_kernel, out_shape=sds((ROWS, 128), F32), in_specs=[vm...]
where the time goes in v10:
time: 171 us
  Pallas kernels  169 us (99%)
    pallas_call x1, Pallas kernels, main(): pl.pallas_call(main_kernel, out_shape=sds((ROWS, 128), F32), in_specs=[vm...  164 us
    pallas_call x1, Pallas kernels, update(): pl.pallas_call(update_kernel, out_shape=[sds((1, 1), F32), sds((64, HID),...  5.47 us

profile of v10, /device:TPU:1, one launch (start us, length us, event | category | flops | bytes accessed | tf_op | source)
XLA Modules:
  0.0 171.2 jit_solution(15792322314200825723)
XLA Ops:
  0.6 0.0 copy-start.2
  0.7 0.0 copy-start.5
  0.7 0.0 copy-start.4
  0.7 0.0 copy-start.3
  0.7 0.0 copy-start.1
  0.7 163.9 %shard_map.222.res = f32[1392,128]{1,0:T(8,128)} custom-call(s32[64,128]{1,0:T(8,128)} %bitcast.28, bf16[8192,128]{1,0:T(8,128)(2,1)} %feat.1, s32[16,2048]{1,0:T(8,128)} %bitcast.25, s32[15,2048]{1,0:T(8,128)} %bitcast.26, s32[11,512]{1,0:T(8,128)} %bitcast.29, s32[10,512]{1,0:T(8,128)} %bitcast.30, s32[1,512]{1,0:T(1,128)} %bitcast.31, s32[1,512]{1,0:T(1,128)} %bitcast.32, ...), custom_call_target="tpu_custom_call" | custom-call | tf_op jit(solution)/shard_map/pallas_call | solution.py:605
  164.6 0.0 copy-done.2
  164.6 0.0 copy-done.5
  164.6 0.0 copy-done.4
  164.6 0.0 copy-done.3
  164.6 0.0 copy-done.1
  164.6 0.0 copy-start
  164.6 1.1 copy-done
  165.7 5.5 %shard_map.223 = (f32[1,1]{1,0:T(1,128)}, f32[64,256]{1,0:T(8,128)}, f32[172,128]{1,0:T(8,128)}, f32[64,256]{1,0:T(8,128)}, f32[172,128]{1,0:T(8,128)}, /*index=...) custom-call(f32[1392,128]{1,0:T(8,128)S(1)} %copy-done, ...), custom_call_target="tpu_custom_call" | custom-call | tf_op jit(solution)/shard_map/pallas_call | solution.py:700
Async XLA Ops:
  0.6 163.9 %copy-start.2 = (f32[64,256]{1,0:T(8,128)S(1)}, f32[64,256]{1,0:T(8,128)}, u32[]{:S(2)}) copy-start(f32[64,256]{1,0:T(8,128)} %w1own.1) | copy-start | bytes 196612
  0.7 163.9 %copy-start.5 = (f32[428]{0:T(512)S(1)}, f32[428]{0:T(512)}, u32[]{:S(2)}) copy-start(f32[428]{0:T(512)} %param.29) | copy-start | bytes 5140
  0.7 163.9 %copy-start.4 = (f32[428]{0:T(512)S(1)}, f32[428]{0:T(512)}, u32[]{:S(2)}) copy-start(f32[428]{0:T(512)} %param.28) | copy-start | bytes 5140
  0.7 163.9 %copy-start.3 = (f32[428]{0:T(512)S(1)}, f32[428]{0:T(512)}, u32[]{:S(2)}) copy-start(f32[428]{0:T(512)} %param.27) | copy-start | bytes 5140
  0.7 163.9 %copy-start.1 = (f32[128,172]{0,1:T(8,128)S(1)}, f32[128,172]{0,1:T(8,128)}, u32[]{:S(2)}) copy-start(f32[128,172]{0,1:T(8,128)} %param.24) | copy-start | bytes 264196
  164.6 1.1 copy-start

commit v11 on v8

--- a/solution.py
+++ b/solution.py
@@ -43,11 +43,12 @@
     return (t // NAR, t % NAR)
 
 
-P1 = 33
-P2 = 44
+PIECE = 32
+P1 = 17
+Q2 = 192
+P2 = 24
 GRP = 32
-ROW_G1 = P1 * 16
-ROW_M2 = ROW_G1 + 512
+ROW_M2 = P1 * PIECE
 ROW_X2 = ROW_M2 + CLS_PAD
 ROWS = ROW_X2 + CLS_PAD
 SEEDS_ALL = SEED * DEV
@@ -87,10 +88,10 @@
 def main_kernel(
     reqt, feat, idx1t, msk1t, idx2t, msk2t, labels, live, w1, w2own, m1, m2own, bias,
     o_all,
-    table, featb, pulled, stage, reqv, reqin, idxv, invv, near, own, z1, a1t, gbuf, fsel, bsel, wants, idc, invc, livec, rbuf, dbuf,
-    gw1, gw2t, gm1, gm2t, gidx2, w2t, b2c, pay1, pay2, misc, inbox1, inbox2, ybox1, ybox2, res2, x2s,
+    table, featb, pulled, stage, reqv, reqin, mid, idxv, invv, near, own, z1, a1t, gbuf, fsel, bsel, wants, idc, invc, livec, rbuf, dbuf,
+    gw1, gw2t, m2pad, gidx2, w2t, b2c, pay1, pay2, misc, inbox1, inbox2, ybox1, ybox2, res2, x2s,
     reqs, idx, inv,
-    feat_sem, loc_sem, ask_sem, req_send, req_recv, row_send, row_recv, nar_send, nar_recv,
+    feat_sem, loc_sem, ask_sem, req_send, mid_recv, req_recv, row_send, row_recv, nar_send, nar_recv,
     h_send, h_recv, r_send, r_recv, d_send, d_recv, rs_send, rs_recv, y_send, y_recv, ag_send, ag_recv,
 ):
     a1, dh1 = pulled, table
@@ -122,39 +123,30 @@
         )
 
     reqv[...] = jnp.concatenate([reqt[...], jnp.zeros((DEV - CAP, DEV), jnp.int32)], axis=0).T
-    ask_rows = reqv.reshape(DEV, 1, 128)
+    ask_rows = reqv.reshape(GRP, NAR, 1, 128)
     got_rows = reqin.reshape(DEV, 1, 128)
 
     gw1[y] = w1[...].astype(BF)
     pad = CLS_PAD - CLS
     gw2t[y] = jnp.concatenate([w2own[...], jnp.zeros((pad, 128), F32)], axis=0).astype(BF)
-    gm1[y] = m1[...]
-    gm2t[y] = jnp.concatenate([m2own[...], jnp.zeros((pad, 128), F32)], axis=0)
+    m2pad[...] = jnp.concatenate([m2own[...], jnp.zeros((Q2 - CLS, 128), F32)], axis=0)
     gidx2[y] = jnp.concatenate(
         [idx2t[0:1, :], jnp.where(msk2t[...] > 0, idx2t[1:, :], -1), jnp.zeros((5, SEED), jnp.int32)], axis=0
     )
-    shared = (gidx2, gw1, gw2t, gm1, gm2t)
+    shared = (gidx2, gw1, gw2t)
 
     pl.semaphore_wait(barrier, DEV - 1)
 
-    def ask_one(t, u, n):
-        row = t * NAR + u
-        pltpu.make_async_remote_copy(
-            src_ref=ask_rows.at[row], dst_ref=got_rows.at[me], send_sem=req_send, recv_sem=req_recv.at[n],
-            device_id=(t, u), device_id_type=MESH,
-        ).start()
-
-    def ask(i, c):
-        n = (i * 13) % GRP
-        t = (g + n) % GRP
-        for d in range(NAR):
-            ask_one(t, ys[d], n)
-        return c
+    def ask_group(d):
+        return pltpu.make_async_remote_copy(
+            src_ref=ask_rows.at[:, ys[d]], dst_ref=mid.at[y], send_sem=req_send.at[d], recv_sem=mid_recv.at[d],
+            device_id=(g, ys[d]), device_id_type=MESH,
+        )
 
     for d in range(1, NAR):
-        ask_one(g, ys[d], 0)
-    lax.fori_loop(1, GRP, ask, 0)
-    reqin[pl.ds(me, 1), :] = reqv[pl.ds(me, 1), :]
+        ask_group(d).start()
+    keep = pltpu.make_async_copy(ask_rows.at[:, y], mid.at[y], loc_sem.at[2])
+    keep.start()
     for n, a in enumerate(shared):
         for d in range(1, NAR):
             link(a.at[y], a.at[y], nar_send.at[n, d - 1], nar_recv.at[n, d - 1], (y + d) % NAR).start()
@@ -167,6 +159,24 @@
     for c in to_smem:
         c.start()
 
+    keep.wait()
+    for d in range(1, NAR):
+        ask_group(d).wait()
+    own_rows = pl.ds(pl.multiple_of(g * NAR, NAR), NAR)
+
+    def ask(i, c):
+        n = (i * 13) % GRP
+        t = (g + n) % GRP
+        pltpu.make_async_remote_copy(
+            src_ref=mid.at[:, t], dst_ref=got_rows.at[own_rows], send_sem=req_send.at[0], recv_sem=req_recv.at[n],
+            device_id=(t, y), device_id_type=MESH,
+        ).start()
+        return c
+
+    lax.fori_loop(1, GRP, ask, 0)
+    keep = pltpu.make_async_copy(mid.at[:, g], got_rows.at[own_rows], loc_sem.at[2])
+    keep.start()
+
     load.wait()
 
     def widen_features(i, c):
@@ -191,8 +201,8 @@
             send_sem=row_send, recv_sem=row_recv, device_id=(t, u), device_id_type=MESH,
         ).start()
 
-    def asked(count, n):
-        rows = got_rows.at[pl.ds(0, count)]
+    def asked(n):
+        rows = got_rows.at[pl.ds(0, NAR)]
         pltpu.make_async_copy(rows, rows, req_recv.at[n]).wait()
 
     def to_scalars(t, n):
@@ -205,7 +215,7 @@
 
     def fetch(i):
         n, t = whose(i)
-        asked(NAR, n)
+        asked(n)
         to_scalars(t, n).start()
 
     def serve(i, c):
@@ -222,7 +232,7 @@
 
     fetch(1)
     lax.fori_loop(1, GRP, serve, 0)
-    asked(NAR - 1, 0)
+    keep.wait()
     to_scalars(g, 0).start()
     to_scalars(g, 0).wait()
     for d in range(1, NAR):
@@ -233,9 +243,6 @@
     for n, a in enumerate(shared):
         for d in range(1, NAR):
             link(a.at[y], a.at[y], nar_send.at[n, d - 1], nar_recv.at[n, d - 1], (y + d) % NAR).wait()
-    for q in range(NAR):
-        o_all[ROW_G1 + q * 64:ROW_G1 + q * 64 + 64, :] = MU * gm1[q, :, 0:128]
-        o_all[ROW_G1 + 256 + q * 64:ROW_G1 + 256 + q * 64 + 64, :] = MU * gm1[q, :, 128:256]
     for q in range(NAR):
         w2t[:, q * 128:(q + 1) * 128] = gw2t[q]
     last = jnp.concatenate([bias[0:1, 384:428], jnp.zeros((1, 84), F32)], axis=1)
@@ -295,8 +302,8 @@
     pltpu.make_async_copy(come, come, row_recv).wait()
     gone = featb.at[pl.ds(CAP, (DEV - 1) * CAP)]
     pltpu.make_async_copy(gone, gone, row_send).wait()
-    sent = ask_rows.at[pl.ds(0, DEV - 1)]
-    pltpu.make_async_copy(sent, sent, req_send).wait()
+    sent = mid.at[:, pl.ds(0, GRP - 1)]
+    pltpu.make_async_copy(sent, sent, req_send.at[0]).wait()
 
     def widen(i, c):
         rows = pl.ds(pl.multiple_of(i * 256, 256), 256)
@@ -436,82 +443,95 @@
     loss = loss + SEEDS_ALL / 2 * jnp.sum(pull_apart * diff, keepdims=True)
     g2t = dot(dlog, act2).astype(BF)
     for q in range(NAR):
-        pay2[q * CLS_PAD:(q + 1) * CLS_PAD, :] = g2t[:, q * 128:(q + 1) * 128]
-
-    def plane(i):
-        return ((g + i) % GRP, y)
-
-    def to_owner(pay, inbox, count, n):
+        pay2[q * Q2:q * Q2 + CLS_PAD, :] = g2t[:, q * 128:(q + 1) * 128]
+        pay2[q * Q2 + CLS_PAD:(q + 1) * Q2, :] = jnp.zeros((Q2 - CLS_PAD, 128), BF)
+
+    def to_owner(pay, inbox, first, count, n):
         def body(i, c):
             t = (g + i) % GRP
-            for slot in range(2):
-                p = t + slot * GRP
-
-                @pl.when(p < count)
-                def _():
-                    pltpu.make_async_remote_copy(
-                        src_ref=pay.at[pl.ds(pl.multiple_of(p * 16, 16), 16)], dst_ref=inbox.at[slot, g],
-                        send_sem=rs_send.at[n], recv_sem=rs_recv.at[n, slot], device_id=(t, y), device_id_type=MESH,
-                    ).start()
+            p = t - first
+
+            @pl.when((p >= 0) & (p < count))
+            def _():
+                pltpu.make_async_remote_copy(
+                    src_ref=pay.at[pl.ds(pl.multiple_of(p * PIECE, PIECE), PIECE)], dst_ref=inbox.at[g],
+                    send_sem=rs_send.at[n], recv_sem=rs_recv.at[n], device_id=(t, y), device_id_type=MESH,
+                ).start()
 
             return c
 
         lax.fori_loop(1, GRP, body, 0)
 
-    def add_plane(pay, inbox, ybox, count, n):
-        for slot in range(2):
-            p = g + slot * GRP
-
-            @pl.when(p < count)
-            def _():
-                got = inbox.at[slot, pl.ds(0, GRP - 1)]
-                pltpu.make_async_copy(got, got, rs_recv.at[n, slot]).wait()
-                inbox[slot, g] = pay[pl.ds(pl.multiple_of(p * 16, 16), 16), :]
-                ybox[slot, y] = jnp.sum(inbox[slot].astype(F32), axis=0)
-                blk = ybox.at[slot, y]
-                for d in range(1, NAR):
-                    link(blk, blk, y_send.at[n, slot, d - 1], y_recv.at[n, slot, d - 1], (y + d) % NAR).start()
-
-    def add_group(ybox, res, count, n):
-        for slot in range(2):
-            p = g + slot * GRP
-
-            @pl.when(p < count)
-            def _():
-                blk = ybox.at[slot, y]
-                for d in range(1, NAR):
-                    link(blk, blk, y_send.at[n, slot, d - 1], y_recv.at[n, slot, d - 1], (y + d) % NAR).wait()
-                rows16 = pl.ds(pl.multiple_of(p * 16, 16), 16)
-                res[rows16, :] = (ybox[slot, 0] + ybox[slot, 1]) + (ybox[slot, 2] + ybox[slot, 3])
-
-                def tell(i, c):
-                    pltpu.make_async_remote_copy(
-                        src_ref=res.at[rows16], dst_ref=res.at[rows16], send_sem=ag_send.at[n], recv_sem=ag_recv.at[n],
-                        device_id=plane(i), device_id_type=MESH,
-                    ).start()
-                    return c
-
-                lax.fori_loop(1, GRP, tell, 0)
-
-    def take(res, count, n):
-        two_here = g + GRP < count
-        for own, here in ((2, two_here), (1, jnp.logical_not(two_here))):
-            @pl.when(here)
-            def _(own=own):
-                got = res.at[pl.ds(0, (count - own) * 16)]
+    def mine(first, count):
+        p = g - first
+        return (p >= 0) & (p < count), pl.ds(pl.multiple_of(p * PIECE, PIECE), PIECE)
+
+    def add_first_momentum(p):
+        rows = pl.ds(pl.multiple_of(p % 2 * PIECE, PIECE), PIECE)
+        for h in range(2):
+            @pl.when((y == p % 8 // 2) & (p // 8 == h))
+            def _(h=h):
+                ybox1[y] = ybox1[y] + MU * m1[rows, h * 128:(h + 1) * 128]
+
+    def add_second_momentum(p):
+        @pl.when(y == p // (Q2 // PIECE))
+        def _():
+            rows = pl.ds(pl.multiple_of(p % (Q2 // PIECE) * PIECE, PIECE), PIECE)
+            ybox2[y] = ybox2[y] + MU * m2pad[rows, :]
+
+    def add_plane(pay, inbox, ybox, first, count, n, add_momentum):
+        here, rows = mine(first, count)
+
+        @pl.when(here)
+        def _():
+            got = inbox.at[pl.ds(0, GRP - 1)]
+            pltpu.make_async_copy(got, got, rs_recv.at[n]).wait()
+            inbox[g] = pay[rows, :]
+            ybox[y] = jnp.sum(inbox[...].astype(F32), axis=0)
+            add_momentum(g - first)
+            for d in range(1, NAR):
+                link(ybox.at[y], ybox.at[y], y_send.at[n, d - 1], y_recv.at[n, d - 1], ys[d]).start()
+
+    def add_group(ybox, res, first, count, n):
+        here, rows = mine(first, count)
+
+        @pl.when(here)
+        def _():
+            for d in range(1, NAR):
+                link(ybox.at[y], ybox.at[y], y_send.at[n, d - 1], y_recv.at[n, d - 1], ys[d]).wait()
+            res[rows, :] = (ybox[0] + ybox[1]) + (ybox[2] + ybox[3])
+
+            def tell(i, c):
+                pltpu.make_async_remote_copy(
+                    src_ref=res.at[rows], dst_ref=res.at[rows], send_sem=ag_send.at[n], recv_sem=ag_recv.at[n],
+                    device_id=((g + i) % GRP, y), device_id_type=MESH,
+                ).start()
+                return c
+
+            lax.fori_loop(1, GRP, tell, 0)
+
+    def take(res, first, count, n):
+        here, rows = mine(first, count)
+        for less, when in ((1, here), (0, jnp.logical_not(here))):
+            @pl.when(when)
+            def _(less=less):
+                got = res.at[pl.ds(0, (count - less) * PIECE)]
                 pltpu.make_async_copy(got, got, ag_recv.at[n]).wait()
 
-    def sums_sent(pay, count, n):
-        two_here = g + GRP < count
-        for own, here in ((2, two_here), (1, jnp.logical_not(two_here))):
-            @pl.when(here)
-            def _(own=own):
-                gone = pay.at[pl.ds(0, (count - own) * 16)]
+    def sums_sent(pay, first, count, n):
+        here, rows = mine(first, count)
+        for less, when in ((1, here), (0, jnp.logical_not(here))):
+            @pl.when(when)
+            def _(less=less):
+                gone = pay.at[pl.ds(0, (count - less) * PIECE)]
                 pltpu.make_async_copy(gone, gone, rs_send.at[n]).wait()
-                gone = table.at[pl.ds(0, own * (GRP - 1) * 16)]
-                pltpu.make_async_copy(gone, gone, ag_send.at[n]).wait()
-
-    to_owner(pay2, inbox2, P2, 1)
+
+        @pl.when(here)
+        def _():
+            gone = table.at[pl.ds(0, (GRP - 1) * PIECE)]
+            pltpu.make_async_copy(gone, gone, ag_send.at[n]).wait()
+
+    to_owner(pay2, inbox2, GRP - P2, P2, 1)
 
     def add_grads(q, fresh=False):
         da = dot(dbuf[q], w2t[...], TN)
@@ -539,10 +559,10 @@
     swap_forward(dbuf, d_send, d_recv, 96)
     add_grads(left)
     add_grads(right)
-    add_plane(pay2, inbox2, ybox2, P2, 1)
+    add_plane(pay2, inbox2, ybox2, GRP - P2, P2, 1, add_second_momentum)
     swap_end(rbuf, r_send, r_recv, SEED // 2)
     swap_end(dbuf, d_send, d_recv, 96)
-    add_group(ybox2, res2, P2, 1)
+    add_group(ybox2, res2, GRP - P2, P2, 1)
     add_grads(opp)
 
     def to_z(i, db):
@@ -562,7 +582,7 @@
     g1 = dot(a1t[...], dz).astype(BF)
     pay1[0:256, :] = g1[:, :128]
     pay1[256:512, :] = g1[:, 128:]
-    misc[...] = jnp.zeros((16, 128), F32)
+    misc[...] = jnp.zeros((PIECE, 128), F32)
 
     def two(rows, v):
         hi = v.astype(BF).astype(F32)
@@ -576,27 +596,25 @@
     hi = loss.astype(BF).astype(F32)
     misc[8:9, 0:1] = hi
     misc[9:10, 0:1] = loss - hi
-    pay1[512:528, :] = misc[...].astype(BF)
-    to_owner(pay1, inbox1, P1, 0)
-
-    take(res2, P2, 1)
-    mom2 = jnp.concatenate(
-        [MU * gm2t[q] + res2[q * CLS_PAD:(q + 1) * CLS_PAD, :] for q in range(NAR)], axis=1
-    )
+    pay1[512:544, :] = misc[...].astype(BF)
+    to_owner(pay1, inbox1, 0, P1, 0)
+
+    take(res2, GRP - P2, P2, 1)
+    mom2 = jnp.concatenate([res2[q * Q2:q * Q2 + CLS_PAD, :] for q in range(NAR)], axis=1)
     for q in range(NAR):
         x2s[q] = mom2[:, q * 128:(q + 1) * 128]
     o_all[ROW_M2:ROW_M2 + CLS_PAD, :] = x2s[y]
     x2 = mom2 * (1.0 / (jnp.sqrt(jnp.sum(mom2 * mom2, keepdims=True)) + 1e-07))
     x2 = ns_step(x2)
-    add_plane(pay1, inbox1, ybox1, P1, 0)
+    add_plane(pay1, inbox1, ybox1, 0, P1, 0, add_first_momentum)
     x2 = ns_step(x2)
-    add_group(ybox1, o_all, P1, 0)
+    add_group(ybox1, o_all, 0, P1, 0)
     for _ in range(NS_ITERS - 2):
         x2 = ns_step(x2)
     for q in range(NAR):
         x2s[q] = x2[:, q * 128:(q + 1) * 128]
     o_all[ROW_X2:ROW_X2 + CLS_PAD, :] = x2s[y]
-    take(o_all, P1, 0)
+    take(o_all, 0, P1, 0)
 
     for b in range(8):
         blk = gbuf.at[y, b * 256:(b + 1) * 256, :]
@@ -607,8 +625,8 @@
     swap_sent(rbuf, r_send, r_recv, SEED // 2)
     swap_sent(dbuf, d_send, d_recv, 96)
 
-    sums_sent(pay2, P2, 1)
-    sums_sent(pay1, P1, 0)
+    sums_sent(pay2, GRP - P2, P2, 1)
+    sums_sent(pay1, 0, P1, 0)
 
 
 def main(reqt, feat, idx1t, msk1t, idx2t, msk2t, labels, live, w1, w2own, m1, m2own, bias):
@@ -628,6 +646,7 @@
             V((CAP, D_IN), F32),
             V((DEV, 128), jnp.int32),
             V((DEV, 128), jnp.int32),
+            V((NAR, GRP, 1, 128), jnp.int32),
             V((16, FRONT), jnp.int32),
             V((1, FRONT), F32),
             V((256, D_IN), F32),
@@ -645,26 +664,25 @@
             V((NAR, CLS_PAD, SEED), BF),
             V((NAR, 64, HID), BF),
             V((NAR, CLS_PAD, 128), BF),
-            V((NAR, 64, HID), F32),
-            V((NAR, CLS_PAD, 128), F32),
+            V((Q2, 128), F32),
             V((NAR, 16, SEED), jnp.int32),
             V((CLS_PAD, 2 * HID), BF),
             V((HID, 128), F32),
-            V((P1 * 16, 128), BF),
-            V((P2 * 16, 128), BF),
-            V((16, 128), F32),
-            V((2, GRP, 16, 128), BF),
-            V((2, GRP, 16, 128), BF),
-            V((2, NAR, 16, 128), F32),
-            V((2, NAR, 16, 128), F32),
-            V((P2 * 16, 128), F32),
+            V((P1 * PIECE, 128), BF),
+            V((P2 * PIECE, 128), BF),
+            V((PIECE, 128), F32),
+            V((GRP, PIECE, 128), BF),
+            V((GRP, PIECE, 128), BF),
+            V((NAR, PIECE, 128), F32),
+            V((NAR, PIECE, 128), F32),
+            V((P2 * PIECE, 128), F32),
             V((NAR, CLS_PAD, 128), F32),
             pltpu.SMEM((DEV, 1, 128), jnp.int32),
             pltpu.SMEM((16, FRONT), jnp.int32),
             pltpu.SMEM((1, FRONT), F32),
-            dma, dma((2,)), dma((GRP,)), dma, dma((GRP,)), dma, dma, dma((5, 3)), dma((5, 3)),
+            dma, dma((3,)), dma((GRP,)), dma((NAR,)), dma((NAR,)), dma((GRP,)), dma, dma, dma((3, 3)), dma((3, 3)),
             dma((3, 8)), dma((3, 8)), dma((4,)), dma((4,)), dma((4,)), dma((4,)),
-            dma((2,)), dma((2, 2)), dma((2, 2, 3)), dma((2, 2, 3)), dma((2,)), dma((2,)),
+            dma((2,)), dma((2,)), dma((2, 3)), dma((2, 3)), dma((2,)), dma((2,)),
         ],
         compiler_params=pltpu.CompilerParams(
             collective_id=0, has_side_effects=True, vmem_limit_bytes=62 * 2**20
@@ -678,9 +696,7 @@
     x1s,
 ):
     y = lax.axis_index("nar")
-    mom1 = jnp.concatenate(
-        [res[i * 256:i * 256 + 256, :] + res[ROW_G1 + i * 256:ROW_G1 + i * 256 + 256, :] for i in range(2)], axis=1
-    )
+    mom1 = jnp.concatenate([res[0:256, :], res[256:512, :]], axis=1)
     x1s[...] = mom1
     block64 = pl.ds(pl.multiple_of(y * 64, 64), 64)
     o_mom1[...] = x1s[block64, :]

time: 168 us -> 160 us (0.952)
  Pallas kernels: 166 us -> 158 us
    pallas_call x1, Pallas kernels: 160 us -> 153 us  [main(): pl.pallas_call(main_kernel, out_shape=sds((ROWS, 128), F32), in_specs=[vm...]
where the time goes in v11:
time: 160 us
  Pallas kernels  158 us (99%)
    pallas_call x1, Pallas kernels, main(): pl.pallas_call(main_kernel, out_shape=sds((ROWS, 128), F32), in_specs=[vm...  153 us
    pallas_call x1, Pallas kernels, update(): pl.pallas_call(update_kernel, out_shape=[sds((1, 1), F32), sds((64, HID),...  5.45 us

profile of v11, /device:TPU:1, one launch (start us, length us, event | category | flops | bytes accessed | tf_op | source)
XLA Modules:
  0.0 159.9 jit_solution(4097760536603844831)
XLA Ops:
  0.6 0.0 copy-start.2
  0.7 0.0 copy-start.5
  0.7 0.0 copy-start.4
  0.7 0.0 copy-start.3
  0.7 0.0 copy-start.1
  0.7 152.7 %shard_map.222.res = f32[896,128]{1,0:T(8,128)} custom-call(s32[64,128]{1,0:T(8,128)} %bitcast.28, bf16[8192,128]{1,0:T(8,128)(2,1)} %feat.1, s32[16,2048]{1,0:T(8,128)} %bitcast.25, s32[15,2048]{1,0:T(8,128)} %bitcast.26, s32[11,512]{1,0:T(8,128)} %bitcast.29, s32[10,512]{1,0:T(8,128)} %bitcast.30, s32[1,512]{1,0:T(1,128)} %bitcast.31, s32[1,512]{1,0:T(1,128)} %bitcast.32, ...), custom_call_target="tpu_custom_call" | custom-call | tf_op jit(solution)/shard_map/pallas_call | solution.py:637
  153.4 0.0 copy-done.2
  153.4 0.0 copy-done.5
  153.4 0.0 copy-done.4
  153.4 0.0 copy-done.3
  153.4 0.0 copy-done.1
  153.4 0.0 copy-start
  153.4 1.0 copy-done
  154.5 5.5 %shard_map.223 = (f32[1,1]{1,0:T(1,128)}, f32[64,256]{1,0:T(8,128)}, f32[172,128]{1,0:T(8,128)}, f32[64,256]{1,0:T(8,128)}, f32[172,128]{1,0:T(8,128)}, /*index=...) custom-call(f32[896,128]{1,0:T(8,128)S(1)} %copy-done, ...), custom_call_target="tpu_custom_call" | custom-call | tf_op jit(solution)/shard_map/pallas_call | solution.py:730
Async XLA Ops:
  0.6 152.7 %copy-start.2 = (f32[64,256]{1,0:T(8,128)S(1)}, f32[64,256]{1,0:T(8,128)}, u32[]{:S(2)}) copy-start(f32[64,256]{1,0:T(8,128)} %w1own.1) | copy-start | bytes 196612
  0.7 152.7 %copy-start.5 = (f32[428]{0:T(512)S(1)}, f32[428]{0:T(512)}, u32[]{:S(2)}) copy-start(f32[428]{0:T(512)} %param.29) | copy-start | bytes 5140
  0.7 152.7 %copy-start.4 = (f32[428]{0:T(512)S(1)}, f32[428]{0:T(512)}, u32[]{:S(2)}) copy-start(f32[428]{0:T(512)} %param.28) | copy-start | bytes 5140
  0.7 152.7 %copy-start.3 = (f32[428]{0:T(512)S(1)}, f32[428]{0:T(512)}, u32[]{:S(2)}) copy-start(f32[428]{0:T(512)} %param.27) | copy-start | bytes 5140
  0.7 152.7 %copy-start.1 = (f32[128,172]{0,1:T(8,128)S(1)}, f32[128,172]{0,1:T(8,128)}, u32[]{:S(2)}) copy-start(f32[128,172]{0,1:T(8,128)} %param.24) | copy-start | bytes 264196
  153.4 1.0 copy-start

commit v12 on v11

--- a/solution.py
+++ b/solution.py
@@ -94,7 +94,7 @@
     feat_sem, loc_sem, ask_sem, req_send, mid_recv, req_recv, row_send, row_recv, nar_send, nar_recv,
     h_send, h_recv, r_send, r_recv, d_send, d_recv, rs_send, rs_recv, y_send, y_recv, ag_send, ag_recv,
 ):
-    a1, dh1 = pulled, table
+    dzs, dh1 = pulled, table
     g = lax.axis_index("grp")
     y = lax.axis_index("nar")
     me = g * NAR + y
@@ -108,9 +108,7 @@
     ys = [(y + d) % NAR for d in range(NAR)]
 
     def greet(i, c):
-        t = (g + i) % GRP
-        for d in range(NAR):
-            pl.semaphore_signal(barrier, inc=1, device_id=(t, ys[d]), device_id_type=MESH)
+        pl.semaphore_signal(barrier, inc=1, device_id=((g + i) % GRP, y), device_id_type=MESH)
         return c
 
     for d in range(1, NAR):
@@ -135,7 +133,7 @@
     )
     shared = (gidx2, gw1, gw2t)
 
-    pl.semaphore_wait(barrier, DEV - 1)
+    pl.semaphore_wait(barrier, GRP + NAR - 2)
 
     def ask_group(d):
         return pltpu.make_async_remote_copy(
@@ -186,6 +184,30 @@
 
     lax.fori_loop(0, OWN // 256, widen_features, 0)
 
+    lane16 = lax.broadcasted_iota(jnp.int32, (16, 128), 1).astype(jnp.int16)
+    iota16 = lax.broadcasted_iota(jnp.int32, (16, 128), 0).astype(jnp.int16)
+    one, zero = jnp.ones((16, 128), BF), jnp.zeros((16, 128), BF)
+
+    def marks(here, want):
+        acc = jnp.where(here == want[1], one, zero)
+        for k in range(2, 1 + F2):
+            acc = acc + jnp.where(here == want[k], one, zero)
+        return acc, jnp.where(here == want[0], one, zero)
+
+    idc[...] = gidx2[y].T
+
+    def seeds16(i):
+        at = pl.multiple_of(i * 16, 16)
+        blk = idc[pl.ds(at, 16), :]
+        return at, [jnp.broadcast_to(blk[:, k:k + 1], (16, 128)).astype(jnp.int16) for k in range(1 + F2)]
+
+    def forward_marks(at, want, q):
+        for c in range(FRONT // 128):
+            here = lane16 + jnp.full((16, 128), q * FRONT + c * 128, jnp.int32).astype(jnp.int16)
+            a, b = marks(here, want)
+            fsel[q, pl.ds(at, 16), c * 128:(c + 1) * 128] = a
+            fsel[q, pl.ds(SEED + at, 16), c * 128:(c + 1) * 128] = b
+
     view = table.reshape(SRC + 8, 1, D_IN)
     my_rows = pl.ds(pl.multiple_of(me * CAP, CAP), CAP)
 
@@ -226,7 +248,9 @@
             fetch(i + 1)
 
         to_scalars(t, n).wait()
+        at, want = seeds16(i)
         for d in range(NAR):
+            forward_marks(at, want, d)
             serve_one(t, ys[d], pl.ds(pl.multiple_of((i * NAR + d) * CAP, CAP), CAP))
         return c
 
@@ -235,6 +259,9 @@
     keep.wait()
     to_scalars(g, 0).start()
     to_scalars(g, 0).wait()
+    at, want = seeds16(0)
+    for d in range(NAR):
+        forward_marks(at, want, d)
     for d in range(1, NAR):
         serve_one(g, ys[d], pl.ds(d * CAP, CAP))
     pick(g, y, pl.ds(0, CAP))
@@ -255,32 +282,6 @@
         n = jnp.sum((gidx2[q, 1:1 + F2, :] >= 0).astype(F32), axis=0, keepdims=True)
         invc[q] = column(1.0 / jnp.maximum(n, 1.0))
     livec[...] = column(2.0 * LAM / HID / SEEDS_ALL * live[...].astype(F32))
-
-    lane16 = lax.broadcasted_iota(jnp.int32, (16, 128), 1).astype(jnp.int16)
-    iota16 = lax.broadcasted_iota(jnp.int32, (16, 128), 0).astype(jnp.int16)
-    one, zero = jnp.ones((16, 128), BF), jnp.zeros((16, 128), BF)
-
-    def marks(here, want):
-        acc = jnp.where(here == want[1], one, zero)
-        for k in range(2, 1 + F2):
-            acc = acc + jnp.where(here == want[k], one, zero)
-        return acc, jnp.where(here == want[0], one, zero)
-
-    idc[...] = gidx2[y].T
-
-    def forward_marks(i, carry):
-        at = pl.multiple_of(i * 16, 16)
-        blk = idc[pl.ds(at, 16), :]
-        want = [jnp.broadcast_to(blk[:, k:k + 1], (16, 128)).astype(jnp.int16) for k in range(1 + F2)]
-        for q in range(NAR):
-            for c in range(FRONT // 128):
-                here = lane16 + jnp.full((16, 128), q * FRONT + c * 128, jnp.int32).astype(jnp.int16)
-                a, b = marks(here, want)
-                fsel[q, pl.ds(at, 16), c * 128:(c + 1) * 128] = a
-                fsel[q, pl.ds(SEED + at, 16), c * 128:(c + 1) * 128] = b
-        return carry
-
-    lax.fori_loop(0, SEED // 16, forward_marks, 0)
 
     for q in range(NAR):
         ids = gidx2[q] - y * FRONT
@@ -348,8 +349,7 @@
         lax.fori_loop(0, 16, some, 0)
         rows = cols(b)
         act = jnp.concatenate([own[...].astype(BF), near[...].astype(BF)], axis=1)
-        a1[rows, :] = act[:, :128]
-        a1[pl.ds(pl.multiple_of(FRONT + b * 256, 256), 256), :] = act[:, 128:]
+        a1t[:, rows] = act.T
         z = dot(act, gw1[...].reshape(2 * D_IN, HID)) + bias[0:1, 0:HID]
         z1[rows, :] = z
         gbuf[y, rows, :] = (z / (1.0 + jnp.exp(-z))).astype(BF)
@@ -550,8 +550,6 @@
 
         lax.fori_loop(0, FRONT // 512, rows512, 0)
 
-    for c in range(2):
-        a1t[c * 128:(c + 1) * 128, :] = a1[c * FRONT:(c + 1) * FRONT, :].T
     db2 = jnp.sum(dlog.astype(F32), axis=1, keepdims=True)
     db2 = jnp.broadcast_to(db2, (CLS_PAD, 128)).T[0:1, :]
     swap_forward(rbuf, r_send, r_recv, SEED // 2)
@@ -574,11 +572,11 @@
         dz = dh * sig * (1.0 + z * (1.0 - sig))
         low = dz.astype(BF)
         for h in range(2):
-            a1[pl.ds(pl.multiple_of((2 + h) * FRONT + i * 128, 128), 128), :] = low[:, h * 128:(h + 1) * 128]
+            dzs[pl.ds(pl.multiple_of(h * FRONT + i * 128, 128), 128), :] = low[:, h * 128:(h + 1) * 128]
         return db + jnp.sum(low.astype(F32), axis=0, keepdims=True)
 
     db1 = lax.fori_loop(0, FRONT // 128, to_z, jnp.zeros((1, HID), F32))
-    dz = jnp.concatenate([a1[2 * FRONT:3 * FRONT, :], a1[3 * FRONT:4 * FRONT, :]], axis=1)
+    dz = jnp.concatenate([dzs[0:FRONT, :], dzs[FRONT:2 * FRONT, :]], axis=1)
     g1 = dot(a1t[...], dz).astype(BF)
     pay1[0:256, :] = g1[:, :128]
     pay1[256:512, :] = g1[:, 128:]

time: 160 us -> 157 us (0.981)
  Pallas kernels: 158 us -> 155 us
    pallas_call x1, Pallas kernels: 153 us -> 150 us  [main(): pl.pallas_call(main_kernel, out_shape=sds((ROWS, 128), F32), in_specs=[vm...]
where the time goes in v12:
time: 157 us
  Pallas kernels  155 us (99%)
    pallas_call x1, Pallas kernels, main(): pl.pallas_call(main_kernel, out_shape=sds((ROWS, 128), F32), in_specs=[vm...  150 us
    pallas_call x1, Pallas kernels, update(): pl.pallas_call(update_kernel, out_shape=[sds((1, 1), F32), sds((64, HID),...  5.45 us

profile of v12, /device:TPU:1, one launch (start us, length us, event | category | flops | bytes accessed | tf_op | source)
XLA Modules:
  0.0 156.9 jit_solution(10976723177081112971)
XLA Ops:
  0.6 0.0 copy-start.2
  0.7 0.0 copy-start.5
  0.7 0.0 copy-start.4
  0.7 0.0 copy-start.3
  0.7 0.0 copy-start.1
  0.7 149.7 %shard_map.222.res = f32[896,128]{1,0:T(8,128)} custom-call(s32[64,128]{1,0:T(8,128)} %bitcast.28, bf16[8192,128]{1,0:T(8,128)(2,1)} %feat.1, s32[16,2048]{1,0:T(8,128)} %bitcast.25, s32[15,2048]{1,0:T(8,128)} %bitcast.26, s32[11,512]{1,0:T(8,128)} %bitcast.29, s32[10,512]{1,0:T(8,128)} %bitcast.30, s32[1,512]{1,0:T(1,128)} %bitcast.31, s32[1,512]{1,0:T(1,128)} %bitcast.32, ...), custom_call_target="tpu_custom_call" | custom-call | tf_op jit(solution)/shard_map/pallas_call | solution.py:635
  150.4 0.0 copy-done.2
  150.4 0.0 copy-done.5
  150.4 0.0 copy-done.4
  150.5 0.0 copy-done.3
  150.5 0.0 copy-done.1
  150.5 0.0 copy-start
  150.5 1.0 copy-done
  151.5 5.5 %shard_map.223 = (f32[1,1]{1,0:T(1,128)}, f32[64,256]{1,0:T(8,128)}, f32[172,128]{1,0:T(8,128)}, f32[64,256]{1,0:T(8,128)}, f32[172,128]{1,0:T(8,128)}, /*index=...) custom-call(f32[896,128]{1,0:T(8,128)S(1)} %copy-done, ...), custom_call_target="tpu_custom_call" | custom-call | tf_op jit(solution)/shard_map/pallas_call | solution.py:728
Async XLA Ops:
  0.6 149.8 %copy-start.2 = (f32[64,256]{1,0:T(8,128)S(1)}, f32[64,256]{1,0:T(8,128)}, u32[]{:S(2)}) copy-start(f32[64,256]{1,0:T(8,128)} %w1own.1) | copy-start | bytes 196612
  0.7 149.8 %copy-start.5 = (f32[428]{0:T(512)S(1)}, f32[428]{0:T(512)}, u32[]{:S(2)}) copy-start(f32[428]{0:T(512)} %param.29) | copy-start | bytes 5140
  0.7 149.8 %copy-start.4 = (f32[428]{0:T(512)S(1)}, f32[428]{0:T(512)}, u32[]{:S(2)}) copy-start(f32[428]{0:T(512)} %param.28) | copy-start | bytes 5140
  0.7 149.8 %copy-start.3 = (f32[428]{0:T(512)S(1)}, f32[428]{0:T(512)}, u32[]{:S(2)}) copy-start(f32[428]{0:T(512)} %param.27) | copy-start | bytes 5140
  0.7 149.8 %copy-start.1 = (f32[128,172]{0,1:T(8,128)S(1)}, f32[128,172]{0,1:T(8,128)}, u32[]{:S(2)}) copy-start(f32[128,172]{0,1:T(8,128)} %param.24) | copy-start | bytes 264196
  150.5 1.0 copy-start

commit v13 on v12

--- a/solution.py
+++ b/solution.py
@@ -88,13 +88,13 @@
 def main_kernel(
     reqt, feat, idx1t, msk1t, idx2t, msk2t, labels, live, w1, w2own, m1, m2own, bias,
     o_all,
-    table, featb, pulled, stage, reqv, reqin, mid, idxv, invv, near, own, z1, a1t, gbuf, fsel, bsel, wants, idc, invc, livec, rbuf, dbuf,
+    table, featb, pulled, stage, reqv, reqin, mid, idxv, invv, near, own, z1, gbuf, fsel, bsel, wants, idc, ssel, idm, invc, livec, rbuf, dbuf,
     gw1, gw2t, m2pad, gidx2, w2t, b2c, pay1, pay2, misc, inbox1, inbox2, ybox1, ybox2, res2, x2s,
     reqs, idx, inv,
     feat_sem, loc_sem, ask_sem, req_send, mid_recv, req_recv, row_send, row_recv, nar_send, nar_recv,
     h_send, h_recv, r_send, r_recv, d_send, d_recv, rs_send, rs_recv, y_send, y_recv, ag_send, ag_recv,
 ):
-    dzs, dh1 = pulled, table
+    a1t, dh1, tot, gsum = featb, table, table.at[2 * FRONT:3 * FRONT], table.at[3 * FRONT:3 * FRONT + 512]
     g = lax.axis_index("grp")
     y = lax.axis_index("nar")
     me = g * NAR + y
@@ -299,6 +299,33 @@
                 bsel[q, out, c * 128:(c + 1) * 128] = a
                 bsel[q, out, SEED + c * 128:SEED + (c + 1) * 128] = b
 
+    def sum_marks(i):
+        at = pl.multiple_of(i // 2 * 16, 16)
+        half = i % 2
+        blk = idm[pl.ds(at, 16), :]
+        want = [jnp.broadcast_to(blk[:, 1 + k:2 + k], (16, 128)).astype(jnp.int16) for k in range(F1)]
+        base = lane16 + jnp.full((16, 128), half * (SRC // 2), jnp.int32).astype(jnp.int16)
+        for c in range(SRC // 256):
+            here = base + jnp.full((16, 128), c * 128, jnp.int32).astype(jnp.int16)
+            acc = jnp.where(here == want[0], one, zero)
+            for k in range(1, F1):
+                acc = acc + jnp.where(here == want[k], one, zero)
+            col = pl.ds(pl.multiple_of(half * (SRC // 2) + c * 128, 128), 128)
+            ssel[pl.ds(at, 16), col] = acc
+
+    def sum_ids(b):
+        idm[...] = idxv[:, cols(b)].T
+
+    def cols(b):
+        return pl.ds(pl.multiple_of(b * 256, 256), 256)
+
+    def one_mark(i, c):
+        sum_marks(i)
+        return c
+
+    sum_ids(0)
+    lax.fori_loop(0, 32, one_mark, 0)
+
     come = pulled.at[pl.ds(0, (DEV - 1) * CAP)]
     pltpu.make_async_copy(come, come, row_recv).wait()
     gone = featb.at[pl.ds(CAP, (DEV - 1) * CAP)]
@@ -316,9 +343,6 @@
     for c in to_smem:
         c.wait()
 
-    def cols(b):
-        return pl.ds(pl.multiple_of(b * 256, 256), 256)
-
     def forward(b):
         @pl.when(b % 2 == 0)
         def _():
@@ -332,24 +356,47 @@
             link(blk, blk, h_send.at[1, b], h_recv.at[1, b], left).wait_recv()
             link(blk, blk, h_send.at[2, b], h_recv.at[2, b], left).start()
 
-    def block(b, c):
-        def some(i, c2):
+    def own_row(b, i, j):
+        m = b * 256 + i * 16 + j
+        here = pl.ds(pl.multiple_of(i * 16, 16) + j, 1)
+        own[here, :] = view[idx[0, m]]
+        return m, here
+
+    def load_sums(b, mark):
+        def some(i, c):
             backward_marks(b * 16 + i)
-            base = pl.multiple_of(b * 256 + i * 16, 16)
+            mark(i)
             for j in range(16):
-                m = base + j
-                here = pl.ds(pl.multiple_of(i * 16, 16) + j, 1)
-                own[here, :] = view[idx[0, m]]
+                m, here = own_row(b, i, j)
                 rows = [view[idx[1 + k, m]] for k in range(F1)]
                 while len(rows) > 1:
                     rows = [p + q for p, q in zip(rows[::2], rows[1::2])] + ([rows[-1]] if len(rows) % 2 else [])
                 near[here, :] = rows[0] * inv[0, m]
-            return c2
+            return c
 
         lax.fori_loop(0, 16, some, 0)
+        finish(b)
+
+    def multiply_sums(b):
+        def some(i, c):
+            backward_marks(b * 16 + i)
+            for j in range(16):
+                own_row(b, i, j)
+            return c
+
+        lax.fori_loop(0, 16, some, 0)
+        scale = jnp.concatenate(
+            [spread(invv[0:1, pl.ds(pl.multiple_of(b * 256 + c * 128, 128), 128)]) for c in range(2)], axis=0
+        )
+        near[...] = dot(ssel[...], pulled[...]) * scale
+        finish(b)
+
+    def finish(b):
         rows = cols(b)
         act = jnp.concatenate([own[...].astype(BF), near[...].astype(BF)], axis=1)
-        a1t[:, rows] = act.T
+        a1 = act.T
+        for h in range(2):
+            a1t[pl.ds(pl.multiple_of((2 * b + h) * 256, 256), 256), :] = a1[:, h * 128:(h + 1) * 128]
         z = dot(act, gw1[...].reshape(2 * D_IN, HID)) + bias[0:1, 0:HID]
         z1[rows, :] = z
         gbuf[y, rows, :] = (z / (1.0 + jnp.exp(-z))).astype(BF)
@@ -361,33 +408,56 @@
         def _():
             forward(b - 1)
 
+    multiply_sums(0)
+
+    def three(p, c):
+        sum_ids(3 * p + 3)
+
+        def loaded(h, c2):
+            load_sums(3 * p + 1 + h, lambda i: sum_marks(h * 16 + i))
+            return c2
+
+        lax.fori_loop(0, 2, loaded, 0)
+        multiply_sums(3 * p + 3)
         return c
 
-    lax.fori_loop(0, 8, block, 0)
+    lax.fori_loop(0, 2, three, 0)
+    load_sums(7, lambda i: None)
     forward(7)
 
-    def from_source(q):
-        return dot(fsel[q], gbuf[q])
-
-    total = from_source(y)
+    def from_source(q, fresh=False):
+        def rows512(i, c):
+            part = dot(fsel[q, pl.ds(pl.multiple_of(i * SEED, SEED), SEED), :], gbuf[q])
+            for h in range(2):
+                rows = pl.ds(pl.multiple_of(h * 2 * SEED + i * SEED, SEED), SEED)
+                now = part[:, h * 128:(h + 1) * 128]
+                tot[rows, :] = now if fresh else tot[rows, :] + now
+            return c
+
+        lax.fori_loop(0, 2, rows512, 0)
+
+    from_source(y, True)
     for b in range(1, 8, 2):
         blk = gbuf.at[left, b * 256:(b + 1) * 256, :]
         link(blk, blk, h_send.at[0, b], h_recv.at[0, b], right).wait_recv()
-    total = total + from_source(left)
+    from_source(left)
     for b in range(0, 8, 2):
         blk = gbuf.at[right, b * 256:(b + 1) * 256, :]
         link(blk, blk, h_send.at[1, b], h_recv.at[1, b], left).wait_recv()
-    total = total + from_source(right)
+    from_source(right)
     for b in range(8):
         blk = gbuf.at[opp, b * 256:(b + 1) * 256, :]
         link(blk, blk, h_send.at[2, b], h_recv.at[2, b], right).wait_recv()
-    total = total + from_source(opp)
+    from_source(opp)
 
     def wide(a):
         return jnp.concatenate([a, a], axis=1)
 
-    near2 = (total[:SEED, :] * wide(invc[y])).astype(BF)
-    self2 = total[SEED:, :].astype(BF)
+    def seeds(first):
+        return jnp.concatenate([tot[h * 2 * SEED + first:h * 2 * SEED + first + SEED, :] for h in range(2)], axis=1)
+
+    near2 = (seeds(0) * wide(invc[y])).astype(BF)
+    self2 = seeds(SEED).astype(BF)
     alive = live[...].astype(F32)
     diff = self2.astype(F32) - near2.astype(F32)
     pull_apart = wide(livec[...]) * diff
@@ -563,23 +633,26 @@
     add_group(ybox2, res2, GRP - P2, P2, 1)
     add_grads(opp)
 
-    def to_z(i, db):
-        z = z1[pl.ds(pl.multiple_of(i * 128, 128), 128), :]
+    def to_z(b, db):
+        rows = pl.ds(pl.multiple_of(b * 256, 256), 256)
+        z = z1[rows, :]
         sig = 1.0 / (1.0 + jnp.exp(-z))
         dh = jnp.concatenate(
-            [dh1[pl.ds(pl.multiple_of(h * FRONT + i * 128, 128), 128), :] for h in range(2)], axis=1
+            [dh1[pl.ds(pl.multiple_of(h * FRONT + b * 256, 256), 256), :] for h in range(2)], axis=1
         )
-        dz = dh * sig * (1.0 + z * (1.0 - sig))
-        low = dz.astype(BF)
+        dz = (dh * sig * (1.0 + z * (1.0 - sig))).astype(BF)
+        a1 = jnp.concatenate(
+            [a1t[pl.ds(pl.multiple_of((2 * b + h) * 256, 256), 256), :] for h in range(2)], axis=1
+        )
+        part = dot(a1, dz)
         for h in range(2):
-            dzs[pl.ds(pl.multiple_of(h * FRONT + i * 128, 128), 128), :] = low[:, h * 128:(h + 1) * 128]
-        return db + jnp.sum(low.astype(F32), axis=0, keepdims=True)
-
-    db1 = lax.fori_loop(0, FRONT // 128, to_z, jnp.zeros((1, HID), F32))
-    dz = jnp.concatenate([dzs[0:FRONT, :], dzs[FRONT:2 * FRONT, :]], axis=1)
-    g1 = dot(a1t[...], dz).astype(BF)
-    pay1[0:256, :] = g1[:, :128]
-    pay1[256:512, :] = g1[:, 128:]
+            now = slice(h * 256, (h + 1) * 256)
+            gsum[now, :] = gsum[now, :] + part[:, h * 128:(h + 1) * 128]
+        return db + jnp.sum(dz.astype(F32), axis=0, keepdims=True)
+
+    gsum[...] = jnp.zeros((512, 128), F32)
+    db1 = lax.fori_loop(0, FRONT // 256, to_z, jnp.zeros((1, HID), F32))
+    pay1[0:512, :] = gsum[...].astype(BF)
     misc[...] = jnp.zeros((PIECE, 128), F32)
 
     def two(rows, v):
@@ -650,12 +723,13 @@
             V((256, D_IN), F32),
             V((256, D_IN), F32),
             V((FRONT, HID), F32),
-            V((2 * D_IN, FRONT), BF),
             V((NAR, FRONT, HID), BF),
             V((NAR, 2 * SEED, FRONT), BF),
             V((NAR, FRONT, 2 * SEED), BF),
             V((NAR, 4, 1 + F2, 16, 128), jnp.int16),
             V((SEED, 16), jnp.int32),
+            V((256, SRC), BF),
+            V((256, 16), jnp.int32),
             V((NAR, SEED, 128), F32),
             V((SEED, 128), F32),
             V((NAR, SEED, HID), BF),

time: 157 us -> 162 us (1.032)
  Pallas kernels: 155 us -> 160 us
    pallas_call x1, Pallas kernels: 150 us -> 154 us  [main(): pl.pallas_call(main_kernel, out_shape=sds((ROWS, 128), F32), in_specs=[vm...]
where the time goes in v13:
time: 162 us; the launch traced here: 161 us
  Pallas kernels  160 us (99%)
    pallas_call x1, Pallas kernels, main(): pl.pallas_call(main_kernel, out_shape=sds((ROWS, 128), F32), in_specs=[vm...  154 us
    pallas_call x1, Pallas kernels, update(): pl.pallas_call(update_kernel, out_shape=[sds((1, 1), F32), sds((64, HID),...  5.45 us

profile of v13, /device:TPU:1, one launch (start us, length us, event | category | flops | bytes accessed | tf_op | source)
XLA Modules:
  0.0 161.4 jit_solution(7348188808767849897)
XLA Ops:
  0.6 0.0 copy-start.2
  0.7 0.0 copy-start.5
  0.7 0.0 copy-start.4
  0.7 0.0 copy-start.3
  0.7 0.0 copy-start.1
  0.7 154.2 %shard_map.222.res = f32[896,128]{1,0:T(8,128)} custom-call(s32[64,128]{1,0:T(8,128)} %bitcast.28, bf16[8192,128]{1,0:T(8,128)(2,1)} %feat.1, s32[16,2048]{1,0:T(8,128)} %bitcast.25, s32[15,2048]{1,0:T(8,128)} %bitcast.26, s32[11,512]{1,0:T(8,128)} %bitcast.29, s32[10,512]{1,0:T(8,128)} %bitcast.30, s32[1,512]{1,0:T(1,128)} %bitcast.31, s32[1,512]{1,0:T(1,128)} %bitcast.32, ...), custom_call_target="tpu_custom_call" | custom-call | tf_op jit(solution)/shard_map/pallas_call | solution.py:708
  154.9 0.0 copy-done.2
  154.9 0.0 copy-done.5
  154.9 0.0 copy-done.4
  154.9 0.0 copy-done.3
  154.9 0.0 copy-done.1
  154.9 0.0 copy-start
  155.0 1.0 copy-done
  156.0 5.5 %shard_map.223 = (f32[1,1]{1,0:T(1,128)}, f32[64,256]{1,0:T(8,128)}, f32[172,128]{1,0:T(8,128)}, f32[64,256]{1,0:T(8,128)}, f32[172,128]{1,0:T(8,128)}, /*index=...) custom-call(f32[896,128]{1,0:T(8,128)S(1)} %copy-done, ...), custom_call_target="tpu_custom_call" | custom-call | tf_op jit(solution)/shard_map/pallas_call | solution.py:802
Async XLA Ops:
  0.6 154.2 %copy-start.2 = (f32[64,256]{1,0:T(8,128)S(1)}, f32[64,256]{1,0:T(8,128)}, u32[]{:S(2)}) copy-start(f32[64,256]{1,0:T(8,128)} %w1own.1) | copy-start | bytes 196612
  0.7 154.2 %copy-start.5 = (f32[428]{0:T(512)S(1)}, f32[428]{0:T(512)}, u32[]{:S(2)}) copy-start(f32[428]{0:T(512)} %param.29) | copy-start | bytes 5140
  0.7 154.2 %copy-start.4 = (f32[428]{0:T(512)S(1)}, f32[428]{0:T(512)}, u32[]{:S(2)}) copy-start(f32[428]{0:T(512)} %param.28) | copy-start | bytes 5140
  0.7 154.2 %copy-start.3 = (f32[428]{0:T(512)S(1)}, f32[428]{0:T(512)}, u32[]{:S(2)}) copy-start(f32[428]{0:T(512)} %param.27) | copy-start | bytes 5140
  0.7 154.2 %copy-start.1 = (f32[128,172]{0,1:T(8,128)S(1)}, f32[128,172]{0,1:T(8,128)}, u32[]{:S(2)}) copy-start(f32[128,172]{0,1:T(8,128)} %param.24) | copy-start | bytes 264196
  154.9 1.0 copy-start

commit v14 on v13

--- a/solution.py
+++ b/solution.py
@@ -408,21 +408,12 @@
         def _():
             forward(b - 1)
 
+    def loaded(b, c):
+        load_sums(b, lambda i: None)
+        return c
+
     multiply_sums(0)
-
-    def three(p, c):
-        sum_ids(3 * p + 3)
-
-        def loaded(h, c2):
-            load_sums(3 * p + 1 + h, lambda i: sum_marks(h * 16 + i))
-            return c2
-
-        lax.fori_loop(0, 2, loaded, 0)
-        multiply_sums(3 * p + 3)
-        return c
-
-    lax.fori_loop(0, 2, three, 0)
-    load_sums(7, lambda i: None)
+    lax.fori_loop(1, 8, loaded, 0)
     forward(7)
 
     def from_source(q, fresh=False):

time: 162 us -> 151 us (0.932)
  Pallas kernels: 160 us -> 150 us
    pallas_call x1, Pallas kernels: 154 us -> 144 us  [main(): pl.pallas_call(main_kernel, out_shape=sds((ROWS, 128), F32), in_specs=[vm...]
where the time goes in v14:
time: 151 us
  Pallas kernels  150 us (99%)
    pallas_call x1, Pallas kernels, main(): pl.pallas_call(main_kernel, out_shape=sds((ROWS, 128), F32), in_specs=[vm...  144 us
    pallas_call x1, Pallas kernels, update(): pl.pallas_call(update_kernel, out_shape=[sds((1, 1), F32), sds((64, HID),...  5.45 us

profile of v14, /device:TPU:1, one launch (start us, length us, event | category | flops | bytes accessed | tf_op | source)
XLA Modules:
  0.0 151.3 jit_solution(9900882420017713392)
XLA Ops:
  0.6 0.0 copy-start.2
  0.7 0.0 copy-start.5
  0.7 0.0 copy-start.4
  0.7 0.0 copy-start.3
  0.7 0.0 copy-start.1
  0.7 144.1 %shard_map.222.res = f32[896,128]{1,0:T(8,128)} custom-call(s32[64,128]{1,0:T(8,128)} %bitcast.28, bf16[8192,128]{1,0:T(8,128)(2,1)} %feat.1, s32[16,2048]{1,0:T(8,128)} %bitcast.25, s32[15,2048]{1,0:T(8,128)} %bitcast.26, s32[11,512]{1,0:T(8,128)} %bitcast.29, s32[10,512]{1,0:T(8,128)} %bitcast.30, s32[1,512]{1,0:T(1,128)} %bitcast.31, s32[1,512]{1,0:T(1,128)} %bitcast.32, ...), custom_call_target="tpu_custom_call" | custom-call | tf_op jit(solution)/shard_map/pallas_call | solution.py:699
  144.8 0.0 copy-done.2
  144.8 0.0 copy-done.5
  144.8 0.0 copy-done.4
  144.8 0.0 copy-done.3
  144.8 0.0 copy-done.1
  144.8 0.0 copy-start
  144.8 1.0 copy-done
  145.8 5.5 %shard_map.223 = (f32[1,1]{1,0:T(1,128)}, f32[64,256]{1,0:T(8,128)}, f32[172,128]{1,0:T(8,128)}, f32[64,256]{1,0:T(8,128)}, f32[172,128]{1,0:T(8,128)}, /*index=...) custom-call(f32[896,128]{1,0:T(8,128)S(1)} %copy-done, ...), custom_call_target="tpu_custom_call" | custom-call | tf_op jit(solution)/shard_map/pallas_call | solution.py:793
Async XLA Ops:
  0.6 144.1 %copy-start.2 = (f32[64,256]{1,0:T(8,128)S(1)}, f32[64,256]{1,0:T(8,128)}, u32[]{:S(2)}) copy-start(f32[64,256]{1,0:T(8,128)} %w1own.1) | copy-start | bytes 196612
  0.7 144.1 %copy-start.5 = (f32[428]{0:T(512)S(1)}, f32[428]{0:T(512)}, u32[]{:S(2)}) copy-start(f32[428]{0:T(512)} %param.29) | copy-start | bytes 5140
  0.7 144.1 %copy-start.4 = (f32[428]{0:T(512)S(1)}, f32[428]{0:T(512)}, u32[]{:S(2)}) copy-start(f32[428]{0:T(512)} %param.28) | copy-start | bytes 5140
  0.7 144.1 %copy-start.3 = (f32[428]{0:T(512)S(1)}, f32[428]{0:T(512)}, u32[]{:S(2)}) copy-start(f32[428]{0:T(512)} %param.27) | copy-start | bytes 5140
  0.7 144.1 %copy-start.1 = (f32[128,172]{0,1:T(8,128)S(1)}, f32[128,172]{0,1:T(8,128)}, u32[]{:S(2)}) copy-start(f32[128,172]{0,1:T(8,128)} %param.24) | copy-start | bytes 264196
  144.8 1.0 copy-start

commit v15 on v14

--- a/solution.py
+++ b/solution.py
@@ -88,7 +88,7 @@
 def main_kernel(
     reqt, feat, idx1t, msk1t, idx2t, msk2t, labels, live, w1, w2own, m1, m2own, bias,
     o_all,
-    table, featb, pulled, stage, reqv, reqin, mid, idxv, invv, near, own, z1, gbuf, fsel, bsel, wants, idc, ssel, idm, invc, livec, rbuf, dbuf,
+    table, featb, pulled, stage, reqv, reqin, mid, idxv, invv, near, own, z1, gbuf, fsel, bsel, unit_of, lows, selfs, idc, ssel, idm, invc, livec, rbuf, dbuf,
     gw1, gw2t, m2pad, gidx2, w2t, b2c, pay1, pay2, misc, inbox1, inbox2, ybox1, ybox2, res2, x2s,
     reqs, idx, inv,
     feat_sem, loc_sem, ask_sem, req_send, mid_recv, req_recv, row_send, row_recv, nar_send, nar_recv,
@@ -184,29 +184,52 @@
 
     lax.fori_loop(0, OWN // 256, widen_features, 0)
 
-    lane16 = lax.broadcasted_iota(jnp.int32, (16, 128), 1).astype(jnp.int16)
+    lane32 = lax.broadcasted_iota(jnp.int32, (16, 128), 1)
+    sub32 = lax.broadcasted_iota(jnp.int32, (32, 128), 0)
+    lane16 = lane32.astype(jnp.int16)
     iota16 = lax.broadcasted_iota(jnp.int32, (16, 128), 0).astype(jnp.int16)
     one, zero = jnp.ones((16, 128), BF), jnp.zeros((16, 128), BF)
 
-    def marks(here, want):
-        acc = jnp.where(here == want[1], one, zero)
-        for k in range(2, 1 + F2):
-            acc = acc + jnp.where(here == want[k], one, zero)
-        return acc, jnp.where(here == want[0], one, zero)
-
-    idc[...] = gidx2[y].T
+    def unit(digit):
+        v = jnp.ones_like(digit)
+        for j in range(1, 8):
+            v = jnp.where(digit == j, 1 << 4 * j, v)
+        return v
+
+    def count(acc, j):
+        return ((acc >> (4 * j)) & 15).astype(F32).astype(BF)
+
+    def keys_units(ids):
+        return (ids & 127) + (ids >> 10) * 128, unit((ids >> 7) & 7)
+
+    def word(pos, keys, units):
+        acc = jnp.zeros((16, 128), jnp.int32)
+        for k, u in zip(keys, units):
+            acc = acc + jnp.where(pos == k, u, 0)
+        return acc
+
+    def spread_columns(blk, ks):
+        return [jnp.broadcast_to(blk[:, k:k + 1], (16, 128)) for k in ks]
+
+    ids = gidx2[y]
+    keys, units = keys_units(ids)
+    idc[...] = jnp.concatenate([ids[0:1, :], keys[1:, :], units], axis=0).T
 
     def seeds16(i):
         at = pl.multiple_of(i * 16, 16)
         blk = idc[pl.ds(at, 16), :]
-        return at, [jnp.broadcast_to(blk[:, k:k + 1], (16, 128)).astype(jnp.int16) for k in range(1 + F2)]
+        self_row = jnp.broadcast_to(blk[:, 0:1], (16, 128)).astype(jnp.int16)
+        return at, (spread_columns(blk, range(1, 1 + F2)), spread_columns(blk, range(17, 17 + F2)), self_row)
 
     def forward_marks(at, want, q):
-        for c in range(FRONT // 128):
-            here = lane16 + jnp.full((16, 128), q * FRONT + c * 128, jnp.int32).astype(jnp.int16)
-            a, b = marks(here, want)
-            fsel[q, pl.ds(at, 16), c * 128:(c + 1) * 128] = a
-            fsel[q, pl.ds(SEED + at, 16), c * 128:(c + 1) * 128] = b
+        keys, units, self_row = want
+        for w in range(2):
+            acc = word(lane32 + 128 * (2 * q + w), keys, units)
+            for j in range(8):
+                c = w * 8 + j
+                fsel[q, pl.ds(at, 16), c * 128:(c + 1) * 128] = count(acc, j)
+                here = lane16 + jnp.full((16, 128), q * FRONT + c * 128, jnp.int32).astype(jnp.int16)
+                fsel[q, pl.ds(SEED + at, 16), c * 128:(c + 1) * 128] = jnp.where(here == self_row, one, zero)
 
     view = table.reshape(SRC + 8, 1, D_IN)
     my_rows = pl.ds(pl.multiple_of(me * CAP, CAP), CAP)
@@ -283,38 +306,50 @@
         invc[q] = column(1.0 / jnp.maximum(n, 1.0))
     livec[...] = column(2.0 * LAM / HID / SEEDS_ALL * live[...].astype(F32))
 
-    for q in range(NAR):
-        ids = gidx2[q] - y * FRONT
-        for c in range(SEED // 128):
-            for k in range(1 + F2):
-                row = ids[k:k + 1, c * 128:(c + 1) * 128]
-                wants[q, c, k] = jnp.broadcast_to(row, (16, 128)).astype(jnp.int16)
-
-    def backward_marks(i):
-        here = iota16 + jnp.full((16, 128), i * 16, jnp.int32).astype(jnp.int16)
-        out = pl.ds(pl.multiple_of(i * 16, 16), 16)
-        for q in range(NAR):
-            for c in range(SEED // 128):
-                a, b = marks(here, [wants[q, c, k] for k in range(1 + F2)])
-                bsel[q, out, c * 128:(c + 1) * 128] = a
-                bsel[q, out, SEED + c * 128:SEED + (c + 1) * 128] = b
+    def backward_marks(q, carry):
+        r = gidx2[q] - y * FRONT
+        lows[...] = r & 31
+        inside = (r >= 0) & (r < FRONT)
+        units = unit((r >> 5) & 7)
+        for w in range(8):
+            unit_of[w] = jnp.where(inside & ((r >> 8) == w), units, 0)
+        selfs[...] = jnp.broadcast_to(r[0:1, :], (16, SEED))
+
+        def column(c, carry2):
+            lanes = pl.ds(pl.multiple_of(c * 128, 128), 128)
+            accs = [jnp.zeros((32, 128), jnp.int32) for _ in range(8)]
+            for k in range(1, 1 + F2):
+                hit = sub32 == jnp.broadcast_to(lows[k:k + 1, lanes], (32, 128))
+                for w in range(8):
+                    u = jnp.broadcast_to(unit_of[w, k:k + 1, lanes], (32, 128))
+                    accs[w] = accs[w] + jnp.where(hit, u, 0)
+            for w in range(8):
+                for j in range(8):
+                    first = (w * 8 + j) * 32
+                    bsel[q, first:first + 32, lanes] = count(accs[w], j)
+            self_row = selfs[:, lanes].astype(jnp.int16)
+            lanes = pl.ds(pl.multiple_of(SEED + c * 128, 128), 128)
+            for t in range(FRONT // 16):
+                here = iota16 + jnp.full((16, 128), t * 16, jnp.int32).astype(jnp.int16)
+                bsel[q, t * 16:(t + 1) * 16, lanes] = jnp.where(here == self_row, one, zero)
+            return carry2
+
+        lax.fori_loop(0, SEED // 128, column, 0)
+        return carry
 
     def sum_marks(i):
         at = pl.multiple_of(i // 2 * 16, 16)
         half = i % 2
         blk = idm[pl.ds(at, 16), :]
-        want = [jnp.broadcast_to(blk[:, 1 + k:2 + k], (16, 128)).astype(jnp.int16) for k in range(F1)]
-        base = lane16 + jnp.full((16, 128), half * (SRC // 2), jnp.int32).astype(jnp.int16)
-        for c in range(SRC // 256):
-            here = base + jnp.full((16, 128), c * 128, jnp.int32).astype(jnp.int16)
-            acc = jnp.where(here == want[0], one, zero)
-            for k in range(1, F1):
-                acc = acc + jnp.where(here == want[k], one, zero)
-            col = pl.ds(pl.multiple_of(half * (SRC // 2) + c * 128, 128), 128)
-            ssel[pl.ds(at, 16), col] = acc
+        keys, units = spread_columns(blk, range(1, 1 + F1)), spread_columns(blk, range(17, 17 + F1))
+        for w in range(4):
+            acc = word(lane32 + (half * 4 + w) * 128, keys, units)
+            for j in range(8):
+                col = pl.ds(pl.multiple_of(half * (SRC // 2) + (w * 8 + j) * 128, 128), 128)
+                ssel[pl.ds(at, 16), col] = count(acc, j)
 
     def sum_ids(b):
-        idm[...] = idxv[:, cols(b)].T
+        idm[...] = jnp.concatenate(keys_units(idxv[:, cols(b)]), axis=0).T
 
     def cols(b):
         return pl.ds(pl.multiple_of(b * 256, 256), 256)
@@ -325,6 +360,7 @@
 
     sum_ids(0)
     lax.fori_loop(0, 32, one_mark, 0)
+    lax.fori_loop(0, NAR, backward_marks, 0)
 
     come = pulled.at[pl.ds(0, (DEV - 1) * CAP)]
     pltpu.make_async_copy(come, come, row_recv).wait()
@@ -364,7 +400,6 @@
 
     def load_sums(b, mark):
         def some(i, c):
-            backward_marks(b * 16 + i)
             mark(i)
             for j in range(16):
                 m, here = own_row(b, i, j)
@@ -379,7 +414,6 @@
 
     def multiply_sums(b):
         def some(i, c):
-            backward_marks(b * 16 + i)
             for j in range(16):
                 own_row(b, i, j)
             return c
@@ -717,10 +751,12 @@
             V((NAR, FRONT, HID), BF),
             V((NAR, 2 * SEED, FRONT), BF),
             V((NAR, FRONT, 2 * SEED), BF),
-            V((NAR, 4, 1 + F2, 16, 128), jnp.int16),
-            V((SEED, 16), jnp.int32),
+            V((8, 16, SEED), jnp.int32),
+            V((16, SEED), jnp.int32),
+            V((16, SEED), jnp.int32),
+            V((SEED, 32), jnp.int32),
             V((256, SRC), BF),
-            V((256, 16), jnp.int32),
+            V((256, 32), jnp.int32),
             V((NAR, SEED, 128), F32),
             V((SEED, 128), F32),
             V((NAR, SEED, HID), BF),

time: 151 us -> 150 us (level)
  Pallas kernels: 150 us -> 148 us
    pallas_call x1, Pallas kernels: 144 us -> 142 us  [main(): pl.pallas_call(main_kernel, out_shape=sds((ROWS, 128), F32), in_specs=[vm...]
where the time goes in v15:
time: 150 us; the launch traced here: 149 us
  Pallas kernels  148 us (99%)
    pallas_call x1, Pallas kernels, main(): pl.pallas_call(main_kernel, out_shape=sds((ROWS, 128), F32), in_specs=[vm...  142 us
    pallas_call x1, Pallas kernels, update(): pl.pallas_call(update_kernel, out_shape=[sds((1, 1), F32), sds((64, HID),...  5.45 us

profile of v15, /device:TPU:1, one launch (start us, length us, event | category | flops | bytes accessed | tf_op | source)
XLA Modules:
  0.0 149.5 jit_solution(14635994005294336586)
XLA Ops:
  0.6 0.0 copy-start.2
  0.7 0.0 copy-start.5
  0.7 0.0 copy-start.4
  0.7 0.0 copy-start.3
  0.7 0.0 copy-start.1
  0.7 142.2 %shard_map.222.res = f32[896,128]{1,0:T(8,128)} custom-call(s32[64,128]{1,0:T(8,128)} %bitcast.28, bf16[8192,128]{1,0:T(8,128)(2,1)} %feat.1, s32[16,2048]{1,0:T(8,128)} %bitcast.25, s32[15,2048]{1,0:T(8,128)} %bitcast.26, s32[11,512]{1,0:T(8,128)} %bitcast.29, s32[10,512]{1,0:T(8,128)} %bitcast.30, s32[1,512]{1,0:T(1,128)} %bitcast.31, s32[1,512]{1,0:T(1,128)} %bitcast.32, ...), custom_call_target="tpu_custom_call" | custom-call | tf_op jit(solution)/shard_map/pallas_call | solution.py:733
  142.9 0.0 copy-done.2
  143.0 0.0 copy-done.5
  143.0 0.0 copy-done.4
  143.0 0.0 copy-done.3
  143.0 0.0 copy-done.1
  143.0 0.0 copy-start
  143.0 1.0 copy-done
  144.0 5.5 %shard_map.223 = (f32[1,1]{1,0:T(1,128)}, f32[64,256]{1,0:T(8,128)}, f32[172,128]{1,0:T(8,128)}, f32[64,256]{1,0:T(8,128)}, f32[172,128]{1,0:T(8,128)}, /*index=...) custom-call(f32[896,128]{1,0:T(8,128)S(1)} %copy-done, ...), custom_call_target="tpu_custom_call" | custom-call | tf_op jit(solution)/shard_map/pallas_call | solution.py:829
Async XLA Ops:
  0.6 142.3 %copy-start.2 = (f32[64,256]{1,0:T(8,128)S(1)}, f32[64,256]{1,0:T(8,128)}, u32[]{:S(2)}) copy-start(f32[64,256]{1,0:T(8,128)} %w1own.1) | copy-start | bytes 196612
  0.7 142.3 %copy-start.5 = (f32[428]{0:T(512)S(1)}, f32[428]{0:T(512)}, u32[]{:S(2)}) copy-start(f32[428]{0:T(512)} %param.29) | copy-start | bytes 5140
  0.7 142.3 %copy-start.4 = (f32[428]{0:T(512)S(1)}, f32[428]{0:T(512)}, u32[]{:S(2)}) copy-start(f32[428]{0:T(512)} %param.28) | copy-start | bytes 5140
  0.7 142.3 %copy-start.3 = (f32[428]{0:T(512)S(1)}, f32[428]{0:T(512)}, u32[]{:S(2)}) copy-start(f32[428]{0:T(512)} %param.27) | copy-start | bytes 5140
  0.7 142.3 %copy-start.1 = (f32[128,172]{0,1:T(8,128)S(1)}, f32[128,172]{0,1:T(8,128)}, u32[]{:S(2)}) copy-start(f32[128,172]{0,1:T(8,128)} %param.24) | copy-start | bytes 264196
  143.0 1.0 copy-start

commit v16 on v15

--- a/solution.py
+++ b/solution.py
@@ -306,7 +306,8 @@
         invc[q] = column(1.0 / jnp.maximum(n, 1.0))
     livec[...] = column(2.0 * LAM / HID / SEEDS_ALL * live[...].astype(F32))
 
-    def backward_marks(q, carry):
+    def backward_marks(b):
+        q = b // 2
         r = gidx2[q] - y * FRONT
         lows[...] = r & 31
         inside = (r >= 0) & (r < FRONT)
@@ -334,8 +335,7 @@
                 bsel[q, t * 16:(t + 1) * 16, lanes] = jnp.where(here == self_row, one, zero)
             return carry2
 
-        lax.fori_loop(0, SEED // 128, column, 0)
-        return carry
+        lax.fori_loop(b % 2 * 2, b % 2 * 2 + 2, column, 0)
 
     def sum_marks(i):
         at = pl.multiple_of(i // 2 * 16, 16)
@@ -360,7 +360,6 @@
 
     sum_ids(0)
     lax.fori_loop(0, 32, one_mark, 0)
-    lax.fori_loop(0, NAR, backward_marks, 0)
 
     come = pulled.at[pl.ds(0, (DEV - 1) * CAP)]
     pltpu.make_async_copy(come, come, row_recv).wait()
@@ -399,6 +398,8 @@
         return m, here
 
     def load_sums(b, mark):
+        backward_marks(b)
+
         def some(i, c):
             mark(i)
             for j in range(16):
@@ -413,6 +414,8 @@
         finish(b)
 
     def multiply_sums(b):
+        backward_marks(b)
+
         def some(i, c):
             for j in range(16):
                 own_row(b, i, j)

time: 150 us -> 151 us (level)
  no operation moved by 1% of the time
where the time goes in v16:
time: 151 us
  Pallas kernels  149 us (99%)
    pallas_call x1, Pallas kernels, main(): pl.pallas_call(main_kernel, out_shape=sds((ROWS, 128), F32), in_specs=[vm...  144 us
    pallas_call x1, Pallas kernels, update(): pl.pallas_call(update_kernel, out_shape=[sds((1, 1), F32), sds((64, HID),...  5.45 us

profile of v16, /device:TPU:1, one launch (start us, length us, event | category | flops | bytes accessed | tf_op | source)
XLA Modules:
  0.0 150.8 jit_solution(5775746179578795775)
XLA Ops:
  0.6 0.0 copy-start.2
  0.7 0.0 copy-start.5
  0.7 0.0 copy-start.4
  0.7 0.0 copy-start.3
  0.7 0.0 copy-start.1
  0.7 143.5 %shard_map.222.res = f32[896,128]{1,0:T(8,128)} custom-call(s32[64,128]{1,0:T(8,128)} %bitcast.28, bf16[8192,128]{1,0:T(8,128)(2,1)} %feat.1, s32[16,2048]{1,0:T(8,128)} %bitcast.25, s32[15,2048]{1,0:T(8,128)} %bitcast.26, s32[11,512]{1,0:T(8,128)} %bitcast.29, s32[10,512]{1,0:T(8,128)} %bitcast.30, s32[1,512]{1,0:T(1,128)} %bitcast.31, s32[1,512]{1,0:T(1,128)} %bitcast.32, ...), custom_call_target="tpu_custom_call" | custom-call | tf_op jit(solution)/shard_map/pallas_call | solution.py:736
  144.2 0.0 copy-done.2
  144.2 0.0 copy-done.5
  144.2 0.0 copy-done.4
  144.3 0.0 copy-done.3
  144.3 0.0 copy-done.1
  144.3 0.0 copy-start
  144.3 1.0 copy-done
  145.3 5.5 %shard_map.223 = (f32[1,1]{1,0:T(1,128)}, f32[64,256]{1,0:T(8,128)}, f32[172,128]{1,0:T(8,128)}, f32[64,256]{1,0:T(8,128)}, f32[172,128]{1,0:T(8,128)}, /*index=...) custom-call(f32[896,128]{1,0:T(8,128)S(1)} %copy-done, ...), custom_call_target="tpu_custom_call" | custom-call | tf_op jit(solution)/shard_map/pallas_call | solution.py:832
Async XLA Ops:
  0.6 143.6 %copy-start.2 = (f32[64,256]{1,0:T(8,128)S(1)}, f32[64,256]{1,0:T(8,128)}, u32[]{:S(2)}) copy-start(f32[64,256]{1,0:T(8,128)} %w1own.1) | copy-start | bytes 196612
  0.7 143.6 %copy-start.5 = (f32[428]{0:T(512)S(1)}, f32[428]{0:T(512)}, u32[]{:S(2)}) copy-start(f32[428]{0:T(512)} %param.29) | copy-start | bytes 5140
  0.7 143.6 %copy-start.4 = (f32[428]{0:T(512)S(1)}, f32[428]{0:T(512)}, u32[]{:S(2)}) copy-start(f32[428]{0:T(512)} %param.28) | copy-start | bytes 5140
  0.7 143.6 %copy-start.3 = (f32[428]{0:T(512)S(1)}, f32[428]{0:T(512)}, u32[]{:S(2)}) copy-start(f32[428]{0:T(512)} %param.27) | copy-start | bytes 5140
  0.7 143.6 %copy-start.1 = (f32[128,172]{0,1:T(8,128)S(1)}, f32[128,172]{0,1:T(8,128)}, u32[]{:S(2)}) copy-start(f32[128,172]{0,1:T(8,128)} %param.24) | copy-start | bytes 264196
  144.3 1.0 copy-start

commit v17 on v15

--- a/solution.py
+++ b/solution.py
@@ -50,7 +50,7 @@
 GRP = 32
 ROW_M2 = P1 * PIECE
 ROW_X2 = ROW_M2 + CLS_PAD
-ROWS = ROW_X2 + CLS_PAD
+ROWS = ROW_X2 + NAR * CLS_PAD
 SEEDS_ALL = SEED * DEV
 
 
@@ -70,7 +70,9 @@
 
 def dot3(a, b, dims):
     (ah, al), (bh, bl) = a, b
-    return dot(ah, bh, dims) + (dot(ah, bl, dims) + dot(al, bh, dims))
+    return dot(
+        jnp.concatenate([ah, ah, al], axis=dims[0][0]), jnp.concatenate([bh, bl, bh], axis=dims[1][0]), dims
+    )
 
 
 def ns_step(x):
@@ -88,9 +90,9 @@
 def main_kernel(
     reqt, feat, idx1t, msk1t, idx2t, msk2t, labels, live, w1, w2own, m1, m2own, bias,
     o_all,
-    table, featb, pulled, stage, reqv, reqin, mid, idxv, invv, near, own, z1, gbuf, fsel, bsel, unit_of, lows, selfs, idc, ssel, idm, invc, livec, rbuf, dbuf,
+    table, featb, pulled, stage, reqv, reqin, mid, idxv, idxp, invv, near, own, slope, gbuf, fsel, bsel, unit_of, lows, selfs, idc, ssel, idm, invc, livec, rbuf, dbuf,
     gw1, gw2t, m2pad, gidx2, w2t, b2c, pay1, pay2, misc, inbox1, inbox2, ybox1, ybox2, res2, x2s,
-    reqs, idx, inv,
+    reqs, idx,
     feat_sem, loc_sem, ask_sem, req_send, mid_recv, req_recv, row_send, row_recv, nar_send, nar_recv,
     h_send, h_recv, r_send, r_recv, d_send, d_recv, rs_send, rs_recv, y_send, y_recv, ag_send, ag_recv,
 ):
@@ -153,7 +155,14 @@
     idxv[0:1, :] = idx1t[0:1, :]
     idxv[1:16, :] = jnp.where(msk > 0, idx1t[1:16, :], SRC)
     invv[...] = 1.0 / jnp.maximum(jnp.sum(msk.astype(F32), axis=0, keepdims=True), 1.0)
-    to_smem = [pltpu.make_async_copy(idxv, idx, loc_sem.at[0]), pltpu.make_async_copy(invv, inv, loc_sem.at[1])]
+    for half in range(2):
+        parts = []
+        for r in range(8):
+            parts.append(jnp.concatenate(
+                [idxv[:, (half * 4 + b) * 256 + r * 32:(half * 4 + b) * 256 + r * 32 + 32] for b in range(4)], axis=1
+            ))
+        idxp[half * 128:(half + 1) * 128, :] = jnp.concatenate(parts, axis=0).T
+    to_smem = [pltpu.make_async_copy(idxp, idx, loc_sem.at[0])]
     for c in to_smem:
         c.start()
 
@@ -392,21 +401,17 @@
             link(blk, blk, h_send.at[1, b], h_recv.at[1, b], left).wait_recv()
             link(blk, blk, h_send.at[2, b], h_recv.at[2, b], left).start()
 
-    def own_row(b, i, j):
-        m = b * 256 + i * 16 + j
-        here = pl.ds(pl.multiple_of(i * 16, 16) + j, 1)
-        own[here, :] = view[idx[0, m]]
-        return m, here
-
-    def load_sums(b, mark):
+    def load_sums(b):
         def some(i, c):
-            mark(i)
-            for j in range(16):
-                m, here = own_row(b, i, j)
-                rows = [view[idx[1 + k, m]] for k in range(F1)]
-                while len(rows) > 1:
-                    rows = [p + q for p, q in zip(rows[::2], rows[1::2])] + ([rows[-1]] if len(rows) % 2 else [])
-                near[here, :] = rows[0] * inv[0, m]
+            for e in range(2):
+                line = b * 32 + 2 * i + e
+                for r in range(8):
+                    here = pl.ds(r * 32 + 2 * i + e, 1)
+                    own[here, :] = view[idx[line, r * 16]]
+                    rows = [view[idx[line, r * 16 + 1 + k]] for k in range(F1)]
+                    while len(rows) > 1:
+                        rows = [p + q for p, q in zip(rows[::2], rows[1::2])] + ([rows[-1]] if len(rows) % 2 else [])
+                    near[here, :] = rows[0]
             return c
 
         lax.fori_loop(0, 16, some, 0)
@@ -414,26 +419,29 @@
 
     def multiply_sums(b):
         def some(i, c):
-            for j in range(16):
-                own_row(b, i, j)
+            for e in range(2):
+                for r in range(8):
+                    own[pl.ds(r * 32 + 2 * i + e, 1), :] = view[idx[b * 32 + 2 * i + e, r * 16]]
             return c
 
         lax.fori_loop(0, 16, some, 0)
+        near[...] = dot(ssel[...], pulled[...])
+        finish(b)
+
+    def finish(b):
+        rows = cols(b)
         scale = jnp.concatenate(
             [spread(invv[0:1, pl.ds(pl.multiple_of(b * 256 + c * 128, 128), 128)]) for c in range(2)], axis=0
         )
-        near[...] = dot(ssel[...], pulled[...]) * scale
-        finish(b)
-
-    def finish(b):
-        rows = cols(b)
-        act = jnp.concatenate([own[...].astype(BF), near[...].astype(BF)], axis=1)
+        act = jnp.concatenate([own[...].astype(BF), (near[...] * scale).astype(BF)], axis=1)
         a1 = act.T
         for h in range(2):
             a1t[pl.ds(pl.multiple_of((2 * b + h) * 256, 256), 256), :] = a1[:, h * 128:(h + 1) * 128]
         z = dot(act, gw1[...].reshape(2 * D_IN, HID)) + bias[0:1, 0:HID]
-        z1[rows, :] = z
-        gbuf[y, rows, :] = (z / (1.0 + jnp.exp(-z))).astype(BF)
+        sig = 1.0 / (1.0 + jnp.exp(-z))
+        h1 = z * sig
+        slope[rows, :] = sig + h1 * (1.0 - sig)
+        gbuf[y, rows, :] = h1.astype(BF)
         blk = gbuf.at[y, rows, :]
         link(blk, blk, h_send.at[0, b], h_recv.at[0, b], right).start()
         link(blk, blk, h_send.at[1, b], h_recv.at[1, b], left).start()
@@ -443,7 +451,7 @@
             forward(b - 1)
 
     def loaded(b, c):
-        load_sums(b, lambda i: None)
+        load_sums(b)
         return c
 
     multiply_sums(0)
@@ -660,12 +668,10 @@
 
     def to_z(b, db):
         rows = pl.ds(pl.multiple_of(b * 256, 256), 256)
-        z = z1[rows, :]
-        sig = 1.0 / (1.0 + jnp.exp(-z))
         dh = jnp.concatenate(
             [dh1[pl.ds(pl.multiple_of(h * FRONT + b * 256, 256), 256), :] for h in range(2)], axis=1
         )
-        dz = (dh * sig * (1.0 + z * (1.0 - sig))).astype(BF)
+        dz = (dh * slope[rows, :]).astype(BF)
         a1 = jnp.concatenate(
             [a1t[pl.ds(pl.multiple_of((2 * b + h) * 256, 256), 256), :] for h in range(2)], axis=1
         )
@@ -705,11 +711,9 @@
     add_plane(pay1, inbox1, ybox1, 0, P1, 0, add_first_momentum)
     x2 = ns_step(x2)
     add_group(ybox1, o_all, 0, P1, 0)
-    for _ in range(NS_ITERS - 2):
-        x2 = ns_step(x2)
+    x2 = ns_step(x2)
     for q in range(NAR):
-        x2s[q] = x2[:, q * 128:(q + 1) * 128]
-    o_all[ROW_X2:ROW_X2 + CLS_PAD, :] = x2s[y]
+        o_all[ROW_X2 + q * CLS_PAD:ROW_X2 + (q + 1) * CLS_PAD, :] = x2[:, q * 128:(q + 1) * 128]
     take(o_all, 0, P1, 0)
 
     for b in range(8):
@@ -744,6 +748,7 @@
             V((DEV, 128), jnp.int32),
             V((NAR, GRP, 1, 128), jnp.int32),
             V((16, FRONT), jnp.int32),
+            V((256, 128), jnp.int32),
             V((1, FRONT), F32),
             V((256, D_IN), F32),
             V((256, D_IN), F32),
@@ -777,8 +782,7 @@
             V((P2 * PIECE, 128), F32),
             V((NAR, CLS_PAD, 128), F32),
             pltpu.SMEM((DEV, 1, 128), jnp.int32),
-            pltpu.SMEM((16, FRONT), jnp.int32),
-            pltpu.SMEM((1, FRONT), F32),
+            pltpu.SMEM((256, 128), jnp.int32),
             dma, dma((3,)), dma((GRP,)), dma((NAR,)), dma((NAR,)), dma((GRP,)), dma, dma, dma((3, 3)), dma((3, 3)),
             dma((3, 8)), dma((3, 8)), dma((4,)), dma((4,)), dma((4,)), dma((4,)),
             dma((2,)), dma((2,)), dma((2, 3)), dma((2, 3)), dma((2,)), dma((2,)),
@@ -792,7 +796,7 @@
 def update_kernel(
     res, w1own, w2own, bias, biasm, biasv,
     o_loss, o_first, o_second, o_mom1, o_mom2, o_flow, o_slow, o_bias, o_bm, o_bv,
-    x1s,
+    x1s, x2s,
 ):
     y = lax.axis_index("nar")
     mom1 = jnp.concatenate([res[0:256, :], res[256:512, :]], axis=1)
@@ -800,13 +804,18 @@
     block64 = pl.ds(pl.multiple_of(y * 64, 64), 64)
     o_mom1[...] = x1s[block64, :]
     x1 = mom1 * (1.0 / (jnp.sqrt(jnp.sum(mom1 * mom1, keepdims=True)) + 1e-07))
-    for _ in range(NS_ITERS):
+    x2 = jnp.concatenate([res[ROW_X2 + q * CLS_PAD:ROW_X2 + (q + 1) * CLS_PAD, :] for q in range(NAR)], axis=1)
+    for i in range(NS_ITERS):
         x1 = ns_step(x1)
+        if i < 2:
+            x2 = ns_step(x2)
     x1s[...] = x1
+    for q in range(NAR):
+        x2s[q] = x2[:, q * 128:(q + 1) * 128]
     first_new = w1own[...] * (1.0 - WDECAY) - x1s[block64, :]
     o_first[...] = first_new
     o_flow[...] = first_new.astype(BF)
-    second = w2own[...] * (1.0 - WDECAY) - (2 * HID / CLS) ** 0.5 * res[ROW_X2:ROW_X2 + CLS, :]
+    second = w2own[...] * (1.0 - WDECAY) - (2 * HID / CLS) ** 0.5 * x2s[y][0:CLS, :]
     o_second[...] = second
     o_slow[...] = second.astype(BF)
     o_mom2[...] = res[ROW_M2:ROW_M2 + CLS, :]
@@ -834,7 +843,7 @@
         ],
         in_specs=[vm] * 6,
         out_specs=[vm] * 10,
-        scratch_shapes=[pltpu.VMEM((2 * D_IN, HID), F32)],
+        scratch_shapes=[pltpu.VMEM((2 * D_IN, HID), F32), pltpu.VMEM((NAR, CLS_PAD, 128), F32)],
         compiler_params=pltpu.CompilerParams(vmem_limit_bytes=32 * 2**20),
     )(*args)
 

time: 150 us -> 147 us (0.980)
  Pallas kernels: 148 us -> 145 us
    pallas_call x1, Pallas kernels: 142 us -> 139 us  [main(): pl.pallas_call(main_kernel, out_shape=sds((ROWS, 128), F32), in_specs=[vm...]
where the time goes in v17:
time: 147 us
  Pallas kernels  145 us (99%)
    pallas_call x1, Pallas kernels, main(): pl.pallas_call(main_kernel, out_shape=sds((ROWS, 128), F32), in_specs=[vm...  139 us
    pallas_call x1, Pallas kernels, update(): pl.pallas_call(update_kernel, out_shape=[sds((1, 1), F32), sds((64, HID),...  6.42 us

profile of v17, /device:TPU:1, one launch (start us, length us, event | category | flops | bytes accessed | tf_op | source)
XLA Modules:
  0.0 146.8 jit_solution(12967607731873725602)
XLA Ops:
  0.6 0.0 copy-start.2
  0.7 0.0 copy-start.5
  0.7 0.0 copy-start.4
  0.7 0.0 copy-start.3
  0.7 0.0 copy-start.1
  0.7 138.5 %shard_map.222.res = f32[1424,128]{1,0:T(8,128)} custom-call(s32[64,128]{1,0:T(8,128)} %bitcast.28, bf16[8192,128]{1,0:T(8,128)(2,1)} %feat.1, s32[16,2048]{1,0:T(8,128)} %bitcast.25, s32[15,2048]{1,0:T(8,128)} %bitcast.26, s32[11,512]{1,0:T(8,128)} %bitcast.29, s32[10,512]{1,0:T(8,128)} %bitcast.30, s32[1,512]{1,0:T(1,128)} %bitcast.31, s32[1,512]{1,0:T(1,128)} %bitcast.32, ...), custom_call_target="tpu_custom_call" | custom-call | tf_op jit(solution)/shard_map/pallas_call | solution.py:737
  139.2 0.0 copy-done.2
  139.2 0.0 copy-done.5
  139.2 0.0 copy-done.4
  139.2 0.0 copy-done.3
  139.3 0.0 copy-done.1
  139.3 0.0 copy-start
  139.3 1.1 copy-done
  140.4 6.4 %shard_map.223 = (f32[1,1]{1,0:T(1,128)}, f32[64,256]{1,0:T(8,128)}, f32[172,128]{1,0:T(8,128)}, f32[64,256]{1,0:T(8,128)}, f32[172,128]{1,0:T(8,128)}, /*index=...) custom-call(f32[1424,128]{1,0:T(8,128)S(1)} %copy-done, ...), custom_call_target="tpu_custom_call" | custom-call | tf_op jit(solution)/shard_map/pallas_call | solution.py:838
Async XLA Ops:
  0.6 138.6 %copy-start.2 = (f32[64,256]{1,0:T(8,128)S(1)}, f32[64,256]{1,0:T(8,128)}, u32[]{:S(2)}) copy-start(f32[64,256]{1,0:T(8,128)} %w1own.1) | copy-start | bytes 196612
  0.7 138.6 %copy-start.5 = (f32[428]{0:T(512)S(1)}, f32[428]{0:T(512)}, u32[]{:S(2)}) copy-start(f32[428]{0:T(512)} %param.29) | copy-start | bytes 5140
  0.7 138.6 %copy-start.4 = (f32[428]{0:T(512)S(1)}, f32[428]{0:T(512)}, u32[]{:S(2)}) copy-start(f32[428]{0:T(512)} %param.28) | copy-start | bytes 5140
  0.7 138.6 %copy-start.3 = (f32[428]{0:T(512)S(1)}, f32[428]{0:T(512)}, u32[]{:S(2)}) copy-start(f32[428]{0:T(512)} %param.27) | copy-start | bytes 5140
  0.7 138.6 %copy-start.1 = (f32[128,172]{0,1:T(8,128)S(1)}, f32[128,172]{0,1:T(8,128)}, u32[]{:S(2)}) copy-start(f32[128,172]{0,1:T(8,128)} %param.24) | copy-start | bytes 264196
  139.3 1.1 copy-start

commit v18 on v17

--- a/solution.py
+++ b/solution.py
@@ -244,8 +244,10 @@
     my_rows = pl.ds(pl.multiple_of(me * CAP, CAP), CAP)
 
     def pick(t, u, slot):
-        for r in range(CAP):
-            stage[r:r + 1, :] = view[reqs[t * NAR + u, 0, r]]
+        for half in range(0, CAP, 32):
+            rows = [view[reqs[t * NAR + u, 0, half + r]] for r in range(32)]
+            for r in range(32):
+                stage[half + r:half + r + 1, :] = rows[r]
         featb[slot, :] = stage[...].astype(BF)
 
     def serve_one(t, u, slot):
@@ -403,15 +405,18 @@
 
     def load_sums(b):
         def some(i, c):
+            found = []
             for e in range(2):
                 line = b * 32 + 2 * i + e
                 for r in range(8):
-                    here = pl.ds(r * 32 + 2 * i + e, 1)
-                    own[here, :] = view[idx[line, r * 16]]
+                    self_row = view[idx[line, r * 16]]
                     rows = [view[idx[line, r * 16 + 1 + k]] for k in range(F1)]
                     while len(rows) > 1:
                         rows = [p + q for p, q in zip(rows[::2], rows[1::2])] + ([rows[-1]] if len(rows) % 2 else [])
-                    near[here, :] = rows[0]
+                    found.append((r * 32 + 2 * i + e, self_row, rows[0]))
+            for at, self_row, total in found:
+                own[pl.ds(at, 1), :] = self_row
+                near[pl.ds(at, 1), :] = total
             return c
 
         lax.fori_loop(0, 16, some, 0)
@@ -419,9 +424,12 @@
 
     def multiply_sums(b):
         def some(i, c):
+            found = []
             for e in range(2):
                 for r in range(8):
-                    own[pl.ds(r * 32 + 2 * i + e, 1), :] = view[idx[b * 32 + 2 * i + e, r * 16]]
+                    found.append((r * 32 + 2 * i + e, view[idx[b * 32 + 2 * i + e, r * 16]]))
+            for at, self_row in found:
+                own[pl.ds(at, 1), :] = self_row
             return c
 
         lax.fori_loop(0, 16, some, 0)

time: 147 us -> 147 us (level)
  no operation moved by 1% of the time
where the time goes in v18:
time: 147 us
  Pallas kernels  145 us (99%)
    pallas_call x1, Pallas kernels, main(): pl.pallas_call(main_kernel, out_shape=sds((ROWS, 128), F32), in_specs=[vm...  139 us
    pallas_call x1, Pallas kernels, update(): pl.pallas_call(update_kernel, out_shape=[sds((1, 1), F32), sds((64, HID),...  6.42 us

profile of v18, /device:TPU:1, one launch (start us, length us, event | category | flops | bytes accessed | tf_op | source)
XLA Modules:
  0.0 146.8 jit_solution(3589399732232722477)
XLA Ops:
  0.6 0.0 copy-start.2
  0.7 0.0 copy-start.5
  0.7 0.0 copy-start.4
  0.7 0.0 copy-start.3
  0.7 0.0 copy-start.1
  0.7 138.5 %shard_map.222.res = f32[1424,128]{1,0:T(8,128)} custom-call(s32[64,128]{1,0:T(8,128)} %bitcast.28, bf16[8192,128]{1,0:T(8,128)(2,1)} %feat.1, s32[16,2048]{1,0:T(8,128)} %bitcast.25, s32[15,2048]{1,0:T(8,128)} %bitcast.26, s32[11,512]{1,0:T(8,128)} %bitcast.29, s32[10,512]{1,0:T(8,128)} %bitcast.30, s32[1,512]{1,0:T(1,128)} %bitcast.31, s32[1,512]{1,0:T(1,128)} %bitcast.32, ...), custom_call_target="tpu_custom_call" | custom-call | tf_op jit(solution)/shard_map/pallas_call | solution.py:745
  139.2 0.0 copy-done.2
  139.3 0.0 copy-done.5
  139.3 0.0 copy-done.4
  139.3 0.0 copy-done.3
  139.3 0.0 copy-done.1
  139.3 0.0 copy-start
  139.3 1.1 copy-done
  140.4 6.4 %shard_map.223 = (f32[1,1]{1,0:T(1,128)}, f32[64,256]{1,0:T(8,128)}, f32[172,128]{1,0:T(8,128)}, f32[64,256]{1,0:T(8,128)}, f32[172,128]{1,0:T(8,128)}, /*index=...) custom-call(f32[1424,128]{1,0:T(8,128)S(1)} %copy-done, ...), custom_call_target="tpu_custom_call" | custom-call | tf_op jit(solution)/shard_map/pallas_call | solution.py:846
Async XLA Ops:
  0.6 138.6 %copy-start.2 = (f32[64,256]{1,0:T(8,128)S(1)}, f32[64,256]{1,0:T(8,128)}, u32[]{:S(2)}) copy-start(f32[64,256]{1,0:T(8,128)} %w1own.1) | copy-start | bytes 196612
  0.7 138.6 %copy-start.5 = (f32[428]{0:T(512)S(1)}, f32[428]{0:T(512)}, u32[]{:S(2)}) copy-start(f32[428]{0:T(512)} %param.29) | copy-start | bytes 5140
  0.7 138.6 %copy-start.4 = (f32[428]{0:T(512)S(1)}, f32[428]{0:T(512)}, u32[]{:S(2)}) copy-start(f32[428]{0:T(512)} %param.28) | copy-start | bytes 5140
  0.7 138.6 %copy-start.3 = (f32[428]{0:T(512)S(1)}, f32[428]{0:T(512)}, u32[]{:S(2)}) copy-start(f32[428]{0:T(512)} %param.27) | copy-start | bytes 5140
  0.7 138.6 %copy-start.1 = (f32[128,172]{0,1:T(8,128)S(1)}, f32[128,172]{0,1:T(8,128)}, u32[]{:S(2)}) copy-start(f32[128,172]{0,1:T(8,128)} %param.24) | copy-start | bytes 264196
  139.3 1.1 copy-start

commit v19 on v18

--- a/solution.py
+++ b/solution.py
@@ -90,13 +90,13 @@
 def main_kernel(
     reqt, feat, idx1t, msk1t, idx2t, msk2t, labels, live, w1, w2own, m1, m2own, bias,
     o_all,
-    table, featb, pulled, stage, reqv, reqin, mid, idxv, idxp, invv, near, own, slope, gbuf, fsel, bsel, unit_of, lows, selfs, idc, ssel, idm, invc, livec, rbuf, dbuf,
+    sums, table, featb, pulled, stage, reqv, reqin, mid, idxv, idxp, invv, near, own, slope, gbuf, fsel, bsel, unit_of, lows, selfs, idc, ssel, idm, invc, livec, rbuf, dbuf,
     gw1, gw2t, m2pad, gidx2, w2t, b2c, pay1, pay2, misc, inbox1, inbox2, ybox1, ybox2, res2, x2s,
     reqs, idx,
     feat_sem, loc_sem, ask_sem, req_send, mid_recv, req_recv, row_send, row_recv, nar_send, nar_recv,
     h_send, h_recv, r_send, r_recv, d_send, d_recv, rs_send, rs_recv, y_send, y_recv, ag_send, ag_recv,
 ):
-    a1t, dh1, tot, gsum = featb, table, table.at[2 * FRONT:3 * FRONT], table.at[3 * FRONT:3 * FRONT + 512]
+    a1t, dh1, gsum = featb, table, table.at[3 * FRONT:3 * FRONT + 512]
     g = lax.axis_index("grp")
     y = lax.axis_index("nar")
     me = g * NAR + y
@@ -390,18 +390,40 @@
     for c in to_smem:
         c.wait()
 
+    def add_blocks(which):
+        marks = [lambda n, q=q, b=b: fsel[q, pl.ds(n, SEED), cols(b)] for q, b in which]
+        blocks = jnp.concatenate([gbuf[q, cols(b), :] for q, b in which], axis=0)
+
+        def rows512(i, c):
+            n = pl.multiple_of(i * SEED, SEED)
+            part = dot(jnp.concatenate([m(n) for m in marks], axis=1), blocks)
+            for h in range(2):
+                rows = pl.ds(pl.multiple_of(h * 2 * SEED + i * SEED, SEED), SEED)
+                sums[rows, :] = sums[rows, :] + part[:, h * 128:(h + 1) * 128]
+            return c
+
+        lax.fori_loop(0, 2, rows512, 0)
+
     def forward(b):
+        from_left, from_right = gbuf.at[left, cols(b), :], gbuf.at[right, cols(b), :]
+        link(from_left, from_left, h_send.at[0, b], h_recv.at[0, b], right).wait_recv()
+
         @pl.when(b % 2 == 0)
         def _():
-            blk = gbuf.at[left, cols(b), :]
-            link(blk, blk, h_send.at[0, b], h_recv.at[0, b], right).wait_recv()
-            link(blk, blk, h_send.at[2, b], h_recv.at[2, b], right).start()
+            link(from_left, from_left, h_send.at[2, b], h_recv.at[2, b], right).start()
+
+        link(from_right, from_right, h_send.at[1, b], h_recv.at[1, b], left).wait_recv()
 
         @pl.when(b % 2 == 1)
         def _():
-            blk = gbuf.at[right, cols(b), :]
-            link(blk, blk, h_send.at[1, b], h_recv.at[1, b], left).wait_recv()
-            link(blk, blk, h_send.at[2, b], h_recv.at[2, b], left).start()
+            link(from_right, from_right, h_send.at[2, b], h_recv.at[2, b], left).start()
+
+        add_blocks([(left, b), (right, b)])
+
+    def add_opposite(b):
+        blk = gbuf.at[opp, cols(b), :]
+        link(blk, blk, h_send.at[2, b], h_recv.at[2, b], right).wait_recv()
+        add_blocks([(opp, b)])
 
     def load_sums(b):
         def some(i, c):
@@ -454,48 +476,33 @@
         link(blk, blk, h_send.at[0, b], h_recv.at[0, b], right).start()
         link(blk, blk, h_send.at[1, b], h_recv.at[1, b], left).start()
 
+        add_blocks([(y, b)])
+
         @pl.when(b > 0)
         def _():
             forward(b - 1)
 
+        @pl.when(b > 2)
+        def _():
+            add_opposite(b - 3)
+
     def loaded(b, c):
         load_sums(b)
         return c
 
+    sums[...] = jnp.zeros((4 * SEED, 128), F32)
     multiply_sums(0)
     lax.fori_loop(1, 8, loaded, 0)
     forward(7)
 
-    def from_source(q, fresh=False):
-        def rows512(i, c):
-            part = dot(fsel[q, pl.ds(pl.multiple_of(i * SEED, SEED), SEED), :], gbuf[q])
-            for h in range(2):
-                rows = pl.ds(pl.multiple_of(h * 2 * SEED + i * SEED, SEED), SEED)
-                now = part[:, h * 128:(h + 1) * 128]
-                tot[rows, :] = now if fresh else tot[rows, :] + now
-            return c
-
-        lax.fori_loop(0, 2, rows512, 0)
-
-    from_source(y, True)
-    for b in range(1, 8, 2):
-        blk = gbuf.at[left, b * 256:(b + 1) * 256, :]
-        link(blk, blk, h_send.at[0, b], h_recv.at[0, b], right).wait_recv()
-    from_source(left)
-    for b in range(0, 8, 2):
-        blk = gbuf.at[right, b * 256:(b + 1) * 256, :]
-        link(blk, blk, h_send.at[1, b], h_recv.at[1, b], left).wait_recv()
-    from_source(right)
-    for b in range(8):
-        blk = gbuf.at[opp, b * 256:(b + 1) * 256, :]
-        link(blk, blk, h_send.at[2, b], h_recv.at[2, b], right).wait_recv()
-    from_source(opp)
+    for b in range(5, 8):
+        add_opposite(b)
 
     def wide(a):
         return jnp.concatenate([a, a], axis=1)
 
     def seeds(first):
-        return jnp.concatenate([tot[h * 2 * SEED + first:h * 2 * SEED + first + SEED, :] for h in range(2)], axis=1)
+        return jnp.concatenate([sums[h * 2 * SEED + first:h * 2 * SEED + first + SEED, :] for h in range(2)], axis=1)
 
     near2 = (seeds(0) * wide(invc[y])).astype(BF)
     self2 = seeds(SEED).astype(BF)
@@ -748,6 +755,7 @@
         in_specs=[vm, pl.BlockSpec(memory_space=pl.ANY)] + [vm] * 11,
         out_specs=vm,
         scratch_shapes=[
+            V((4 * SEED, 128), F32),
             V((SRC + 8, D_IN), F32),
             V((OWN, D_IN), BF),
             V((SRC, D_IN), BF),

time: 147 us -> 149 us (1.014)
  Pallas kernels: 145 us -> 147 us
    pallas_call x1, Pallas kernels: 139 us -> 141 us  [main(): pl.pallas_call(main_kernel, out_shape=sds((ROWS, 128), F32), in_specs=[vm...]
where the time goes in v19:
time: 149 us
  Pallas kernels  147 us (99%)
    pallas_call x1, Pallas kernels, main(): pl.pallas_call(main_kernel, out_shape=sds((ROWS, 128), F32), in_specs=[vm...  141 us
    pallas_call x1, Pallas kernels, update(): pl.pallas_call(update_kernel, out_shape=[sds((1, 1), F32), sds((64, HID),...  6.42 us

profile of v19, /device:TPU:1, one launch (start us, length us, event | category | flops | bytes accessed | tf_op | source)
XLA Modules:
  0.0 149.2 jit_solution(14824979033460120925)
XLA Ops:
  0.6 0.0 copy-start.2
  0.7 0.0 copy-start.5
  0.7 0.0 copy-start.4
  0.7 0.0 copy-start.3
  0.7 0.0 copy-start.1
  0.7 140.9 %shard_map.222.res = f32[1424,128]{1,0:T(8,128)} custom-call(s32[64,128]{1,0:T(8,128)} %bitcast.28, bf16[8192,128]{1,0:T(8,128)(2,1)} %feat.1, s32[16,2048]{1,0:T(8,128)} %bitcast.25, s32[15,2048]{1,0:T(8,128)} %bitcast.26, s32[11,512]{1,0:T(8,128)} %bitcast.29, s32[10,512]{1,0:T(8,128)} %bitcast.30, s32[1,512]{1,0:T(1,128)} %bitcast.31, s32[1,512]{1,0:T(1,128)} %bitcast.32, ...), custom_call_target="tpu_custom_call" | custom-call | tf_op jit(solution)/shard_map/pallas_call | solution.py:752
  141.6 0.0 copy-done.2
  141.6 0.0 copy-done.5
  141.6 0.0 copy-done.4
  141.6 0.0 copy-done.3
  141.6 0.0 copy-done.1
  141.6 0.0 copy-start
  141.6 1.1 copy-done
  142.7 6.4 %shard_map.223 = (f32[1,1]{1,0:T(1,128)}, f32[64,256]{1,0:T(8,128)}, f32[172,128]{1,0:T(8,128)}, f32[64,256]{1,0:T(8,128)}, f32[172,128]{1,0:T(8,128)}, /*index=...) custom-call(f32[1424,128]{1,0:T(8,128)S(1)} %copy-done, ...), custom_call_target="tpu_custom_call" | custom-call | tf_op jit(solution)/shard_map/pallas_call | solution.py:854
Async XLA Ops:
  0.6 140.9 %copy-start.2 = (f32[64,256]{1,0:T(8,128)S(1)}, f32[64,256]{1,0:T(8,128)}, u32[]{:S(2)}) copy-start(f32[64,256]{1,0:T(8,128)} %w1own.1) | copy-start | bytes 196612
  0.7 140.9 %copy-start.5 = (f32[428]{0:T(512)S(1)}, f32[428]{0:T(512)}, u32[]{:S(2)}) copy-start(f32[428]{0:T(512)} %param.29) | copy-start | bytes 5140
  0.7 140.9 %copy-start.4 = (f32[428]{0:T(512)S(1)}, f32[428]{0:T(512)}, u32[]{:S(2)}) copy-start(f32[428]{0:T(512)} %param.28) | copy-start | bytes 5140
  0.7 140.9 %copy-start.3 = (f32[428]{0:T(512)S(1)}, f32[428]{0:T(512)}, u32[]{:S(2)}) copy-start(f32[428]{0:T(512)} %param.27) | copy-start | bytes 5140
  0.7 140.9 %copy-start.1 = (f32[128,172]{0,1:T(8,128)S(1)}, f32[128,172]{0,1:T(8,128)}, u32[]{:S(2)}) copy-start(f32[128,172]{0,1:T(8,128)} %param.24) | copy-start | bytes 264196
  141.6 1.1 copy-start

commit v20 on v18

--- a/solution.py
+++ b/solution.py
@@ -90,7 +90,7 @@
 def main_kernel(
     reqt, feat, idx1t, msk1t, idx2t, msk2t, labels, live, w1, w2own, m1, m2own, bias,
     o_all,
-    table, featb, pulled, stage, reqv, reqin, mid, idxv, idxp, invv, near, own, slope, gbuf, fsel, bsel, unit_of, lows, selfs, idc, ssel, idm, invc, livec, rbuf, dbuf,
+    table, featb, pulled, stage, reqv, reqin, mid, idxv, idxp, invv, near, own, slope, gbuf, fsel, bsel, unit_of, lows, idc, ssel, idm, invc, livec, rbuf, dbuf,
     gw1, gw2t, m2pad, gidx2, w2t, b2c, pay1, pay2, misc, inbox1, inbox2, ybox1, ybox2, res2, x2s,
     reqs, idx,
     feat_sem, loc_sem, ask_sem, req_send, mid_recv, req_recv, row_send, row_recv, nar_send, nar_recv,
@@ -317,36 +317,29 @@
         invc[q] = column(1.0 / jnp.maximum(n, 1.0))
     livec[...] = column(2.0 * LAM / HID / SEEDS_ALL * live[...].astype(F32))
 
-    def backward_marks(q, carry):
+    for q in range(NAR):
         r = gidx2[q] - y * FRONT
-        lows[...] = r & 31
+        units = unit((r >> 5) & 7)
         inside = (r >= 0) & (r < FRONT)
-        units = unit((r >> 5) & 7)
         for w in range(8):
-            unit_of[w] = jnp.where(inside & ((r >> 8) == w), units, 0)
-        selfs[...] = jnp.broadcast_to(r[0:1, :], (16, SEED))
-
-        def column(c, carry2):
-            lanes = pl.ds(pl.multiple_of(c * 128, 128), 128)
-            accs = [jnp.zeros((32, 128), jnp.int32) for _ in range(8)]
-            for k in range(1, 1 + F2):
-                hit = sub32 == jnp.broadcast_to(lows[k:k + 1, lanes], (32, 128))
-                for w in range(8):
-                    u = jnp.broadcast_to(unit_of[w, k:k + 1, lanes], (32, 128))
-                    accs[w] = accs[w] + jnp.where(hit, u, 0)
-            for w in range(8):
-                for j in range(8):
-                    first = (w * 8 + j) * 32
-                    bsel[q, first:first + 32, lanes] = count(accs[w], j)
-            self_row = selfs[:, lanes].astype(jnp.int16)
-            lanes = pl.ds(pl.multiple_of(SEED + c * 128, 128), 128)
-            for t in range(FRONT // 16):
-                here = iota16 + jnp.full((16, 128), t * 16, jnp.int32).astype(jnp.int16)
-                bsel[q, t * 16:(t + 1) * 16, lanes] = jnp.where(here == self_row, one, zero)
-            return carry2
-
-        lax.fori_loop(0, SEED // 128, column, 0)
-        return carry
+            unit_of[q, w] = jnp.where(inside & ((r >> 8) == w), units, 0)
+        lows[q] = jnp.concatenate([r[0:1, :], r[1:, :] & 31], axis=0)
+
+    def backward_marks(n):
+        q, c, w = n // 32, n // 8 % 4, n % 8
+        lanes = pl.ds(pl.multiple_of(c * 128, 128), 128)
+        acc = jnp.zeros((32, 128), jnp.int32)
+        for k in range(1, 1 + F2):
+            hit = sub32 == jnp.broadcast_to(lows[q, k:k + 1, lanes], (32, 128))
+            acc = acc + jnp.where(hit, jnp.broadcast_to(unit_of[q, w, k:k + 1, lanes], (32, 128)), 0)
+        self_row = jnp.broadcast_to(lows[q, 0:1, lanes], (16, 128)).astype(jnp.int16)
+        for j in range(8):
+            bsel[q, pl.ds(pl.multiple_of(w * 256 + j * 32, 32), 32), lanes] = count(acc, j)
+        lanes = pl.ds(pl.multiple_of(SEED + c * 128, 128), 128)
+        for t in range(16):
+            here = iota16 + jnp.full((16, 128), w * 256 + t * 16, jnp.int32).astype(jnp.int16)
+            rows = pl.ds(pl.multiple_of(w * 256 + t * 16, 16), 16)
+            bsel[q, rows, lanes] = jnp.where(here == self_row, one, zero)
 
     def sum_marks(i):
         at = pl.multiple_of(i // 2 * 16, 16)
@@ -371,7 +364,6 @@
 
     sum_ids(0)
     lax.fori_loop(0, 32, one_mark, 0)
-    lax.fori_loop(0, NAR, backward_marks, 0)
 
     come = pulled.at[pl.ds(0, (DEV - 1) * CAP)]
     pltpu.make_async_copy(come, come, row_recv).wait()
@@ -403,8 +395,10 @@
             link(blk, blk, h_send.at[1, b], h_recv.at[1, b], left).wait_recv()
             link(blk, blk, h_send.at[2, b], h_recv.at[2, b], left).start()
 
-    def load_sums(b):
+    def load_sums(b, mark):
         def some(i, c):
+            backward_marks(b * 16 + i)
+            mark(i)
             found = []
             for e in range(2):
                 line = b * 32 + 2 * i + e
@@ -424,6 +418,7 @@
 
     def multiply_sums(b):
         def some(i, c):
+            backward_marks(b * 16 + i)
             found = []
             for e in range(2):
                 for r in range(8):
@@ -458,12 +453,21 @@
         def _():
             forward(b - 1)
 
-    def loaded(b, c):
-        load_sums(b)
+    multiply_sums(0)
+
+    def three(p, c):
+        sum_ids(3 * p + 3)
+
+        def loaded(h, c2):
+            load_sums(3 * p + 1 + h, lambda i: sum_marks(h * 16 + i))
+            return c2
+
+        lax.fori_loop(0, 2, loaded, 0)
+        multiply_sums(3 * p + 3)
         return c
 
-    multiply_sums(0)
-    lax.fori_loop(1, 8, loaded, 0)
+    lax.fori_loop(0, 2, three, 0)
+    load_sums(7, lambda i: None)
     forward(7)
 
     def from_source(q, fresh=False):
@@ -764,9 +768,8 @@
             V((NAR, FRONT, HID), BF),
             V((NAR, 2 * SEED, FRONT), BF),
             V((NAR, FRONT, 2 * SEED), BF),
-            V((8, 16, SEED), jnp.int32),
-            V((16, SEED), jnp.int32),
-            V((16, SEED), jnp.int32),
+            V((NAR, 8, 16, SEED), jnp.int32),
+            V((NAR, 16, SEED), jnp.int32),
             V((SEED, 32), jnp.int32),
             V((256, SRC), BF),
             V((256, 32), jnp.int32),

time: 147 us -> 162 us (1.10)
  Pallas kernels: 145 us -> 160 us
    pallas_call x1, Pallas kernels: 139 us -> 153 us  [main(): pl.pallas_call(main_kernel, out_shape=sds((ROWS, 128), F32), in_specs=[vm...]
where the time goes in v20:
time: 162 us
  Pallas kernels  160 us (99%)
    pallas_call x1, Pallas kernels, main(): pl.pallas_call(main_kernel, out_shape=sds((ROWS, 128), F32), in_specs=[vm...  153 us
    pallas_call x1, Pallas kernels, update(): pl.pallas_call(update_kernel, out_shape=[sds((1, 1), F32), sds((64, HID),...  6.42 us

profile of v20, /device:TPU:1, one launch (start us, length us, event | category | flops | bytes accessed | tf_op | source)
XLA Modules:
  0.0 161.5 jit_solution(524945786822818677)
XLA Ops:
  0.6 0.0 copy-start.2
  0.7 0.0 copy-start.5
  0.7 0.0 copy-start.4
  0.7 0.0 copy-start.3
  0.7 0.0 copy-start.1
  0.7 153.2 %shard_map.222.res = f32[1424,128]{1,0:T(8,128)} custom-call(s32[64,128]{1,0:T(8,128)} %bitcast.28, bf16[8192,128]{1,0:T(8,128)(2,1)} %feat.1, s32[16,2048]{1,0:T(8,128)} %bitcast.25, s32[15,2048]{1,0:T(8,128)} %bitcast.26, s32[11,512]{1,0:T(8,128)} %bitcast.29, s32[10,512]{1,0:T(8,128)} %bitcast.30, s32[1,512]{1,0:T(1,128)} %bitcast.31, s32[1,512]{1,0:T(1,128)} %bitcast.32, ...), custom_call_target="tpu_custom_call" | custom-call | tf_op jit(solution)/shard_map/pallas_call | solution.py:749
  153.9 0.0 copy-done.2
  154.0 0.0 copy-done.5
  154.0 0.0 copy-done.4
  154.0 0.0 copy-done.3
  154.0 0.0 copy-done.1
  154.0 0.0 copy-start
  154.0 1.1 copy-done
  155.1 6.4 %shard_map.223 = (f32[1,1]{1,0:T(1,128)}, f32[64,256]{1,0:T(8,128)}, f32[172,128]{1,0:T(8,128)}, f32[64,256]{1,0:T(8,128)}, f32[172,128]{1,0:T(8,128)}, /*index=...) custom-call(f32[1424,128]{1,0:T(8,128)S(1)} %copy-done, ...), custom_call_target="tpu_custom_call" | custom-call | tf_op jit(solution)/shard_map/pallas_call | solution.py:849
Async XLA Ops:
  0.6 153.3 %copy-start.2 = (f32[64,256]{1,0:T(8,128)S(1)}, f32[64,256]{1,0:T(8,128)}, u32[]{:S(2)}) copy-start(f32[64,256]{1,0:T(8,128)} %w1own.1) | copy-start | bytes 196612
  0.7 153.3 %copy-start.5 = (f32[428]{0:T(512)S(1)}, f32[428]{0:T(512)}, u32[]{:S(2)}) copy-start(f32[428]{0:T(512)} %param.29) | copy-start | bytes 5140
  0.7 153.3 %copy-start.4 = (f32[428]{0:T(512)S(1)}, f32[428]{0:T(512)}, u32[]{:S(2)}) copy-start(f32[428]{0:T(512)} %param.28) | copy-start | bytes 5140
  0.7 153.3 %copy-start.3 = (f32[428]{0:T(512)S(1)}, f32[428]{0:T(512)}, u32[]{:S(2)}) copy-start(f32[428]{0:T(512)} %param.27) | copy-start | bytes 5140
  0.7 153.3 %copy-start.1 = (f32[128,172]{0,1:T(8,128)S(1)}, f32[128,172]{0,1:T(8,128)}, u32[]{:S(2)}) copy-start(f32[128,172]{0,1:T(8,128)} %param.24) | copy-start | bytes 264196
  154.0 1.1 copy-start

commit v21 on v18

--- a/solution.py
+++ b/solution.py
@@ -43,14 +43,12 @@
     return (t // NAR, t % NAR)
 
 
-PIECE = 32
-P1 = 17
-Q2 = 192
-P2 = 24
 GRP = 32
-ROW_M2 = P1 * PIECE
-ROW_X2 = ROW_M2 + CLS_PAD
-ROWS = ROW_X2 + NAR * CLS_PAD
+PIECE = 48
+PIECES = 26
+ROW_2 = 512
+ROW_MISC = ROW_2 + NAR * CLS_PAD
+ROWS = PIECES * PIECE
 SEEDS_ALL = SEED * DEV
 
 
@@ -91,7 +89,7 @@
     reqt, feat, idx1t, msk1t, idx2t, msk2t, labels, live, w1, w2own, m1, m2own, bias,
     o_all,
     table, featb, pulled, stage, reqv, reqin, mid, idxv, idxp, invv, near, own, slope, gbuf, fsel, bsel, unit_of, lows, selfs, idc, ssel, idm, invc, livec, rbuf, dbuf,
-    gw1, gw2t, m2pad, gidx2, w2t, b2c, pay1, pay2, misc, inbox1, inbox2, ybox1, ybox2, res2, x2s,
+    gw1, gw2t, momenta, gidx2, w2t, b2c, pay, misc, inbox, ybox,
     reqs, idx,
     feat_sem, loc_sem, ask_sem, req_send, mid_recv, req_recv, row_send, row_recv, nar_send, nar_recv,
     h_send, h_recv, r_send, r_recv, d_send, d_recv, rs_send, rs_recv, y_send, y_recv, ag_send, ag_recv,
@@ -129,7 +127,12 @@
     gw1[y] = w1[...].astype(BF)
     pad = CLS_PAD - CLS
     gw2t[y] = jnp.concatenate([w2own[...], jnp.zeros((pad, 128), F32)], axis=0).astype(BF)
-    m2pad[...] = jnp.concatenate([m2own[...], jnp.zeros((Q2 - CLS, 128), F32)], axis=0)
+    momenta[...] = jnp.zeros((ROWS, 128), F32)
+    for h in range(2):
+        momenta[pl.ds(pl.multiple_of(h * 256 + y * 64, 64), 64), :] = MU * m1[:, h * 128:(h + 1) * 128]
+    momenta[pl.ds(pl.multiple_of(ROW_2 + y * CLS_PAD, 16), CLS_PAD), :] = jnp.concatenate(
+        [MU * m2own[...], jnp.zeros((pad, 128), F32)], axis=0
+    )
     gidx2[y] = jnp.concatenate(
         [idx2t[0:1, :], jnp.where(msk2t[...] > 0, idx2t[1:, :], -1), jnp.zeros((5, SEED), jnp.int32)], axis=0
     )
@@ -554,95 +557,7 @@
     loss = loss + SEEDS_ALL / 2 * jnp.sum(pull_apart * diff, keepdims=True)
     g2t = dot(dlog, act2).astype(BF)
     for q in range(NAR):
-        pay2[q * Q2:q * Q2 + CLS_PAD, :] = g2t[:, q * 128:(q + 1) * 128]
-        pay2[q * Q2 + CLS_PAD:(q + 1) * Q2, :] = jnp.zeros((Q2 - CLS_PAD, 128), BF)
-
-    def to_owner(pay, inbox, first, count, n):
-        def body(i, c):
-            t = (g + i) % GRP
-            p = t - first
-
-            @pl.when((p >= 0) & (p < count))
-            def _():
-                pltpu.make_async_remote_copy(
-                    src_ref=pay.at[pl.ds(pl.multiple_of(p * PIECE, PIECE), PIECE)], dst_ref=inbox.at[g],
-                    send_sem=rs_send.at[n], recv_sem=rs_recv.at[n], device_id=(t, y), device_id_type=MESH,
-                ).start()
-
-            return c
-
-        lax.fori_loop(1, GRP, body, 0)
-
-    def mine(first, count):
-        p = g - first
-        return (p >= 0) & (p < count), pl.ds(pl.multiple_of(p * PIECE, PIECE), PIECE)
-
-    def add_first_momentum(p):
-        rows = pl.ds(pl.multiple_of(p % 2 * PIECE, PIECE), PIECE)
-        for h in range(2):
-            @pl.when((y == p % 8 // 2) & (p // 8 == h))
-            def _(h=h):
-                ybox1[y] = ybox1[y] + MU * m1[rows, h * 128:(h + 1) * 128]
-
-    def add_second_momentum(p):
-        @pl.when(y == p // (Q2 // PIECE))
-        def _():
-            rows = pl.ds(pl.multiple_of(p % (Q2 // PIECE) * PIECE, PIECE), PIECE)
-            ybox2[y] = ybox2[y] + MU * m2pad[rows, :]
-
-    def add_plane(pay, inbox, ybox, first, count, n, add_momentum):
-        here, rows = mine(first, count)
-
-        @pl.when(here)
-        def _():
-            got = inbox.at[pl.ds(0, GRP - 1)]
-            pltpu.make_async_copy(got, got, rs_recv.at[n]).wait()
-            inbox[g] = pay[rows, :]
-            ybox[y] = jnp.sum(inbox[...].astype(F32), axis=0)
-            add_momentum(g - first)
-            for d in range(1, NAR):
-                link(ybox.at[y], ybox.at[y], y_send.at[n, d - 1], y_recv.at[n, d - 1], ys[d]).start()
-
-    def add_group(ybox, res, first, count, n):
-        here, rows = mine(first, count)
-
-        @pl.when(here)
-        def _():
-            for d in range(1, NAR):
-                link(ybox.at[y], ybox.at[y], y_send.at[n, d - 1], y_recv.at[n, d - 1], ys[d]).wait()
-            res[rows, :] = (ybox[0] + ybox[1]) + (ybox[2] + ybox[3])
-
-            def tell(i, c):
-                pltpu.make_async_remote_copy(
-                    src_ref=res.at[rows], dst_ref=res.at[rows], send_sem=ag_send.at[n], recv_sem=ag_recv.at[n],
-                    device_id=((g + i) % GRP, y), device_id_type=MESH,
-                ).start()
-                return c
-
-            lax.fori_loop(1, GRP, tell, 0)
-
-    def take(res, first, count, n):
-        here, rows = mine(first, count)
-        for less, when in ((1, here), (0, jnp.logical_not(here))):
-            @pl.when(when)
-            def _(less=less):
-                got = res.at[pl.ds(0, (count - less) * PIECE)]
-                pltpu.make_async_copy(got, got, ag_recv.at[n]).wait()
-
-    def sums_sent(pay, first, count, n):
-        here, rows = mine(first, count)
-        for less, when in ((1, here), (0, jnp.logical_not(here))):
-            @pl.when(when)
-            def _(less=less):
-                gone = pay.at[pl.ds(0, (count - less) * PIECE)]
-                pltpu.make_async_copy(gone, gone, rs_send.at[n]).wait()
-
-        @pl.when(here)
-        def _():
-            gone = table.at[pl.ds(0, (GRP - 1) * PIECE)]
-            pltpu.make_async_copy(gone, gone, ag_send.at[n]).wait()
-
-    to_owner(pay2, inbox2, GRP - P2, P2, 1)
+        pay[ROW_2 + q * CLS_PAD:ROW_2 + (q + 1) * CLS_PAD, :] = g2t[:, q * 128:(q + 1) * 128]
 
     def add_grads(q, fresh=False):
         da = dot(dbuf[q], w2t[...], TN)
@@ -668,10 +583,8 @@
     swap_forward(dbuf, d_send, d_recv, 96)
     add_grads(left)
     add_grads(right)
-    add_plane(pay2, inbox2, ybox2, GRP - P2, P2, 1, add_second_momentum)
     swap_end(rbuf, r_send, r_recv, SEED // 2)
     swap_end(dbuf, d_send, d_recv, 96)
-    add_group(ybox2, res2, GRP - P2, P2, 1)
     add_grads(opp)
 
     def to_z(b, db):
@@ -691,8 +604,8 @@
 
     gsum[...] = jnp.zeros((512, 128), F32)
     db1 = lax.fori_loop(0, FRONT // 256, to_z, jnp.zeros((1, HID), F32))
-    pay1[0:512, :] = gsum[...].astype(BF)
-    misc[...] = jnp.zeros((PIECE, 128), F32)
+    pay[0:512, :] = gsum[...].astype(BF)
+    misc[...] = jnp.zeros((32, 128), F32)
 
     def two(rows, v):
         hi = v.astype(BF).astype(F32)
@@ -706,23 +619,54 @@
     hi = loss.astype(BF).astype(F32)
     misc[8:9, 0:1] = hi
     misc[9:10, 0:1] = loss - hi
-    pay1[512:544, :] = misc[...].astype(BF)
-    to_owner(pay1, inbox1, 0, P1, 0)
-
-    take(res2, GRP - P2, P2, 1)
-    mom2 = jnp.concatenate([res2[q * Q2:q * Q2 + CLS_PAD, :] for q in range(NAR)], axis=1)
-    for q in range(NAR):
-        x2s[q] = mom2[:, q * 128:(q + 1) * 128]
-    o_all[ROW_M2:ROW_M2 + CLS_PAD, :] = x2s[y]
-    x2 = mom2 * (1.0 / (jnp.sqrt(jnp.sum(mom2 * mom2, keepdims=True)) + 1e-07))
-    x2 = ns_step(x2)
-    add_plane(pay1, inbox1, ybox1, 0, P1, 0, add_first_momentum)
-    x2 = ns_step(x2)
-    add_group(ybox1, o_all, 0, P1, 0)
-    x2 = ns_step(x2)
-    for q in range(NAR):
-        o_all[ROW_X2 + q * CLS_PAD:ROW_X2 + (q + 1) * CLS_PAD, :] = x2[:, q * 128:(q + 1) * 128]
-    take(o_all, 0, P1, 0)
+    pay[ROW_MISC:ROWS, :] = misc[...].astype(BF)
+
+    def to_owner(i, c):
+        t = (g + i) % GRP
+
+        @pl.when(t < PIECES)
+        def _():
+            pltpu.make_async_remote_copy(
+                src_ref=pay.at[pl.ds(pl.multiple_of(t * PIECE, 16), PIECE)], dst_ref=inbox.at[g],
+                send_sem=rs_send, recv_sem=rs_recv, device_id=(t, y), device_id_type=MESH,
+            ).start()
+
+        return c
+
+    lax.fori_loop(1, GRP, to_owner, 0)
+    mine = pl.ds(pl.multiple_of(g * PIECE, 16), PIECE)
+
+    @pl.when(g < PIECES)
+    def _():
+        got = inbox.at[pl.ds(0, GRP - 1)]
+        pltpu.make_async_copy(got, got, rs_recv).wait()
+        inbox[g] = pay[mine, :]
+        ybox[y] = jnp.sum(inbox[...].astype(F32), axis=0) + momenta[mine, :]
+        for d in range(1, NAR):
+            link(ybox.at[y], ybox.at[y], y_send.at[d - 1], y_recv.at[d - 1], ys[d]).start()
+        for d in range(1, NAR):
+            link(ybox.at[y], ybox.at[y], y_send.at[d - 1], y_recv.at[d - 1], ys[d]).wait()
+        o_all[mine, :] = (ybox[0] + ybox[1]) + (ybox[2] + ybox[3])
+
+        def tell(i, c):
+            pltpu.make_async_remote_copy(
+                src_ref=o_all.at[mine], dst_ref=o_all.at[mine], send_sem=ag_send, recv_sem=ag_recv,
+                device_id=((g + i) % GRP, y), device_id_type=MESH,
+            ).start()
+            return c
+
+        lax.fori_loop(1, GRP, tell, 0)
+        got = o_all.at[pl.ds(0, (PIECES - 1) * PIECE)]
+        pltpu.make_async_copy(got, got, ag_recv).wait()
+        gone = pay.at[pl.ds(0, (PIECES - 1) * PIECE)]
+        pltpu.make_async_copy(gone, gone, rs_send).wait()
+        gone = table.at[pl.ds(0, (GRP - 1) * PIECE)]
+        pltpu.make_async_copy(gone, gone, ag_send).wait()
+
+    @pl.when(g >= PIECES)
+    def _():
+        pltpu.make_async_copy(o_all, o_all, ag_recv).wait()
+        pltpu.make_async_copy(pay, pay, rs_send).wait()
 
     for b in range(8):
         blk = gbuf.at[y, b * 256:(b + 1) * 256, :]
@@ -732,9 +676,6 @@
         link(blk, blk, h_send.at[2, b], h_recv.at[2, b], right).wait_send()
     swap_sent(rbuf, r_send, r_recv, SEED // 2)
     swap_sent(dbuf, d_send, d_recv, 96)
-
-    sums_sent(pay2, GRP - P2, P2, 1)
-    sums_sent(pay1, 0, P1, 0)
 
 
 def main(reqt, feat, idx1t, msk1t, idx2t, msk2t, labels, live, w1, w2own, m1, m2own, bias):
@@ -776,24 +717,19 @@
             V((NAR, CLS_PAD, SEED), BF),
             V((NAR, 64, HID), BF),
             V((NAR, CLS_PAD, 128), BF),
-            V((Q2, 128), F32),
+            V((ROWS, 128), F32),
             V((NAR, 16, SEED), jnp.int32),
             V((CLS_PAD, 2 * HID), BF),
             V((HID, 128), F32),
-            V((P1 * PIECE, 128), BF),
-            V((P2 * PIECE, 128), BF),
-            V((PIECE, 128), F32),
-            V((GRP, PIECE, 128), BF),
+            V((ROWS, 128), BF),
+            V((32, 128), F32),
             V((GRP, PIECE, 128), BF),
             V((NAR, PIECE, 128), F32),
-            V((NAR, PIECE, 128), F32),
-            V((P2 * PIECE, 128), F32),
-            V((NAR, CLS_PAD, 128), F32),
             pltpu.SMEM((DEV, 1, 128), jnp.int32),
             pltpu.SMEM((256, 128), jnp.int32),
             dma, dma((3,)), dma((GRP,)), dma((NAR,)), dma((NAR,)), dma((GRP,)), dma, dma, dma((3, 3)), dma((3, 3)),
             dma((3, 8)), dma((3, 8)), dma((4,)), dma((4,)), dma((4,)), dma((4,)),
-            dma((2,)), dma((2,)), dma((2, 3)), dma((2, 3)), dma((2,)), dma((2,)),
+            dma, dma, dma((3,)), dma((3,)), dma, dma,
         ],
         compiler_params=pltpu.CompilerParams(
             collective_id=0, has_side_effects=True, vmem_limit_bytes=62 * 2**20
@@ -812,11 +748,11 @@
     block64 = pl.ds(pl.multiple_of(y * 64, 64), 64)
     o_mom1[...] = x1s[block64, :]
     x1 = mom1 * (1.0 / (jnp.sqrt(jnp.sum(mom1 * mom1, keepdims=True)) + 1e-07))
-    x2 = jnp.concatenate([res[ROW_X2 + q * CLS_PAD:ROW_X2 + (q + 1) * CLS_PAD, :] for q in range(NAR)], axis=1)
+    mom2 = jnp.concatenate([res[ROW_2 + q * CLS_PAD:ROW_2 + (q + 1) * CLS_PAD, :] for q in range(NAR)], axis=1)
+    x2 = mom2 * (1.0 / (jnp.sqrt(jnp.sum(mom2 * mom2, keepdims=True)) + 1e-07))
     for i in range(NS_ITERS):
         x1 = ns_step(x1)
-        if i < 2:
-            x2 = ns_step(x2)
+        x2 = ns_step(x2)
     x1s[...] = x1
     for q in range(NAR):
         x2s[q] = x2[:, q * 128:(q + 1) * 128]
@@ -826,9 +762,9 @@
     second = w2own[...] * (1.0 - WDECAY) - (2 * HID / CLS) ** 0.5 * x2s[y][0:CLS, :]
     o_second[...] = second
     o_slow[...] = second.astype(BF)
-    o_mom2[...] = res[ROW_M2:ROW_M2 + CLS, :]
-
-    gb = res[512:516, :] + res[516:520, :]
+    o_mom2[...] = res[pl.ds(pl.multiple_of(ROW_2 + y * CLS_PAD, 16), CLS_PAD), :][0:CLS, :]
+
+    gb = res[ROW_MISC + 0:ROW_MISC + 4, :] + res[ROW_MISC + 4:ROW_MISC + 8, :]
     gb = jnp.concatenate([gb[0:1, :], gb[1:2, :], gb[2:3, :], gb[3:4, 0:44]], axis=1)
     m_new = BETA_ONE * biasm[...] + (1.0 - BETA_ONE) * gb
     v_new = BETA_TWO * biasv[...] + (1.0 - BETA_TWO) * gb * gb
@@ -837,7 +773,7 @@
     o_bias[...] = bias[...] * (1.0 - LR_BIAS * WDECAY) - LR_BIAS * m_hat / (jnp.sqrt(v_hat) + EPSILON)
     o_bm[...] = m_new
     o_bv[...] = v_new
-    o_loss[...] = res[520:521, 0:1] + res[521:522, 0:1]
+    o_loss[...] = res[ROW_MISC + 8:ROW_MISC + 9, 0:1] + res[ROW_MISC + 9:ROW_MISC + 10, 0:1]
 
 
 def update(*args):

time: 147 us -> 147 us (level)
    pallas_call x1, Pallas kernels: 6.42 us -> 8.06 us  [update(): pl.pallas_call(update_kernel, out_shape=[sds((1, 1), F32), sds((64, HID),...]
where the time goes in v21:
time: 147 us
  Pallas kernels  145 us (99%)
    pallas_call x1, Pallas kernels, main(): pl.pallas_call(main_kernel, out_shape=sds((ROWS, 128), F32), in_specs=[vm...  137 us
    pallas_call x1, Pallas kernels, update(): pl.pallas_call(update_kernel, out_shape=[sds((1, 1), F32), sds((64, HID),...  8.06 us

profile of v21, /device:TPU:1, one launch (start us, length us, event | category | flops | bytes accessed | tf_op | source)
XLA Modules:
  0.0 147.2 jit_solution(5096782696288302239)
XLA Ops:
  0.6 0.0 copy-start.2
  0.7 0.0 copy-start.5
  0.7 0.0 copy-start.4
  0.7 0.0 copy-start.3
  0.7 0.0 copy-start.1
  0.7 137.3 %shard_map.222.res = f32[1248,128]{1,0:T(8,128)} custom-call(s32[64,128]{1,0:T(8,128)} %bitcast.28, bf16[8192,128]{1,0:T(8,128)(2,1)} %feat.1, s32[16,2048]{1,0:T(8,128)} %bitcast.25, s32[15,2048]{1,0:T(8,128)} %bitcast.26, s32[11,512]{1,0:T(8,128)} %bitcast.29, s32[10,512]{1,0:T(8,128)} %bitcast.30, s32[1,512]{1,0:T(1,128)} %bitcast.31, s32[1,512]{1,0:T(1,128)} %bitcast.32, ...), custom_call_target="tpu_custom_call" | custom-call | tf_op jit(solution)/shard_map/pallas_call | solution.py:686
  138.0 0.0 copy-done.2
  138.1 0.0 copy-done.5
  138.1 0.0 copy-done.4
  138.1 0.0 copy-done.3
  138.1 0.0 copy-done.1
  138.1 0.0 copy-start
  138.1 1.1 copy-done
  139.2 8.1 %shard_map.223 = (f32[1,1]{1,0:T(1,128)}, f32[64,256]{1,0:T(8,128)}, f32[172,128]{1,0:T(8,128)}, f32[64,256]{1,0:T(8,128)}, f32[172,128]{1,0:T(8,128)}, /*index=...) custom-call(f32[1248,128]{1,0:T(8,128)S(1)} %copy-done, ...), custom_call_target="tpu_custom_call" | custom-call | tf_op jit(solution)/shard_map/pallas_call | solution.py:782
Async XLA Ops:
  0.6 137.4 %copy-start.2 = (f32[64,256]{1,0:T(8,128)S(1)}, f32[64,256]{1,0:T(8,128)}, u32[]{:S(2)}) copy-start(f32[64,256]{1,0:T(8,128)} %w1own.1) | copy-start | bytes 196612
  0.7 137.4 %copy-start.5 = (f32[428]{0:T(512)S(1)}, f32[428]{0:T(512)}, u32[]{:S(2)}) copy-start(f32[428]{0:T(512)} %param.29) | copy-start | bytes 5140
  0.7 137.4 %copy-start.4 = (f32[428]{0:T(512)S(1)}, f32[428]{0:T(512)}, u32[]{:S(2)}) copy-start(f32[428]{0:T(512)} %param.28) | copy-start | bytes 5140
  0.7 137.4 %copy-start.3 = (f32[428]{0:T(512)S(1)}, f32[428]{0:T(512)}, u32[]{:S(2)}) copy-start(f32[428]{0:T(512)} %param.27) | copy-start | bytes 5140
  0.7 137.4 %copy-start.1 = (f32[128,172]{0,1:T(8,128)S(1)}, f32[128,172]{0,1:T(8,128)}, u32[]{:S(2)}) copy-start(f32[128,172]{0,1:T(8,128)} %param.24) | copy-start | bytes 264196
  138.1 1.1 copy-start

commit v22 on v21

--- a/solution.py
+++ b/solution.py
@@ -88,7 +88,7 @@
 def main_kernel(
     reqt, feat, idx1t, msk1t, idx2t, msk2t, labels, live, w1, w2own, m1, m2own, bias,
     o_all,
-    table, featb, pulled, stage, reqv, reqin, mid, idxv, idxp, invv, near, own, slope, gbuf, fsel, bsel, unit_of, lows, selfs, idc, ssel, idm, invc, livec, rbuf, dbuf,
+    table, featb, pulled, stage, reqv, reqin, mid, idxv, idxp, invv, near, own, slope, gbuf, fsel, bsel, wants, idc, ssel, idm, invc, livec, rbuf, dbuf,
     gw1, gw2t, momenta, gidx2, w2t, b2c, pay, misc, inbox, ybox,
     reqs, idx,
     feat_sem, loc_sem, ask_sem, req_send, mid_recv, req_recv, row_send, row_recv, nar_send, nar_recv,
@@ -197,7 +197,6 @@
     lax.fori_loop(0, OWN // 256, widen_features, 0)
 
     lane32 = lax.broadcasted_iota(jnp.int32, (16, 128), 1)
-    sub32 = lax.broadcasted_iota(jnp.int32, (32, 128), 0)
     lane16 = lane32.astype(jnp.int16)
     iota16 = lax.broadcasted_iota(jnp.int32, (16, 128), 0).astype(jnp.int16)
     one, zero = jnp.ones((16, 128), BF), jnp.zeros((16, 128), BF)
@@ -320,36 +319,27 @@
         invc[q] = column(1.0 / jnp.maximum(n, 1.0))
     livec[...] = column(2.0 * LAM / HID / SEEDS_ALL * live[...].astype(F32))
 
-    def backward_marks(q, carry):
-        r = gidx2[q] - y * FRONT
-        lows[...] = r & 31
-        inside = (r >= 0) & (r < FRONT)
-        units = unit((r >> 5) & 7)
-        for w in range(8):
-            unit_of[w] = jnp.where(inside & ((r >> 8) == w), units, 0)
-        selfs[...] = jnp.broadcast_to(r[0:1, :], (16, SEED))
-
-        def column(c, carry2):
-            lanes = pl.ds(pl.multiple_of(c * 128, 128), 128)
-            accs = [jnp.zeros((32, 128), jnp.int32) for _ in range(8)]
-            for k in range(1, 1 + F2):
-                hit = sub32 == jnp.broadcast_to(lows[k:k + 1, lanes], (32, 128))
-                for w in range(8):
-                    u = jnp.broadcast_to(unit_of[w, k:k + 1, lanes], (32, 128))
-                    accs[w] = accs[w] + jnp.where(hit, u, 0)
-            for w in range(8):
-                for j in range(8):
-                    first = (w * 8 + j) * 32
-                    bsel[q, first:first + 32, lanes] = count(accs[w], j)
-            self_row = selfs[:, lanes].astype(jnp.int16)
-            lanes = pl.ds(pl.multiple_of(SEED + c * 128, 128), 128)
-            for t in range(FRONT // 16):
-                here = iota16 + jnp.full((16, 128), t * 16, jnp.int32).astype(jnp.int16)
-                bsel[q, t * 16:(t + 1) * 16, lanes] = jnp.where(here == self_row, one, zero)
-            return carry2
-
-        lax.fori_loop(0, SEED // 128, column, 0)
-        return carry
+    for q in range(NAR):
+        ids = gidx2[q] - y * FRONT
+        for c in range(SEED // 128):
+            for k in range(1 + F2):
+                row = ids[k:k + 1, c * 128:(c + 1) * 128]
+                wants[q, c, k] = jnp.broadcast_to(row, (16, 128)).astype(jnp.int16)
+
+    def backward_marks(i):
+        here = iota16 + jnp.full((16, 128), i * 16, jnp.int32).astype(jnp.int16)
+        out = pl.ds(pl.multiple_of(i * 16, 16), 16)
+        for q in range(NAR):
+            for c in range(SEED // 128):
+                acc = jnp.where(here == wants[q, c, 1], one, zero)
+                for k in range(2, 1 + F2):
+                    acc = acc + jnp.where(here == wants[q, c, k], one, zero)
+                bsel[q, out, c * 128:(c + 1) * 128] = acc
+                bsel[q, out, SEED + c * 128:SEED + (c + 1) * 128] = jnp.where(here == wants[q, c, 0], one, zero)
+
+    def some_marks(i, c):
+        backward_marks(i)
+        return c
 
     def sum_marks(i):
         at = pl.multiple_of(i // 2 * 16, 16)
@@ -374,7 +364,7 @@
 
     sum_ids(0)
     lax.fori_loop(0, 32, one_mark, 0)
-    lax.fori_loop(0, NAR, backward_marks, 0)
+    lax.fori_loop(0, 16, some_marks, 0)
 
     come = pulled.at[pl.ds(0, (DEV - 1) * CAP)]
     pltpu.make_async_copy(come, come, row_recv).wait()
@@ -408,6 +398,7 @@
 
     def load_sums(b):
         def some(i, c):
+            backward_marks(b * 16 + i)
             found = []
             for e in range(2):
                 line = b * 32 + 2 * i + e
@@ -705,9 +696,7 @@
             V((NAR, FRONT, HID), BF),
             V((NAR, 2 * SEED, FRONT), BF),
             V((NAR, FRONT, 2 * SEED), BF),
-            V((8, 16, SEED), jnp.int32),
-            V((16, SEED), jnp.int32),
-            V((16, SEED), jnp.int32),
+            V((NAR, 4, 1 + F2, 16, 128), jnp.int16),
             V((SEED, 32), jnp.int32),
             V((256, SRC), BF),
             V((256, 32), jnp.int32),

time: 147 us -> 147 us (level)
  no operation moved by 1% of the time
where the time goes in v22:
time: 147 us
  Pallas kernels  145 us (99%)
    pallas_call x1, Pallas kernels, main(): pl.pallas_call(main_kernel, out_shape=sds((ROWS, 128), F32), in_specs=[vm...  137 us
    pallas_call x1, Pallas kernels, update(): pl.pallas_call(update_kernel, out_shape=[sds((1, 1), F32), sds((64, HID),...  8.06 us

profile of v22, /device:TPU:1, one launch (start us, length us, event | category | flops | bytes accessed | tf_op | source)
XLA Modules:
  0.0 146.8 jit_solution(13505299859111891883)
XLA Ops:
  0.6 0.0 copy-start.2
  0.7 0.0 copy-start.5
  0.7 0.0 copy-start.4
  0.7 0.0 copy-start.3
  0.7 0.0 copy-start.1
  0.7 136.9 %shard_map.222.res = f32[1248,128]{1,0:T(8,128)} custom-call(s32[64,128]{1,0:T(8,128)} %bitcast.28, bf16[8192,128]{1,0:T(8,128)(2,1)} %feat.1, s32[16,2048]{1,0:T(8,128)} %bitcast.25, s32[15,2048]{1,0:T(8,128)} %bitcast.26, s32[11,512]{1,0:T(8,128)} %bitcast.29, s32[10,512]{1,0:T(8,128)} %bitcast.30, s32[1,512]{1,0:T(1,128)} %bitcast.31, s32[1,512]{1,0:T(1,128)} %bitcast.32, ...), custom_call_target="tpu_custom_call" | custom-call | tf_op jit(solution)/shard_map/pallas_call | solution.py:677
  137.6 0.0 copy-done.2
  137.6 0.0 copy-done.5
  137.6 0.0 copy-done.4
  137.6 0.0 copy-done.3
  137.6 0.0 copy-done.1
  137.6 0.0 copy-start
  137.6 1.1 copy-done
  138.7 8.1 %shard_map.223 = (f32[1,1]{1,0:T(1,128)}, f32[64,256]{1,0:T(8,128)}, f32[172,128]{1,0:T(8,128)}, f32[64,256]{1,0:T(8,128)}, f32[172,128]{1,0:T(8,128)}, /*index=...) custom-call(f32[1248,128]{1,0:T(8,128)S(1)} %copy-done, ...), custom_call_target="tpu_custom_call" | custom-call | tf_op jit(solution)/shard_map/pallas_call | solution.py:771
Async XLA Ops:
  0.6 136.9 %copy-start.2 = (f32[64,256]{1,0:T(8,128)S(1)}, f32[64,256]{1,0:T(8,128)}, u32[]{:S(2)}) copy-start(f32[64,256]{1,0:T(8,128)} %w1own.1) | copy-start | bytes 196612
  0.7 136.9 %copy-start.5 = (f32[428]{0:T(512)S(1)}, f32[428]{0:T(512)}, u32[]{:S(2)}) copy-start(f32[428]{0:T(512)} %param.29) | copy-start | bytes 5140
  0.7 136.9 %copy-start.4 = (f32[428]{0:T(512)S(1)}, f32[428]{0:T(512)}, u32[]{:S(2)}) copy-start(f32[428]{0:T(512)} %param.28) | copy-start | bytes 5140
  0.7 136.9 %copy-start.3 = (f32[428]{0:T(512)S(1)}, f32[428]{0:T(512)}, u32[]{:S(2)}) copy-start(f32[428]{0:T(512)} %param.27) | copy-start | bytes 5140
  0.7 136.9 %copy-start.1 = (f32[128,172]{0,1:T(8,128)S(1)}, f32[128,172]{0,1:T(8,128)}, u32[]{:S(2)}) copy-start(f32[128,172]{0,1:T(8,128)} %param.24) | copy-start | bytes 264196
  137.6 1.1 copy-start

commit v23 on v22

--- a/solution.py
+++ b/solution.py
@@ -92,7 +92,7 @@
     gw1, gw2t, momenta, gidx2, w2t, b2c, pay, misc, inbox, ybox,
     reqs, idx,
     feat_sem, loc_sem, ask_sem, req_send, mid_recv, req_recv, row_send, row_recv, nar_send, nar_recv,
-    h_send, h_recv, r_send, r_recv, d_send, d_recv, rs_send, rs_recv, y_send, y_recv, ag_send, ag_recv,
+    h_send, h_recv, r_send, r_recv, d_send, d_recv, rs_send, rs_recv, y_send, y_recv, ag_send, ag_recv, pair_send, pair_recv,
 ):
     a1t, dh1, tot, gsum = featb, table, table.at[2 * FRONT:3 * FRONT], table.at[3 * FRONT:3 * FRONT + 512]
     g = lax.axis_index("grp")
@@ -642,21 +642,35 @@
         def tell(i, c):
             pltpu.make_async_remote_copy(
                 src_ref=o_all.at[mine], dst_ref=o_all.at[mine], send_sem=ag_send, recv_sem=ag_recv,
-                device_id=((g + i) % GRP, y), device_id_type=MESH,
+                device_id=((g + 2 * i) % GRP, y), device_id_type=MESH,
             ).start()
             return c
 
-        lax.fori_loop(1, GRP, tell, 0)
-        got = o_all.at[pl.ds(0, (PIECES - 1) * PIECE)]
+        lax.fori_loop(1, GRP // 2, tell, 0)
+        got = o_all.at[pl.ds(0, (PIECES // 2 - 1) * PIECE)]
         pltpu.make_async_copy(got, got, ag_recv).wait()
+
+    @pl.when(g >= PIECES)
+    def _():
+        got = o_all.at[pl.ds(0, PIECES // 2 * PIECE)]
+        pltpu.make_async_copy(got, got, ag_recv).wait()
+
+    pairs = o_all.reshape(PIECES // 2, 2, PIECE, 128)
+    half = pltpu.make_async_remote_copy(
+        src_ref=pairs.at[:, g % 2], dst_ref=pairs.at[:, g % 2], send_sem=pair_send, recv_sem=pair_recv,
+        device_id=(g + 1 - 2 * (g % 2), y), device_id_type=MESH,
+    )
+    half.start()
+
+    @pl.when(g < PIECES)
+    def _():
         gone = pay.at[pl.ds(0, (PIECES - 1) * PIECE)]
         pltpu.make_async_copy(gone, gone, rs_send).wait()
-        gone = table.at[pl.ds(0, (GRP - 1) * PIECE)]
+        gone = table.at[pl.ds(0, (GRP // 2 - 1) * PIECE)]
         pltpu.make_async_copy(gone, gone, ag_send).wait()
 
     @pl.when(g >= PIECES)
     def _():
-        pltpu.make_async_copy(o_all, o_all, ag_recv).wait()
         pltpu.make_async_copy(pay, pay, rs_send).wait()
 
     for b in range(8):
@@ -667,6 +681,7 @@
         link(blk, blk, h_send.at[2, b], h_recv.at[2, b], right).wait_send()
     swap_sent(rbuf, r_send, r_recv, SEED // 2)
     swap_sent(dbuf, d_send, d_recv, 96)
+    half.wait()
 
 
 def main(reqt, feat, idx1t, msk1t, idx2t, msk2t, labels, live, w1, w2own, m1, m2own, bias):
@@ -718,7 +733,7 @@
             pltpu.SMEM((256, 128), jnp.int32),
             dma, dma((3,)), dma((GRP,)), dma((NAR,)), dma((NAR,)), dma((GRP,)), dma, dma, dma((3, 3)), dma((3, 3)),
             dma((3, 8)), dma((3, 8)), dma((4,)), dma((4,)), dma((4,)), dma((4,)),
-            dma, dma, dma((3,)), dma((3,)), dma, dma,
+            dma, dma, dma((3,)), dma((3,)), dma, dma, dma, dma,
         ],
         compiler_params=pltpu.CompilerParams(
             collective_id=0, has_side_effects=True, vmem_limit_bytes=62 * 2**20

time: 147 us -> 144 us (0.980)
  Pallas kernels: 145 us -> 142 us
    pallas_call x1, Pallas kernels: 137 us -> 134 us  [main(): pl.pallas_call(main_kernel, out_shape=sds((ROWS, 128), F32), in_specs=[vm...]
where the time goes in v23:
time: 144 us
  Pallas kernels  142 us (99%)
    pallas_call x1, Pallas kernels, main(): pl.pallas_call(main_kernel, out_shape=sds((ROWS, 128), F32), in_specs=[vm...  134 us
    pallas_call x1, Pallas kernels, update(): pl.pallas_call(update_kernel, out_shape=[sds((1, 1), F32), sds((64, HID),...  8.06 us

profile of v23, /device:TPU:1, one launch (start us, length us, event | category | flops | bytes accessed | tf_op | source)
XLA Modules:
  0.0 144.2 jit_solution(1076949243275487369)
XLA Ops:
  0.6 0.0 copy-start.2
  0.7 0.0 copy-start.5
  0.7 0.0 copy-start.4
  0.7 0.0 copy-start.3
  0.7 0.0 copy-start.1
  0.7 134.3 %shard_map.222.res = f32[1248,128]{1,0:T(8,128)} custom-call(s32[64,128]{1,0:T(8,128)} %bitcast.28, bf16[8192,128]{1,0:T(8,128)(2,1)} %feat.1, s32[16,2048]{1,0:T(8,128)} %bitcast.25, s32[15,2048]{1,0:T(8,128)} %bitcast.26, s32[11,512]{1,0:T(8,128)} %bitcast.29, s32[10,512]{1,0:T(8,128)} %bitcast.30, s32[1,512]{1,0:T(1,128)} %bitcast.31, s32[1,512]{1,0:T(1,128)} %bitcast.32, ...), custom_call_target="tpu_custom_call" | custom-call | tf_op jit(solution)/shard_map/pallas_call | solution.py:692
  135.1 0.0 copy-done.2
  135.1 0.0 copy-done.5
  135.1 0.0 copy-done.4
  135.1 0.0 copy-done.3
  135.1 0.0 copy-done.1
  135.1 0.0 copy-start
  135.1 1.1 copy-done
  136.2 8.1 %shard_map.223 = (f32[1,1]{1,0:T(1,128)}, f32[64,256]{1,0:T(8,128)}, f32[172,128]{1,0:T(8,128)}, f32[64,256]{1,0:T(8,128)}, f32[172,128]{1,0:T(8,128)}, /*index=...) custom-call(f32[1248,128]{1,0:T(8,128)S(1)} %copy-done, ...), custom_call_target="tpu_custom_call" | custom-call | tf_op jit(solution)/shard_map/pallas_call | solution.py:786
Async XLA Ops:
  0.6 134.4 %copy-start.2 = (f32[64,256]{1,0:T(8,128)S(1)}, f32[64,256]{1,0:T(8,128)}, u32[]{:S(2)}) copy-start(f32[64,256]{1,0:T(8,128)} %w1own.1) | copy-start | bytes 196612
  0.7 134.4 %copy-start.5 = (f32[428]{0:T(512)S(1)}, f32[428]{0:T(512)}, u32[]{:S(2)}) copy-start(f32[428]{0:T(512)} %param.29) | copy-start | bytes 5140
  0.7 134.4 %copy-start.4 = (f32[428]{0:T(512)S(1)}, f32[428]{0:T(512)}, u32[]{:S(2)}) copy-start(f32[428]{0:T(512)} %param.28) | copy-start | bytes 5140
  0.7 134.4 %copy-start.3 = (f32[428]{0:T(512)S(1)}, f32[428]{0:T(512)}, u32[]{:S(2)}) copy-start(f32[428]{0:T(512)} %param.27) | copy-start | bytes 5140
  0.7 134.4 %copy-start.1 = (f32[128,172]{0,1:T(8,128)S(1)}, f32[128,172]{0,1:T(8,128)}, u32[]{:S(2)}) copy-start(f32[128,172]{0,1:T(8,128)} %param.24) | copy-start | bytes 264196
  135.1 1.1 copy-start

commit v24 on v23

--- a/solution.py
+++ b/solution.py
@@ -550,6 +550,25 @@
     for q in range(NAR):
         pay[ROW_2 + q * CLS_PAD:ROW_2 + (q + 1) * CLS_PAD, :] = g2t[:, q * 128:(q + 1) * 128]
 
+    def to_owners(first, last):
+        def one_owner(t, c):
+            @pl.when(t != g)
+            def _():
+                pltpu.make_async_remote_copy(
+                    src_ref=pay.at[pl.ds(pl.multiple_of(t * PIECE, 16), PIECE)], dst_ref=inbox.at[g],
+                    send_sem=rs_send, recv_sem=rs_recv, device_id=(t, y), device_id_type=MESH,
+                ).start()
+
+            return c
+
+        def turned(i, c):
+            return one_owner(first + (i + g) % (last - first), c)
+
+        lax.fori_loop(0, last - first, turned, 0)
+
+    early, late = -(-ROW_2 // PIECE), ROW_MISC // PIECE
+    to_owners(early, late)
+
     def add_grads(q, fresh=False):
         da = dot(dbuf[q], w2t[...], TN)
         r = rbuf[q].astype(F32)
@@ -612,19 +631,8 @@
     misc[9:10, 0:1] = loss - hi
     pay[ROW_MISC:ROWS, :] = misc[...].astype(BF)
 
-    def to_owner(i, c):
-        t = (g + i) % GRP
-
-        @pl.when(t < PIECES)
-        def _():
-            pltpu.make_async_remote_copy(
-                src_ref=pay.at[pl.ds(pl.multiple_of(t * PIECE, 16), PIECE)], dst_ref=inbox.at[g],
-                send_sem=rs_send, recv_sem=rs_recv, device_id=(t, y), device_id_type=MESH,
-            ).start()
-
-        return c
-
-    lax.fori_loop(1, GRP, to_owner, 0)
+    to_owners(0, early)
+    to_owners(late, PIECES)
     mine = pl.ds(pl.multiple_of(g * PIECE, 16), PIECE)
 
     @pl.when(g < PIECES)

time: 144 us -> 144 us (level)
  no operation moved by 1% of the time
where the time goes in v24:
time: 144 us
  Pallas kernels  142 us (99%)
    pallas_call x1, Pallas kernels, main(): pl.pallas_call(main_kernel, out_shape=sds((ROWS, 128), F32), in_specs=[vm...  134 us
    pallas_call x1, Pallas kernels, update(): pl.pallas_call(update_kernel, out_shape=[sds((1, 1), F32), sds((64, HID),...  8.06 us

profile of v24, /device:TPU:1, one launch (start us, length us, event | category | flops | bytes accessed | tf_op | source)
XLA Modules:
  0.0 143.5 jit_solution(18379755476622710822)
XLA Ops:
  0.6 0.0 copy-start.2
  0.7 0.0 copy-start.5
  0.7 0.0 copy-start.4
  0.7 0.0 copy-start.3
  0.7 0.0 copy-start.1
  0.7 133.6 %shard_map.222.res = f32[1248,128]{1,0:T(8,128)} custom-call(s32[64,128]{1,0:T(8,128)} %bitcast.28, bf16[8192,128]{1,0:T(8,128)(2,1)} %feat.1, s32[16,2048]{1,0:T(8,128)} %bitcast.25, s32[15,2048]{1,0:T(8,128)} %bitcast.26, s32[11,512]{1,0:T(8,128)} %bitcast.29, s32[10,512]{1,0:T(8,128)} %bitcast.30, s32[1,512]{1,0:T(1,128)} %bitcast.31, s32[1,512]{1,0:T(1,128)} %bitcast.32, ...), custom_call_target="tpu_custom_call" | custom-call | tf_op jit(solution)/shard_map/pallas_call | solution.py:700
  134.3 0.0 copy-done.2
  134.4 0.0 copy-done.5
  134.4 0.0 copy-done.4
  134.4 0.0 copy-done.3
  134.4 0.0 copy-done.1
  134.4 0.0 copy-start
  134.4 1.1 copy-done
  135.5 8.1 %shard_map.223 = (f32[1,1]{1,0:T(1,128)}, f32[64,256]{1,0:T(8,128)}, f32[172,128]{1,0:T(8,128)}, f32[64,256]{1,0:T(8,128)}, f32[172,128]{1,0:T(8,128)}, /*index=...) custom-call(f32[1248,128]{1,0:T(8,128)S(1)} %copy-done, ...), custom_call_target="tpu_custom_call" | custom-call | tf_op jit(solution)/shard_map/pallas_call | solution.py:794
Async XLA Ops:
  0.6 133.7 %copy-start.2 = (f32[64,256]{1,0:T(8,128)S(1)}, f32[64,256]{1,0:T(8,128)}, u32[]{:S(2)}) copy-start(f32[64,256]{1,0:T(8,128)} %w1own.1) | copy-start | bytes 196612
  0.7 133.7 %copy-start.5 = (f32[428]{0:T(512)S(1)}, f32[428]{0:T(512)}, u32[]{:S(2)}) copy-start(f32[428]{0:T(512)} %param.29) | copy-start | bytes 5140
  0.7 133.7 %copy-start.4 = (f32[428]{0:T(512)S(1)}, f32[428]{0:T(512)}, u32[]{:S(2)}) copy-start(f32[428]{0:T(512)} %param.28) | copy-start | bytes 5140
  0.7 133.7 %copy-start.3 = (f32[428]{0:T(512)S(1)}, f32[428]{0:T(512)}, u32[]{:S(2)}) copy-start(f32[428]{0:T(512)} %param.27) | copy-start | bytes 5140
  0.7 133.7 %copy-start.1 = (f32[128,172]{0,1:T(8,128)S(1)}, f32[128,172]{0,1:T(8,128)}, u32[]{:S(2)}) copy-start(f32[128,172]{0,1:T(8,128)} %param.24) | copy-start | bytes 264196
  134.4 1.1 copy-start

commit v25 on v24

--- a/solution.py
+++ b/solution.py
@@ -88,7 +88,7 @@
 def main_kernel(
     reqt, feat, idx1t, msk1t, idx2t, msk2t, labels, live, w1, w2own, m1, m2own, bias,
     o_all,
-    table, featb, pulled, stage, reqv, reqin, mid, idxv, idxp, invv, near, own, slope, gbuf, fsel, bsel, wants, idc, ssel, idm, invc, livec, rbuf, dbuf,
+    table, featb, pulled, stage, reqv, reqin, mid, idxv, idxp, invv, scale, near, own, slope, gbuf, fsel, bsel, wants, idc, ssel, idm, invc, livec, rbuf, dbuf,
     gw1, gw2t, momenta, gidx2, w2t, b2c, pay, misc, inbox, ybox,
     reqs, idx,
     feat_sem, loc_sem, ask_sem, req_send, mid_recv, req_recv, row_send, row_recv, nar_send, nar_recv,
@@ -365,6 +365,13 @@
     sum_ids(0)
     lax.fori_loop(0, 32, one_mark, 0)
     lax.fori_loop(0, 16, some_marks, 0)
+
+    def scales(i, c):
+        at = pl.multiple_of(i * 128, 128)
+        scale[pl.ds(at, 128), :] = spread(invv[0:1, pl.ds(at, 128)])
+        return c
+
+    lax.fori_loop(0, FRONT // 128, scales, 0)
 
     come = pulled.at[pl.ds(0, (DEV - 1) * CAP)]
     pltpu.make_async_copy(come, come, row_recv).wait()
@@ -432,10 +439,7 @@
 
     def finish(b):
         rows = cols(b)
-        scale = jnp.concatenate(
-            [spread(invv[0:1, pl.ds(pl.multiple_of(b * 256 + c * 128, 128), 128)]) for c in range(2)], axis=0
-        )
-        act = jnp.concatenate([own[...].astype(BF), (near[...] * scale).astype(BF)], axis=1)
+        act = jnp.concatenate([own[...].astype(BF), (near[...] * scale[rows, :]).astype(BF)], axis=1)
         a1 = act.T
         for h in range(2):
             a1t[pl.ds(pl.multiple_of((2 * b + h) * 256, 256), 256), :] = a1[:, h * 128:(h + 1) * 128]
@@ -460,9 +464,10 @@
     lax.fori_loop(1, 8, loaded, 0)
     forward(7)
 
-    def from_source(q, fresh=False):
+    def from_sources(qs, fresh=False):
         def rows512(i, c):
-            part = dot(fsel[q, pl.ds(pl.multiple_of(i * SEED, SEED), SEED), :], gbuf[q])
+            n = pl.multiple_of(i * SEED, SEED)
+            part = sum(dot(fsel[q, pl.ds(n, SEED), :], gbuf[q]) for q in qs)
             for h in range(2):
                 rows = pl.ds(pl.multiple_of(h * 2 * SEED + i * SEED, SEED), SEED)
                 now = part[:, h * 128:(h + 1) * 128]
@@ -471,19 +476,18 @@
 
         lax.fori_loop(0, 2, rows512, 0)
 
-    from_source(y, True)
+    from_sources([y], True)
     for b in range(1, 8, 2):
         blk = gbuf.at[left, b * 256:(b + 1) * 256, :]
         link(blk, blk, h_send.at[0, b], h_recv.at[0, b], right).wait_recv()
-    from_source(left)
     for b in range(0, 8, 2):
         blk = gbuf.at[right, b * 256:(b + 1) * 256, :]
         link(blk, blk, h_send.at[1, b], h_recv.at[1, b], left).wait_recv()
-    from_source(right)
+    from_sources([left, right])
     for b in range(8):
         blk = gbuf.at[opp, b * 256:(b + 1) * 256, :]
         link(blk, blk, h_send.at[2, b], h_recv.at[2, b], right).wait_recv()
-    from_source(opp)
+    from_sources([opp])
 
     def wide(a):
         return jnp.concatenate([a, a], axis=1)
@@ -569,15 +573,17 @@
     early, late = -(-ROW_2 // PIECE), ROW_MISC // PIECE
     to_owners(early, late)
 
-    def add_grads(q, fresh=False):
-        da = dot(dbuf[q], w2t[...], TN)
-        r = rbuf[q].astype(F32)
-        ds = (da[:, :HID] + r).astype(BF)
-        dn = ((da[:, HID:] - r) * wide(invc[q])).astype(BF)
-        both = jnp.concatenate([dn, ds], axis=0)
+    def add_grads(qs, fresh=False):
+        both = []
+        for q in qs:
+            da = dot(dbuf[q], w2t[...], TN)
+            r = rbuf[q].astype(F32)
+            near_part = ((da[:, HID:] - r) * wide(invc[q])).astype(BF)
+            both.append(jnp.concatenate([near_part, (da[:, :HID] + r).astype(BF)], axis=0))
 
         def rows512(i, c):
-            part = dot(bsel[q, pl.ds(pl.multiple_of(i * 512, 512), 512), :], both)
+            n = pl.multiple_of(i * 512, 512)
+            part = sum(dot(bsel[q, pl.ds(n, 512), :], d) for q, d in zip(qs, both))
             for h in range(2):
                 rows = pl.ds(pl.multiple_of(h * FRONT + i * 512, 512), 512)
                 now = part[:, h * 128:(h + 1) * 128]
@@ -589,13 +595,12 @@
     db2 = jnp.sum(dlog.astype(F32), axis=1, keepdims=True)
     db2 = jnp.broadcast_to(db2, (CLS_PAD, 128)).T[0:1, :]
     swap_forward(rbuf, r_send, r_recv, SEED // 2)
-    add_grads(y, True)
+    add_grads([y], True)
     swap_forward(dbuf, d_send, d_recv, 96)
-    add_grads(left)
-    add_grads(right)
+    add_grads([left, right])
     swap_end(rbuf, r_send, r_recv, SEED // 2)
     swap_end(dbuf, d_send, d_recv, 96)
-    add_grads(opp)
+    add_grads([opp])
 
     def to_z(b, db):
         rows = pl.ds(pl.multiple_of(b * 256, 256), 256)
@@ -713,6 +718,7 @@
             V((16, FRONT), jnp.int32),
             V((256, 128), jnp.int32),
             V((1, FRONT), F32),
+            V((FRONT, 128), F32),
             V((256, D_IN), F32),
             V((256, D_IN), F32),
             V((FRONT, HID), F32),

time: 144 us -> 143 us (level)
  no operation moved by 1% of the time
where the time goes in v25:
time: 143 us; the launch traced here: 142 us
  Pallas kernels  141 us (99%)
    pallas_call x1, Pallas kernels, main(): pl.pallas_call(main_kernel, out_shape=sds((ROWS, 128), F32), in_specs=[vm...  132 us
    pallas_call x1, Pallas kernels, update(): pl.pallas_call(update_kernel, out_shape=[sds((1, 1), F32), sds((64, HID),...  8.06 us

profile of v25, /device:TPU:1, one launch (start us, length us, event | category | flops | bytes accessed | tf_op | source)
XLA Modules:
  0.0 142.4 jit_solution(10828479263475790638)
XLA Ops:
  0.6 0.0 copy-start.2
  0.7 0.0 copy-start.5
  0.7 0.0 copy-start.4
  0.7 0.0 copy-start.3
  0.7 0.0 copy-start.1
  0.7 132.5 %shard_map.222.res = f32[1248,128]{1,0:T(8,128)} custom-call(s32[64,128]{1,0:T(8,128)} %bitcast.28, bf16[8192,128]{1,0:T(8,128)(2,1)} %feat.1, s32[16,2048]{1,0:T(8,128)} %bitcast.25, s32[15,2048]{1,0:T(8,128)} %bitcast.26, s32[11,512]{1,0:T(8,128)} %bitcast.29, s32[10,512]{1,0:T(8,128)} %bitcast.30, s32[1,512]{1,0:T(1,128)} %bitcast.31, s32[1,512]{1,0:T(1,128)} %bitcast.32, ...), custom_call_target="tpu_custom_call" | custom-call | tf_op jit(solution)/shard_map/pallas_call | solution.py:705
  133.2 0.0 copy-done.2
  133.2 0.0 copy-done.5
  133.2 0.0 copy-done.4
  133.2 0.0 copy-done.3
  133.2 0.0 copy-done.1
  133.2 0.0 copy-start
  133.3 1.1 copy-done
  134.3 8.1 %shard_map.223 = (f32[1,1]{1,0:T(1,128)}, f32[64,256]{1,0:T(8,128)}, f32[172,128]{1,0:T(8,128)}, f32[64,256]{1,0:T(8,128)}, f32[172,128]{1,0:T(8,128)}, /*index=...) custom-call(f32[1248,128]{1,0:T(8,128)S(1)} %copy-done, ...), custom_call_target="tpu_custom_call" | custom-call | tf_op jit(solution)/shard_map/pallas_call | solution.py:800
Async XLA Ops:
  0.6 132.5 %copy-start.2 = (f32[64,256]{1,0:T(8,128)S(1)}, f32[64,256]{1,0:T(8,128)}, u32[]{:S(2)}) copy-start(f32[64,256]{1,0:T(8,128)} %w1own.1) | copy-start | bytes 196612
  0.7 132.5 %copy-start.5 = (f32[428]{0:T(512)S(1)}, f32[428]{0:T(512)}, u32[]{:S(2)}) copy-start(f32[428]{0:T(512)} %param.29) | copy-start | bytes 5140
  0.7 132.5 %copy-start.4 = (f32[428]{0:T(512)S(1)}, f32[428]{0:T(512)}, u32[]{:S(2)}) copy-start(f32[428]{0:T(512)} %param.28) | copy-start | bytes 5140
  0.7 132.5 %copy-start.3 = (f32[428]{0:T(512)S(1)}, f32[428]{0:T(512)}, u32[]{:S(2)}) copy-start(f32[428]{0:T(512)} %param.27) | copy-start | bytes 5140
  0.7 132.5 %copy-start.1 = (f32[128,172]{0,1:T(8,128)S(1)}, f32[128,172]{0,1:T(8,128)}, u32[]{:S(2)}) copy-start(f32[128,172]{0,1:T(8,128)} %param.24) | copy-start | bytes 264196
  133.2 1.1 copy-start
